TPU v7x, 32 devices: a whole 2x2x4 slice. The times are simulated.
32 devices in a mesh: seg: 8 (over z, x), rep: 4 (over y, core).
Axes of the slice: x: 2, y: 2, z: 4, core: 2. Of those that a mesh axis runs over, the one named last changes fastest.
Arguments:
- tokens: bfloat16 [2, 4, 64, 128, 768], P(None, 'rep', 'seg'), may hold values from -6 to 6
- cotangent: bfloat16 [2, 4, 64, 128, 768], P(None, 'rep', 'seg'), may hold values from -6 to 6
- doc_counts: int32 [2, 4, 3], P(None, 'rep'), may hold values from 1 to 57, 64 in all within a row
- w_qkv: bfloat16 [768, 2304], P('seg'), may hold values from -0.21875 to 0.21875
- w_out: bfloat16 [768, 768], P('seg'), may hold values from -0.625 to 0.625
- w_up: bfloat16 [768, 3072], P('seg'), may hold values from -0.21875 to 0.21875
- w_down: bfloat16 [3072, 768], P('seg'), may hold values from -0.109375 to 0.109375
- c_qkv: bfloat16 [768, 2304], P('seg'), may hold values from -0.21875 to 0.21875
- c_out: bfloat16 [768, 768], P('seg'), may hold values from -0.625 to 0.625
- pos_table: bfloat16 [64, 768], P('seg'), may hold values from -6 to 6
- norm_gains: bfloat16 [3, 768], P(None, 'seg'), may hold values from 0.5 to 1.5
- norm_shifts: bfloat16 [3, 768], P(None, 'seg'), may hold values from -1.5 to 1.5
Outputs:
- layer_out: bfloat16 [2, 4, 64, 128, 768], P(None, 'rep', 'seg')
- input_grad: float32 [2, 4, 64, 128, 768], P(None, 'rep', 'seg')
- grad_w_qkv: float32 [768, 2304], P('seg')
- grad_w_out: float32 [768, 768], P('seg')
- grad_w_up: float32 [768, 3072], P('seg')
- grad_w_down: float32 [3072, 768], P('seg')
- grad_c_qkv: float32 [768, 2304], P('seg')
- grad_c_out: float32 [768, 768], P('seg')
- grad_pos_table: float32 [64, 768], P('seg')
- grad_norm_gains: float32 [3, 768], P(None, 'seg')
- grad_norm_shifts: float32 [3, 768], P(None, 'seg')
Inputs may be any that keep to these rules, and one draw needn't show every extreme that they name: `doc_counts`: for each micro-batch and group the 3 counts sum to 64, and one of them is exactly 57.
All inputs are finite; a program needn't handle non-finite values.
Results may differ from a plain program's by a relative error of at most 0.03.
Values may be sent and summed in bfloat16 or wider, within the bound.
No kernel may reach another device: no remote copies, remote signals or barrier semaphores. Data moves between devices by JAX's collectives and lax.ppermute only.
A program may use at most 320 MiB of HBM per device.

v0:
```python
from functools import partial

import jax
import jax.numpy as jnp
from jax import lax
from jax.sharding import PartitionSpec as P

HEAD_DIM = 64


EPSILON = 1e-05
NEGATIVE = -1e30
HIGHEST = lax.Precision.HIGHEST


def for_sending(shard):
    return jax.tree.map(lambda a: a.astype(jnp.bfloat16) if a.dtype == jnp.float32 else a, shard)


def layer_norm(values, gain, shift):
    center = values - jnp.mean(values, axis=-1, keepdims=True)
    spread = jnp.mean(center * center, axis=-1, keepdims=True)
    return center * lax.rsqrt(spread + EPSILON) * gain + shift


def inner_rows(left, right):
    return lax.dot_general(
        left, right, (((0,), (0,)), ((), ())), preferred_element_type=jnp.float32
    )


def outer_cols(left, right):
    return lax.dot_general(
        left, right, (((1,), (1,)), ((), ())), preferred_element_type=jnp.float32
    )


def soft_rows(scores):
    peak = jnp.max(scores, axis=-1, keepdims=True)
    raised = jnp.exp(scores - peak)
    summed = jnp.sum(raised, axis=-1, keepdims=True)
    return (raised / summed, peak + jnp.log(summed))


def doc_layout(counts, seg_total):
    doc_ends = jnp.cumsum(counts)
    doc_starts = doc_ends - counts
    seg_index = jnp.arange(seg_total, dtype=jnp.int32)
    doc_ids = jnp.sum((seg_index[:, None] >= doc_ends[None, :]).astype(jnp.int32), axis=1)
    owned = doc_ids[:, None] == jnp.arange(counts.shape[0], dtype=jnp.int32)[None, :]
    positions = seg_index - jnp.sum(jnp.where(owned, doc_starts[None, :], 0), axis=1)
    return (doc_ids, positions)


def forward_pass(token_block, full, doc_ids, positions, seg_first):
    w_qkv, w_out, w_up, w_down, c_qkv, c_out, pos_table, norm_gains, norm_shifts = full
    gains = norm_gains.astype(jnp.float32)
    shifts = norm_shifts.astype(jnp.float32)
    seg_local, seg_length, model_width = token_block.shape
    head_count = model_width // HEAD_DIM
    score_scale = HEAD_DIM ** (-0.5)
    row_count = seg_local * seg_length
    flat_rows = token_block.reshape(row_count, model_width)
    projected = jnp.dot(flat_rows, w_qkv, preferred_element_type=jnp.float32).astype(jnp.bfloat16)
    split_rows = projected.reshape(seg_local, seg_length, 3, head_count, HEAD_DIM)
    scores = (
        jnp.einsum(
            "bqhd,bkhd->bhqk",
            split_rows[:, :, 0],
            split_rows[:, :, 1],
            preferred_element_type=jnp.float32,
        )
        * score_scale
    )
    soft_probs, log_total = soft_rows(scores)
    mixed_rows = jnp.einsum(
        "bhqk,bkhd->bqhd",
        soft_probs.astype(jnp.bfloat16),
        split_rows[:, :, 2],
        preferred_element_type=jnp.float32,
    )
    mixed_rows = mixed_rows.reshape(row_count, model_width).astype(jnp.bfloat16)
    attended = jnp.dot(mixed_rows, w_out, preferred_element_type=jnp.float32)
    pre_first = flat_rows.astype(jnp.float32) + attended
    first_norm = layer_norm(pre_first, gains[0], shifts[0])
    first_low = first_norm.astype(jnp.bfloat16)
    hidden_pre = jnp.dot(first_low, w_up, preferred_element_type=jnp.float32)
    activated = jax.nn.gelu(hidden_pre, approximate=False).astype(jnp.bfloat16)
    branch_out = jnp.dot(activated, w_down, preferred_element_type=jnp.float32)
    pre_second = first_norm + branch_out
    second_norm = layer_norm(pre_second, gains[1], shifts[1]).reshape(
        seg_local, seg_length, model_width
    )
    local_docs = lax.dynamic_slice_in_dim(doc_ids, seg_first, seg_local)
    local_pos = lax.dynamic_slice_in_dim(positions, seg_first, seg_local)
    pick_table = (
        local_pos[:, None] == jnp.arange(pos_table.shape[0], dtype=jnp.int32)[None, :]
    ).astype(jnp.bfloat16)
    embedded = second_norm[:, 0, :] + jnp.dot(
        pick_table, pos_table, preferred_element_type=jnp.float32
    )
    embed_low = embedded.astype(jnp.bfloat16)
    cross_proj = jnp.dot(embed_low, c_qkv, preferred_element_type=jnp.float32).astype(jnp.bfloat16)
    key_value = cross_proj[:, model_width:]
    all_kv = lax.all_gather(key_value, "seg", axis=0, tiled=True)
    seg_total = all_kv.shape[0]
    all_split = all_kv.reshape(seg_total, 2, head_count, HEAD_DIM)
    cross_query = cross_proj[:, :model_width].reshape(seg_local, head_count, HEAD_DIM)
    same_doc = local_docs[:, None] == doc_ids[None, :]
    cross_scores = (
        jnp.einsum("qhd,khd->hqk", cross_query, all_split[:, 0], preferred_element_type=jnp.float32)
        * score_scale
    )
    cross_scores = jnp.where(same_doc[None], cross_scores, NEGATIVE)
    cross_probs, cross_log = soft_rows(cross_scores)
    cross_mixed = jnp.einsum(
        "hqk,khd->qhd",
        cross_probs.astype(jnp.bfloat16),
        all_split[:, 1],
        preferred_element_type=jnp.float32,
    )
    cross_mixed = cross_mixed.reshape(seg_local, model_width).astype(jnp.bfloat16)
    cross_att = jnp.dot(cross_mixed, c_out, preferred_element_type=jnp.float32)
    pre_third = embedded + cross_att
    cls_new = layer_norm(pre_third, gains[2], shifts[2])
    layer_rows = second_norm.at[:, 0, :].set(cls_new).astype(jnp.bfloat16)
    saved = {
        "flat_rows": flat_rows,
        "split_rows": split_rows,
        "log_total": log_total,
        "mixed_rows": mixed_rows,
        "pre_first": pre_first,
        "first_low": first_low,
        "hidden_pre": hidden_pre,
        "activated": activated,
        "pre_second": pre_second,
        "pick_table": pick_table,
        "embed_low": embed_low,
        "all_split": all_split,
        "cross_query": cross_query,
        "same_doc": same_doc,
        "cross_log": cross_log,
        "cross_mixed": cross_mixed,
        "pre_third": pre_third,
    }
    return (saved, layer_rows)


def backward_pass(saved, full, grad_rows):
    w_qkv, w_out, w_up, w_down, c_qkv, c_out, pos_table, norm_gains, norm_shifts = full
    gains = norm_gains.astype(jnp.float32)
    shifts = norm_shifts.astype(jnp.float32)
    seg_local, seg_length, model_width = grad_rows.shape
    head_count = model_width // HEAD_DIM
    score_scale = HEAD_DIM ** (-0.5)
    row_count = seg_local * seg_length
    unused, third_pull = jax.vjp(layer_norm, saved["pre_third"], gains[2], shifts[2])
    grad_pre_third, grad_gain_third, grad_shift_third = third_pull(grad_rows[:, 0, :])
    grad_cross_att = grad_pre_third.astype(jnp.bfloat16)
    grad_c_out = inner_rows(saved["cross_mixed"], grad_cross_att)
    grad_cross_mixed = (
        outer_cols(grad_cross_att, c_out)
        .astype(jnp.bfloat16)
        .reshape(seg_local, head_count, HEAD_DIM)
    )
    all_split = saved["all_split"]
    cross_query = saved["cross_query"]
    cross_scores = (
        jnp.einsum("qhd,khd->hqk", cross_query, all_split[:, 0], preferred_element_type=jnp.float32)
        * score_scale
    )
    cross_scores = jnp.where(saved["same_doc"][None], cross_scores, NEGATIVE)
    cross_probs = jnp.exp(cross_scores - saved["cross_log"])
    grad_cross_probs = jnp.einsum(
        "qhd,khd->hqk", grad_cross_mixed, all_split[:, 1], preferred_element_type=jnp.float32
    )
    grad_cross_scores = cross_probs * (
        grad_cross_probs - jnp.sum(grad_cross_probs * cross_probs, axis=-1, keepdims=True)
    )
    grad_cross_low = grad_cross_scores.astype(jnp.bfloat16)
    cross_probs_low = cross_probs.astype(jnp.bfloat16)
    grad_cross_query = (
        jnp.einsum(
            "hqk,khd->qhd", grad_cross_low, all_split[:, 0], preferred_element_type=jnp.float32
        )
        * score_scale
    )
    rows = lax.axis_size("seg") * seg_local
    grad_keys = (
        jnp.einsum("hqk,qhd->khd", grad_cross_low, cross_query, preferred_element_type=jnp.float32)
        * score_scale
    )
    grad_values = jnp.einsum(
        "hqk,qhd->khd", cross_probs_low, grad_cross_mixed, preferred_element_type=jnp.float32
    )
    grad_kv = lax.psum_scatter(
        jnp.concatenate(
            [grad_keys.reshape(rows, model_width), grad_values.reshape(rows, model_width)], axis=1
        ).astype(jnp.bfloat16),
        "seg",
        scatter_dimension=0,
        tiled=True,
    ).astype(jnp.float32)
    grad_cross_proj = jnp.concatenate(
        [grad_cross_query.reshape(seg_local, model_width), grad_kv], axis=1
    ).astype(jnp.bfloat16)
    grad_c_qkv = inner_rows(saved["embed_low"], grad_cross_proj)
    grad_embed = grad_pre_third + outer_cols(grad_cross_proj, c_qkv)
    grad_pos = lax.dot_general(
        saved["pick_table"].astype(jnp.float32),
        grad_embed,
        (((0,), (0,)), ((), ())),
        precision=HIGHEST,
    )
    grad_second = grad_rows.at[:, 0, :].set(grad_embed).reshape(row_count, model_width)
    unused, second_pull = jax.vjp(layer_norm, saved["pre_second"], gains[1], shifts[1])
    grad_pre_second, grad_gain_second, grad_shift_second = second_pull(grad_second)
    grad_branch = grad_pre_second.astype(jnp.bfloat16)
    grad_w_down = inner_rows(saved["activated"], grad_branch)
    grad_active = outer_cols(grad_branch, w_down)
    unused, gelu_pull = jax.vjp(partial(jax.nn.gelu, approximate=False), saved["hidden_pre"])
    grad_hidden = gelu_pull(grad_active)[0].astype(jnp.bfloat16)
    grad_w_up = inner_rows(saved["first_low"], grad_hidden)
    grad_first = grad_pre_second + outer_cols(grad_hidden, w_up)
    unused, first_pull = jax.vjp(layer_norm, saved["pre_first"], gains[0], shifts[0])
    grad_pre_first, grad_gain_first, grad_shift_first = first_pull(grad_first)
    grad_attended = grad_pre_first.astype(jnp.bfloat16)
    grad_w_out = inner_rows(saved["mixed_rows"], grad_attended)
    grad_mixed = (
        outer_cols(grad_attended, w_out)
        .astype(jnp.bfloat16)
        .reshape(seg_local, seg_length, head_count, HEAD_DIM)
    )
    split_rows = saved["split_rows"]
    queries = split_rows[:, :, 0]
    keys_all = split_rows[:, :, 1]
    values_all = split_rows[:, :, 2]
    scores = (
        jnp.einsum("bqhd,bkhd->bhqk", queries, keys_all, preferred_element_type=jnp.float32)
        * score_scale
    )
    soft_probs = jnp.exp(scores - saved["log_total"])
    grad_probs = jnp.einsum(
        "bqhd,bkhd->bhqk", grad_mixed, values_all, preferred_element_type=jnp.float32
    )
    grad_values = jnp.einsum(
        "bhqk,bqhd->bkhd",
        soft_probs.astype(jnp.bfloat16),
        grad_mixed,
        preferred_element_type=jnp.float32,
    )
    grad_scores = (
        soft_probs * (grad_probs - jnp.sum(grad_probs * soft_probs, axis=-1, keepdims=True))
    ).astype(jnp.bfloat16)
    grad_queries = (
        jnp.einsum("bhqk,bkhd->bqhd", grad_scores, keys_all, preferred_element_type=jnp.float32)
        * score_scale
    )
    grad_keys = (
        jnp.einsum("bhqk,bqhd->bkhd", grad_scores, queries, preferred_element_type=jnp.float32)
        * score_scale
    )
    grad_proj = (
        jnp.stack([grad_queries, grad_keys, grad_values], axis=2)
        .reshape(row_count, 3 * model_width)
        .astype(jnp.bfloat16)
    )
    grad_w_qkv = inner_rows(saved["flat_rows"], grad_proj)
    input_rows = (grad_pre_first + outer_cols(grad_proj, w_qkv)).reshape(
        seg_local, seg_length, model_width
    )
    grad_gains = jnp.stack([grad_gain_first, grad_gain_second, grad_gain_third], axis=0)
    grad_shifts = jnp.stack([grad_shift_first, grad_shift_second, grad_shift_third], axis=0)
    grad_full = (
        grad_w_qkv,
        grad_w_out,
        grad_w_up,
        grad_w_down,
        grad_c_qkv,
        grad_c_out,
        grad_pos,
        grad_gains,
        grad_shifts,
    )
    return (input_rows, grad_full)


def body(
    tokens,
    cotangent,
    doc_counts,
    w_qkv,
    w_out,
    w_up,
    w_down,
    c_qkv,
    c_out,
    pos_table,
    norm_gains,
    norm_shifts,
):
    shards = (w_qkv, w_out, w_up, w_down, c_qkv, c_out, pos_table, norm_gains, norm_shifts)
    micro_count = tokens.shape[0]
    seg_local = tokens.shape[2]
    seg_total = seg_local * lax.axis_size("seg")
    seg_first = lax.axis_index("seg") * seg_local
    grad_totals = None
    layer_list = []
    input_list = []
    for micro in range(micro_count):
        full_fwd = (
            lax.all_gather(shards[0], "seg", axis=0, tiled=True),
            lax.all_gather(shards[1], "seg", axis=0, tiled=True),
            lax.all_gather(shards[2], "seg", axis=0, tiled=True),
            lax.all_gather(shards[3], "seg", axis=0, tiled=True),
            lax.all_gather(shards[4], "seg", axis=0, tiled=True),
            lax.all_gather(shards[5], "seg", axis=0, tiled=True),
            lax.all_gather(shards[6], "seg", axis=0, tiled=True),
            lax.all_gather(shards[7], "seg", axis=1, tiled=True),
            lax.all_gather(shards[8], "seg", axis=1, tiled=True),
        )
        doc_ids, positions = doc_layout(doc_counts[micro, 0], seg_total)
        saved, layer_rows = forward_pass(tokens[micro, 0], full_fwd, doc_ids, positions, seg_first)
        full_back = (
            lax.all_gather(shards[0], "seg", axis=0, tiled=True),
            lax.all_gather(shards[1], "seg", axis=0, tiled=True),
            lax.all_gather(shards[2], "seg", axis=0, tiled=True),
            lax.all_gather(shards[3], "seg", axis=0, tiled=True),
            lax.all_gather(shards[4], "seg", axis=0, tiled=True),
            lax.all_gather(shards[5], "seg", axis=0, tiled=True),
            lax.all_gather(shards[6], "seg", axis=0, tiled=True),
            lax.all_gather(shards[7], "seg", axis=1, tiled=True),
            lax.all_gather(shards[8], "seg", axis=1, tiled=True),
        )
        input_rows, grad_full = backward_pass(
            saved, full_back, cotangent[micro, 0].astype(jnp.float32)
        )
        grad_part = (
            lax.psum_scatter(
                grad_full[0].astype(jnp.bfloat16), "seg", scatter_dimension=0, tiled=True
            ).astype(jnp.float32),
            lax.psum_scatter(
                grad_full[1].astype(jnp.bfloat16), "seg", scatter_dimension=0, tiled=True
            ).astype(jnp.float32),
            lax.psum_scatter(
                grad_full[2].astype(jnp.bfloat16), "seg", scatter_dimension=0, tiled=True
            ).astype(jnp.float32),
            lax.psum_scatter(
                grad_full[3].astype(jnp.bfloat16), "seg", scatter_dimension=0, tiled=True
            ).astype(jnp.float32),
            lax.psum_scatter(
                grad_full[4].astype(jnp.bfloat16), "seg", scatter_dimension=0, tiled=True
            ).astype(jnp.float32),
            lax.psum_scatter(
                grad_full[5].astype(jnp.bfloat16), "seg", scatter_dimension=0, tiled=True
            ).astype(jnp.float32),
            lax.psum_scatter(
                grad_full[6].astype(jnp.bfloat16), "seg", scatter_dimension=0, tiled=True
            ).astype(jnp.float32),
            lax.psum_scatter(
                grad_full[7].astype(jnp.bfloat16), "seg", scatter_dimension=1, tiled=True
            ).astype(jnp.float32),
            lax.psum_scatter(
                grad_full[8].astype(jnp.bfloat16), "seg", scatter_dimension=1, tiled=True
            ).astype(jnp.float32),
        )
        if grad_totals is None:
            grad_totals = tuple(grad_part)
        else:
            grad_totals = tuple((left + right for left, right in zip(grad_totals, grad_part)))
        layer_list.append(layer_rows)
        input_list.append(input_rows)
    grad_totals = jax.tree.map(
        lambda part: part.astype(jnp.float32), lax.psum(for_sending(grad_totals), "rep")
    )
    layer_out = jnp.stack(layer_list, axis=0)[:, None]
    input_grad = jnp.stack(input_list, axis=0)[:, None]
    return (
        layer_out,
        input_grad,
        grad_totals[0],
        grad_totals[1],
        grad_totals[2],
        grad_totals[3],
        grad_totals[4],
        grad_totals[5],
        grad_totals[6],
        grad_totals[7],
        grad_totals[8],
    )


def solution(mesh):
    placed = (
        P(None, "rep", "seg", None, None),
        P(None, "rep", "seg", None, None),
        P(None, "rep", None),
        P("seg", None),
        P("seg", None),
        P("seg", None),
        P("seg", None),
        P("seg", None),
        P("seg", None),
        P("seg", None),
        P(None, "seg"),
        P(None, "seg"),
    )
    return jax.shard_map(
        body,
        mesh=mesh,
        in_specs=placed,
        out_specs=(
            P(None, "rep", "seg", None, None),
            P(None, "rep", "seg", None, None),
            P("seg", None),
            P("seg", None),
            P("seg", None),
            P("seg", None),
            P("seg", None),
            P("seg", None),
            P("seg", None),
            P(None, "seg"),
            P(None, "seg"),
        ),
        check_vma=False,
    )
```

profile of v0, /device:TPU:0, one launch (start us, length us, event | category | flops | bytes accessed | tf_op | source)
XLA Modules:
  0.0 2038.5 jit_solution(15620252068364495566)
XLA Ops:
  15.8 22.5 %all-gather = bf16[8,96,3]{1,2,0:T(4,128)(2,1)S(1)} all-gather(bf16[1,96,3]{1,2,0:T(4,128)(2,1)} %bitcast.404), channel_id=1, replica_groups=mesh['seg'=8,'rep'=4] {'seg'}, dimensions={0}, use_global_device_ids=true | all-gather | bytes 5184 | tf_op jit(solution)/shard_map/all_gather | solution.py:319
  39.0 16.8 all-gather.1
  56.5 33.0 %all_gather.28 = bf16[64,768]{1,0:T(8,128)(2,1)} all-gather(bf16[8,768]{1,0:T(8,128)(2,1)} %param.29), channel_id=1, replica_groups=mesh['seg'=8,'rep'=4] {'seg'}, dimensions={0}, use_global_device_ids=true | all-gather | bytes 110592 | tf_op jit(solution)/shard_map/all_gather | solution.py:318
  89.5 3.4 fusion.157
  93.2 4.4 fusion.66
  97.6 7.4 convolution_convert_fusion
  105.0 6.6 copy.241
  111.6 3.6 copy.322
  119.4 5.4 convolution_convert_fusion.1
  124.8 6.8 copy.227
  131.6 3.6 copy.320
  143.8 3.9 fusion.160
  159.7 42.4 %all-gather.13.cloned.1.call-done = bf16[768,3072]{1,0:T(8,128)(2,1)} async-done(((bf16[96,3072]{1,0:T(8,128)(2,1)}), bf16[768,3072]{1,0:T(8,128)(2,1)}) %all-gather.13.cloned.1.call-update) | async-done | bytes 4718608 | tf_op jit(solution)/shard_map/all_gather | solution.py:314
  202.1 35.3 %multiply_convert_fusion = (bf16[1024,3072]{1,0:T(8,128)(2,1)}, f32[1024,3072]{1,0:T(8,128)}, f32[1024,3072]{1,0:T(8,128)}) fusion(bf16[768,3072]{1,0:T(8,128)(2,1)} %all-gather.13.cloned.1.call-done, f32[1024,768]{1,0:T(8,128)S(1)} %get-tuple-element.209, f32[1024]{0:T(1024)S(1)} %fusion.128, f32[1024]{0:T(1024)S(1)} %broadcast_multiply_fusion.1, ...), kind=kOutput, calls=%fused_computation.6 | convolution fusion | flops 5040242688 | bytes 39335936 | tf_op jit(solution)/shard_map/dot_general | solution.py:87
  237.4 44.8 %all-gather.15.cloned.1.call-done = bf16[3072,768]{1,0:T(8,128)(2,1)} async-done(((bf16[384,768]{1,0:T(8,128)(2,1)}), bf16[3072,768]{1,0:T(8,128)(2,1)}) %all-gather.15.cloned.1.call-update) | async-done | bytes 4718608 | tf_op jit(solution)/shard_map/all_gather | solution.py:315
  282.2 8.9 fusion.163
  291.2 34.8 %multiply_convert_fusion.1 = (bf16[1024,3072]{1,0:T(8,128)(2,1)S(1)}, f32[1024,3072]{1,0:T(8,128)}, f32[1024,3072]{1,0:T(8,128)}) fusion(bf16[768,3072]{1,0:T(8,128)(2,1)S(1)} %copy-done.145, f32[1024,768]{1,0:T(8,128)S(1)} %copy-done.24, f32[768]{0:T(1024)S(1)} %get-tuple-element.133, f32[768]{0:T(1024)S(1)} %get-tuple-element.130, f32[1024]{0:T(1024)S(1)} %fusion.126, ...), kind=kOutput, calls=%fused_computation.19 | convolution fusion | flops 5040242688 | bytes 39335936 | tf_op jit(solution)/shard_map/dot_general | solution.py:87
  326.0 5.4 fusion.161
  337.9 9.7 all-gather.17.cloned.1.call-done
  357.5 33.2 %all_gather.30 = bf16[64,1536]{1,0:T(8,128)(2,1)} all-gather(bf16[8,1536]{1,0:T(8,128)(2,1)} %slice.232), channel_id=1, replica_groups=mesh['seg'=8,'rep'=4] {'seg'}, dimensions={0}, use_global_device_ids=true | all-gather | bytes 221184 | tf_op jit(solution)/shard_map/all_gather | solution.py:105
  398.0 33.1 %all_gather.32 = bf16[64,1536]{1,0:T(8,128)(2,1)} all-gather(bf16[8,1536]{1,0:T(8,128)(2,1)} %slice.242), channel_id=1, replica_groups=mesh['seg'=8,'rep'=4] {'seg'}, dimensions={0}, use_global_device_ids=true | all-gather | bytes 221184 | tf_op jit(solution)/shard_map/all_gather | solution.py:105
  492.6 39.6 %reduce-scatter.61.cloned.1.call-done = bf16[8,1536]{1,0:T(8,128)(2,1)} async-done(((bf16[64,1536]{1,0:T(8,128)(2,1)}), bf16[8,1536]{1,0:T(8,128)(2,1)}) %reduce-scatter.61.cloned.1.call-update) | async-done | bytes 24592 | tf_op jit(solution)/shard_map/reduce_scatter | solution.py:196
  536.6 4.6 copy.259
  541.2 54.9 %reduce-scatter.63.cloned.1.call-done = bf16[8,1536]{1,0:T(8,128)(2,1)} async-done(((bf16[64,1536]{1,0:T(8,128)(2,1)}), bf16[8,1536]{1,0:T(8,128)(2,1)}) %reduce-scatter.63.cloned.1.call-update) | async-done | bytes 24592 | tf_op jit(solution)/shard_map/reduce_scatter | solution.py:196
  607.9 4.1 fusion.147
  612.1 17.9 add_convert_fusion
  629.9 9.7 add_add_fusion.5
  639.7 18.2 add_convert_fusion.1
  658.0 12.8 multiply_reduce_fusion.5
  670.9 3.5 fusion.146
  678.9 3.9 convolution_convert_fusion.12
  687.8 4.5 fusion.71
  692.9 5.5 multiply_reduce_fusion
  707.2 9.3 copy.280
  718.6 4.1 fusion.23
  722.7 3.9 copy.296
  728.6 3.9 convolution_convert_fusion.13
  734.9 4.7 multiply_reduce_fusion.1
  749.4 9.3 copy.266
  760.8 4.1 fusion.20
  764.9 4.1 copy.294
  775.8 9.9 convolution_convert_fusion.4
  787.5 9.8 convolution_convert_fusion.5
  799.2 10.2 convolution_convert_fusion.3
  811.4 10.2 convolution_convert_fusion.2
  838.6 8.5 add_add_fusion.4
  848.8 14.1 reduce-scatter.39.cloned.1.call-done
  864.6 80.1 %reduce-scatter.67.cloned.1.call-done = bf16[96,2304]{1,0:T(8,128)(2,1)} async-done(((bf16[768,2304]{1,0:T(8,128)(2,1)}), bf16[96,2304]{1,0:T(8,128)(2,1)}) %reduce-scatter.67.cloned.1.call-update) | async-done | bytes 442384
  946.7 80.1 %reduce-scatter.65.cloned.1.call-done = bf16[96,2304]{1,0:T(8,128)(2,1)} async-done(((bf16[768,2304]{1,0:T(8,128)(2,1)}), bf16[96,2304]{1,0:T(8,128)(2,1)}) %reduce-scatter.65.cloned.1.call-update) | async-done | bytes 442384
  1031.2 77.8 %reduce-scatter.51.cloned.1.call-done = bf16[96,2304]{1,0:T(8,128)(2,1)} async-done(((bf16[768,2304]{1,0:T(8,128)(2,1)}), bf16[96,2304]{1,0:T(8,128)(2,1)}) %reduce-scatter.51.cloned.1.call-update) | async-done | bytes 442384 | tf_op jit(solution)/shard_map/reduce_scatter | solution.py:351
  1109.0 82.2 %reduce-scatter.49.cloned.1.call-done = bf16[96,2304]{1,0:T(8,128)(2,1)} async-done(((bf16[768,2304]{1,0:T(8,128)(2,1)}), bf16[96,2304]{1,0:T(8,128)(2,1)}) %reduce-scatter.49.cloned.1.call-update) | async-done | bytes 442384 | tf_op jit(solution)/shard_map/reduce_scatter | solution.py:351
  1193.2 96.3 %reduce-scatter.43.cloned.1.call-done = bf16[96,3072]{1,0:T(8,128)(2,1)} async-done(((bf16[768,3072]{1,0:T(8,128)(2,1)}), bf16[96,3072]{1,0:T(8,128)(2,1)}) %reduce-scatter.43.cloned.1.call-update) | async-done | bytes 589840 | tf_op jit(solution)/shard_map/reduce_scatter | solution.py:345
  1289.4 98.5 %reduce-scatter.41.cloned.1.call-done = bf16[96,3072]{1,0:T(8,128)(2,1)} async-done(((bf16[768,3072]{1,0:T(8,128)(2,1)}), bf16[96,3072]{1,0:T(8,128)(2,1)}) %reduce-scatter.41.cloned.1.call-update) | async-done | bytes 589840 | tf_op jit(solution)/shard_map/reduce_scatter | solution.py:345
  1390.1 96.5 %reduce-scatter.45.cloned.1.call-done = bf16[384,768]{1,0:T(8,128)(2,1)} async-done(((bf16[3072,768]{1,0:T(8,128)(2,1)}), bf16[384,768]{1,0:T(8,128)(2,1)}) %reduce-scatter.45.cloned.1.call-update) | async-done | bytes 589840 | tf_op jit(solution)/shard_map/reduce_scatter | solution.py:348
  1486.6 98.5 %reduce-scatter.47.cloned.1.call-done = bf16[384,768]{1,0:T(8,128)(2,1)} async-done(((bf16[3072,768]{1,0:T(8,128)(2,1)}), bf16[384,768]{1,0:T(8,128)(2,1)}) %reduce-scatter.47.cloned.1.call-update) | async-done | bytes 589840 | tf_op jit(solution)/shard_map/reduce_scatter | solution.py:348
  1587.3 8.5 add_add_fusion.6
  1599.1 50.8 %reduce-scatter.71.cloned.1.call-done = bf16[96,3]{1,0:T(8,128)(2,1)} async-done(((bf16[768,3]{1,0:T(8,128)(2,1)}), bf16[96,3]{1,0:T(8,128)(2,1)}) %reduce-scatter.71.cloned.1.call-update) | async-done | bytes 592
  1650.7 62.6 %reduce-scatter.75.cloned.1.call-done = bf16[96,3]{1,0:T(8,128)(2,1)} async-done(((bf16[768,3]{1,0:T(8,128)(2,1)}), bf16[96,3]{1,0:T(8,128)(2,1)}) %reduce-scatter.75.cloned.1.call-update) | async-done | bytes 592
  1714.1 62.6 %reduce-scatter.73.cloned.1.call-done = bf16[96,3]{1,0:T(8,128)(2,1)} async-done(((bf16[768,3]{1,0:T(8,128)(2,1)}), bf16[96,3]{1,0:T(8,128)(2,1)}) %reduce-scatter.73.cloned.1.call-update) | async-done | bytes 592
  1777.5 63.0 %reduce-scatter.69.cloned.1.call-done = bf16[96,3]{1,0:T(8,128)(2,1)} async-done(((bf16[768,3]{1,0:T(8,128)(2,1)}), bf16[96,3]{1,0:T(8,128)(2,1)}) %reduce-scatter.69.cloned.1.call-update) | async-done | bytes 592
  1841.3 59.0 %reduce-scatter.57.cloned.1.call-done = bf16[8,768]{1,0:T(8,128)(2,1)} async-done(((bf16[64,768]{1,0:T(8,128)(2,1)}), bf16[8,768]{1,0:T(8,128)(2,1)}) %reduce-scatter.57.cloned.1.call-update) | async-done | bytes 12304 | tf_op jit(solution)/shard_map/reduce_scatter | solution.py:357
  1900.3 59.8 %reduce-scatter.59.cloned.1.call-done = bf16[8,768]{1,0:T(8,128)(2,1)} async-done(((bf16[64,768]{1,0:T(8,128)(2,1)}), bf16[8,768]{1,0:T(8,128)(2,1)}) %reduce-scatter.59.cloned.1.call-update) | async-done | bytes 12304 | tf_op jit(solution)/shard_map/reduce_scatter | solution.py:357
  1960.9 10.1 all-reduce
  1972.8 48.8 %all-reduce.4.cloned.1.call-done = (bf16[96,2304]{0,1:T(8,128)(2,1)}, bf16[96,768]{1,0:T(8,128)(2,1)}, bf16[96,3072]{1,0:T(8,128)(2,1)}, bf16[384,768]{1,0:T(8,1...) async-done(((bf16[96,2304]{0,1:T(8,128)(2,1)}, bf16[96,768]{1,0:T(8,128)(2,1)}, bf16[96,3072]{1,0:T(8,128)(2,1)}, bf16[384,768]{1,0:T(8,128)(2,1)}, ...) | async-done | bytes 2359312 | tf_op jit(solution)/shard_map/psum | solution.py:374
  (576 shorter events, 236.3 us)
Async XLA Ops:
  7.2 90.4 %all-gather.9.cloned.1.call-start = ((), (), s32[]{:S(2)}) async-start(), calls=%async_computation.20 | async-start | bytes 3981312 | tf_op jit(solution)/shard_map/all_gather | solution.py:312
  7.9 135.9 %all-gather.11.cloned.1.call-start = ((), (), s32[]{:S(2)}) async-start(), calls=%async_computation.21 | async-start | bytes 1327104 | tf_op jit(solution)/shard_map/all_gather | solution.py:313
  8.7 193.4 %all-gather.13.cloned.1.call-start = ((), (), s32[]{:S(2)}) async-start(), calls=%async_computation.22 | async-start | bytes 5308416 | tf_op jit(solution)/shard_map/all_gather | solution.py:314
  9.4 272.8 %all-gather.15.cloned.1.call-start = ((), (), s32[]{:S(2)}) async-start(), calls=%async_computation.23 | async-start | bytes 5308416 | tf_op jit(solution)/shard_map/all_gather | solution.py:315
  10.0 337.6 %all-gather.17.cloned.1.call-start = ((), (), s32[]{:S(2)}) async-start(), calls=%async_computation.24 | async-start | bytes 3981312 | tf_op jit(solution)/shard_map/all_gather | solution.py:316
  10.6 421.2 %all-gather.19.cloned.1.call-start = ((), (), s32[]{:S(2)}) async-start(), calls=%async_computation.25 | async-start | bytes 1327104 | tf_op jit(solution)/shard_map/all_gather | solution.py:317
  11.1 521.0 %reduce-scatter.61.cloned.1.call-start = ((), (), s32[]{:S(2)}) async-start(), calls=%async_computation.38 | async-start | bytes 221184 | tf_op jit(solution)/shard_map/reduce_scatter | solution.py:196
  39.0 287.0 %copy-start.111 = (f32[768]{0:T(1024)}, f32[768]{0:T(1024)S(1)}, u32[]{:S(2)}) copy-start(f32[768]{0:T(1024)S(1)} %get-tuple-element.130) | copy-start | bytes 9220
  56.5 269.4 %copy-start.134 = (f32[768]{0:T(1024)}, f32[768]{0:T(1024)S(1)}, u32[]{:S(2)}) copy-start(f32[768]{0:T(1024)S(1)} %get-tuple-element.133) | copy-start | bytes 9220
  116.8 32.5 %copy-start.13 = (bf16[8,128,1,12,64]{1,0,4,3,2:T(8,128)(2,1)}, bf16[8,128,1,12,64]{1,0,4,3,2:T(8,128)(2,1)S(1)}, u32[]{:S(2)}) copy-start(bf16[8,128,1,12,64]{1,0,4,3,2:T(8,128)(2,1)S(1)} %get-tuple-element.164) | copy-start | bytes 4718596
  116.8 32.5 %copy-start.15 = (bf16[8,128,1,12,64]{1,0,4,3,2:T(8,128)(2,1)}, bf16[8,128,1,12,64]{1,0,4,3,2:T(8,128)(2,1)S(1)}, u32[]{:S(2)}) copy-start(bf16[8,128,1,12,64]{1,0,4,3,2:T(8,128)(2,1)S(1)} %get-tuple-element.163) | copy-start | bytes 4718596
  147.7 178.3 %copy-start.101 = (f32[1024]{0:T(1024)}, f32[1024]{0:T(1024)S(1)}, u32[]{:S(2)}) copy-start(f32[1024]{0:T(1024)S(1)} %broadcast_multiply_fusion.3) | copy-start | bytes 12292
  148.2 177.7 %copy-start.107 = (f32[1024]{0:T(1024)}, f32[1024]{0:T(1024)S(1)}, u32[]{:S(2)}) copy-start(f32[1024]{0:T(1024)S(1)} %fusion.126) | copy-start | bytes 12292
  158.2 124.0 %copy-start.27 = (f32[1024,768]{1,0:T(8,128)}, f32[1024,768]{1,0:T(8,128)S(1)}, u32[]{:S(2)}) copy-start(f32[1024,768]{1,0:T(8,128)S(1)} %get-tuple-element.209) | copy-start | bytes 9437188
  158.2 124.0 %copy-start.103 = (f32[1024]{0:T(1024)}, f32[1024]{0:T(1024)S(1)}, u32[]{:S(2)}) copy-start(f32[1024]{0:T(1024)S(1)} %broadcast_multiply_fusion.1) | copy-start | bytes 12292
  159.7 122.5 %copy-start.109 = (f32[1024]{0:T(1024)}, f32[1024]{0:T(1024)S(1)}, u32[]{:S(2)}) copy-start(f32[1024]{0:T(1024)S(1)} %fusion.128) | copy-start | bytes 12292
  282.2 9.0 copy-start.24
  282.2 9.0 copy-start.145
  282.2 43.8 %slice-start.5 = ((s8[4718592]{0:T(1024)(128)(4,1)}), s8[4194304]{0:T(1024)(128)(4,1)S(1)}, s32[]{:S(2)}) async-start(s8[4718592]{0:T(1024)(128)(4,1)} %bitcast.408), calls=%async_computation.52 | async-start | bytes 8388608
  291.1 42.0 %copy-start.3 = (f32[1024,768]{1,0:T(8,128)}, f32[1024,768]{1,0:T(8,128)S(1)}, u32[]{:S(2)}) copy-start(f32[1024,768]{1,0:T(8,128)S(1)} %get-tuple-element.212) | copy-start | bytes 9437188
  291.2 41.9 %copy-start.77 = (f32[1024]{0:T(1024)}, f32[1024]{0:T(1024)S(1)}, u32[]{:S(2)}) copy-start(f32[1024]{0:T(1024)S(1)} %broadcast_multiply_fusion) | copy-start | bytes 12292
  291.2 34.8 %slice-start.6 = ((s8[4718592]{0:T(1024)(128)(4,1)}), s8[524288]{0:T(1024)(128)(4,1)S(1)}, s32[]{:S(2)}) async-start(s8[4718592]{0:T(1024)(128)(4,1)} %bitcast.408), calls=%async_computation.53 | async-start | bytes 1048576
  335.4 16.4 copy-start.136
  472.5 123.6 %reduce-scatter.63.cloned.1.call-start = ((), (), s32[]{:S(2)}) async-start(), calls=%async_computation.39 | async-start | bytes 221184 | tf_op jit(solution)/shard_map/reduce_scatter | solution.py:196
  474.1 16.1 copy-start.76
  476.9 56.7 %copy-start.123 = (f32[8]{0:T(128)S(1)}, f32[8]{0:T(128)}, u32[]{:S(2)}) copy-start(f32[8]{0:T(128)} %copy-done.122) | copy-start | bytes 100
  478.7 368.3 %reduce-scatter.55.cloned.1.call-start = ((), (), s32[]{:S(2)}) async-start(), calls=%async_computation.35 | async-start | bytes 1327104 | tf_op jit(solution)/shard_map/reduce_scatter | solution.py:354
  481.1 366.0 %reduce-scatter.53.cloned.1.call-start = ((), (), s32[]{:S(2)}) async-start(), calls=%async_computation.34 | async-start | bytes 1327104 | tf_op jit(solution)/shard_map/reduce_scatter | solution.py:354
  492.5 356.3 %reduce-scatter.37.cloned.1.call-start = ((), (), s32[]{:S(2)}) async-start(), calls=%async_computation.26 | async-start | bytes 1327104 | tf_op jit(solution)/shard_map/reduce_scatter | solution.py:342
  536.6 60.9 %copy-start.121 = (f32[8]{0:T(128)S(1)}, f32[8]{0:T(128)}, u32[]{:S(2)}) copy-start(f32[8]{0:T(128)} %copy-done.120) | copy-start | bytes 100
  612.0 17.9 copy-start.40
  612.0 45.9 %copy-start.132 = (f32[1024]{0:T(1024)}, f32[1024]{0:T(1024)S(1)}, u32[]{:S(2)}) copy-start(f32[1024]{0:T(1024)S(1)} %negate_multiply_fusion.5) | copy-start | bytes 12292
  612.0 17.9 copy-start.130
  639.7 18.2 copy-start.25
  639.7 18.3 copy-start.102
  639.7 18.3 copy-start.104
  639.7 18.3 copy-start.108
  639.7 18.3 copy-start.110
  639.7 18.3 copy-start.112
  658.0 12.9 copy-start.96
  658.0 12.9 copy-start.94
  658.0 12.9 copy-start.28
  658.0 12.9 copy-start.43
  678.8 184.1 %reduce-scatter.39.cloned.1.call-start = ((), (), s32[]{:S(2)}) async-start(), calls=%async_computation.27 | async-start | bytes 1327104 | tf_op jit(solution)/shard_map/reduce_scatter | solution.py:342
  678.9 8.5 copy-start.128
  692.4 252.3 %reduce-scatter.67.cloned.1.call-start = ((), (), s32[]{:S(2)}) async-start(), calls=%async_computation.41 | async-start | bytes 3981312
  707.2 11.4 copy-start.50
  726.7 300.2 %reduce-scatter.65.cloned.1.call-start = ((), (), s32[]{:S(2)}) async-start(), calls=%async_computation.40 | async-start | bytes 3981312
  749.4 11.4 copy-start.47
  769.0 340.0 %reduce-scatter.51.cloned.1.call-start = ((), (), s32[]{:S(2)}) async-start(), calls=%async_computation.33 | async-start | bytes 3981312 | tf_op jit(solution)/shard_map/reduce_scatter | solution.py:351
  772.7 418.5 %reduce-scatter.49.cloned.1.call-start = ((), (), s32[]{:S(2)}) async-start(), calls=%async_computation.32 | async-start | bytes 3981312 | tf_op jit(solution)/shard_map/reduce_scatter | solution.py:351
  775.7 513.7 %reduce-scatter.43.cloned.1.call-start = ((), (), s32[]{:S(2)}) async-start(), calls=%async_computation.29 | async-start | bytes 5308416 | tf_op jit(solution)/shard_map/reduce_scatter | solution.py:345
  785.6 602.3 %reduce-scatter.41.cloned.1.call-start = ((), (), s32[]{:S(2)}) async-start(), calls=%async_computation.28 | async-start | bytes 5308416 | tf_op jit(solution)/shard_map/reduce_scatter | solution.py:345
  797.4 689.2 %reduce-scatter.45.cloned.1.call-start = ((), (), s32[]{:S(2)}) async-start(), calls=%async_computation.30 | async-start | bytes 5308416 | tf_op jit(solution)/shard_map/reduce_scatter | solution.py:348
  809.5 775.6 %reduce-scatter.47.cloned.1.call-start = ((), (), s32[]{:S(2)}) async-start(), calls=%async_computation.31 | async-start | bytes 5308416 | tf_op jit(solution)/shard_map/reduce_scatter | solution.py:348
  821.6 828.3 %reduce-scatter.71.cloned.1.call-start = ((), (), s32[]{:S(2)}) async-start(), calls=%async_computation.43 | async-start | bytes 221184
  831.3 882.0 %reduce-scatter.75.cloned.1.call-start = ((), (), s32[]{:S(2)}) async-start(), calls=%async_computation.45 | async-start | bytes 221184
  834.4 942.3 %reduce-scatter.73.cloned.1.call-start = ((), (), s32[]{:S(2)}) async-start(), calls=%async_computation.44 | async-start | bytes 221184
  835.4 1005.1 %reduce-scatter.69.cloned.1.call-start = ((), (), s32[]{:S(2)}) async-start(), calls=%async_computation.42 | async-start | bytes 221184
  836.3 1064.0 %reduce-scatter.57.cloned.1.call-start = ((), (), s32[]{:S(2)}) async-start(), calls=%async_computation.36 | async-start | bytes 110592 | tf_op jit(solution)/shard_map/reduce_scatter | solution.py:357
  837.4 1122.7 %reduce-scatter.59.cloned.1.call-start = ((), (), s32[]{:S(2)}) async-start(), calls=%async_computation.37 | async-start | bytes 110592 | tf_op jit(solution)/shard_map/reduce_scatter | solution.py:357
  838.5 1183.1 %all-reduce.4.cloned.1.call-start = ((), (), s32[]{:S(2)}) async-start(), calls=%async_computation.46 | async-start | bytes 5013504 | tf_op jit(solution)/shard_map/psum | solution.py:374
  1193.2 394.2 %copy-start.127 = (f32[1024]{0:T(1024)S(1)}, f32[1024]{0:T(1024)}, u32[]{:S(2)}) copy-start(f32[1024]{0:T(1024)} %copy-done.125) | copy-start | bytes 12292
  2021.6 8.7 copy-start.62
  (119 other events, 332.5 us)
Sparse Core Ops, SparseCore 0:
  10.2 69.2 all-gather.8
  81.6 39.5 all-gather.10
  123.4 78.6 all-gather.12
  204.1 78.0 all-gather.14
  284.2 63.3 all-gather.16
  349.6 40.2 all-gather.18
  472.6 59.5 reduce-scatter.60
  536.0 60.0 reduce-scatter.62
  599.5 63.0 reduce-scatter.54
  665.8 62.9 reduce-scatter.52
  732.8 63.2 reduce-scatter.36
  799.9 62.9 reduce-scatter.38
  866.5 78.0 reduce-scatter.66
  948.1 78.6 reduce-scatter.64
  1030.3 78.5 reduce-scatter.50
  1112.5 78.6 reduce-scatter.48
  1194.6 94.7 reduce-scatter.42
  1292.9 94.9 reduce-scatter.40
  1391.6 94.9 reduce-scatter.44
  1490.1 94.9 reduce-scatter.46
  1589.0 60.8 reduce-scatter.70
  1653.1 60.0 reduce-scatter.74
  1716.5 60.0 reduce-scatter.72
  1780.3 60.0 reduce-scatter.68
  1843.7 56.5 reduce-scatter.56
  1903.5 56.6 reduce-scatter.58
  1963.4 58.1 all-reduce.3
where the time goes:
time: 2050 us; the launch traced here: 2040 us
  waiting for transfers between devices  1330 us (65%)
  matrix products  315 us (15%)
  local copies, waits for them, and re-layouts  154 us (8%)
  blocking collectives  149 us (7%)
  other arithmetic  76 us (4%)
    unnamed x33, waiting for transfers between devices  403 us
    reduce_scatter x2, waiting for transfers between devices, body(): lax.psum_scatter(grad_full[3].astype(jnp.bfloat16), 'seg', scatter_dimens...  195 us
    reduce_scatter x2, waiting for transfers between devices, body(): lax.psum_scatter(grad_full[2].astype(jnp.bfloat16), 'seg', scatter_dimens...  195 us
    reduce_scatter x2, waiting for transfers between devices, body(): lax.psum_scatter(grad_full[4].astype(jnp.bfloat16), 'seg', scatter_dimens...  160 us
    reduce_scatter x2, waiting for transfers between devices, body(): lax.psum_scatter(grad_full[6].astype(jnp.bfloat16), 'seg', scatter_dimens...  119 us
    reduce_scatter x2, waiting for transfers between devices, backward_pass(): lax.psum_scatter(jnp.concatenate([grad_keys.reshape(rows, model_width), g...  94.6 us
    dot_general x12, matrix products, outer_cols(): lax.dot_general(left, right, (((1,), (1,)), ((), ())), preferred_element_...  94.3 us
    dot_general x2, matrix products, forward_pass(): hidden_pre = jnp.dot(first_low, w_up, preferred_element_type=jnp.float32)  70.1 us
  transfers between devices with their start and end apart: 27, of which 21 were waited for; matrix products, arithmetic and copies ran while one was open for 23% of the time, Pallas kernels for 0%

commit v1 on v0

v1 whole, which is shorter than its diff:
```python
from functools import partial
import jax
import jax.numpy as jnp
from jax import lax
from jax.experimental import pallas as pl
from jax.experimental.pallas import tpu as pltpu
from jax.sharding import PartitionSpec as P

HEAD_DIM = 64
PAIR = 2 * HEAD_DIM
EPSILON = 1e-05
NEGATIVE = -1e30
F32 = jnp.float32
BF16 = jnp.bfloat16
MIB = 1 << 20


def dot_nn(left, right):
    return lax.dot_general(left, right, (((1,), (0,)), ((), ())), preferred_element_type=F32)


def dot_nt(left, right):
    return lax.dot_general(left, right, (((1,), (1,)), ((), ())), preferred_element_type=F32)


def dot_tn(left, right):
    return lax.dot_general(left, right, (((0,), (0,)), ((), ())), preferred_element_type=F32)


def norm_parts(values):
    center = values - jnp.mean(values, axis=-1, keepdims=True)
    spread = jnp.mean(center * center, axis=-1, keepdims=True)
    inverse = lax.rsqrt(spread + EPSILON)
    return center * inverse, inverse


def norm_back(grad, unit, inverse, gain):
    scaled = grad * gain
    first = jnp.mean(scaled, axis=-1, keepdims=True)
    second = jnp.mean(scaled * unit, axis=-1, keepdims=True)
    return inverse * (scaled - first - unit * second)


def gelu_parts(hidden):
    size = jnp.abs(hidden)
    bell = jnp.exp(hidden * hidden * -0.5)
    base = size * (0.3275911 * 0.7071067811865476) + 1.0
    inv = pl.reciprocal(base, approx=True)
    inv = inv * (2.0 - base * inv)
    poly = inv * (0.5 * 1.061405429) + (0.5 * -1.453152027)
    poly = poly * inv + (0.5 * 1.421413741)
    poly = poly * inv + (0.5 * -0.284496736)
    poly = poly * inv + (0.5 * 0.254829592)
    tail = poly * inv * bell
    phi = jnp.where(hidden < 0.0, tail, 1.0 - tail)
    return hidden * phi, phi + hidden * bell * 0.3989422804014327


def halves(pair, first_half):
    zero = jnp.zeros_like(pair)
    return jnp.concatenate([jnp.where(first_half, pair, zero), jnp.where(first_half, zero, pair)], axis=0)


def pair_forward(query, key, value, first_half, same=None):
    rows = query.shape[0]
    scores = dot_nt(key, halves(query * BF16(HEAD_DIM ** -0.5), first_half))
    if same is not None:
        scores = jnp.where(same, scores, NEGATIVE)
    raised = jnp.exp(scores - jnp.max(scores, axis=0, keepdims=True))
    probs = (raised * (1.0 / jnp.sum(raised, axis=0, keepdims=True))).astype(BF16)
    both = dot_tn(probs, value)
    return probs, jnp.where(first_half, both[:rows], both[rows:])


def pair_backward(query, key, value, probs, grad_mixed, first_half):
    rows = query.shape[0]
    grad_both = halves(grad_mixed, first_half)
    query_both = halves(query * BF16(HEAD_DIM ** -0.5), first_half)
    grad_probs = dot_nt(value, grad_both)
    wide = probs.astype(F32)
    grad_scores = (wide * (grad_probs - jnp.sum(grad_probs * wide, axis=0, keepdims=True))).astype(BF16)
    grad_value = dot_nn(probs, grad_both)
    grad_key = dot_nn(grad_scores, query_both)
    both = dot_tn(grad_scores, key)
    grad_query = jnp.where(first_half, both[:rows], both[rows:]) * (HEAD_DIM ** -0.5)
    return grad_query, grad_key, grad_value


def lane_half(shape):
    return lax.broadcasted_iota(jnp.int32, shape, 1) % PAIR < HEAD_DIM


def attention_kernel(seg_length, x_ref, wqo_ref, proj_ref, probs_ref, mixed_ref, pre_ref):
    rows, width = x_ref.shape
    pairs = width // PAIR
    for part in range(3):
        proj_ref[:, part * width : (part + 1) * width] = dot_nn(x_ref[...], square(wqo_ref[part])).astype(BF16)
    first_half = lane_half((seg_length, PAIR))
    for seg in range(rows // seg_length):
        span = slice(seg * seg_length, (seg + 1) * seg_length)
        for pair in range(pairs):
            cols = [slice(part * width + pair * PAIR, part * width + (pair + 1) * PAIR) for part in range(3)]
            probs, mixed = pair_forward(
                proj_ref[span, cols[0]], proj_ref[span, cols[1]], proj_ref[span, cols[2]], first_half
            )
            probs_ref[seg, pair] = probs
            mixed_ref[span, cols[0]] = mixed.astype(BF16)
    pre_ref[...] = x_ref[...].astype(F32) + dot_nn(mixed_ref[...], square(wqo_ref[3]))


def square(value):
    return value.reshape(-1, value.shape[-1])


def up_block(ref, part):
    return square(ref[:, part])


def down_block(ref, part):
    count = ref.shape[0] // 4
    return square(ref[part * count : (part + 1) * count])


def whole(shape):
    return pl.BlockSpec(shape, lambda i: (0,) * len(shape), pipeline_mode=pl.Buffered(1))


def by_rows(block, width):
    return pl.BlockSpec((block, width), lambda i: (i, 0))


def attention_forward(rows_in, w_qo, seg_length, block):
    rows, width = rows_in.shape
    pairs = width // PAIR
    segs = block // seg_length
    shapes = (
        jax.ShapeDtypeStruct((rows, 3 * width), BF16),
        jax.ShapeDtypeStruct((rows // seg_length, pairs, seg_length, 2 * seg_length), BF16),
        jax.ShapeDtypeStruct((rows, width), BF16),
        jax.ShapeDtypeStruct((rows, width), F32),
    )
    flops = 2 * rows * width * (4 * width + 4 * seg_length)
    return pl.pallas_call(
        partial(attention_kernel, seg_length),
        out_shape=shapes,
        grid=(rows // block,),
        in_specs=[by_rows(block, width), whole(w_qo.shape)],
        out_specs=[
            by_rows(block, 3 * width),
            pl.BlockSpec((segs, pairs, seg_length, 2 * seg_length), lambda i: (i, 0, 0, 0)),
            by_rows(block, width),
            by_rows(block, width),
        ],
        compiler_params=pltpu.CompilerParams(vmem_limit_bytes=56 * MIB),
        cost_estimate=pl.CostEstimate(flops=2 * flops, bytes_accessed=rows * width * 26, transcendentals=0),
        name="attention_forward",
    )(rows_in, w_qo)


def ffn_kernel(pre_ref, wup_ref, wdown_ref, gains_ref, shifts_ref, low_ref, act_ref, slope_ref, pre2_ref):
    rows, width = pre_ref.shape
    unit, unused = norm_parts(pre_ref[...])
    first = unit * gains_ref[0:1].astype(F32) + shifts_ref[0:1].astype(F32)
    low = first.astype(BF16)
    low_ref[...] = low
    total = first
    for part in range(4):
        cols = slice(part * width, (part + 1) * width)
        act, slope = gelu_parts(dot_nn(low, up_block(wup_ref, part)))
        act = act.astype(BF16)
        act_ref[:, cols] = act
        slope_ref[:, cols] = slope.astype(BF16)
        total = total + dot_nn(act, down_block(wdown_ref, part))
    pre2_ref[...] = total


def ffn_forward(pre_first, w_up, w_down, gains, shifts, block):
    rows, width = pre_first.shape
    hidden = 4 * width
    shapes = (
        jax.ShapeDtypeStruct((rows, width), BF16),
        jax.ShapeDtypeStruct((rows, hidden), BF16),
        jax.ShapeDtypeStruct((rows, hidden), BF16),
        jax.ShapeDtypeStruct((rows, width), F32),
    )
    return pl.pallas_call(
        ffn_kernel,
        out_shape=shapes,
        grid=(rows // block,),
        in_specs=[by_rows(block, width), w_up[1], w_down[1], whole(gains.shape), whole(shifts.shape)],
        out_specs=[
            by_rows(block, width),
            by_rows(block, hidden),
            by_rows(block, hidden),
            by_rows(block, width),
        ],
        compiler_params=pltpu.CompilerParams(vmem_limit_bytes=56 * MIB),
        cost_estimate=pl.CostEstimate(flops=8 * rows * width * hidden, bytes_accessed=rows * width * 28, transcendentals=0),
        name="ffn_forward",
    )(pre_first, w_up[0], w_down[0], gains, shifts)


def ffn_back_kernel(
    seg_length, cot_ref, edge_ref, cls_ref, pre1_ref, pre2_ref, slope_ref, wup_ref, wdown_ref, gains_ref, shifts_ref,
    out_ref, branch_ref, gradh_ref, grad1_ref, low1_ref, sums_ref,
):
    rows, width = cot_ref.shape
    segs = rows // seg_length
    step = pl.program_id(0)
    gain1 = gains_ref[1:2].astype(F32)
    gain0 = gains_ref[0:1].astype(F32)

    def with_edge(values, edge):
        parts = []
        top = lax.broadcasted_iota(jnp.int32, (seg_length, width), 0) == 0
        for seg in range(segs):
            parts.append(jnp.where(top, edge[seg], values[seg * seg_length : (seg + 1) * seg_length]))
        return jnp.concatenate(parts, axis=0) if segs > 1 else parts[0]

    unit2, inverse2 = norm_parts(pre2_ref[...])
    out_ref[...] = with_edge(unit2 * gain1 + shifts_ref[1:2].astype(F32), cls_ref).astype(BF16)
    grad2 = with_edge(cot_ref[...].astype(F32), edge_ref)
    sums = [jnp.sum(grad2 * unit2, axis=0, keepdims=True), jnp.sum(grad2, axis=0, keepdims=True)]
    pre_grad = norm_back(grad2, unit2, inverse2, gain1)
    branch = pre_grad.astype(BF16)
    branch_ref[...] = branch
    total = pre_grad
    for part in range(4):
        cols = slice(part * width, (part + 1) * width)
        grad_act = dot_nt(branch, down_block(wdown_ref, part))
        grad_hidden = (grad_act * slope_ref[:, cols].astype(F32)).astype(BF16)
        gradh_ref[:, cols] = grad_hidden
        total = total + dot_nt(grad_hidden, up_block(wup_ref, part))
    unit1, inverse1 = norm_parts(pre1_ref[...])
    sums += [jnp.sum(total * unit1, axis=0, keepdims=True), jnp.sum(total, axis=0, keepdims=True)]
    grad1 = norm_back(total, unit1, inverse1, gain0)
    grad1_ref[...] = grad1
    low1_ref[...] = grad1.astype(BF16)

    @pl.when(step == 0)
    def start_sums():
        sums_ref[...] = jnp.zeros_like(sums_ref)

    for row, part in zip((1, 4, 0, 3), sums):
        sums_ref[row : row + 1] += part


def ffn_backward(cot, edge, cls_new, pre_first, pre_second, slope, w_up, w_down, gains, shifts, seg_length, block):
    rows, width = cot.shape
    hidden = 4 * width
    segs = block // seg_length
    small = pl.BlockSpec((segs, 1, width), lambda i: (i, 0, 0))
    shapes = (
        jax.ShapeDtypeStruct((rows, width), BF16),
        jax.ShapeDtypeStruct((rows, width), BF16),
        jax.ShapeDtypeStruct((rows, hidden), BF16),
        jax.ShapeDtypeStruct((rows, width), F32),
        jax.ShapeDtypeStruct((rows, width), BF16),
        jax.ShapeDtypeStruct((8, width), F32),
    )
    return pl.pallas_call(
        partial(ffn_back_kernel, seg_length),
        out_shape=shapes,
        grid=(rows // block,),
        in_specs=[
            by_rows(block, width), small, small, by_rows(block, width), by_rows(block, width), by_rows(block, hidden),
            w_up[1], w_down[1], whole(gains.shape), whole(shifts.shape),
        ],
        out_specs=[
            by_rows(block, width), by_rows(block, width), by_rows(block, hidden), by_rows(block, width), by_rows(block, width),
            pl.BlockSpec((8, width), lambda i: (0, 0)),
        ],
        compiler_params=pltpu.CompilerParams(vmem_limit_bytes=56 * MIB),
        cost_estimate=pl.CostEstimate(flops=8 * rows * width * hidden, bytes_accessed=rows * width * 40, transcendentals=0),
        name="ffn_backward",
    )(cot, edge, cls_new, pre_first, pre_second, slope, w_up[0], w_down[0], gains, shifts)


def attention_back_kernel(seg_length, grad1_ref, low1_ref, proj_ref, probs_ref, wqo_ref, gradp_ref, input_ref, gradm_ref):
    rows, width = grad1_ref.shape
    pairs = width // PAIR
    gradm_ref[...] = dot_nt(low1_ref[...], square(wqo_ref[3])).astype(BF16)
    first_half = lane_half((seg_length, PAIR))
    for seg in range(rows // seg_length):
        span = slice(seg * seg_length, (seg + 1) * seg_length)
        for pair in range(pairs):
            cols = [slice(part * width + pair * PAIR, part * width + (pair + 1) * PAIR) for part in range(3)]
            grads = pair_backward(
                proj_ref[span, cols[0]], proj_ref[span, cols[1]], proj_ref[span, cols[2]],
                probs_ref[seg, pair], gradm_ref[span, cols[0]], first_half,
            )
            for place, grad in zip(cols, grads):
                gradp_ref[span, place] = grad.astype(BF16)
    total = grad1_ref[...]
    for part in range(3):
        total = total + dot_nt(gradp_ref[:, part * width : (part + 1) * width], square(wqo_ref[part]))
    input_ref[...] = total


def attention_backward(grad1, low1, proj, probs, w_qo, seg_length, block):
    rows, width = grad1.shape
    pairs = width // PAIR
    segs = block // seg_length
    return pl.pallas_call(
        partial(attention_back_kernel, seg_length),
        out_shape=(jax.ShapeDtypeStruct((rows, 3 * width), BF16), jax.ShapeDtypeStruct((rows, width), F32)),
        grid=(rows // block,),
        in_specs=[
            by_rows(block, width), by_rows(block, width), by_rows(block, 3 * width),
            pl.BlockSpec((segs, pairs, seg_length, 2 * seg_length), lambda i: (i, 0, 0, 0)),
            whole(w_qo.shape),
        ],
        out_specs=[by_rows(block, 3 * width), by_rows(block, width)],
        scratch_shapes=[pltpu.VMEM((block, width), BF16)],
        compiler_params=pltpu.CompilerParams(vmem_limit_bytes=56 * MIB),
        cost_estimate=pl.CostEstimate(flops=2 * rows * width * (8 * width), bytes_accessed=rows * width * 30, transcendentals=0),
        name="attention_backward",
    )(grad1, low1, proj, probs, w_qo)


def edge_kernel(pre_ref, wup_ref, wdown_ref, gains_ref, shifts_ref, out_ref):
    unit, unused = norm_parts(pre_ref[...])
    total = unit * gains_ref[0:1].astype(F32) + shifts_ref[0:1].astype(F32)
    low = total.astype(BF16)
    for part in range(4):
        act, unused = gelu_parts(dot_nn(low, up_block(wup_ref, part)))
        total = total + dot_nn(act.astype(BF16), down_block(wdown_ref, part))
    unit, unused = norm_parts(total)
    out_ref[...] = unit * gains_ref[1:2].astype(F32) + shifts_ref[1:2].astype(F32)


def edge_forward(pre_edge, w_up, w_down, gains, shifts):
    rows, width = pre_edge.shape
    return pl.pallas_call(
        edge_kernel,
        out_shape=jax.ShapeDtypeStruct((rows, width), F32),
        grid=(1,),
        in_specs=[by_rows(rows, width), w_up[1], w_down[1], whole(gains.shape), whole(shifts.shape)],
        out_specs=by_rows(rows, width),
        compiler_params=pltpu.CompilerParams(vmem_limit_bytes=56 * MIB),
        cost_estimate=pl.CostEstimate(flops=200 * rows * width * width, bytes_accessed=20 * width * width, transcendentals=0),
        name="edge_forward",
    )(pre_edge, w_up[0], w_down[0], gains, shifts)


def cross_kernel(
    local, rows_ref, cot_ref, keyc_ref, keyr_ref, place_ref, table_ref, wc_ref, gains_ref, shifts_ref,
    new_ref, edge_ref, low_ref, gradp_ref, mixed_ref, gradz_ref, sums_ref, table_grad_ref, proj_ref, probs_ref, gradm_ref,
):
    count, width = rows_ref.shape
    pairs = width // PAIR
    entries = table_ref.shape[0]
    picks = place_ref[...] == lax.broadcasted_iota(jnp.int32, (count, entries), 1)
    embedded = rows_ref[...] + dot_nn(picks.astype(BF16), table_ref[...])
    low = embedded.astype(BF16)
    low_ref[...] = low
    for part in range(3):
        proj_ref[:, part * width : (part + 1) * width] = dot_nn(low, up_block(wc_ref, part)).astype(BF16)
    first_half = lane_half((count, PAIR))
    same = keyc_ref[...] == keyr_ref[...]
    places = [
        [slice(part * width + pair * PAIR, part * width + (pair + 1) * PAIR) for part in range(3)] for pair in range(pairs)
    ]
    for pair, cols in enumerate(places):
        probs, mixed = pair_forward(proj_ref[:, cols[0]], proj_ref[:, cols[1]], proj_ref[:, cols[2]], first_half, same)
        probs_ref[pair] = probs
        mixed_ref[:, cols[0]] = mixed.astype(BF16)
    pre_third = embedded + dot_nn(mixed_ref[...], up_block(wc_ref, 3))
    unit, inverse = norm_parts(pre_third)
    gain = gains_ref[2:3].astype(F32)
    new_ref[...] = unit[:local] * gain + shifts_ref[2:3].astype(F32)
    grad_out = cot_ref[...]
    grad_third = norm_back(grad_out, unit, inverse, gain)
    sums_ref[...] = jnp.zeros_like(sums_ref)
    sums_ref[2:3] = jnp.sum(grad_out[:local] * unit[:local], axis=0, keepdims=True)
    sums_ref[5:6] = jnp.sum(grad_out[:local], axis=0, keepdims=True)
    gradz = grad_third.astype(BF16)
    gradz_ref[...] = gradz
    gradm_ref[...] = dot_nt(gradz, up_block(wc_ref, 3)).astype(BF16)
    for pair, cols in enumerate(places):
        grads = pair_backward(
            proj_ref[:, cols[0]], proj_ref[:, cols[1]], proj_ref[:, cols[2]], probs_ref[pair], gradm_ref[:, cols[0]], first_half
        )
        for place, grad in zip(cols, grads):
            gradp_ref[:, place] = grad.astype(BF16)
    grad_edge = grad_third[:local]
    for part in range(3):
        grad_edge = grad_edge + dot_nt(gradp_ref[:local, part * width : (part + 1) * width], up_block(wc_ref, part))
    edge_ref[...] = grad_edge
    table_grad_ref[...] = lax.dot_general(
        picks[:local].astype(F32), grad_edge, (((0,), (0,)), ((), ())),
        precision=lax.Precision.HIGHEST, preferred_element_type=F32,
    )


def cross_block(local, edge_rows, edge_cot, key_col, key_row, place, table, w_cross, gains, shifts):
    count, width = edge_rows.shape
    shapes = (
        jax.ShapeDtypeStruct((local, width), F32),
        jax.ShapeDtypeStruct((local, width), F32),
        jax.ShapeDtypeStruct((count, width), BF16),
        jax.ShapeDtypeStruct((count, 3 * width), BF16),
        jax.ShapeDtypeStruct((count, width), BF16),
        jax.ShapeDtypeStruct((count, width), BF16),
        jax.ShapeDtypeStruct((8, width), F32),
        jax.ShapeDtypeStruct(table.shape, F32),
    )
    return pl.pallas_call(
        partial(cross_kernel, local),
        out_shape=shapes,
        grid=(1,),
        in_specs=[
            whole(edge_rows.shape), whole(edge_cot.shape), whole(key_col.shape), whole(key_row.shape), whole(place.shape),
            whole(table.shape), w_cross[1], whole(gains.shape), whole(shifts.shape),
        ],
        out_specs=[whole(shape.shape) for shape in shapes],
        scratch_shapes=[
            pltpu.VMEM((count, 3 * width), BF16),
            pltpu.VMEM((width // PAIR, count, 2 * count), BF16),
            pltpu.VMEM((count, width), BF16),
        ],
        compiler_params=pltpu.CompilerParams(vmem_limit_bytes=56 * MIB),
        cost_estimate=pl.CostEstimate(flops=10_000_000_000, bytes_accessed=width * width * 8, transcendentals=0),
        name="cross_block",
    )(edge_rows, edge_cot, key_col, key_row, place, table, w_cross[0], gains, shifts)


def cols_grad_kernel(ids_ref, left_ref, right_ref, send_ref, keep_ref):
    step = pl.program_id(0)
    product = dot_tn(left_ref[...], right_ref[...]).astype(BF16)

    @pl.when(step < 2)
    def to_send():
        send_ref[0] = product

    @pl.when(step >= 2)
    def to_keep():
        keep_ref[0] = product


def joint_grad_kernel(ids_ref, left_ref, last_left_ref, right_ref, last_right_ref, send_ref, keep_ref):
    step = pl.program_id(0)
    block = step ^ (2 * (1 - (ids_ref[1] & 1)))

    def put(product):
        @pl.when(step < 2)
        def to_send():
            send_ref[0] = product

        @pl.when(step >= 2)
        def to_keep():
            keep_ref[0] = product

    @pl.when(block < 3)
    def main():
        put(dot_tn(left_ref[...], right_ref[...]).astype(BF16))

    @pl.when(block == 3)
    def last():
        put(dot_tn(last_left_ref[...], last_right_ref[...]).astype(BF16))


def send_keep_specs(width):
    return [
        pl.BlockSpec((1, width, width), lambda j, ids: (jnp.minimum(j, 1), 0, 0)),
        pl.BlockSpec((1, width, width), lambda j, ids: (jnp.maximum(j - 2, 0), 0, 0)),
    ]


def other_core_first(j, ids):
    return j ^ (2 * (1 - (ids[1] & 1)))


def cols_grads(ids, left, right):
    rows, width = left.shape
    fixed = pl.BlockSpec((rows, width), lambda j, ids: (0, 0), pipeline_mode=pl.Buffered(1))
    half = jax.ShapeDtypeStruct((2, width, width), BF16)
    return pl.pallas_call(
        cols_grad_kernel,
        out_shape=(half, half),
        grid_spec=pltpu.PrefetchScalarGridSpec(
            num_scalar_prefetch=1,
            grid=(4,),
            in_specs=[fixed, pl.BlockSpec((rows, width), lambda j, ids: (0, other_core_first(j, ids)))],
            out_specs=send_keep_specs(width),
        ),
        compiler_params=pltpu.CompilerParams(vmem_limit_bytes=56 * MIB),
        cost_estimate=pl.CostEstimate(flops=8 * rows * width * width, bytes_accessed=10 * rows * width, transcendentals=0),
        name="cols_grads",
    )(ids, left, right)


def joint_grads(ids, left, last_left, right, last_right):
    rows, width = left.shape
    fixed = pl.BlockSpec((rows, width), lambda j, ids: (0, 0), pipeline_mode=pl.Buffered(1))
    half = jax.ShapeDtypeStruct((2, width, width), BF16)
    return pl.pallas_call(
        joint_grad_kernel,
        out_shape=(half, half),
        grid_spec=pltpu.PrefetchScalarGridSpec(
            num_scalar_prefetch=1,
            grid=(4,),
            in_specs=[
                fixed, fixed,
                pl.BlockSpec((rows, width), lambda j, ids: (0, jnp.minimum(other_core_first(j, ids), 2))),
                fixed,
            ],
            out_specs=send_keep_specs(width),
        ),
        compiler_params=pltpu.CompilerParams(vmem_limit_bytes=56 * MIB),
        cost_estimate=pl.CostEstimate(flops=8 * rows * width * width, bytes_accessed=12 * rows * width, transcendentals=0),
        name="joint_grads",
    )(ids, left, last_left, right, last_right)


def rows_grad_kernel(ids_ref, left_ref, right_ref, send_ref, keep_ref, held_ref):
    core = ids_ref[1] & 1
    held_ref[...] = dot_tn(left_ref[...], right_ref[...]).reshape(held_ref.shape)
    for share in range(2):
        send_ref[share] = held_ref[:, 2 * (1 - core) + share].astype(BF16)
        keep_ref[share] = held_ref[:, 2 * core + share].astype(BF16)


def rows_grads(ids, left, right, count):
    rows, width = right.shape
    hidden = left.shape[1]
    shard_rows = hidden // count // 4
    owners = count // 4
    half = jax.ShapeDtypeStruct((2, count, shard_rows, width), BF16)
    out_spec = pl.BlockSpec((2, owners, shard_rows, width), lambda j, ids: (0, j, 0, 0))
    return pl.pallas_call(
        rows_grad_kernel,
        out_shape=(half, half),
        grid_spec=pltpu.PrefetchScalarGridSpec(
            num_scalar_prefetch=1,
            grid=(4,),
            in_specs=[
                pl.BlockSpec((rows, hidden // 4), lambda j, ids: (0, j)),
                pl.BlockSpec((rows, width), lambda j, ids: (0, 0), pipeline_mode=pl.Buffered(1)),
            ],
            out_specs=[out_spec, out_spec],
            scratch_shapes=[pltpu.VMEM((owners, 4, shard_rows, width), F32)],
        ),
        compiler_params=pltpu.CompilerParams(vmem_limit_bytes=56 * MIB),
        cost_estimate=pl.CostEstimate(flops=2 * rows * width * hidden, bytes_accessed=10 * rows * width, transcendentals=0),
        name="rows_grads",
    )(ids, left, right)


def seg_swap(value, mask):
    count = lax.axis_size("seg")
    return lax.ppermute(value, "seg", [(i, i ^ mask) for i in range(count)])


def rep_swap(value, mask):
    count = lax.axis_size("rep")
    return lax.ppermute(value, "rep", [(i, i ^ mask) for i in range(count)])


def both_swap(value, seg_mask, rep_mask):
    reps = lax.axis_size("rep")
    total = lax.axis_size("seg") * reps
    pairs = [(i, ((i // reps) ^ seg_mask) * reps + ((i % reps) ^ rep_mask)) for i in range(total)]
    return lax.ppermute(value, ("seg", "rep"), pairs)


def place_kernel(count, ids_ref, *refs):
    parts, out_ref, sems = refs[:-2], refs[-2], refs[-1]
    me, core = ids_ref[0], ids_ref[1] & 1
    copies = []
    for number, part in enumerate(parts):
        mask, side = number % count, number // count
        owner_core = core if side == 0 else 1 - core
        for share in range(2):
            target = out_ref.at[2 * owner_core + share, me ^ mask]
            copies.append(pltpu.make_async_copy(part.at[share], target, sems.at[2 * number + share]))
    for copy in copies:
        copy.start()
    for copy in copies:
        copy.wait()


def put_in_place(ids, parts, count):
    unused, rows, width = parts[0].shape
    return pl.pallas_call(
        partial(place_kernel, count),
        out_shape=jax.ShapeDtypeStruct((4, count, rows, width), parts[0].dtype),
        in_specs=[pl.BlockSpec(memory_space=pltpu.SMEM)] + [pl.BlockSpec(memory_space=pl.ANY)] * len(parts),
        out_specs=pl.BlockSpec(memory_space=pltpu.VMEM),
        scratch_shapes=[pltpu.SemaphoreType.DMA((2 * len(parts),))],
        compiler_params=pltpu.CompilerParams(vmem_limit_bytes=32 * MIB),
        cost_estimate=pl.CostEstimate(flops=0, bytes_accessed=16 * count * rows * width, transcendentals=0),
        name="put_in_place",
    )(ids, *parts)


def gather_halves(ids, blocks):
    count = lax.axis_size("seg")
    piece = lax.dynamic_slice_in_dim(blocks, 2 * (ids[1] & 1), 2, 0)
    held = {0: piece}
    for mask in range(2, count, 2):
        held[mask] = seg_swap(piece, mask)
    for mask in range(0, count, 2):
        held[mask + 1] = seg_swap(held[mask], 1)
    mine = [held[mask] for mask in range(count)]
    return put_in_place(ids, mine + [rep_swap(part, 1) for part in mine], count)


def spread_kernel(ids_ref, keep_ref, came_ref, stay_ref, x_ref, y_ref, xy_ref):
    near, across = ids_ref[0] & 1, ids_ref[1] >> 1

    def total(share, side):
        return (keep_ref[share, 0, side].astype(F32) + came_ref[share, 0, side].astype(F32)).astype(BF16)

    stay_ref[0] = total(across, near)
    x_ref[0] = total(across, 1 - near)
    y_ref[0] = total(1 - across, near)
    xy_ref[0] = total(1 - across, 1 - near)


def spread(ids, keep, came):
    unused, count, rows, width = keep.shape
    far = count // 2
    shape = (2, far, 2, rows, width)
    in_spec = pl.BlockSpec((2, 1, 2, rows, width), lambda j: (0, j, 0, 0, 0))
    out_spec = pl.BlockSpec((1, rows, width), lambda j: (j, 0, 0))
    out = jax.ShapeDtypeStruct((far, rows, width), BF16)
    return pl.pallas_call(
        spread_kernel,
        out_shape=(out,) * 4,
        grid=(far,),
        in_specs=[pl.BlockSpec(memory_space=pltpu.SMEM), in_spec, in_spec],
        out_specs=[out_spec] * 4,
        compiler_params=pltpu.CompilerParams(vmem_limit_bytes=32 * MIB),
        cost_estimate=pl.CostEstimate(flops=0, bytes_accessed=12 * count * rows * width, transcendentals=0),
        name="spread",
    )(ids, keep.reshape(shape), came.reshape(shape))


def settle_kernel(ids_ref, a_ref, b_ref, c_ref, d_ref, *outs):
    far = ids_ref[0] >> 1
    for mask, out in enumerate(outs):
        place = far ^ mask
        total = (a_ref[place].astype(F32) + b_ref[place].astype(F32)) + (c_ref[place].astype(F32) + d_ref[place].astype(F32))
        out[...] = total.astype(BF16)


def settle(ids, parts):
    far, rows, width = parts[0].shape
    whole_spec = pl.BlockSpec(memory_space=pltpu.VMEM)
    return pl.pallas_call(
        settle_kernel,
        out_shape=(jax.ShapeDtypeStruct((rows, width), BF16),) * far,
        in_specs=[pl.BlockSpec(memory_space=pltpu.SMEM)] + [whole_spec] * 4,
        out_specs=[whole_spec] * far,
        compiler_params=pltpu.CompilerParams(vmem_limit_bytes=32 * MIB),
        cost_estimate=pl.CostEstimate(flops=0, bytes_accessed=10 * far * rows * width, transcendentals=0),
        name="settle",
    )(ids, *parts)


def reduce_group(ids, send, keep):
    count = lax.axis_size("seg")
    width = send.shape[-1]
    shape = (2, count, send.shape[-2] if send.ndim == 4 else send.shape[1] // count, width)
    stay, to_x, to_y, to_xy = spread(ids, keep.reshape(shape), rep_swap(send, 1).reshape(shape))
    own, *others = settle(ids, [stay, seg_swap(to_x, 1), rep_swap(to_y, 2), both_swap(to_xy, 1, 2)])
    total = own.astype(F32)
    for mask, other in enumerate(others, 1):
        total = total + seg_swap(other, 2 * mask).astype(F32)
    return total.astype(BF16)


def share_out(ids, share):
    rep = ids[1]
    held = jnp.stack([share, rep_swap(share, 2)], axis=0)
    held = jnp.concatenate([held, rep_swap(held, 1)], axis=0)
    order = jnp.array([0, 2, 1, 3], jnp.int32)
    return [
        lax.dynamic_index_in_dim(held, order[rep ^ owner], 0, keepdims=False).astype(F32) for owner in (0, 2, 1, 3)
    ]


def halve(value, axis, bit):
    own = lax.dynamic_index_in_dim(value, bit, axis, keepdims=False)
    other = lax.dynamic_index_in_dim(value, 1 - bit, axis, keepdims=False)
    return own, other


def reduce_small(ids, value):
    mask = lax.axis_size("seg") // 2
    while mask:
        bit = (ids[0] // mask) & 1
        own, other = halve(value.reshape((2, mask) + value.shape[1:]), 0, bit)
        value = own + seg_swap(other, mask)
        mask //= 2
    value = value[0]
    for mask in (1, 2):
        value = value + rep_swap(value, mask)
    return value


def body(tokens, cotangent, doc_counts, w_qkv, w_out, w_up, w_down, c_qkv, c_out, pos_table, norm_gains, norm_shifts):
    micro_count, unused, seg_local, seg_length, width = tokens.shape
    count = lax.axis_size("seg")
    me = lax.axis_index("seg").astype(jnp.int32)
    rep = lax.axis_index("rep").astype(jnp.int32)
    ids = jnp.stack([me, rep])
    shard_rows = w_qkv.shape[0]
    local = micro_count * seg_local
    rows = local * seg_length
    table_rows = pos_table.shape[0]
    norm_cols = norm_gains.shape[1]

    def shares_of(matrix):
        return matrix.reshape(shard_rows, 4, width).transpose(1, 0, 2)

    def own_share(matrix):
        return lax.dynamic_slice_in_dim(matrix, rep * width, width, 1)

    packed = jnp.concatenate(
        [
            own_share(w_up),
            lax.dynamic_slice_in_dim(w_down, rep * shard_rows, shard_rows, 0),
            own_share(jnp.concatenate([c_qkv, c_out], axis=1)),
            pos_table,
            jnp.pad(jnp.concatenate([norm_gains, norm_shifts], axis=0), ((0, 2), (0, width - norm_cols))),
        ],
        axis=0,
    )
    gathered = lax.all_gather(packed, ("seg", "rep"), axis=0).reshape(count, 4, -1, width)
    small = gathered[:, 0, 3 * shard_rows :]
    table = small[:, :table_rows].reshape(count * table_rows, width)
    norms = small[:, table_rows : table_rows + 6, :norm_cols].transpose(1, 0, 2).reshape(6, width)
    gains, shifts = norms[:3], norms[3:]

    if shard_rows % 16 == 0:
        def part_of(place):
            spec = pl.BlockSpec(
                (count, 4, shard_rows, width), lambda i: (0, 0, place, 0), pipeline_mode=pl.Buffered(1)
            )
            return gathered, spec

        full_up, full_down, full_cross = part_of(0), part_of(1), part_of(2)
    else:
        def part_of(place):
            return gathered[:, :, place * shard_rows : (place + 1) * shard_rows]

        def joined(value):
            value = value.transpose(1, 0, 2, 3).reshape(1, 4, width, width)
            return value, whole(value.shape)

        full_up, full_cross = joined(part_of(0)), joined(part_of(2))
        full_down = part_of(1).reshape(4, 1, width, width)
        full_down = (full_down, whole(full_down.shape))
    full_qo = gather_halves(ids, shares_of(jnp.concatenate([w_qkv, w_out], axis=1))).reshape(4, width, width)

    counts = doc_counts[:, 0]
    ends = jnp.cumsum(counts, axis=1)
    owners = me ^ jnp.arange(count, dtype=jnp.int32)
    seg_ids = owners[:, None, None] * seg_local + jnp.arange(seg_local, dtype=jnp.int32)[None, None, :]
    seg_ids = jnp.broadcast_to(seg_ids, (count, micro_count, seg_local))
    past = seg_ids[..., None] >= ends[None, :, None, :]
    doc_ids = jnp.sum(past.astype(jnp.int32), axis=-1)
    starts = jnp.sum(jnp.where(past, counts[None, :, None, :], 0), axis=-1)
    places = (seg_ids - starts).reshape(-1, 1)
    keys = (doc_ids + (counts.shape[1] + 1) * jnp.arange(micro_count, dtype=jnp.int32)[None, :, None]).reshape(-1)

    flat = tokens.reshape(rows, width)
    cot = cotangent.reshape(rows, width)
    proj, probs, mixed, pre_first = attention_forward(flat, full_qo, seg_length, 2 * seg_length)
    pre_edge = pre_first.reshape(local, seg_length, width)[:, 0]
    edge = edge_forward(pre_edge, full_up, full_down, gains, shifts)
    edge_cot = cot.reshape(local, seg_length, width)[:, 0].astype(F32)
    edges = jnp.stack([edge, edge_cot], axis=0)
    edges = jnp.stack([edges] + [seg_swap(edges, mask) for mask in range(1, count)], axis=0)
    low, act, slope, pre_second = ffn_forward(pre_first, full_up, full_down, gains, shifts, 2 * seg_length)
    cls_new, grad_edge, c_low, c_gradp, c_mixed, c_gradz, c_sums, table_grad = cross_block(
        local, edges[:, 0].reshape(-1, width), edges[:, 1].reshape(-1, width),
        keys[:, None], jnp.concatenate([keys, keys])[None, :], places, table, full_cross, gains, shifts,
    )
    layer_out, branch, grad_hidden, grad1, low1, sums = ffn_backward(
        cot, grad_edge[:, None], cls_new[:, None], pre_first, pre_second, slope, full_up, full_down, gains, shifts,
        seg_length, 2 * seg_length,
    )
    down_share = reduce_group(ids, *rows_grads(ids, act, branch, count))
    up_share = reduce_group(ids, *cols_grads(ids, low, grad_hidden))
    grad_proj, input_grad = attention_backward(grad1, low1, proj, probs, full_qo, seg_length, 2 * seg_length)
    qo_share = reduce_group(ids, *joint_grads(ids, flat, mixed, grad_proj, low1))

    own_low = lax.dynamic_slice_in_dim(c_low, me * shard_rows, shard_rows, 1)
    own_mixed = lax.dynamic_slice_in_dim(c_mixed, me * shard_rows, shard_rows, 1)
    grad_c = shares_of(jnp.concatenate([dot_tn(own_low, c_gradp), dot_tn(own_mixed, c_gradz)], axis=1)).astype(BF16)
    own, other = halve(grad_c.reshape(2, 2, shard_rows, width), 0, rep & 1)
    own, other = halve(own.astype(F32) + rep_swap(other, 1).astype(F32), 0, rep >> 1)
    c_share = (own + rep_swap(other.astype(BF16), 2).astype(F32)).astype(BF16)

    norm_sums = (sums + c_sums).reshape(8, count, norm_cols).transpose(1, 0, 2)
    norm_sums = jnp.pad(norm_sums, ((0, 0), (0, 0), (0, width - norm_cols)))
    summed = reduce_small(ids, jnp.concatenate([norm_sums, table_grad.reshape(count, table_rows, width)], axis=1))

    early = share_out(ids, jnp.stack([down_share, up_share, c_share], axis=0))
    late = share_out(ids, qo_share)

    def side_by_side(parts):
        return jnp.concatenate(parts, axis=1)

    return (
        layer_out.reshape(tokens.shape),
        input_grad.reshape(tokens.shape),
        side_by_side(late[:3]),
        late[3],
        side_by_side([part[1] for part in early]),
        jnp.concatenate([part[0] for part in early], axis=0),
        side_by_side([part[2] for part in early[:3]]),
        early[3][2],
        summed[8:],
        summed[:3, :norm_cols],
        summed[3:6, :norm_cols],
    )


def solution(mesh):
    rows = P(None, "rep", "seg", None, None)
    split = P("seg", None)
    last = P(None, "seg")
    return jax.shard_map(
        body,
        mesh=mesh,
        in_specs=(rows, rows, P(None, "rep", None)) + (split,) * 7 + (last, last),
        out_specs=(rows, rows) + (split,) * 7 + (last, last),
        check_vma=False,
    )
```

time: 2050 us -> 535 us (0.26)
  waiting for transfers between devices: 1330 us -> 153 us
  matrix products: 315 us -> 2.5 us
  Pallas kernels: 0 us -> 233 us
  blocking collectives: 149 us -> 0 us
  local copies, waits for them, and re-layouts: 154 us -> 35.8 us
  starting transfers between devices: 1.95 us -> 68.2 us
  other arithmetic: 76 us -> 14.3 us
    reduce_scatter x14 -> x0, waiting for transfers between devices: 777 us -> none  [the longest x2 195 us: body(): lax.psum_scatter(grad_full[3].astype(jnp.bfloat16), 'seg', scatter_dimens...]
    unnamed x33 -> x1, waiting for transfers between devices: 403 us -> 0.02 us
    dot_general x64 -> x2, matrix products: 315 us -> 2.5 us  [dot_tn(): lax.dot_general(left, right, (((0,), (0,)), ((), ())), preferred_element_...]
    pallas_call x0 -> x16, Pallas kernels: none -> 233 us  [the longest x1 45.7 us: ffn_forward(): pl.pallas_call(ffn_kernel, out_shape=shapes, grid=(rows // block,), in_sp...]
    all_gather x5 -> x0, blocking collectives: 139 us -> none  [the longest x2 66.3 us: forward_pass(): all_kv = lax.all_gather(key_value, 'seg', axis=0, tiled=True)]
    ppermute x0 -> x54, waiting for transfers between devices: none -> 128 us  [the longest x29 85.7 us: seg_swap(): return lax.ppermute(value, 'seg', [(i, i ^ mask) for i in range(count)])]
    all_gather x6 -> x1, waiting for transfers between devices: 96.8 us -> 25.3 us  [body(): lax.all_gather(packed, ('seg', 'rep'), axis=0).reshape(count, 4, -1, width)]
    ppermute x0 -> x54, starting transfers between devices: none -> 68.1 us  [the longest x29 55 us: seg_swap(): return lax.ppermute(value, 'seg', [(i, i ^ mask) for i in range(count)])]
  transfers between devices with their start and end apart: 27 -> 55, of which waited for: 21 -> 18; matrix products, arithmetic and copies ran while one was open for 23% -> 4% of each run, Pallas kernels for 0% -> 24%
where the time goes in v1:
time: 535 us; the launch traced here: 530 us
  Pallas kernels  233 us (44%)
  waiting for transfers between devices  153 us (29%)
  starting transfers between devices  68.2 us (13%)
  local copies, waits for them, and re-layouts  35.8 us (7%)
  between operations  22.8 us (4%)
  other arithmetic  14.3 us (3%)
    ppermute x29, waiting for transfers between devices, seg_swap(): return lax.ppermute(value, 'seg', [(i, i ^ mask) for i in range(count)])  85.7 us
    ppermute x29, starting transfers between devices, seg_swap(): return lax.ppermute(value, 'seg', [(i, i ^ mask) for i in range(count)])  55 us
    pallas_call x1, Pallas kernels, ffn_forward(): pl.pallas_call(ffn_kernel, out_shape=shapes, grid=(rows // block,), in_sp...  45.7 us
    pallas_call x1, Pallas kernels, attention_backward(): pl.pallas_call(partial(attention_back_kernel, seg_length), out_shape=(jax...  39.4 us
    pallas_call x1, Pallas kernels, ffn_backward(): pl.pallas_call(partial(ffn_back_kernel, seg_length), out_shape=shapes, gr...  35.3 us
    ppermute x22, waiting for transfers between devices, rep_swap(): return lax.ppermute(value, 'rep', [(i, i ^ mask) for i in range(count)])  33.5 us
    all_gather x1, waiting for transfers between devices, body(): lax.all_gather(packed, ('seg', 'rep'), axis=0).reshape(count, 4, -1, width)  25.3 us
    pallas_call x1, Pallas kernels, attention_forward(): pl.pallas_call(partial(attention_kernel, seg_length), out_shape=shapes, g...  24.7 us
  transfers between devices with their start and end apart: 55, of which 18 were waited for; matrix products, arithmetic and copies ran while one was open for 4% of the time, Pallas kernels for 24%

profile of v1, /device:TPU:0, one launch (start us, length us, event | category | flops | bytes accessed | tf_op | source)
XLA Modules:
  0.0 529.6 jit_solution(3096440018742236207)
XLA Ops:
  14.8 4.7 collective-permute-start.5
  20.1 1.6 collective-permute-start
  22.1 6.9 %collective-permute-done.5.refs_6_ = bf16[2,96,768]{2,1,0:T(8,128)(2,1)S(1)} collective-permute-done((bf16[2,96,768]{2,1,0:T(8,128)(2,1)S(1)}, bf16[2,96,768]{2,1,0:T(8,128)(2,1)S(1)}, u32[]{:S(2)}, u32[]{:S(2)}) %collective-permute-start.5) | collective-permute-done | bytes 294944 | tf_op jit(solution)/shard_map/ppermute | solution.py:552
  30.3 24.9 %collective-permute-done.3.refs_4_ = bf16[2,96,768]{2,1,0:T(8,128)(2,1)S(1)} collective-permute-done((bf16[2,96,768]{2,1,0:T(8,128)(2,1)S(1)}, bf16[2,96,768]{2,1,0:T(8,128)(2,1)S(1)}, u32[]{:S(2)}, u32[]{:S(2)}) %collective-permute-start.3) | collective-permute-done | bytes 294944 | tf_op jit(solution)/shard_map/ppermute | solution.py:552
  55.2 1.5 collective-permute-start.4
  58.8 3.6 copy.68
  63.6 7.3 %collective-permute-done.4.refs_5_ = bf16[2,96,768]{2,1,0:T(8,128)(2,1)S(1)} collective-permute-done((bf16[2,96,768]{2,1,0:T(8,128)(2,1)S(1)}, bf16[2,96,768]{2,1,0:T(8,128)(2,1)S(1)}, u32[]{:S(2)}, u32[]{:S(2)}) %collective-permute-start.4) | collective-permute-done | bytes 294944 | tf_op jit(solution)/shard_map/ppermute | solution.py:552
  70.9 12.6 %collective-permute-done.2.refs_3_ = bf16[2,96,768]{2,1,0:T(8,128)(2,1)S(1)} collective-permute-done((bf16[2,96,768]{2,1,0:T(8,128)(2,1)S(1)}, bf16[2,96,768]{2,1,0:T(8,128)(2,1)S(1)}, u32[]{:S(2)}, u32[]{:S(2)}) %collective-permute-start.2) | collective-permute-done | bytes 294944 | tf_op jit(solution)/shard_map/ppermute | solution.py:552
  83.6 1.4 collective-permute-done.10.refs_11_
  85.0 8.0 %put_in_place.1 = bf16[4,8,96,768]{3,2,1,0:T(8,128)(2,1)S(1)} custom-call(s32[2]{0:T(128)S(1)} %pad_add_fusion.1.ids_ref, bf16[2,96,768]{2,1,0:T(8,128)(2,1)S(1)} %bitcast.157, bf16[2,96,768]{2,1,0:T(8,128)(2,1)S(1)} %collective-permute-done.refs_1_, bf16[2,96,768]{2,1,0:T(8,128)(2,1)S(1)} %collective-permute-done.1.refs_2_, ...), custom_call_target="tpu_custom_call" | custom-call | bytes 9437184 | tf_op jit(solution)/shard_map/put_in_place/pallas_call | solution.py:585
  93.0 2.1 copy-done
  95.2 24.7 %attention_forward.1 = (bf16[2048,2304]{1,0:T(8,128)(2,1)}, bf16[16,6,128,256]{3,2,1,0:T(8,128)(2,1)}, bf16[2048,768]{1,0:T(8,128)(2,1)}, f32[2048,768]{1,0:T(8,128)}) custom-call(bf16[2048,768]{1,0:T(8,128)(2,1)} %bitcast.192, bf16[4,768,768]{2,1,0:T(8,128)(2,1)} %bitcast.146), custom_call_target="tpu_custom_call" | custom-call | flops 22548578304 | bytes 40894464 | tf_op jit(solution)/shard_map/attention_forward/pallas_call | solution.py:143
  121.5 25.3 %all-gather.3.cloned.1.call-done = bf16[9728,768]{1,0:T(8,128)(2,1)} async-done(((bf16[304,768]{1,0:T(8,128)(2,1)}), bf16[9728,768]{1,0:T(8,128)(2,1)}) %all-gather.3.cloned.1.call-update) | async-done | bytes 14942224 | tf_op jit(solution)/shard_map/all_gather | solution.py:731
  149.8 6.4 %edge_forward.1 = f32[16,768]{1,0:T(8,128)} custom-call(f32[16,768]{1,0:T(8,128)} %bitcast.187, bf16[8,4,304,768]{3,2,1,0:T(8,128)(2,1)} %bitcast.159, bf16[8,4,304,768]{3,2,1,0:T(8,128)(2,1)} %bitcast.160, bf16[3,768]{1,0:T(4,128)(2,1)} %slice.94.gains_ref, bf16[3,768]{1,0:T(4,128)(2,1)} %slice.96.shifts_ref), custom_call_target="tpu_custom_call" | custom-call | flops 1887436800 | bytes 11796480 | tf_op jit(solution)/shard_map/edge_forward/pallas_call | solution.py:334
  157.1 1.5 collective-permute-start.20
  158.6 1.5 collective-permute-start.19
  160.0 2.3 collective-permute-start.18
  163.0 1.4 collective-permute-start.15
  164.5 45.7 %ffn_forward.1 = (bf16[2048,768]{1,0:T(8,128)(2,1)}, bf16[2048,3072]{1,0:T(8,128)(2,1)}, bf16[2048,3072]{1,0:T(8,128)(2,1)}, f32[2048,768]{1,0:T(8,128)}) custom-call(f32[2048,768]{1,0:T(8,128)} %get-tuple-element.65.pre_ref.pre1_ref, bf16[8,4,304,768]{3,2,1,0:T(8,128)(2,1)} %bitcast.161, bf16[8,4,304,768]{3,2,1,0:T(8,128)(2,1)} %bitcast.162, ...), custom_call_target="tpu_custom_call" | custom-call | flops 38654705664 | bytes 44040192 | tf_op jit(solution)/shard_map/ffn_forward/pallas_call | solution.py:186
  210.2 1.4 collective-permute-start.16
  211.6 3.2 collective-permute-done.16
  214.9 1.8 collective-permute-start.21
  216.8 5.5 %collective-permute-done.21 = f32[2,16,768]{2,1,0:T(8,128)S(1)} collective-permute-done((f32[2,16,768]{2,1,0:T(8,128)S(1)}, f32[2,16,768]{2,1,0:T(8,128)S(1)}, u32[]{:S(2)}, u32[]{:S(2)}) %collective-permute-start.21) | collective-permute-done | bytes 98336 | tf_op jit(solution)/shard_map/ppermute | solution.py:552
  223.2 8.3 %cross_block.1 = (f32[16,768]{1,0:T(8,128)}, f32[16,768]{1,0:T(8,128)}, bf16[128,768]{1,0:T(8,128)(2,1)}, bf16[128,2304]{1,0:T(8,128)(2,1)}, bf16[128,768]{1,0:T...) custom-call(f32[128,768]{1,0:T(8,128)} %bitcast.186, f32[128,768]{1,0:T(8,128)} %bitcast.185, ...), custom_call_target="tpu_custom_call" | custom-call | flops 10000000000 | bytes 4718592 | tf_op jit(solution)/shard_map/cross_block/pallas_call | solution.py:408
  231.5 1.5 broadcast_in_dim.34.edge_ref
  232.9 1.5 broadcast_in_dim.35.cls_ref
  234.4 35.3 %ffn_backward.1 = (bf16[2048,768]{1,0:T(8,128)(2,1)}, bf16[2048,768]{1,0:T(8,128)(2,1)}, bf16[2048,3072]{1,0:T(8,128)(2,1)}, f32[2048,768]{1,0:T(8,128)}, bf16[2048,768]{1,0:T(8,128)(2,1)}, /*index=5*/f32[8,768]{1,0:T(8,128)}) custom-call(bf16[2048,768]{1,0:T(8,128)(2,1)} %bitcast.167, f32[16,1,768]{2,1,0:T(1,128)} %broadcast_in_dim.34.edge_ref, ...), custom_call_target="tpu_custom_call" | custom-call | flops 38654705664 | bytes 62914560 | tf_op jit(solution)/shard_map/ffn_backward/pallas_call | solution.py:261
  269.7 39.4 %attention_backward.1 = (bf16[2048,2304]{1,0:T(8,128)(2,1)}, f32[2048,768]{1,0:T(8,128)}) custom-call(f32[2048,768]{1,0:T(8,128)} %get-tuple-element.71.grad1_ref, bf16[2048,768]{1,0:T(8,128)(2,1)} %get-tuple-element.72.low1_ref.last_right_ref, bf16[2048,2304]{1,0:T(8,128)(2,1)} %get-tuple-element.73.proj_ref, ...), custom_call_target="tpu_custom_call" | custom-call | flops 19327352832 | bytes 47185920 | tf_op jit(solution)/shard_map/attention_backward/pallas_call | solution.py:304
  309.1 18.3 %joint_grads.1 = (bf16[2,768,768]{2,1,0:T(8,128)(2,1)}, bf16[2,768,768]{2,1,0:T(8,128)(2,1)}) custom-call(s32[2]{0:T(128)} %copy-done.14, bf16[2048,768]{1,0:T(8,128)(2,1)} %bitcast.193, bf16[2048,768]{1,0:T(8,128)(2,1)} %get-tuple-element.76.last_left_ref, bf16[2048,2304]{1,0:T(8,128)(2,1)} %get-tuple-element.77.right_ref, ...), custom_call_target="tpu_custom_call" | custom-call | flops 9663676416 | bytes 18874368 | tf_op jit(solution)/shard_map/joint_grads/pallas_call | solution.py:497
  327.4 16.2 %cols_grads.1 = (bf16[2,768,768]{2,1,0:T(8,128)(2,1)}, bf16[2,768,768]{2,1,0:T(8,128)(2,1)}) custom-call(s32[2]{0:T(128)} %copy-done.14, bf16[2048,768]{1,0:T(8,128)(2,1)} %get-tuple-element.100.left_ref, bf16[2048,3072]{1,0:T(8,128)(2,1)} %get-tuple-element.101.right_ref), custom_call_target="tpu_custom_call" | custom-call | flops 9663676416 | bytes 15728640 | tf_op jit(solution)/shard_map/cols_grads/pallas_call | solution.py:478
  344.1 16.6 %rows_grads.1 = (bf16[2,8,96,768]{3,2,1,0:T(8,128)(2,1)}, bf16[2,8,96,768]{3,2,1,0:T(8,128)(2,1)}) custom-call(s32[2]{0:T(128)} %copy-done.14, bf16[2048,3072]{1,0:T(8,128)(2,1)} %get-tuple-element.88.left_ref, bf16[2048,768]{1,0:T(8,128)(2,1)} %get-tuple-element.89.right_ref), custom_call_target="tpu_custom_call" | custom-call | flops 9663676416 | bytes 15728640 | tf_op jit(solution)/shard_map/rows_grads/pallas_call | solution.py:531
  360.9 1.6 collective-permute-start.49
  363.6 1.4 convolution_convert_fusion
  366.1 6.4 %collective-permute-done.49 = f32[4,16,768]{2,1,0:T(8,128)S(1)} collective-permute-done((f32[4,16,768]{2,1,0:T(8,128)S(1)}, f32[4,16,768]{2,1,0:T(8,128)S(1)}, u32[]{:S(2)}, u32[]{:S(2)}) %collective-permute-start.49) | collective-permute-done | bytes 196640 | tf_op jit(solution)/shard_map/ppermute | solution.py:552
  373.3 4.0 spread.3
  378.0 1.5 copy-done.3
  379.4 1.7 copy-done.4
  381.1 2.3 spread.5
  386.0 1.4 collective-permute-start.39
  388.1 1.4 collective-permute-start.41
  390.7 1.5 collective-permute-start.46
  392.2 4.2 spread.4
  397.3 9.2 %collective-permute-done.46 = bf16[96,768]{1,0:T(8,128)(2,1)S(1)} collective-permute-done((bf16[96,768]{1,0:T(8,128)(2,1)S(1)}, bf16[96,768]{1,0:T(8,128)(2,1)S(1)}, u32[]{:S(2)}, u32[]{:S(2)}) %collective-permute-start.46) | collective-permute-done | bytes 147488 | tf_op jit(solution)/shard_map/ppermute | solution.py:557
  406.5 1.6 collective-permute-start.25
  408.0 1.9 collective-permute-start.32
  410.8 8.3 %collective-permute-done.41.d_ref = bf16[4,96,768]{2,1,0:T(8,128)(2,1)S(1)} collective-permute-done((bf16[4,96,768]{2,1,0:T(8,128)(2,1)}, bf16[4,96,768]{2,1,0:T(8,128)(2,1)S(1)}, u32[]{:S(2)}, u32[]{:S(2)}) %collective-permute-start.41) | collective-permute-done | bytes 589856 | tf_op jit(solution)/shard_map/ppermute | solution.py:564
  420.0 1.5 collective-permute-start.34
  425.7 1.5 settle.5
  427.1 17.3 %collective-permute-done.24.c_ref = bf16[4,96,768]{2,1,0:T(8,128)(2,1)S(1)} collective-permute-done((bf16[4,96,768]{2,1,0:T(8,128)(2,1)}, bf16[4,96,768]{2,1,0:T(8,128)(2,1)S(1)}, u32[]{:S(2)}, u32[]{:S(2)}) %collective-permute-start.24) | collective-permute-done | bytes 589856 | tf_op jit(solution)/shard_map/ppermute | solution.py:557
  444.5 2.1 collective-permute-start.42
  446.5 16.3 %collective-permute-start.43 = (bf16[96,768]{1,0:T(8,128)(2,1)S(1)}, bf16[96,768]{1,0:T(8,128)(2,1)S(1)}, u32[]{:S(2)}, u32[]{:S(2)}) collective-permute-start(bf16[96,768]{1,0:T(8,128)(2,1)S(1)} %get-tuple-element.110), channel_id=1, source_target_pairs={{0,16},{4,20},{8,24},{12,28},{16,0},{20,4},{24,8},{28,12},{1,17},{... | collective-permute-start | bytes 442376 | tf_op jit(solution)/shard_map/ppermute | solution.py:552
  462.8 1.5 collective-permute-start.44
  464.4 1.4 settle.3
  465.8 3.0 collective-permute-done.33.c_ref
  468.8 1.3 collective-permute-start.51
  470.1 1.4 collective-permute-start.26
  473.1 1.9 collective-permute-start.36
  474.9 1.9 collective-permute-start.37
  476.9 5.0 collective-permute-done.35
  481.9 9.7 %collective-permute-done.36 = bf16[96,768]{1,0:T(8,128)(2,1)S(1)} collective-permute-done((bf16[96,768]{1,0:T(8,128)(2,1)S(1)}, bf16[96,768]{1,0:T(8,128)(2,1)S(1)}, u32[]{:S(2)}, u32[]{:S(2)}) %collective-permute-start.36) | collective-permute-done | bytes 147488 | tf_op jit(solution)/shard_map/ppermute | solution.py:552
  491.6 1.5 collective-permute-start.28
  493.3 1.8 collective-permute-start.47
  495.1 4.3 collective-permute-done.27
  503.5 1.3 collective-permute-done.29
  (216 shorter events, 51.3 us)
Async XLA Ops:
  7.2 139.7 %all-gather.3.cloned.1.call-start = ((), (), s32[]{:S(2)}) async-start(), calls=%async_computation | async-start | bytes 15409152 | tf_op jit(solution)/shard_map/all_gather | solution.py:731
  14.2 14.7 %collective-permute-start.7 = (bf16[2,96,768]{2,1,0:T(8,128)(2,1)S(1)}, bf16[2,96,768]{2,1,0:T(8,128)(2,1)S(1)}, u32[]{:S(2)}, u32[]{:S(2)}) collective-permute-start(bf16[2,96,768]{2,1,0:T(8,128)(2,1)S(1)} %bitcast.152), channel_id=1, source_target_pairs={{0,1},{1,0},{2,3},{3,2},{4,5},{5,4},{6,7},{7,6},{8,9},{9,8},{10,11... | collective-permute-start | bytes 884744 | tf_op jit(solution)/shard_map/ppermute | solution.py:557
  14.8 14.2 %collective-permute-start.5 = (bf16[2,96,768]{2,1,0:T(8,128)(2,1)S(1)}, bf16[2,96,768]{2,1,0:T(8,128)(2,1)S(1)}, u32[]{:S(2)}, u32[]{:S(2)}) collective-permute-start(bf16[2,96,768]{2,1,0:T(8,128)(2,1)S(1)} %bitcast.153), channel_id=1, source_target_pairs={{0,24},{4,28},{8,16},{12,20},{16,8},{20,12},{24,0},{28,4},{1,25},{... | collective-permute-start | bytes 884744 | tf_op jit(solution)/shard_map/ppermute | solution.py:552
  19.4 35.7 %collective-permute-start.3 = (bf16[2,96,768]{2,1,0:T(8,128)(2,1)S(1)}, bf16[2,96,768]{2,1,0:T(8,128)(2,1)S(1)}, u32[]{:S(2)}, u32[]{:S(2)}) collective-permute-start(bf16[2,96,768]{2,1,0:T(8,128)(2,1)S(1)} %bitcast.154), channel_id=1, source_target_pairs={{0,16},{4,20},{8,24},{12,28},{16,0},{20,4},{24,8},{28,12},{1,17},{... | collective-permute-start | bytes 884744 | tf_op jit(solution)/shard_map/ppermute | solution.py:552
  19.4 35.7 %collective-permute-start.1 = (bf16[2,96,768]{2,1,0:T(8,128)(2,1)S(1)}, bf16[2,96,768]{2,1,0:T(8,128)(2,1)S(1)}, u32[]{:S(2)}, u32[]{:S(2)}) collective-permute-start(bf16[2,96,768]{2,1,0:T(8,128)(2,1)S(1)} %bitcast.155), channel_id=1, source_target_pairs={{0,8},{4,12},{8,0},{12,4},{16,24},{20,28},{24,16},{28,20},{1,9},{5... | collective-permute-start | bytes 884744 | tf_op jit(solution)/shard_map/ppermute | solution.py:552
  20.1 36.6 %collective-permute-start = (bf16[2,96,768]{2,1,0:T(8,128)(2,1)S(1)}, bf16[2,96,768]{2,1,0:T(8,128)(2,1)S(1)}, u32[]{:S(2)}, u32[]{:S(2)}) collective-permute-start(bf16[2,96,768]{2,1,0:T(8,128)(2,1)S(1)} %bitcast.156), channel_id=1, source_target_pairs={{0,4},{4,0},{8,12},{12,8},{16,20},{20,16},{24,28},{28,24},{1,5},{5... | collective-permute-start | bytes 884744 | tf_op jit(solution)/shard_map/ppermute | solution.py:552
  29.0 34.0 %collective-permute-start.13 = (bf16[2,96,768]{2,1,0:T(8,128)(2,1)S(1)}, bf16[2,96,768]{2,1,0:T(8,128)(2,1)S(1)}, u32[]{:S(2)}, u32[]{:S(2)}) collective-permute-start(bf16[2,96,768]{2,1,0:T(8,128)(2,1)S(1)} %collective-permute-done.5.refs_6_), channel_id=1, source_target_pairs={{0,1},{1,0},{2,3},{3,2},{4,5},{5,4},{6,7},{7,6},{8,9},{9,8},{10,11... | collective-permute-start | bytes 884744 | tf_op jit(solution)/shard_map/ppermute | solution.py:557
  29.0 34.0 %collective-permute-start.6 = (bf16[2,96,768]{2,1,0:T(8,128)(2,1)S(1)}, bf16[2,96,768]{2,1,0:T(8,128)(2,1)S(1)}, u32[]{:S(2)}, u32[]{:S(2)}) collective-permute-start(bf16[2,96,768]{2,1,0:T(8,128)(2,1)S(1)} %collective-permute-done.5.refs_6_), channel_id=1, source_target_pairs={{0,4},{4,0},{8,12},{12,8},{16,20},{20,16},{24,28},{28,24},{1,5},{5... | collective-permute-start | bytes 884744 | tf_op jit(solution)/shard_map/ppermute | solution.py:552
  55.2 8.4 %collective-permute-start.11 = (bf16[2,96,768]{2,1,0:T(8,128)(2,1)S(1)}, bf16[2,96,768]{2,1,0:T(8,128)(2,1)S(1)}, u32[]{:S(2)}, u32[]{:S(2)}) collective-permute-start(bf16[2,96,768]{2,1,0:T(8,128)(2,1)S(1)} %collective-permute-done.3.refs_4_), channel_id=1, source_target_pairs={{0,1},{1,0},{2,3},{3,2},{4,5},{5,4},{6,7},{7,6},{8,9},{9,8},{10,11... | collective-permute-start | bytes 884744 | tf_op jit(solution)/shard_map/ppermute | solution.py:557
  55.2 15.7 %collective-permute-start.4 = (bf16[2,96,768]{2,1,0:T(8,128)(2,1)S(1)}, bf16[2,96,768]{2,1,0:T(8,128)(2,1)S(1)}, u32[]{:S(2)}, u32[]{:S(2)}) collective-permute-start(bf16[2,96,768]{2,1,0:T(8,128)(2,1)S(1)} %collective-permute-done.3.refs_4_), channel_id=1, source_target_pairs={{0,4},{4,0},{8,12},{12,8},{16,20},{20,16},{24,28},{28,24},{1,5},{5... | collective-permute-start | bytes 884744 | tf_op jit(solution)/shard_map/ppermute | solution.py:552
  56.7 26.8 %collective-permute-start.2 = (bf16[2,96,768]{2,1,0:T(8,128)(2,1)S(1)}, bf16[2,96,768]{2,1,0:T(8,128)(2,1)S(1)}, u32[]{:S(2)}, u32[]{:S(2)}) collective-permute-start(bf16[2,96,768]{2,1,0:T(8,128)(2,1)S(1)} %collective-permute-done.1.refs_2_), channel_id=1, source_target_pairs={{0,4},{4,0},{8,12},{12,8},{16,20},{20,16},{24,28},{28,24},{1,5},{5... | collective-permute-start | bytes 884744 | tf_op jit(solution)/shard_map/ppermute | solution.py:552
  63.0 20.5 %collective-permute-start.9 = (bf16[2,96,768]{2,1,0:T(8,128)(2,1)S(1)}, bf16[2,96,768]{2,1,0:T(8,128)(2,1)S(1)}, u32[]{:S(2)}, u32[]{:S(2)}) collective-permute-start(bf16[2,96,768]{2,1,0:T(8,128)(2,1)S(1)} %collective-permute-done.1.refs_2_), channel_id=1, source_target_pairs={{0,1},{1,0},{2,3},{3,2},{4,5},{5,4},{6,7},{7,6},{8,9},{9,8},{10,11... | collective-permute-start | bytes 884744 | tf_op jit(solution)/shard_map/ppermute | solution.py:557
  63.0 20.5 %collective-permute-start.8 = (bf16[2,96,768]{2,1,0:T(8,128)(2,1)S(1)}, bf16[2,96,768]{2,1,0:T(8,128)(2,1)S(1)}, u32[]{:S(2)}, u32[]{:S(2)}) collective-permute-start(bf16[2,96,768]{2,1,0:T(8,128)(2,1)S(1)} %collective-permute-done.refs_1_), channel_id=1, source_target_pairs={{0,1},{1,0},{2,3},{3,2},{4,5},{5,4},{6,7},{7,6},{8,9},{9,8},{10,11... | collective-permute-start | bytes 884744 | tf_op jit(solution)/shard_map/ppermute | solution.py:557
  63.5 20.0 %collective-permute-start.14 = (bf16[2,96,768]{2,1,0:T(8,128)(2,1)S(1)}, bf16[2,96,768]{2,1,0:T(8,128)(2,1)S(1)}, u32[]{:S(2)}, u32[]{:S(2)}) collective-permute-start(bf16[2,96,768]{2,1,0:T(8,128)(2,1)S(1)} %collective-permute-done.6.refs_7_), channel_id=1, source_target_pairs={{0,1},{1,0},{2,3},{3,2},{4,5},{5,4},{6,7},{7,6},{8,9},{9,8},{10,11... | collective-permute-start | bytes 884744 | tf_op jit(solution)/shard_map/ppermute | solution.py:557
  70.9 12.7 %collective-permute-start.12 = (bf16[2,96,768]{2,1,0:T(8,128)(2,1)S(1)}, bf16[2,96,768]{2,1,0:T(8,128)(2,1)S(1)}, u32[]{:S(2)}, u32[]{:S(2)}) collective-permute-start(bf16[2,96,768]{2,1,0:T(8,128)(2,1)S(1)} %collective-permute-done.4.refs_5_), channel_id=1, source_target_pairs={{0,1},{1,0},{2,3},{3,2},{4,5},{5,4},{6,7},{7,6},{8,9},{9,8},{10,11... | collective-permute-start | bytes 884744 | tf_op jit(solution)/shard_map/ppermute | solution.py:557
  83.4 1.6 collective-permute-start.10
  157.1 53.1 %copy-start.25 = (f32[16,768]{1,0:T(8,128)S(1)}, f32[16,768]{1,0:T(8,128)}, u32[]{:S(2)}) copy-start(f32[16,768]{1,0:T(8,128)} %edge_forward.1) | copy-start | bytes 147460
  157.1 59.7 %collective-permute-start.20 = (f32[2,16,768]{2,1,0:T(8,128)S(1)}, f32[2,16,768]{2,1,0:T(8,128)S(1)}, u32[]{:S(2)}, u32[]{:S(2)}) collective-permute-start(f32[2,16,768]{2,1,0:T(8,128)S(1)} %pad_maximum_fusion.10), channel_id=1, source_target_pairs={{0,24},{4,28},{8,16},{12,20},{16,8},{20,12},{24,0},{28,4},{1,25},{... | collective-permute-start | bytes 294920 | tf_op jit(solution)/shard_map/ppermute | solution.py:552
  158.6 58.1 %collective-permute-start.19 = (f32[2,16,768]{2,1,0:T(8,128)S(1)}, f32[2,16,768]{2,1,0:T(8,128)S(1)}, u32[]{:S(2)}, u32[]{:S(2)}) collective-permute-start(f32[2,16,768]{2,1,0:T(8,128)S(1)} %pad_maximum_fusion.10), channel_id=1, source_target_pairs={{0,20},{4,16},{8,28},{12,24},{16,4},{20,0},{24,12},{28,8},{1,21},{... | collective-permute-start | bytes 294920 | tf_op jit(solution)/shard_map/ppermute | solution.py:552
  160.0 56.6 %collective-permute-start.18 = (f32[2,16,768]{2,1,0:T(8,128)S(1)}, f32[2,16,768]{2,1,0:T(8,128)S(1)}, u32[]{:S(2)}, u32[]{:S(2)}) collective-permute-start(f32[2,16,768]{2,1,0:T(8,128)S(1)} %pad_maximum_fusion.10), channel_id=1, source_target_pairs={{0,16},{4,20},{8,24},{12,28},{16,0},{20,4},{24,8},{28,12},{1,17},{... | collective-permute-start | bytes 294920 | tf_op jit(solution)/shard_map/ppermute | solution.py:552
  162.4 54.3 %collective-permute-start.17 = (f32[2,16,768]{2,1,0:T(8,128)S(1)}, f32[2,16,768]{2,1,0:T(8,128)S(1)}, u32[]{:S(2)}, u32[]{:S(2)}) collective-permute-start(f32[2,16,768]{2,1,0:T(8,128)S(1)} %pad_maximum_fusion.10), channel_id=1, source_target_pairs={{0,12},{4,8},{8,4},{12,0},{16,28},{20,24},{24,20},{28,16},{1,13},{... | collective-permute-start | bytes 294920 | tf_op jit(solution)/shard_map/ppermute | solution.py:552
  163.0 47.1 %collective-permute-start.15 = (f32[2,16,768]{2,1,0:T(8,128)S(1)}, f32[2,16,768]{2,1,0:T(8,128)S(1)}, u32[]{:S(2)}, u32[]{:S(2)}) collective-permute-start(f32[2,16,768]{2,1,0:T(8,128)S(1)} %pad_maximum_fusion.10), channel_id=1, source_target_pairs={{0,4},{4,0},{8,12},{12,8},{16,20},{20,16},{24,28},{28,24},{1,5},{5... | collective-permute-start | bytes 294920 | tf_op jit(solution)/shard_map/ppermute | solution.py:552
  210.2 4.7 collective-permute-start.16
  214.9 7.4 %collective-permute-start.21 = (f32[2,16,768]{2,1,0:T(8,128)S(1)}, f32[2,16,768]{2,1,0:T(8,128)S(1)}, u32[]{:S(2)}, u32[]{:S(2)}) collective-permute-start(f32[2,16,768]{2,1,0:T(8,128)S(1)} %pad_maximum_fusion.10), channel_id=1, source_target_pairs={{0,28},{4,24},{8,20},{12,16},{16,12},{20,8},{24,4},{28,0},{1,29},{... | collective-permute-start | bytes 294920 | tf_op jit(solution)/shard_map/ppermute | solution.py:552
  327.4 45.9 %collective-permute-start.22 = (bf16[2,768,768]{2,1,0:T(8,128)(2,1)}, bf16[2,768,768]{2,1,0:T(8,128)(2,1)}, u32[]{:S(2)}, u32[]{:S(2)}) collective-permute-start(bf16[2,768,768]{2,1,0:T(8,128)(2,1)} %get-tuple-element.79), channel_id=1, source_target_pairs={{0,1},{1,0},{2,3},{3,2},{4,5},{5,4},{6,7},{7,6},{8,9},{9,8},{10,11... | collective-permute-start | bytes 7077896 | tf_op jit(solution)/shard_map/ppermute | solution.py:557
  343.5 34.4 %collective-permute-start.38 = (bf16[2,768,768]{2,1,0:T(8,128)(2,1)}, bf16[2,768,768]{2,1,0:T(8,128)(2,1)S(1)}, u32[]{:S(2)}, u32[]{:S(2)}) collective-permute-start(bf16[2,768,768]{2,1,0:T(8,128)(2,1)} %get-tuple-element.103), channel_id=1, source_target_pairs={{0,1},{1,0},{2,3},{3,2},{4,5},{5,4},{6,7},{7,6},{8,9},{9,8},{10,11... | collective-permute-start | bytes 7077896 | tf_op jit(solution)/shard_map/ppermute | solution.py:557
  344.0 16.7 %copy-start.29 = (f32[8,768]{1,0:T(8,128)S(1)}, f32[8,768]{1,0:T(8,128)}, u32[]{:S(2)}) copy-start(f32[8,768]{1,0:T(8,128)} %get-tuple-element.117) | copy-start | bytes 73732
  344.0 16.7 %copy-start.30 = (f32[8,768]{1,0:T(8,128)S(1)}, f32[8,768]{1,0:T(8,128)}, u32[]{:S(2)}) copy-start(f32[8,768]{1,0:T(8,128)} %get-tuple-element.116) | copy-start | bytes 73732
  344.0 16.8 %copy-start.22 = (f32[64,768]{1,0:T(8,128)S(1)}, f32[64,768]{1,0:T(8,128)}, u32[]{:S(2)}) copy-start(f32[64,768]{1,0:T(8,128)} %get-tuple-element.118) | copy-start | bytes 589828
  344.0 18.4 %copy-start.26 = (bf16[128,768]{1,0:T(8,128)(2,1)S(1)}, bf16[128,768]{1,0:T(8,128)(2,1)}, u32[]{:S(2)}) copy-start(bf16[128,768]{1,0:T(8,128)(2,1)} %get-tuple-element.115) | copy-start | bytes 589828
  344.1 19.6 %copy-start.24 = (bf16[128,2304]{1,0:T(8,128)(2,1)S(1)}, bf16[128,2304]{1,0:T(8,128)(2,1)}, u32[]{:S(2)}) copy-start(bf16[128,2304]{1,0:T(8,128)(2,1)} %get-tuple-element.113) | copy-start | bytes 1769476
  360.7 30.0 %collective-permute-start.31 = (bf16[2,8,96,768]{3,2,1,0:T(8,128)(2,1)}, bf16[2,8,96,768]{3,2,1,0:T(8,128)(2,1)}, u32[]{:S(2)}, u32[]{:S(2)}) collective-permute-start(bf16[2,8,96,768]{3,2,1,0:T(8,128)(2,1)} %get-tuple-element.91), channel_id=1, source_target_pairs={{0,1},{1,0},{2,3},{3,2},{4,5},{5,4},{6,7},{7,6},{8,9},{9,8},{10,11... | collective-permute-start | bytes 7077896 | tf_op jit(solution)/shard_map/ppermute | solution.py:557
  360.9 11.6 %collective-permute-start.49 = (f32[4,16,768]{2,1,0:T(8,128)S(1)}, f32[4,16,768]{2,1,0:T(8,128)S(1)}, u32[]{:S(2)}, u32[]{:S(2)}) collective-permute-start(f32[4,16,768]{2,1,0:T(8,128)S(1)} %fusion.2), channel_id=1, source_target_pairs={{0,16},{4,20},{8,24},{12,28},{16,0},{20,4},{24,8},{28,12},{1,17},{... | collective-permute-start | bytes 589832 | tf_op jit(solution)/shard_map/ppermute | solution.py:552
  365.9 21.5 %collective-permute-start.45 = (bf16[2,96,768]{2,1,0:T(8,128)(2,1)}, bf16[2,96,768]{2,1,0:T(8,128)(2,1)}, u32[]{:S(2)}, u32[]{:S(2)}) collective-permute-start(bf16[2,96,768]{2,1,0:T(8,128)(2,1)} %dynamic-slice_bitcast_fusion), channel_id=1, source_target_pairs={{0,1},{1,0},{2,3},{3,2},{4,5},{5,4},{6,7},{7,6},{8,9},{9,8},{10,11... | collective-permute-start | bytes 884744 | tf_op jit(solution)/shard_map/ppermute | solution.py:557
  373.3 14.8 %collective-permute-start.50 = (f32[2,16,768]{2,1,0:T(8,128)}, f32[2,16,768]{2,1,0:T(8,128)}, u32[]{:S(2)}, u32[]{:S(2)}) collective-permute-start(f32[2,16,768]{2,1,0:T(8,128)} %dynamic-slice_bitcast_fusion.4), channel_id=1, source_target_pairs={{0,8},{4,12},{8,0},{12,4},{16,24},{20,28},{24,16},{28,20},{1,9},{5... | collective-permute-start | bytes 294920 | tf_op jit(solution)/shard_map/ppermute | solution.py:552
  377.4 29.1 %collective-permute-start.23 = (bf16[4,96,768]{2,1,0:T(8,128)(2,1)}, bf16[4,96,768]{2,1,0:T(8,128)(2,1)S(1)}, u32[]{:S(2)}, u32[]{:S(2)}) collective-permute-start(bf16[4,96,768]{2,1,0:T(8,128)(2,1)} %get-tuple-element.81), channel_id=1, source_target_pairs={{0,4},{4,0},{8,12},{12,8},{16,20},{20,16},{24,28},{28,24},{1,5},{5... | collective-permute-start | bytes 1769480 | tf_op jit(solution)/shard_map/ppermute | solution.py:552
  386.0 22.0 %collective-permute-start.39 = (bf16[4,96,768]{2,1,0:T(8,128)(2,1)}, bf16[4,96,768]{2,1,0:T(8,128)(2,1)}, u32[]{:S(2)}, u32[]{:S(2)}) collective-permute-start(bf16[4,96,768]{2,1,0:T(8,128)(2,1)} %get-tuple-element.105), channel_id=1, source_target_pairs={{0,4},{4,0},{8,12},{12,8},{16,20},{20,16},{24,28},{28,24},{1,5},{5... | collective-permute-start | bytes 1769480 | tf_op jit(solution)/shard_map/ppermute | solution.py:552
  387.5 22.5 %collective-permute-start.40 = (bf16[4,96,768]{2,1,0:T(8,128)(2,1)}, bf16[4,96,768]{2,1,0:T(8,128)(2,1)S(1)}, u32[]{:S(2)}, u32[]{:S(2)}) collective-permute-start(bf16[4,96,768]{2,1,0:T(8,128)(2,1)} %copy-done.17), channel_id=1, source_target_pairs={{0,2},{1,3},{2,0},{3,1},{4,6},{5,7},{6,4},{7,5},{8,10},{9,11},{10,... | collective-permute-start | bytes 1769480 | tf_op jit(solution)/shard_map/ppermute | solution.py:557
  388.1 31.1 %collective-permute-start.41 = (bf16[4,96,768]{2,1,0:T(8,128)(2,1)}, bf16[4,96,768]{2,1,0:T(8,128)(2,1)S(1)}, u32[]{:S(2)}, u32[]{:S(2)}) collective-permute-start(bf16[4,96,768]{2,1,0:T(8,128)(2,1)} %copy-done.16), channel_id=1, source_target_pairs={{0,6},{1,7},{2,4},{3,5},{4,2},{5,3},{6,0},{7,1},{8,14},{9,15},{10,... | collective-permute-start | bytes 1769480 | tf_op jit(solution)/shard_map/ppermute | solution.py:564
  390.7 15.8 %collective-permute-start.46 = (bf16[96,768]{1,0:T(8,128)(2,1)S(1)}, bf16[96,768]{1,0:T(8,128)(2,1)S(1)}, u32[]{:S(2)}, u32[]{:S(2)}) collective-permute-start(bf16[96,768]{1,0:T(8,128)(2,1)S(1)} %fusion.8), channel_id=1, source_target_pairs={{0,2},{1,3},{2,0},{3,1},{4,6},{5,7},{6,4},{7,5},{8,10},{9,11},{10,... | collective-permute-start | bytes 442376 | tf_op jit(solution)/shard_map/ppermute | solution.py:557
  406.5 38.0 %collective-permute-start.24 = (bf16[4,96,768]{2,1,0:T(8,128)(2,1)}, bf16[4,96,768]{2,1,0:T(8,128)(2,1)S(1)}, u32[]{:S(2)}, u32[]{:S(2)}) collective-permute-start(bf16[4,96,768]{2,1,0:T(8,128)(2,1)} %get-tuple-element.82), channel_id=1, source_target_pairs={{0,2},{1,3},{2,0},{3,1},{4,6},{5,7},{6,4},{7,5},{8,10},{9,11},{10,... | collective-permute-start | bytes 1769480 | tf_op jit(solution)/shard_map/ppermute | solution.py:557
  406.5 40.0 %collective-permute-start.25 = (bf16[4,96,768]{2,1,0:T(8,128)(2,1)}, bf16[4,96,768]{2,1,0:T(8,128)(2,1)}, u32[]{:S(2)}, u32[]{:S(2)}) collective-permute-start(bf16[4,96,768]{2,1,0:T(8,128)(2,1)} %get-tuple-element.83), channel_id=1, source_target_pairs={{0,6},{1,7},{2,4},{3,5},{4,2},{5,3},{6,0},{7,1},{8,14},{9,15},{10,... | collective-permute-start | bytes 1769480 | tf_op jit(solution)/shard_map/ppermute | solution.py:564
  408.0 54.8 %collective-permute-start.32 = (bf16[4,96,768]{2,1,0:T(8,128)(2,1)}, bf16[4,96,768]{2,1,0:T(8,128)(2,1)S(1)}, u32[]{:S(2)}, u32[]{:S(2)}) collective-permute-start(bf16[4,96,768]{2,1,0:T(8,128)(2,1)} %get-tuple-element.93), channel_id=1, source_target_pairs={{0,4},{4,0},{8,12},{12,8},{16,20},{20,16},{24,28},{28,24},{1,5},{5... | collective-permute-start | bytes 1769480 | tf_op jit(solution)/shard_map/ppermute | solution.py:552
  410.8 58.0 %collective-permute-start.33 = (bf16[4,96,768]{2,1,0:T(8,128)(2,1)}, bf16[4,96,768]{2,1,0:T(8,128)(2,1)S(1)}, u32[]{:S(2)}, u32[]{:S(2)}) collective-permute-start(bf16[4,96,768]{2,1,0:T(8,128)(2,1)} %get-tuple-element.94), channel_id=1, source_target_pairs={{0,2},{1,3},{2,0},{3,1},{4,6},{5,7},{6,4},{7,5},{8,10},{9,11},{10,... | collective-permute-start | bytes 1769480 | tf_op jit(solution)/shard_map/ppermute | solution.py:557
  420.0 50.1 %collective-permute-start.34 = (bf16[4,96,768]{2,1,0:T(8,128)(2,1)}, bf16[4,96,768]{2,1,0:T(8,128)(2,1)S(1)}, u32[]{:S(2)}, u32[]{:S(2)}) collective-permute-start(bf16[4,96,768]{2,1,0:T(8,128)(2,1)} %get-tuple-element.95), channel_id=1, source_target_pairs={{0,6},{1,7},{2,4},{3,5},{4,2},{5,3},{6,0},{7,1},{8,14},{9,15},{10,... | collective-permute-start | bytes 1769480 | tf_op jit(solution)/shard_map/ppermute | solution.py:564
  421.4 42.9 %copy-start.28 = (bf16[96,768]{1,0:T(8,128)(2,1)S(1)}, bf16[96,768]{1,0:T(8,128)(2,1)}, u32[]{:S(2)}) copy-start(bf16[96,768]{1,0:T(8,128)(2,1)} %copy-done.27) | copy-start | bytes 442372
  425.7 38.7 %copy-start.20 = (f32[2,96,768]{2,1,0:T(8,128)S(1)}, f32[2,96,768]{2,1,0:T(8,128)}, u32[]{:S(2)}) copy-start(f32[2,96,768]{2,1,0:T(8,128)} %copy-done.19) | copy-start | bytes 1769476
  425.7 45.9 %copy-start.7 = (bf16[4,96,768]{2,1,0:T(8,128)(2,1)S(1)}, bf16[4,96,768]{2,1,0:T(8,128)(2,1)}, u32[]{:S(2)}) copy-start(bf16[4,96,768]{2,1,0:T(8,128)(2,1)} %copy-done.6) | copy-start | bytes 1769476
  444.5 27.9 %collective-permute-start.42 = (bf16[96,768]{1,0:T(8,128)(2,1)S(1)}, bf16[96,768]{1,0:T(8,128)(2,1)S(1)}, u32[]{:S(2)}, u32[]{:S(2)}) collective-permute-start(bf16[96,768]{1,0:T(8,128)(2,1)S(1)} %get-tuple-element.109), channel_id=1, source_target_pairs={{0,8},{4,12},{8,0},{12,4},{16,24},{20,28},{24,16},{28,20},{1,9},{5... | collective-permute-start | bytes 442376 | tf_op jit(solution)/shard_map/ppermute | solution.py:552
  446.5 26.6 %collective-permute-start.43 = (bf16[96,768]{1,0:T(8,128)(2,1)S(1)}, bf16[96,768]{1,0:T(8,128)(2,1)S(1)}, u32[]{:S(2)}, u32[]{:S(2)}) collective-permute-start(bf16[96,768]{1,0:T(8,128)(2,1)S(1)} %get-tuple-element.110), channel_id=1, source_target_pairs={{0,16},{4,20},{8,24},{12,28},{16,0},{20,4},{24,8},{28,12},{1,17},{... | collective-permute-start | bytes 442376 | tf_op jit(solution)/shard_map/ppermute | solution.py:552
  462.8 12.1 %collective-permute-start.44 = (bf16[96,768]{1,0:T(8,128)(2,1)S(1)}, bf16[96,768]{1,0:T(8,128)(2,1)S(1)}, u32[]{:S(2)}, u32[]{:S(2)}) collective-permute-start(bf16[96,768]{1,0:T(8,128)(2,1)S(1)} %get-tuple-element.111), channel_id=1, source_target_pairs={{0,24},{4,28},{8,16},{12,20},{16,8},{20,12},{24,0},{28,4},{1,25},{... | collective-permute-start | bytes 442376 | tf_op jit(solution)/shard_map/ppermute | solution.py:552
  468.8 31.7 %collective-permute-start.51 = (f32[1,16,768]{2,1,0:T(8,128)S(1)}, f32[1,16,768]{2,1,0:T(8,128)S(1)}, u32[]{:S(2)}, u32[]{:S(2)}) collective-permute-start(f32[1,16,768]{2,1,0:T(8,128)S(1)} %constant_dynamic-slice_fusion), channel_id=1, source_target_pairs={{0,4},{4,0},{8,12},{12,8},{16,20},{20,16},{24,28},{28,24},{1,5},{5... | collective-permute-start | bytes 147464 | tf_op jit(solution)/shard_map/ppermute | solution.py:552
  470.1 25.0 %collective-permute-start.26 = (bf16[96,768]{1,0:T(8,128)(2,1)S(1)}, bf16[96,768]{1,0:T(8,128)(2,1)S(1)}, u32[]{:S(2)}, u32[]{:S(2)}) collective-permute-start(bf16[96,768]{1,0:T(8,128)(2,1)S(1)} %get-tuple-element.85), channel_id=1, source_target_pairs={{0,8},{4,12},{8,0},{12,4},{16,24},{20,28},{24,16},{28,20},{1,9},{5... | collective-permute-start | bytes 442376 | tf_op jit(solution)/shard_map/ppermute | solution.py:552
  472.4 9.5 %collective-permute-start.35 = (bf16[96,768]{1,0:T(8,128)(2,1)S(1)}, bf16[96,768]{1,0:T(8,128)(2,1)S(1)}, u32[]{:S(2)}, u32[]{:S(2)}) collective-permute-start(bf16[96,768]{1,0:T(8,128)(2,1)S(1)} %get-tuple-element.97), channel_id=1, source_target_pairs={{0,8},{4,12},{8,0},{12,4},{16,24},{20,28},{24,16},{28,20},{1,9},{5... | collective-permute-start | bytes 442376 | tf_op jit(solution)/shard_map/ppermute | solution.py:552
  473.1 18.5 %collective-permute-start.36 = (bf16[96,768]{1,0:T(8,128)(2,1)S(1)}, bf16[96,768]{1,0:T(8,128)(2,1)S(1)}, u32[]{:S(2)}, u32[]{:S(2)}) collective-permute-start(bf16[96,768]{1,0:T(8,128)(2,1)S(1)} %get-tuple-element.98), channel_id=1, source_target_pairs={{0,16},{4,20},{8,24},{12,28},{16,0},{20,4},{24,8},{28,12},{1,17},{... | collective-permute-start | bytes 442376 | tf_op jit(solution)/shard_map/ppermute | solution.py:552
  474.9 18.2 %collective-permute-start.37 = (bf16[96,768]{1,0:T(8,128)(2,1)S(1)}, bf16[96,768]{1,0:T(8,128)(2,1)S(1)}, u32[]{:S(2)}, u32[]{:S(2)}) collective-permute-start(bf16[96,768]{1,0:T(8,128)(2,1)S(1)} %get-tuple-element.99), channel_id=1, source_target_pairs={{0,24},{4,28},{8,16},{12,20},{16,8},{20,12},{24,0},{28,4},{1,25},{... | collective-permute-start | bytes 442376 | tf_op jit(solution)/shard_map/ppermute | solution.py:552
  481.9 17.4 %collective-permute-start.27 = (bf16[96,768]{1,0:T(8,128)(2,1)S(1)}, bf16[96,768]{1,0:T(8,128)(2,1)S(1)}, u32[]{:S(2)}, u32[]{:S(2)}) collective-permute-start(bf16[96,768]{1,0:T(8,128)(2,1)S(1)} %get-tuple-element.86), channel_id=1, source_target_pairs={{0,16},{4,20},{8,24},{12,28},{16,0},{20,4},{24,8},{28,12},{1,17},{... | collective-permute-start | bytes 442376 | tf_op jit(solution)/shard_map/ppermute | solution.py:552
  491.6 7.8 %collective-permute-start.28 = (bf16[96,768]{1,0:T(8,128)(2,1)S(1)}, bf16[96,768]{1,0:T(8,128)(2,1)S(1)}, u32[]{:S(2)}, u32[]{:S(2)}) collective-permute-start(bf16[96,768]{1,0:T(8,128)(2,1)S(1)} %get-tuple-element.87), channel_id=1, source_target_pairs={{0,24},{4,28},{8,16},{12,20},{16,8},{20,12},{24,0},{28,4},{1,25},{... | collective-permute-start | bytes 442376 | tf_op jit(solution)/shard_map/ppermute | solution.py:552
  493.3 11.6 %collective-permute-start.47 = (bf16[3,96,768]{2,1,0:T(8,128)(2,1)S(1)}, bf16[3,96,768]{2,1,0:T(8,128)(2,1)S(1)}, u32[]{:S(2)}, u32[]{:S(2)}) collective-permute-start(bf16[3,96,768]{2,1,0:T(8,128)(2,1)S(1)} %get-tuple-element.177), channel_id=1, source_target_pairs={{0,2},{1,3},{2,0},{3,1},{4,6},{5,7},{6,4},{7,5},{8,10},{9,11},{10,... | collective-permute-start | bytes 1327112 | tf_op jit(solution)/shard_map/ppermute | solution.py:557
  499.4 5.3 %collective-permute-start.29 = (bf16[96,768]{1,0:T(8,128)(2,1)S(1)}, bf16[96,768]{1,0:T(8,128)(2,1)S(1)}, u32[]{:S(2)}, u32[]{:S(2)}) collective-permute-start(bf16[96,768]{1,0:T(8,128)(2,1)S(1)} %add_convert_fusion.2), channel_id=1, source_target_pairs={{0,2},{1,3},{2,0},{3,1},{4,6},{5,7},{6,4},{7,5},{8,10},{9,11},{10,... | collective-permute-start | bytes 442376 | tf_op jit(solution)/shard_map/ppermute | solution.py:557
  500.5 1.3 collective-permute-start.52
  502.4 11.5 %collective-permute-start.53 = (f32[16,768]{1,0:T(8,128)}, f32[16,768]{1,0:T(8,128)}, u32[]{:S(2)}, u32[]{:S(2)}) collective-permute-start(f32[16,768]{1,0:T(8,128)} %add.243), channel_id=1, source_target_pairs={{0,2},{1,3},{2,0},{3,1},{4,6},{5,7},{6,4},{7,5},{8,10},{9,11},{10,... | collective-permute-start | bytes 147464 | tf_op jit(solution)/shard_map/ppermute | solution.py:557
  504.8 11.1 %collective-permute-start.30 = (bf16[2,96,768]{2,1,0:T(8,128)(2,1)S(1)}, bf16[2,96,768]{2,1,0:T(8,128)(2,1)S(1)}, u32[]{:S(2)}, u32[]{:S(2)}) collective-permute-start(bf16[2,96,768]{2,1,0:T(8,128)(2,1)S(1)} %pad_maximum_fusion.9), channel_id=1, source_target_pairs={{0,1},{1,0},{2,3},{3,2},{4,5},{5,4},{6,7},{7,6},{8,9},{9,8},{10,11... | collective-permute-start | bytes 884744 | tf_op jit(solution)/shard_map/ppermute | solution.py:557
  505.0 12.8 %collective-permute-start.48 = (bf16[2,3,96,768]{3,2,1,0:T(8,128)(2,1)S(1)}, bf16[2,3,96,768]{3,2,1,0:T(8,128)(2,1)S(1)}, u32[]{:S(2)}, u32[]{:S(2)}) collective-permute-start(bf16[2,3,96,768]{3,2,1,0:T(8,128)(2,1)S(1)} %pad_maximum_fusion.3), channel_id=1, source_target_pairs={{0,1},{1,0},{2,3},{3,2},{4,5},{5,4},{6,7},{7,6},{8,9},{9,8},{10,11... | collective-permute-start | bytes 2654216 | tf_op jit(solution)/shard_map/ppermute | solution.py:557
  (24 other events, 108.5 us)
Sparse Core Ops, SparseCore 0:
  12.4 134.3 all-gather.2

commit v2 on v1

v2 whole, which is shorter than its diff:
```python
from functools import partial
import jax
import jax.numpy as jnp
from jax import lax
from jax.experimental import pallas as pl
from jax.experimental.pallas import tpu as pltpu
from jax.sharding import PartitionSpec as P

HEAD_DIM = 64
PAIR = 2 * HEAD_DIM
EPSILON = 1e-05
NEGATIVE = -1e30
F32 = jnp.float32
BF16 = jnp.bfloat16
MIB = 1 << 20
LONG, SHORT = 6.0, 0.001


def dot_nn(left, right):
    return lax.dot_general(left, right, (((1,), (0,)), ((), ())), preferred_element_type=F32)


def dot_nt(left, right):
    return lax.dot_general(left, right, (((1,), (1,)), ((), ())), preferred_element_type=F32)


def dot_tn(left, right):
    return lax.dot_general(left, right, (((0,), (0,)), ((), ())), preferred_element_type=F32)


def norm_parts(values):
    center = values - jnp.mean(values, axis=-1, keepdims=True)
    spread = jnp.mean(center * center, axis=-1, keepdims=True)
    inverse = lax.rsqrt(spread + EPSILON)
    return center * inverse, inverse


def norm_back(grad, unit, inverse, gain):
    scaled = grad * gain
    first = jnp.mean(scaled, axis=-1, keepdims=True)
    second = jnp.mean(scaled * unit, axis=-1, keepdims=True)
    return inverse * (scaled - first - unit * second)


def gelu_parts(hidden):
    phi = 0.5 + 0.5 * lax.erf(hidden * 0.5 ** 0.5)
    bell = jnp.exp(hidden * hidden * -0.5) * 0.3989422804014327
    return hidden * phi, phi + hidden * bell


def halves(pair, first_half):
    zero = jnp.zeros_like(pair)
    return jnp.concatenate([jnp.where(first_half, pair, zero), jnp.where(first_half, zero, pair)], axis=0)


def pair_forward(query, key, value, first_half, same=None):
    rows = query.shape[0]
    scores = dot_nt(key, halves(query * BF16(HEAD_DIM ** -0.5), first_half))
    if same is not None:
        scores = jnp.where(same, scores, NEGATIVE)
    raised = jnp.exp(scores - jnp.max(scores, axis=0, keepdims=True))
    probs = (raised * (1.0 / jnp.sum(raised, axis=0, keepdims=True))).astype(BF16)
    both = dot_tn(probs, value)
    return probs, jnp.where(first_half, both[:rows], both[rows:])


def pair_backward(query, key, value, probs, grad_mixed, first_half):
    rows = query.shape[0]
    grad_both = halves(grad_mixed, first_half)
    query_both = halves(query * BF16(HEAD_DIM ** -0.5), first_half)
    grad_probs = dot_nt(value, grad_both)
    wide = probs.astype(F32)
    grad_scores = (wide * (grad_probs - jnp.sum(grad_probs * wide, axis=0, keepdims=True))).astype(BF16)
    grad_value = dot_nn(probs, grad_both)
    grad_key = dot_nn(grad_scores, query_both)
    both = dot_tn(grad_scores, key)
    grad_query = jnp.where(first_half, both[:rows], both[rows:]) * (HEAD_DIM ** -0.5)
    return grad_query, grad_key, grad_value


def lane_half(shape):
    return lax.broadcasted_iota(jnp.int32, shape, 1) % PAIR < HEAD_DIM


def square(value):
    return value.reshape(-1, value.shape[-1])


def up_block(ref, part):
    return square(ref[:, part])


def down_block(ref, part):
    count = ref.shape[0] // 4
    return square(ref[part * count : (part + 1) * count])


def whole(shape):
    return pl.BlockSpec(shape, lambda *at: (0,) * len(shape), pipeline_mode=pl.Buffered(1))


ANYWHERE = pl.BlockSpec(memory_space=pl.ANY)


def cost(flops, moved, weight=1.0):
    return pl.CostEstimate(flops=int(flops * weight), bytes_accessed=int(moved * weight), transcendentals=0)


def rows_call(kernel, name, block, span, rowed, fixed, outs, flops, prior=(), after=(), extra=(), ids=None, scratch=(), weight=1.0):
    first, steps = span

    def cut(value):
        array, ratio = value if isinstance(value, tuple) else (value, 1)
        shape = (block // ratio,) + array.shape[1:]
        return array, pl.BlockSpec(shape, lambda i, *ids: (i + first,) + (0,) * (len(shape) - 1))

    ins = [cut(value) for value in rowed] + list(fixed)
    results = [cut(value) for value in outs] + [(shape, whole(shape.shape)) for shape in extra]
    unread = list(prior) + list(after)
    lead = 0 if ids is None else 1
    moved = sum(value.size * value.dtype.itemsize for value, unused in ins + results) // 2

    def run(*refs):
        start = lead + len(ins)
        kernel(*refs[:start], *refs[start + len(unread) :])

    return pl.pallas_call(
        run,
        out_shape=tuple(jax.ShapeDtypeStruct(shape.shape, shape.dtype) for shape, unused in results),
        grid_spec=pltpu.PrefetchScalarGridSpec(
            num_scalar_prefetch=lead,
            grid=(steps,),
            in_specs=[spec for unused, spec in ins] + [ANYWHERE] * len(unread),
            out_specs=[spec for unused, spec in results],
            scratch_shapes=list(scratch),
        ),
        input_output_aliases={lead + len(ins) + i: i for i in range(len(prior))},
        compiler_params=pltpu.CompilerParams(vmem_limit_bytes=58 * MIB),
        cost_estimate=cost(2 * flops * steps * block, moved, weight),
        name=name,
    )(*([] if ids is None else [ids]), *[array for array, unused in ins], *unread)


def shape_of(shape, dtype):
    return jax.ShapeDtypeStruct(shape, dtype)


def fetch_pieces(ids_ref, plan, parts, out_ref, sems, start=0, owner_first=False):
    me, core = ids_ref[0], ids_ref[1] & 1
    rows = out_ref.shape[2]
    base = 2 * len(plan) if owner_first else 0
    copies = []
    for number, (which, mask, side) in enumerate(plan):
        part = parts[which]
        owner_core = core if side == 0 else 1 - core
        for share in range(2):
            piece = part.at[share] if part.shape[-2] == rows else part.at[share, pl.ds(start, rows)]
            place = (2 * owner_core + share, me ^ mask)
            target = out_ref.at[place[::-1] if owner_first else place]
            copies.append(pltpu.make_async_copy(piece, target, sems.at[base + 2 * number + share]))
    for copy in copies:
        copy.start()
    return copies


def fetch_halves(ids_ref, parts, out_ref, sems, start=0, owner_first=False):
    core = ids_ref[1] & 1
    rows = out_ref.shape[2]
    base = 4 if owner_first else 0
    copies = []
    for side, part in enumerate(parts):
        owner_core = core if side == 0 else 1 - core
        for share in range(2):
            piece = part.at[:, share] if part.shape[-2] == rows else part.at[:, share, pl.ds(start, rows)]
            block = 2 * owner_core + share
            target = out_ref.at[:, block] if owner_first else out_ref.at[block]
            copies.append(pltpu.make_async_copy(piece, target, sems.at[base + 2 * side + share]))
    for copy in copies:
        copy.start()
    return copies


def attention_rows(seg_length, x_ref, wqo_ref, proj_ref, probs_ref, mixed_ref, pre_ref):
    rows, width = x_ref.shape
    pairs = width // PAIR
    for part in range(3):
        proj_ref[:, part * width : (part + 1) * width] = dot_nn(x_ref[...], square(wqo_ref[part])).astype(BF16)
    first_half = lane_half((seg_length, PAIR))
    for seg in range(rows // seg_length):
        span = slice(seg * seg_length, (seg + 1) * seg_length)
        for pair in range(pairs):
            cols = [slice(part * width + pair * PAIR, part * width + (pair + 1) * PAIR) for part in range(3)]
            probs, mixed = pair_forward(
                proj_ref[span, cols[0]], proj_ref[span, cols[1]], proj_ref[span, cols[2]], first_half
            )
            probs_ref[seg, pair] = probs
            mixed_ref[span, cols[0]] = mixed.astype(BF16)
    pre_ref[...] = x_ref[...].astype(F32) + dot_nn(mixed_ref[...], square(wqo_ref[3]))


def attention_first_kernel(seg_length, plan, count, ids_ref, x_ref, *refs):
    parts, (proj_ref, probs_ref, mixed_ref, pre_ref, wqo_ref, sems) = refs[:count], refs[count:]

    @pl.when(pl.program_id(0) == 0)
    def fetch():
        for copy in fetch_pieces(ids_ref, plan, parts, wqo_ref, sems):
            copy.wait()

    attention_rows(seg_length, x_ref, wqo_ref, proj_ref, probs_ref, mixed_ref, pre_ref)


def attention_shapes(rows, width, seg_length):
    probs = shape_of((rows // seg_length, width // PAIR, seg_length, 2 * seg_length), BF16)
    return [
        shape_of((rows, 3 * width), BF16), (probs, seg_length), shape_of((rows, width), BF16), shape_of((rows, width), F32),
    ]


def attention_forward(rows_in, weight, seg_length, block, span, prior=(), after=(), pieces=None, ids=None):
    rows, width = rows_in.shape
    outs = attention_shapes(rows, width, seg_length)
    flops = width * (4 * width + 8 * seg_length)
    if pieces is None:
        return rows_call(
            partial(attention_rows, seg_length), "attention_forward", block, span, [rows_in],
            [(weight, whole(weight.shape))], outs, flops, prior, after, weight=SHORT,
        )
    plan, parts, shape = pieces
    return rows_call(
        partial(attention_first_kernel, seg_length, plan, len(parts)), "attention_forward", block, span, [rows_in],
        [(part, ANYWHERE) for part in parts], outs, flops, prior, after, [shape], ids,
        [pltpu.SemaphoreType.DMA((2 * len(plan),))], SHORT,
    )


def ffn_rows(pre_ref, wup_ref, wdown_ref, gains_ref, shifts_ref, low_ref, act_ref, slope_ref, pre2_ref):
    width = pre_ref.shape[1]
    unit, unused = norm_parts(pre_ref[...])
    total = unit * gains_ref[0:1].astype(F32) + shifts_ref[0:1].astype(F32)
    low = total.astype(BF16)
    low_ref[...] = low
    held = dot_nn(low, square(wup_ref[0]))
    for part in range(4):
        cols = slice(part * width, (part + 1) * width)
        ahead = dot_nn(low, square(wup_ref[part + 1])) if part < 3 else None
        act, slope = gelu_parts(held)
        act_ref[:, cols] = act.astype(BF16)
        slope_ref[:, cols] = slope.astype(BF16)
        total = total + dot_nn(act_ref[:, cols], down_block(wdown_ref, part))
        held = ahead
    pre2_ref[...] = total


def ffn_forward(pre_first, w_up, w_down, gains, shifts, block, span, prior=(), after=()):
    rows, width = pre_first.shape
    wide = shape_of((rows, 4 * width), BF16)
    return rows_call(
        ffn_rows, "ffn_forward", block, span, [pre_first],
        [(value, whole(value.shape)) for value in (w_up, w_down, gains, shifts)],
        [shape_of((rows, width), BF16), wide, wide, shape_of((rows, width), F32)], 8 * width * width, prior, after,
    )


def edge_rows(pre_ref, wup_ref, wdown_ref, gains_ref, shifts_ref, out_ref):
    unit, unused = norm_parts(pre_ref[...])
    total = unit * gains_ref[0:1].astype(F32) + shifts_ref[0:1].astype(F32)
    low = total.astype(BF16)
    for part in range(4):
        act, unused = gelu_parts(dot_nn(low, square(wup_ref[part])))
        total = total + dot_nn(act.astype(BF16), down_block(wdown_ref, part))
    unit, unused = norm_parts(total)
    out_ref[...] = unit * gains_ref[1:2].astype(F32) + shifts_ref[1:2].astype(F32)


def edge_first_kernel(ids_ref, pre_ref, gains_ref, shifts_ref, half_ref, other_ref, out_ref, wup_ref, wdown_ref, sems):
    parts = (half_ref, other_ref)
    up = fetch_halves(ids_ref, parts, wup_ref, sems)
    down = fetch_halves(ids_ref, parts, wdown_ref, sems, wup_ref.shape[2], True)
    for copy in up + down:
        copy.wait()
    edge_rows(pre_ref, wup_ref, wdown_ref, gains_ref, shifts_ref, out_ref)


def edge_forward(pre_edge, weights, gains, shifts, pieces=None, ids=None):
    rows, width = pre_edge.shape
    norms = [(gains, whole(gains.shape)), (shifts, whole(shifts.shape))]
    outs = [shape_of((rows, width), F32)]
    if pieces is None:
        return rows_call(
            edge_rows, "edge_forward", rows, (0, 1), [pre_edge], [(value, whole(value.shape)) for value in weights] + norms,
            outs, 60 * width * width,
        )
    parts, shapes = pieces
    return rows_call(
        edge_first_kernel, "edge_forward", rows, (0, 1), [pre_edge], norms + [(part, ANYWHERE) for part in parts], outs,
        60 * width * width, extra=shapes, ids=ids, scratch=[pltpu.SemaphoreType.DMA((8,))],
    )


def norm_rows(seg_length, cot_ref, pre2_ref, edge_ref, cls_ref, gains_ref, shifts_ref, out_ref, branch_ref, grad_ref, sums_ref):
    rows, width = cot_ref.shape
    top = lax.broadcasted_iota(jnp.int32, (seg_length, width), 0) == 0

    def with_edge(values, edge):
        parts = [
            jnp.where(top, edge[seg], values[seg * seg_length : (seg + 1) * seg_length]) for seg in range(rows // seg_length)
        ]
        return jnp.concatenate(parts, axis=0) if len(parts) > 1 else parts[0]

    gain = gains_ref[1:2].astype(F32)
    unit, inverse = norm_parts(pre2_ref[...])
    out_ref[...] = with_edge(unit * gain + shifts_ref[1:2].astype(F32), cls_ref).astype(BF16)
    grad = with_edge(cot_ref[...].astype(F32), edge_ref)
    pre_grad = norm_back(grad, unit, inverse, gain)
    grad_ref[...] = pre_grad
    branch_ref[...] = pre_grad.astype(BF16)

    @pl.when(pl.program_id(0) == 0)
    def start_sums():
        sums_ref[...] = jnp.zeros_like(sums_ref)

    sums_ref[1:2] += jnp.sum(grad * unit, axis=0, keepdims=True)
    sums_ref[4:5] += jnp.sum(grad, axis=0, keepdims=True)


def norm_backward(cot, pre_second, edge, cls_new, gains, shifts, seg_length, block, after):
    rows, width = cot.shape
    return rows_call(
        partial(norm_rows, seg_length), "norm_backward", block, (0, rows // block),
        [cot, pre_second, (edge, seg_length), (cls_new, seg_length)],
        [(gains, whole(gains.shape)), (shifts, whole(shifts.shape))],
        [shape_of((rows, width), BF16), shape_of((rows, width), BF16), shape_of((rows, width), F32)], 2 * width,
        after=after, extra=[shape_of((8, width), F32)],
    )


def ffn_back_rows(branch_ref, grad2_ref, pre1_ref, slope_ref, wup_ref, wdown_ref, gains_ref, gradh_ref, grad1_ref, low1_ref, sums_ref):
    width = branch_ref.shape[1]
    total = grad2_ref[...]
    for part in range(4):
        cols = slice(part * width, (part + 1) * width)
        grad_act = dot_nt(branch_ref[...], down_block(wdown_ref, part))
        grad_hidden = (grad_act * slope_ref[:, cols].astype(F32)).astype(BF16)
        gradh_ref[:, cols] = grad_hidden
        total = total + dot_nt(grad_hidden, square(wup_ref[part]))
    unit, inverse = norm_parts(pre1_ref[...])
    grad1 = norm_back(total, unit, inverse, gains_ref[0:1].astype(F32))
    grad1_ref[...] = grad1
    low1_ref[...] = grad1.astype(BF16)

    @pl.when(pl.program_id(0) == 0)
    def start_sums():
        sums_ref[...] = jnp.zeros_like(sums_ref)

    sums_ref[0:1] += jnp.sum(total * unit, axis=0, keepdims=True)
    sums_ref[3:4] += jnp.sum(total, axis=0, keepdims=True)


def ffn_backward(branch, grad2, pre_first, slope, w_up, w_down, gains, block, span, weight, prior=(), after=()):
    rows, width = branch.shape
    return rows_call(
        ffn_back_rows, "ffn_backward", block, span, [branch, grad2, pre_first, slope],
        [(w_up, whole(w_up.shape)), (w_down, whole(w_down.shape)), (gains, whole(gains.shape))],
        [shape_of((rows, 4 * width), BF16), shape_of((rows, width), F32), shape_of((rows, width), BF16)],
        8 * width * width, prior, after, [shape_of((8, width), F32)], weight=weight,
    )


def attention_back_rows(seg_length, grad1_ref, low1_ref, proj_ref, probs_ref, wqo_ref, gradp_ref, input_ref, gradm_ref):
    rows, width = grad1_ref.shape
    pairs = width // PAIR
    gradm_ref[...] = dot_nt(low1_ref[...], square(wqo_ref[3])).astype(BF16)
    first_half = lane_half((seg_length, PAIR))
    for seg in range(rows // seg_length):
        span = slice(seg * seg_length, (seg + 1) * seg_length)
        for pair in range(pairs):
            cols = [slice(part * width + pair * PAIR, part * width + (pair + 1) * PAIR) for part in range(3)]
            grads = pair_backward(
                proj_ref[span, cols[0]], proj_ref[span, cols[1]], proj_ref[span, cols[2]],
                probs_ref[seg, pair], gradm_ref[span, cols[0]], first_half,
            )
            for place, grad in zip(cols, grads):
                gradp_ref[span, place] = grad.astype(BF16)
    total = grad1_ref[...]
    for part in range(3):
        total = total + dot_nt(gradp_ref[:, part * width : (part + 1) * width], square(wqo_ref[part]))
    input_ref[...] = total


def attention_backward(grad1, low1, proj, probs, w_qo, seg_length, block, span, prior=(), after=()):
    rows, width = grad1.shape
    return rows_call(
        partial(attention_back_rows, seg_length), "attention_backward", block, span,
        [grad1, low1, proj, (probs, seg_length)], [(w_qo, whole(w_qo.shape))],
        [shape_of((rows, 3 * width), BF16), shape_of((rows, width), F32)],
        width * (4 * width + 16 * seg_length), prior, after, scratch=[pltpu.VMEM((block, width), BF16)], weight=SHORT,
    )


def cross_kernel(
    local, fetch, ids_ref, rows_ref, cot_ref, keyc_ref, keyr_ref, place_ref, table_ref, gains_ref, shifts_ref, *refs
):
    parts, refs = (refs[:2], refs[2:]) if fetch else (refs[:1], refs[1:])
    new_ref, edge_ref, low_ref, gradp_ref, mixed_ref, gradz_ref, sums_ref, table_grad_ref, proj_ref, probs_ref, gradm_ref = refs[:11]
    wc_ref = parts[0]
    if fetch:
        wc_ref, sems = refs[11:]
        for copy in fetch_halves(ids_ref, parts, wc_ref, sems):
            copy.wait()
    count, width = rows_ref.shape
    pairs = width // PAIR
    entries = table_ref.shape[0]
    picks = place_ref[...] == lax.broadcasted_iota(jnp.int32, (count, entries), 1)
    embedded = rows_ref[...] + dot_nn(picks.astype(BF16), table_ref[...])
    low = embedded.astype(BF16)
    low_ref[...] = low
    for part in range(3):
        proj_ref[:, part * width : (part + 1) * width] = dot_nn(low, square(wc_ref[part])).astype(BF16)
    first_half = lane_half((count, PAIR))
    same = keyc_ref[...] == keyr_ref[...]
    places = [
        [slice(part * width + pair * PAIR, part * width + (pair + 1) * PAIR) for part in range(3)] for pair in range(pairs)
    ]
    for pair, cols in enumerate(places):
        probs, mixed = pair_forward(proj_ref[:, cols[0]], proj_ref[:, cols[1]], proj_ref[:, cols[2]], first_half, same)
        probs_ref[pair] = probs
        mixed_ref[:, cols[0]] = mixed.astype(BF16)
    pre_third = embedded + dot_nn(mixed_ref[...], square(wc_ref[3]))
    unit, inverse = norm_parts(pre_third)
    gain = gains_ref[2:3].astype(F32)
    new_ref[...] = unit[:local] * gain + shifts_ref[2:3].astype(F32)
    grad_out = cot_ref[...]
    grad_third = norm_back(grad_out, unit, inverse, gain)
    sums_ref[...] = jnp.zeros_like(sums_ref)
    sums_ref[2:3] = jnp.sum(grad_out[:local] * unit[:local], axis=0, keepdims=True)
    sums_ref[5:6] = jnp.sum(grad_out[:local], axis=0, keepdims=True)
    gradz = grad_third.astype(BF16)
    gradz_ref[...] = gradz
    gradm_ref[...] = dot_nt(gradz, square(wc_ref[3])).astype(BF16)
    for pair, cols in enumerate(places):
        grads = pair_backward(
            proj_ref[:, cols[0]], proj_ref[:, cols[1]], proj_ref[:, cols[2]], probs_ref[pair], gradm_ref[:, cols[0]], first_half
        )
        for place, grad in zip(cols, grads):
            gradp_ref[:, place] = grad.astype(BF16)
    grad_edge = grad_third[:local]
    for part in range(3):
        grad_edge = grad_edge + dot_nt(gradp_ref[:local, part * width : (part + 1) * width], square(wc_ref[part]))
    edge_ref[...] = grad_edge
    table_grad_ref[...] = lax.dot_general(
        picks[:local].astype(F32), grad_edge, (((0,), (0,)), ((), ())),
        precision=lax.Precision.HIGHEST, preferred_element_type=F32,
    )


def cross_block(ids, local, edge_rows, edge_cot, key_col, key_row, place, table, gains, shifts, parts, shape):
    count, width = edge_rows.shape
    read = [edge_rows, edge_cot, key_col, key_row, place, table, gains, shifts]
    part_specs, fetched = [whole(part.shape) for part in parts], []
    if shape is not None:
        part_specs = [ANYWHERE] * len(parts)
        fetched = [pltpu.VMEM(shape.shape, BF16), pltpu.SemaphoreType.DMA((4,))]
    shapes = (
        jax.ShapeDtypeStruct((local, width), F32),
        jax.ShapeDtypeStruct((local, width), F32),
        jax.ShapeDtypeStruct((count, width), BF16),
        jax.ShapeDtypeStruct((count, 3 * width), BF16),
        jax.ShapeDtypeStruct((count, width), BF16),
        jax.ShapeDtypeStruct((count, width), BF16),
        jax.ShapeDtypeStruct((8, width), F32),
        jax.ShapeDtypeStruct(table.shape, F32),
    )
    return pl.pallas_call(
        partial(cross_kernel, local, shape is not None),
        out_shape=shapes,
        grid_spec=pltpu.PrefetchScalarGridSpec(
            num_scalar_prefetch=1,
            grid=(1,),
            in_specs=[whole(value.shape) for value in read] + part_specs,
            out_specs=[whole(value.shape) for value in shapes],
            scratch_shapes=[
                pltpu.VMEM((count, 3 * width), BF16),
                pltpu.VMEM((width // PAIR, count, 2 * count), BF16),
                pltpu.VMEM((count, width), BF16),
            ] + fetched,
        ),
        compiler_params=pltpu.CompilerParams(vmem_limit_bytes=56 * MIB),
        cost_estimate=cost(10_000_000_000, width * width * 8),
        name="cross_block",
    )(ids, *read, *parts)


def cols_grad_kernel(ids_ref, left_ref, right_ref, *refs):
    refs[-1][0] = dot_tn(left_ref[...], right_ref[...]).astype(BF16)


def joint_grad_kernel(side, ids_ref, left_ref, last_left_ref, right_ref, last_right_ref, *refs):
    block = half_block(side, pl.program_id(0), ids_ref)

    @pl.when(block < 3)
    def main():
        refs[-1][0] = dot_tn(left_ref[...], right_ref[...]).astype(BF16)

    @pl.when(block == 3)
    def last():
        refs[-1][0] = dot_tn(last_left_ref[...], last_right_ref[...]).astype(BF16)


def half_block(side, step, ids):
    return 2 * ((ids[1] & 1) ^ side) + step


def half_grads(kernel, name, side, ids, operands, specs, after, weight):
    rows, width = operands[0].shape
    return pl.pallas_call(
        kernel,
        out_shape=jax.ShapeDtypeStruct((2, width, width), BF16),
        grid_spec=pltpu.PrefetchScalarGridSpec(
            num_scalar_prefetch=1,
            grid=(2,),
            in_specs=specs + [ANYWHERE] * len(after),
            out_specs=pl.BlockSpec((1, width, width), lambda j, ids: (j, 0, 0)),
        ),
        compiler_params=pltpu.CompilerParams(vmem_limit_bytes=56 * MIB),
        cost_estimate=cost(4 * rows * width * width, 10 * rows * width, weight),
        name=name,
    )(ids, *operands, *after)


def cols_grads(side, ids, left, right, after, weight):
    rows, width = left.shape
    specs = [
        whole(left.shape),
        pl.BlockSpec((rows, width), lambda j, ids: (0, half_block(side, j, ids))),
    ]
    return half_grads(cols_grad_kernel, "cols_grads", side, ids, [left, right], specs, after, weight)


def joint_grads(side, ids, left, last_left, right, last_right, after, weight):
    rows, width = left.shape
    specs = [
        whole(left.shape),
        whole(left.shape),
        pl.BlockSpec((rows, width), lambda j, ids: (0, jnp.minimum(half_block(side, j, ids), 2))),
        whole(left.shape),
    ]
    operands = [left, last_left, right, last_right]
    return half_grads(partial(joint_grad_kernel, side), "joint_grads", side, ids, operands, specs, after, weight)


def rows_grad_kernel(ids_ref, left_ref, right_ref, *refs):
    send_ref, keep_ref, held_ref = refs[-3:]
    core = ids_ref[1] & 1
    held_ref[...] = dot_tn(left_ref[...], right_ref[...]).reshape(held_ref.shape)
    for share in range(2):
        send_ref[share] = held_ref[:, 2 * (1 - core) + share].astype(BF16)
        keep_ref[share] = held_ref[:, 2 * core + share].astype(BF16)


def rows_grads(ids, left, right, count, after):
    rows, width = right.shape
    hidden = left.shape[1]
    shard_rows = hidden // count // 4
    owners = count // 4
    half = jax.ShapeDtypeStruct((2, count, shard_rows, width), BF16)
    out_spec = pl.BlockSpec((2, owners, shard_rows, width), lambda j, ids: (0, j, 0, 0))
    return pl.pallas_call(
        rows_grad_kernel,
        out_shape=(half, half),
        grid_spec=pltpu.PrefetchScalarGridSpec(
            num_scalar_prefetch=1,
            grid=(4,),
            in_specs=[
                pl.BlockSpec((rows, hidden // 4), lambda j, ids: (0, j)),
                pl.BlockSpec((rows, width), lambda j, ids: (0, 0), pipeline_mode=pl.Buffered(1)),
            ] + [ANYWHERE] * len(after),
            out_specs=[out_spec, out_spec],
            scratch_shapes=[pltpu.VMEM((owners, 4, shard_rows, width), F32)],
        ),
        compiler_params=pltpu.CompilerParams(vmem_limit_bytes=56 * MIB),
        cost_estimate=cost(2 * rows * width * hidden, 10 * rows * width),
        name="rows_grads",
    )(ids, left, right, *after)


def later(value, *first):
    return lax.optimization_barrier((value,) + first)[0]


def seg_swap(value, mask):
    count = lax.axis_size("seg")
    return lax.ppermute(value, "seg", [(i, i ^ mask) for i in range(count)])


def rep_swap(value, mask):
    count = lax.axis_size("rep")
    return lax.ppermute(value, "rep", [(i, i ^ mask) for i in range(count)])


def both_swap(value, seg_mask, rep_mask):
    reps = lax.axis_size("rep")
    total = lax.axis_size("seg") * reps
    pairs = [(i, ((i // reps) ^ seg_mask) * reps + ((i % reps) ^ rep_mask)) for i in range(total)]
    return lax.ppermute(value, ("seg", "rep"), pairs)


def place_kernel(plan, count, owner_first, ids_ref, *refs):
    for copy in fetch_pieces(ids_ref, plan, refs[:count], refs[count], refs[count + 1], 0, owner_first):
        copy.wait()


def put_in_place(ids, pieces, owner_first=False):
    plan, parts, shape = pieces
    return pl.pallas_call(
        partial(place_kernel, plan, len(parts), owner_first),
        out_shape=shape,
        in_specs=[pl.BlockSpec(memory_space=pltpu.SMEM)] + [ANYWHERE] * len(parts),
        out_specs=pl.BlockSpec(memory_space=pltpu.VMEM),
        scratch_shapes=[pltpu.SemaphoreType.DMA((4 * len(plan),))],
        compiler_params=pltpu.CompilerParams(vmem_limit_bytes=32 * MIB),
        cost_estimate=cost(0, 4 * shape.size),
        name="put_in_place",
    )(ids, *parts)


def own_half(ids, blocks):
    return lax.dynamic_slice_in_dim(blocks, 2 * (ids[1] & 1), 2, 0)


def far_pieces(piece):
    return [piece] + [seg_swap(piece, mask) for mask in range(2, lax.axis_size("seg"), 2)]


def after_all(value, first):
    return later(value, *first) if first else value


def gather_singly(piece, evens, firsts):
    held, crossed = [], []
    for number, even in enumerate(evens):
        before = held[-1:] + [rep_swap(part, 1) for part in held[-4:-2]]
        crossed += before[1:]
        held += [even, seg_swap(after_all(even, before + firsts.get(number, [])), 1)]
    crossed += [rep_swap(part, 1) for part in held[-4:-1]] + [rep_swap(after_all(held[-1], firsts.get(-1, [])), 1)]
    return held, crossed


def pieces_of(held, crossed, shapes):
    count = len(held)
    return [(i, i % count, i // count) for i in range(2 * count)], held + crossed, shapes


class Gather:
    def __init__(self, piece):
        self.piece, self.came = piece, far_pieces(piece)

    def across(self, *first):
        self.evens = jnp.stack(self.came[:1] + [later(value, *first) for value in self.came[1:]], axis=0)
        self.came = seg_swap(self.evens, 1)

    def finish(self, *first):
        return jnp.stack([self.evens, later(self.came, *first)], axis=1).reshape((-1,) + self.piece.shape)


def spread_kernel(ids_ref, keep_ref, came_ref, stay_ref, x_ref, y_ref, xy_ref):
    near, across = ids_ref[0] & 1, ids_ref[1] >> 1

    def total(share, side):
        return (keep_ref[share, 0, side].astype(F32) + came_ref[share, 0, side].astype(F32)).astype(BF16)

    stay_ref[0] = total(across, near)
    x_ref[0] = total(across, 1 - near)
    y_ref[0] = total(1 - across, near)
    xy_ref[0] = total(1 - across, 1 - near)


def spread(ids, keep, came):
    unused, count, rows, width = keep.shape
    far = count // 2
    shape = (2, far, 2, rows, width)
    in_spec = pl.BlockSpec((2, 1, 2, rows, width), lambda j: (0, j, 0, 0, 0))
    out_spec = pl.BlockSpec((1, rows, width), lambda j: (j, 0, 0))
    out = jax.ShapeDtypeStruct((far, rows, width), BF16)
    return pl.pallas_call(
        spread_kernel,
        out_shape=(out,) * 4,
        grid=(far,),
        in_specs=[pl.BlockSpec(memory_space=pltpu.SMEM), in_spec, in_spec],
        out_specs=[out_spec] * 4,
        compiler_params=pltpu.CompilerParams(vmem_limit_bytes=32 * MIB),
        cost_estimate=cost(0, 12 * count * rows * width),
        name="spread",
    )(ids, keep.reshape(shape), came.reshape(shape))


def settle_kernel(ids_ref, a_ref, b_ref, c_ref, d_ref, *outs):
    far = ids_ref[0] >> 1
    for mask, out in enumerate(outs):
        place = far ^ mask
        total = (a_ref[place].astype(F32) + b_ref[place].astype(F32)) + (c_ref[place].astype(F32) + d_ref[place].astype(F32))
        out[...] = total.astype(BF16)


def settle(ids, parts):
    far, rows, width = parts[0].shape
    whole_spec = pl.BlockSpec(memory_space=pltpu.VMEM)
    return pl.pallas_call(
        settle_kernel,
        out_shape=(jax.ShapeDtypeStruct((rows, width), BF16),) * far,
        in_specs=[pl.BlockSpec(memory_space=pltpu.SMEM)] + [whole_spec] * 4,
        out_specs=[whole_spec] * far,
        compiler_params=pltpu.CompilerParams(vmem_limit_bytes=32 * MIB),
        cost_estimate=cost(0, 10 * far * rows * width),
        name="settle",
    )(ids, *parts)


def halve(value, axis, bit):
    own = lax.dynamic_index_in_dim(value, bit, axis, keepdims=False)
    other = lax.dynamic_index_in_dim(value, 1 - bit, axis, keepdims=False)
    return own, other


class Reduction:
    def __init__(self, ids, send, keep):
        count = lax.axis_size("seg")
        self.ids = ids
        self.shape = (2, count, send.size // (2 * count * send.shape[-1]), send.shape[-1])
        self.keep = keep
        self.came = rep_swap(send, 1)

    def spread(self, *first):
        came = later(self.came, *first)
        self.stay, *sends = spread(self.ids, self.keep.reshape(self.shape), came.reshape(self.shape))
        self.came = [seg_swap(sends[0], 1), rep_swap(sends[1], 2), both_swap(sends[2], 1, 2)]

    def settle(self, *first):
        self.own, *others = settle(self.ids, [self.stay] + [later(value, *first) for value in self.came])
        self.came = [seg_swap(other, 2 * mask) for mask, other in enumerate(others, 1)]

    def finish(self, *first):
        total = self.own.astype(F32)
        for value in self.came:
            total = total + later(value, *first).astype(F32)
        return total.astype(BF16)


class Sharing:
    def __init__(self, ids, value):
        self.ids, self.value = ids, value
        self.came = rep_swap(value, 2)

    def step(self, *first):
        self.value = jnp.stack([self.value, later(self.came, *first)], axis=0)
        self.came = rep_swap(self.value, 1)

    def finish(self, *first):
        held = jnp.concatenate([self.value, later(self.came, *first)], axis=0)
        order = jnp.array([0, 2, 1, 3], jnp.int32)
        return [
            lax.dynamic_index_in_dim(held, order[self.ids[1] ^ owner], 0, keepdims=False).astype(F32)
            for owner in (0, 2, 1, 3)
        ]


class SmallReduction:
    def __init__(self, ids, value):
        self.ids, self.mask = ids, lax.axis_size("seg") // 2
        self.split(value)

    def split(self, value):
        bit = (self.ids[0] // self.mask) & 1
        self.own, self.other = halve(value.reshape((2, self.mask) + value.shape[1:]), 0, bit)
        self.came = seg_swap(self.other, self.mask)
        self.mask //= 2

    def step(self, *first):
        value = self.own + later(self.came, *first)
        if self.mask:
            self.split(value)
        elif value.ndim == 3:
            self.own = self.other = value[0]
            self.came = rep_swap(self.own, 1)
        else:
            self.own = self.other = value
            self.came = rep_swap(self.own, 2)
            self.last = True

    def finish(self, *first):
        while not getattr(self, "last", False):
            self.step(*first)
        return self.own + later(self.came, *first)


def body(tokens, cotangent, doc_counts, w_qkv, w_out, w_up, w_down, c_qkv, c_out, pos_table, norm_gains, norm_shifts):
    micro_count, unused, seg_local, seg_length, width = tokens.shape
    count = lax.axis_size("seg")
    me = lax.axis_index("seg").astype(jnp.int32)
    rep = lax.axis_index("rep").astype(jnp.int32)
    ids = jnp.stack([me, rep])
    shard_rows = w_qkv.shape[0]
    local = micro_count * seg_local
    rows = local * seg_length
    table_rows = pos_table.shape[0]
    norm_cols = norm_gains.shape[1]
    aligned = shard_rows % 16 == 0

    def shares_of(matrix):
        return matrix.reshape(shard_rows, 4, width).transpose(1, 0, 2)

    def own_share(matrix):
        return lax.dynamic_slice_in_dim(matrix, rep * width, width, 1)

    norms = jnp.pad(jnp.concatenate([norm_gains, norm_shifts], axis=0), ((0, 2), (0, width - norm_cols)))
    small = jnp.pad(jnp.stack([pos_table, norms], axis=0), ((0, 0), (0, 16 - table_rows), (0, 0)))
    ffn_piece = jnp.concatenate(
        [own_half(ids, shares_of(w_up)), own_half(ids, w_down.reshape(4, shard_rows, width)), small], axis=1
    )
    ffn_half = lax.all_gather(ffn_piece, "seg", axis=0)
    qo_piece = own_half(ids, shares_of(jnp.concatenate([w_qkv, w_out], axis=1)))
    qo_evens = far_pieces(qo_piece)
    shapes = [shape_of((4, count, shard_rows, width), BF16), shape_of((count, 4, shard_rows, width), BF16)]
    qo_pieces = pieces_of(*gather_singly(qo_piece, qo_evens, {}), shapes[0])
    cross_piece = own_half(ids, shares_of(jnp.concatenate([c_qkv, c_out], axis=1)))
    cross_half = lax.all_gather(later(cross_piece, qo_evens[1]), "seg", axis=0)

    counts = doc_counts[:, 0]
    ends = jnp.cumsum(counts, axis=1)
    owners = me ^ jnp.arange(count, dtype=jnp.int32)
    seg_ids = owners[:, None, None] * seg_local + jnp.arange(seg_local, dtype=jnp.int32)[None, None, :]
    seg_ids = jnp.broadcast_to(seg_ids, (count, micro_count, seg_local))
    past = seg_ids[..., None] >= ends[None, :, None, :]
    doc_ids = jnp.sum(past.astype(jnp.int32), axis=-1)
    starts = jnp.sum(jnp.where(past, counts[None, :, None, :], 0), axis=-1)
    places = (seg_ids - starts).reshape(-1, 1)
    keys = (doc_ids + (counts.shape[1] + 1) * jnp.arange(micro_count, dtype=jnp.int32)[None, :, None]).reshape(-1)

    flat = tokens.reshape(rows, width)
    cot = cotangent.reshape(rows, width)
    block = 4 * seg_length
    steps = rows // block
    halves_of = ((0, steps // 2), (steps // 2, steps - steps // 2))

    everything = (0, steps)
    if aligned:
        proj, probs, mixed, pre_first, full_qo = attention_forward(
            flat, None, seg_length, block, everything, pieces=qo_pieces, ids=ids
        )
    else:
        full_qo = put_in_place(ids, qo_pieces).reshape(4, 1, width, width)
        proj, probs, mixed, pre_first = attention_forward(flat, full_qo, seg_length, block, everything)
    ffn_half = later(ffn_half, proj)
    small = ffn_half[:, :, 2 * shard_rows :]
    table = small[:, 0, :table_rows].reshape(count * table_rows, width)
    norms = small[:, 1, :6, :norm_cols].transpose(1, 0, 2).reshape(6, width)
    gains, shifts = norms[:3], norms[3:]
    ffn_other = rep_swap(ffn_half, 1)

    def joined(parts, start, owner_first):
        own, other = [part[:, :, start : start + shard_rows] for part in parts]
        both = jnp.where((rep & 1) == 0, jnp.concatenate([own, other], axis=1), jnp.concatenate([other, own], axis=1))
        return (both if owner_first else both.transpose(1, 0, 2, 3)).reshape(4, 1, width, width)

    pre_edge = pre_first.reshape(local, seg_length, width)[:, 0]
    if aligned:
        edge, full_up, full_down = edge_forward(
            pre_edge, None, gains, shifts, ([ffn_half, ffn_other], shapes), ids
        )
    else:
        full_up = joined([ffn_half, ffn_other], 0, False)
        full_down = joined([ffn_half, ffn_other], shard_rows, True)
        edge = edge_forward(pre_edge, [full_up, full_down], gains, shifts)[0]
    edge_cot = cot.reshape(local, seg_length, width)[:, 0].astype(F32)
    edges = Gather(jnp.stack([edge, edge_cot], axis=0))
    kept = ffn_forward(pre_first, full_up, full_down, gains, shifts, block, halves_of[0], after=[edge])
    edges.across(kept[0])
    low, act, slope, pre_second = ffn_forward(
        pre_first, full_up, full_down, gains, shifts, block, halves_of[1], prior=kept, after=[edges.evens]
    )
    edges = edges.finish(pre_second)
    cross_half = later(cross_half, pre_second)
    cross_parts, cross_shape = [cross_half, rep_swap(cross_half, 1)], shapes[0]
    if not aligned:
        cross_parts, cross_shape = [joined(cross_parts, 0, False)], None
    cls_new, grad_edge, c_low, c_gradp, c_mixed, c_gradz, c_sums, table_grad = cross_block(
        ids, local, edges[:, 0].reshape(-1, width), edges[:, 1].reshape(-1, width),
        keys[:, None], jnp.concatenate([keys, keys])[None, :], places, table, gains, shifts, cross_parts, cross_shape,
    )
    own_low = lax.dynamic_slice_in_dim(c_low, me * shard_rows, shard_rows, 1)
    own_mixed = lax.dynamic_slice_in_dim(c_mixed, me * shard_rows, shard_rows, 1)
    grad_c = shares_of(jnp.concatenate([dot_tn(own_low, c_gradp), dot_tn(own_mixed, c_gradz)], axis=1)).astype(BF16)
    c_own, c_other = halve(grad_c.reshape(2, 2, shard_rows, width), 0, rep & 1)
    c_came = rep_swap(c_other, 1)
    layer_out, branch, grad2, sums2 = norm_backward(
        cot, pre_second, grad_edge[:, None], cls_new[:, None], gains, shifts, seg_length, block, [c_other]
    )
    c_own, c_other = halve(c_own.astype(F32) + later(c_came, branch).astype(F32), 0, rep >> 1)
    c_other = c_other.astype(BF16)
    c_came = rep_swap(c_other, 2)
    send_down, keep_down = rows_grads(ids, act, branch, count, [c_other])
    c_share = (c_own + later(c_came, send_down).astype(F32)).astype(BF16)
    down = Reduction(ids, send_down, keep_down)
    grad_hidden, grad1, low1, sums1 = ffn_backward(
        branch, grad2, pre_first, slope, full_up, full_down, gains, block, everything, LONG, after=[send_down, c_share]
    )
    down.spread(grad1)
    send_up = cols_grads(1, ids, low, grad_hidden, [down.stay], SHORT)
    norm_sums = (later(sums2, send_up) + sums1 + c_sums).reshape(8, count, norm_cols).transpose(1, 0, 2)
    norm_sums = jnp.pad(norm_sums, ((0, 0), (0, 0), (0, width - norm_cols)))
    tiny = SmallReduction(ids, jnp.concatenate([norm_sums, table_grad.reshape(count, table_rows, width)], axis=1))
    keep_up = cols_grads(0, ids, low, grad_hidden, [send_up, tiny.other], LONG)
    up = Reduction(ids, send_up, keep_up)
    up.spread(keep_up)
    grad_proj, input_grad = attention_backward(
        grad1, low1, proj, probs, full_qo, seg_length, block, everything, after=[up.stay]
    )
    down.settle(grad_proj)
    up.settle(grad_proj)
    send_qo = joint_grads(1, ids, flat, mixed, grad_proj, low1, [up.own, down.own], SHORT)
    keep_qo = joint_grads(0, ids, flat, mixed, grad_proj, low1, [send_qo], LONG)
    qo = Reduction(ids, send_qo, keep_qo)
    tiny.step(send_qo)
    early = Sharing(ids, jnp.stack([down.finish(keep_qo), up.finish(keep_qo), c_share], axis=0))
    tiny.step(keep_qo)
    qo.spread(early.value, tiny.other)
    early.step(qo.came[0])
    tiny.step(qo.came[0])
    qo.settle()
    early_shares = early.finish(qo.own)
    tiny.step(qo.own)
    qo_share = qo.finish()
    summed = tiny.finish(qo_share)
    late = Sharing(ids, qo_share)
    late.step()
    late_shares = late.finish()

    def side_by_side(parts):
        return jnp.concatenate(parts, axis=1)

    return (
        layer_out.reshape(tokens.shape),
        input_grad.reshape(tokens.shape),
        side_by_side(late_shares[:3]),
        late_shares[3],
        side_by_side([part[1] for part in early_shares]),
        jnp.concatenate([part[0] for part in early_shares], axis=0),
        side_by_side([part[2] for part in early_shares[:3]]),
        early_shares[3][2],
        summed[8:],
        summed[:3, :norm_cols],
        summed[3:6, :norm_cols],
    )


def solution(mesh):
    rows = P(None, "rep", "seg", None, None)
    split = P("seg", None)
    last = P(None, "seg")
    return jax.shard_map(
        body,
        mesh=mesh,
        in_specs=(rows, rows, P(None, "rep", None)) + (split,) * 7 + (last, last),
        out_specs=(rows, rows) + (split,) * 7 + (last, last),
        check_vma=False,
    )
```

time: 535 us -> 479 us (0.90)
  waiting for transfers between devices: 153 us -> 113 us
  starting transfers between devices: 68.2 us -> 55.7 us
  local copies, waits for them, and re-layouts: 35.8 us -> 29.4 us
    ppermute x22 -> x24, waiting for transfers between devices: 33.5 us -> 6.47 us  [rep_swap(): return lax.ppermute(value, 'rep', [(i, i ^ mask) for i in range(count)])]
    ppermute x29 -> x26, starting transfers between devices: 55 us -> 39.4 us  [seg_swap(): return lax.ppermute(value, 'seg', [(i, i ^ mask) for i in range(count)])]
    unnamed x79 -> x105, local copies, waits for them, and re-layouts: 21.3 us -> 8.93 us
    ppermute x29 -> x26, waiting for transfers between devices: 85.7 us -> 74.6 us  [seg_swap(): return lax.ppermute(value, 'seg', [(i, i ^ mask) for i in range(count)])]
    pallas_call x9 -> x12, Pallas kernels: 202 us -> 209 us  [the longest x7 155 us: rows_call(): pl.pallas_call(run, out_shape=tuple((jax.ShapeDtypeStruct(shape.shape, sh...]
    all_gather x1 -> x2, waiting for transfers between devices: 25.3 us -> 21.4 us  [the longest x1 21.3 us: body(): ffn_half = lax.all_gather(ffn_piece, 'seg', axis=0)]
  transfers between devices with their start and end apart: 55 -> 55, of which waited for: 18 -> 18; matrix products, arithmetic and copies ran while one was open for 4% -> 6% of each run, Pallas kernels for 24% -> 46%
where the time goes in v2:
time: 479 us; the launch traced here: 474 us
  Pallas kernels  235 us (49%)
  waiting for transfers between devices  113 us (24%)
  starting transfers between devices  55.7 us (12%)
  local copies, waits for them, and re-layouts  29.4 us (6%)
  between operations  23.1 us (5%)
  other arithmetic  15.6 us (3%)
    pallas_call x7, Pallas kernels, rows_call(): pl.pallas_call(run, out_shape=tuple((jax.ShapeDtypeStruct(shape.shape, sh...  155 us
    ppermute x26, waiting for transfers between devices, seg_swap(): return lax.ppermute(value, 'seg', [(i, i ^ mask) for i in range(count)])  74.6 us
    pallas_call x4, Pallas kernels, half_grads(): pl.pallas_call(kernel, out_shape=jax.ShapeDtypeStruct((2, width, width),...  43.9 us
    ppermute x26, starting transfers between devices, seg_swap(): return lax.ppermute(value, 'seg', [(i, i ^ mask) for i in range(count)])  39.4 us
    all_gather x1, waiting for transfers between devices, body(): ffn_half = lax.all_gather(ffn_piece, 'seg', axis=0)  21.3 us
    pallas_call x1, Pallas kernels, rows_grads(): pl.pallas_call(rows_grad_kernel, out_shape=(half, half), grid_spec=pltpu....  16.5 us
    ppermute x3, waiting for transfers between devices, both_swap(): return lax.ppermute(value, ('seg', 'rep'), pairs)  10.2 us
    pallas_call x1, Pallas kernels, cross_block(): pl.pallas_call(partial(cross_kernel, local, shape is not None), out_shape...  9.82 us
  transfers between devices with their start and end apart: 55, of which 18 were waited for; matrix products, arithmetic and copies ran while one was open for 6% of the time, Pallas kernels for 46%

profile of v2, /device:TPU:0, one launch (start us, length us, event | category | flops | bytes accessed | tf_op | source)
XLA Modules:
  0.0 474.3 jit_solution(18428011734309798310)
XLA Ops:
  9.2 1.8 reshape.225
  11.6 1.3 dynamic-slice_bitcast_fusion.1
  15.8 3.1 collective-permute-start.1
  18.9 1.5 collective-permute-start
  20.4 2.6 collective-permute-start.3
  23.0 7.7 %collective-permute-done.1.refs_4_ = bf16[2,96,768]{2,1,0:T(8,128)(2,1)S(1)} collective-permute-done((bf16[2,96,768]{2,1,0:T(8,128)(2,1)S(1)}, bf16[2,96,768]{2,1,0:T(8,128)(2,1)S(1)}, u32[]{:S(2)}, u32[]{:S(2)}) %collective-permute-start.1) | collective-permute-done | bytes 294944 | tf_op jit(solution)/shard_map/ppermute | solution.py:592
  30.7 5.2 %collective-permute-start.2 = (bf16[2,96,768]{2,1,0:T(8,128)(2,1)S(1)}, bf16[2,96,768]{2,1,0:T(8,128)(2,1)S(1)}, u32[]{:S(2)}, u32[]{:S(2)}) collective-permute-start(bf16[2,96,768]{2,1,0:T(8,128)(2,1)S(1)} %collective-permute-done.1.refs_4_), channel_id=1, source_target_pairs={{0,4},{4,0},{8,12},{12,8},{16,20},{20,16},{24,28},{28,24},{1,5},{5... | collective-permute-start | bytes 884744 | tf_op jit(solution)/shard_map/ppermute | solution.py:592
  35.9 3.8 collective-permute-start.7
  39.9 12.9 %collective-permute-done.3.refs_6_ = bf16[2,96,768]{2,1,0:T(8,128)(2,1)S(1)} collective-permute-done((bf16[2,96,768]{2,1,0:T(8,128)(2,1)S(1)}, bf16[2,96,768]{2,1,0:T(8,128)(2,1)S(1)}, u32[]{:S(2)}, u32[]{:S(2)}) %collective-permute-start.3) | collective-permute-done | bytes 294944 | tf_op jit(solution)/shard_map/ppermute | solution.py:592
  53.0 1.4 collective-permute-done.9.refs_13_
  54.4 7.8 %collective-permute-done.6.refs_7_ = bf16[2,96,768]{2,1,0:T(8,128)(2,1)S(1)} collective-permute-done((bf16[2,96,768]{2,1,0:T(8,128)(2,1)S(1)}, bf16[2,96,768]{2,1,0:T(8,128)(2,1)S(1)}, u32[]{:S(2)}, u32[]{:S(2)}) %collective-permute-start.6) | collective-permute-done | bytes 294944 | tf_op jit(solution)/shard_map/ppermute | solution.py:592
  63.1 7.9 %collective-permute-done.10.refs_9_ = bf16[2,96,768]{2,1,0:T(8,128)(2,1)S(1)} collective-permute-done((bf16[2,96,768]{2,1,0:T(8,128)(2,1)S(1)}, bf16[2,96,768]{2,1,0:T(8,128)(2,1)S(1)}, u32[]{:S(2)}, u32[]{:S(2)}) %collective-permute-start.10) | collective-permute-done | bytes 294944 | tf_op jit(solution)/shard_map/ppermute | solution.py:592
  71.6 1.0 collective-permute-done.14.refs_17_
  72.8 28.6 %attention_forward.1 = (bf16[2048,2304]{1,0:T(8,128)(2,1)}, bf16[16,6,128,256]{3,2,1,0:T(8,128)(2,1)}, bf16[2048,768]{1,0:T(8,128)(2,1)}, f32[2048,768]{1,0:T(8,128)}, bf16[4,8,96,768]{3,2,1,0:T(8,128)(2,1)}) custom-call(s32[2]{0:T(128)} %pad_add_fusion.1.refs_0_.ids_ref, bf16[2048,768]{1,0:T(8,128)(2,1)} %bitcast.151, bf16[2,96,768]{2,1,0:T(8,128)(2,1)} %bitcast.176, ...), custom_call_target="tpu_custom_call" | custom-call | flops 12884901 | bytes 18874 | tf_op jit(solution)/shard_map/attention_forward/pallas_call | solution.py:127
  101.4 21.3 %all-gather.5.cloned.1.call-done = bf16[16,208,768]{2,1,0:T(8,128)(2,1)} async-done(((bf16[2,208,768]{2,1,0:T(8,128)(2,1)}), bf16[16,208,768]{2,1,0:T(8,128)(2,1)}) %all-gather.5.cloned.1.call-update) | async-done | bytes 5111824 | tf_op jit(solution)/shard_map/all_gather | solution.py:819
  122.7 1.7 copy.110
  124.5 1.7 copy.126
  130.0 1.5 collective-permute-done.15.refs_5_
  131.5 8.9 %edge_forward.1 = (f32[16,768]{1,0:T(8,128)}, bf16[4,8,96,768]{3,2,1,0:T(8,128)(2,1)}, bf16[8,4,96,768]{3,2,1,0:T(8,128)(2,1)}) custom-call(s32[2]{0:T(128)} %pad_add_fusion.1.refs_0_.ids_ref, f32[16,768]{1,0:T(8,128)} %bitcast.187, bf16[3,768]{1,0:T(4,128)(2,1)} %slice.93.refs_2_.refs_3_.gains_ref.refs_4_.refs_6_, ...), custom_call_target="tpu_custom_call" | custom-call | flops 1132462080 | bytes 9884160 | tf_op jit(solution)/shard_map/edge_forward/pallas_call | solution.py:127
  141.2 1.4 collective-permute-start.17
  143.5 2.2 collective-permute-start.18
  145.7 18.9 %ffn_forward.2 = (bf16[2048,768]{1,0:T(8,128)(2,1)}, bf16[2048,3072]{1,0:T(8,128)(2,1)}, bf16[2048,3072]{1,0:T(8,128)(2,1)}, f32[2048,768]{1,0:T(8,128)}) custom-call(f32[2048,768]{1,0:T(8,128)} %get-tuple-element.109.refs_0_.refs_2_, bf16[4,8,96,768]{3,2,1,0:T(8,128)(2,1)} %get-tuple-element.112.refs_1_.refs_4_, ...), custom_call_target="tpu_custom_call" | custom-call | flops 9663676416 | bytes 25170432 | tf_op jit(solution)/shard_map/ffn_forward/pallas_call | solution.py:127
  165.4 19.1 %ffn_forward.3 = (bf16[2048,768]{1,0:T(8,128)(2,1)}, bf16[2048,3072]{1,0:T(8,128)(2,1)}, bf16[2048,3072]{1,0:T(8,128)(2,1)}, f32[2048,768]{1,0:T(8,128)}) custom-call(f32[2048,768]{1,0:T(8,128)} %get-tuple-element.109.refs_0_.refs_2_, ...), custom_call_target="tpu_custom_call", output_to_operand_aliasing={{0}: (5, {}), {1}: (6, {}), {2}: (7, {}), {3}: (8, {})} | custom-call | flops 9663676416 | bytes 25170432 | tf_op jit(solution)/shard_map/ffn_forward/pallas_call | solution.py:127
  187.6 1.5 slice_bitcast_fusion.12.table_ref
  189.1 7.4 %collective-permute-done.19 = f32[4,2,16,768]{3,2,1,0:T(8,128)S(1)} collective-permute-done((f32[4,2,16,768]{3,2,1,0:T(8,128)S(1)}, f32[4,2,16,768]{3,2,1,0:T(8,128)S(1)}, u32[]{:S(2)}, u32[]{:S(2)}) %collective-permute-start.19) | collective-permute-done | bytes 393248 | tf_op jit(solution)/shard_map/ppermute | solution.py:592
  197.6 9.8 %cross_block.1 = (f32[16,768]{1,0:T(8,128)}, f32[16,768]{1,0:T(8,128)}, bf16[128,768]{1,0:T(8,128)(2,1)}, bf16[128,2304]{1,0:T(8,128)(2,1)}, bf16[128,768]{1,0:T...) custom-call(s32[2]{0:T(128)} %pad_add_fusion.1.refs_0_.ids_ref, ...), custom_call_target="tpu_custom_call" | custom-call | flops 10000000000 | bytes 4718592 | tf_op jit(solution)/shard_map/cross_block/pallas_call | solution.py:473
  207.5 1.3 convolution_convert_fusion.1
  208.7 1.5 convolution_convert_fusion
  211.8 10.9 %norm_backward.1 = (bf16[2048,768]{1,0:T(8,128)(2,1)}, bf16[2048,768]{1,0:T(8,128)(2,1)}, f32[2048,768]{1,0:T(8,128)}, f32[8,768]{1,0:T(8,128)}) custom-call(bf16[2048,768]{1,0:T(8,128)(2,1)} %bitcast.154, f32[2048,768]{1,0:T(8,128)} %get-tuple-element.122.refs_1_, f32[16,1,768]{2,1,0:T(1,128)} %broadcast_in_dim.34.refs_2_, ...), custom_call_target="tpu_custom_call" | custom-call | flops 6291456 | bytes 11076096 | tf_op jit(solution)/shard_map/norm_backward/pallas_call | solution.py:127
  222.9 1.6 collective-permute-start.22
  224.5 16.5 %rows_grads.1 = (bf16[2,8,96,768]{3,2,1,0:T(8,128)(2,1)}, bf16[2,8,96,768]{3,2,1,0:T(8,128)(2,1)}) custom-call(s32[2]{0:T(128)} %pad_add_fusion.1.refs_0_.ids_ref, bf16[2048,3072]{1,0:T(8,128)(2,1)} %get-tuple-element.136.left_ref, bf16[2048,768]{1,0:T(8,128)(2,1)} %get-tuple-element.133.right_ref.refs_0_, bf16[96,768]{1,0:T(8,128)(2,1)} %copy-done.42), custom_call_target="tpu_custom_call" | custom-call | flops 9663676416 | bytes 15728640 | tf_op jit(solution)/shard_map/rows_grads/pallas_call | solution.py:567
  241.8 32.7 %ffn_backward.1 = (bf16[2048,3072]{1,0:T(8,128)(2,1)}, f32[2048,768]{1,0:T(8,128)}, bf16[2048,768]{1,0:T(8,128)(2,1)}, f32[8,768]{1,0:T(8,128)}) custom-call(bf16[2048,768]{1,0:T(8,128)(2,1)} %get-tuple-element.133.right_ref.refs_0_, f32[2048,768]{1,0:T(8,128)} %get-tuple-element.134.refs_1_, f32[2048,768]{1,0:T(8,128)} %get-tuple-element.109.refs_0_.refs_2_, ...), custom_call_target="tpu_custom_call" | custom-call | flops 115964116992 | bytes 179394048 | tf_op jit(solution)/shard_map/ffn_backward/pallas_call | solution.py:127
  274.5 2.5 spread.3
  279.0 2.4 collective-permute-start.30
  281.4 10.0 %cols_grads.2.refs_0_ = bf16[2,768,768]{2,1,0:T(8,128)(2,1)} custom-call(s32[2]{0:T(128)} %pad_add_fusion.1.refs_0_.ids_ref, bf16[2048,768]{1,0:T(8,128)(2,1)} %get-tuple-element.144.left_ref, bf16[2048,3072]{1,0:T(8,128)(2,1)} %get-tuple-element.145.right_ref, bf16[4,96,768]{2,1,0:T(8,128)(2,1)} %copy-done.2), custom_call_target="tpu_custom_call" | custom-call | flops 4831838 | bytes 15728 | tf_op jit(solution)/shard_map/cols_grads/pallas_call | solution.py:515
  292.0 1.4 reshape.233
  294.9 1.6 fusion.5.refs_1_
  296.5 10.0 %cols_grads.3 = bf16[2,768,768]{2,1,0:T(8,128)(2,1)} custom-call(s32[2]{0:T(128)} %pad_add_fusion.1.refs_0_.ids_ref, bf16[2048,768]{1,0:T(8,128)(2,1)} %get-tuple-element.144.left_ref, bf16[2048,3072]{1,0:T(8,128)(2,1)} %get-tuple-element.145.right_ref, bf16[2,768,768]{2,1,0:T(8,128)(2,1)} %cols_grads.2.refs_0_, f32[4,16,768]{2,1,0:T(8,128)} %fusion.5.refs_1_), custom_call_target="tpu_custom_call" | custom-call | flops 28991029248 | bytes 94371840 | tf_op jit(solution)/shard_map/cols_grads/pallas_call | solution.py:515
  306.5 1.7 copy-done.6
  308.1 2.5 spread.4
  312.6 2.4 collective-permute-start.27
  315.0 36.4 %attention_backward.1 = (bf16[2048,2304]{1,0:T(8,128)(2,1)}, f32[2048,768]{1,0:T(8,128)}) custom-call(f32[2048,768]{1,0:T(8,128)} %get-tuple-element.140.refs_0_, bf16[2048,768]{1,0:T(8,128)(2,1)} %get-tuple-element.141.refs_1_.last_right_ref, bf16[2048,2304]{1,0:T(8,128)(2,1)} %get-tuple-element.110.refs_2_, ...), custom_call_target="tpu_custom_call" | custom-call | flops 16106127 | bytes 22806 | tf_op jit(solution)/shard_map/attention_backward/pallas_call | solution.py:127
  351.8 1.4 settle.4
  353.8 1.8 collective-permute-start.32
  356.5 1.8 collective-permute-start.34
  359.7 11.8 %joint_grads.2.refs_0_ = bf16[2,768,768]{2,1,0:T(8,128)(2,1)} custom-call(s32[2]{0:T(128)} %pad_add_fusion.1.refs_0_.ids_ref, bf16[2048,768]{1,0:T(8,128)(2,1)} %bitcast.152, bf16[2048,768]{1,0:T(8,128)(2,1)} %get-tuple-element.157.last_left_ref, bf16[2048,2304]{1,0:T(8,128)(2,1)} %get-tuple-element.158.right_ref, ...), custom_call_target="tpu_custom_call" | custom-call | flops 4831838 | bytes 15728 | tf_op jit(solution)/shard_map/joint_grads/pallas_call | solution.py:515
  371.6 12.1 %joint_grads.3 = bf16[2,768,768]{2,1,0:T(8,128)(2,1)} custom-call(s32[2]{0:T(128)} %pad_add_fusion.1.refs_0_.ids_ref, bf16[2048,768]{1,0:T(8,128)(2,1)} %bitcast.153, bf16[2048,768]{1,0:T(8,128)(2,1)} %get-tuple-element.157.last_left_ref, bf16[2048,2304]{1,0:T(8,128)(2,1)} %get-tuple-element.158.right_ref, ...), custom_call_target="tpu_custom_call" | custom-call | flops 28991029248 | bytes 94371840 | tf_op jit(solution)/shard_map/joint_grads/pallas_call | solution.py:515
  384.8 1.7 collective-permute-start.36
  386.5 1.8 collective-permute-start.37
  388.5 9.3 %collective-permute-done.39 = f32[2,16,768]{2,1,0:T(8,128)S(1)} collective-permute-done((f32[2,16,768]{2,1,0:T(8,128)S(1)}, f32[2,16,768]{2,1,0:T(8,128)S(1)}, u32[]{:S(2)}, u32[]{:S(2)}) %collective-permute-start.39) | collective-permute-done | bytes 98336 | tf_op jit(solution)/shard_map/ppermute | solution.py:592
  399.0 1.5 spread.5
  401.7 2.3 collective-permute-start.42
  404.0 12.8 %collective-permute-done.40.b_ref = bf16[4,96,768]{2,1,0:T(8,128)(2,1)S(1)} collective-permute-done((bf16[4,96,768]{2,1,0:T(8,128)(2,1)S(1)}, bf16[4,96,768]{2,1,0:T(8,128)(2,1)S(1)}, u32[]{:S(2)}, u32[]{:S(2)}) %collective-permute-start.40) | collective-permute-done | bytes 589856 | tf_op jit(solution)/shard_map/ppermute | solution.py:592
  416.8 10.2 %collective-permute-done.42.d_ref = bf16[4,96,768]{2,1,0:T(8,128)(2,1)S(1)} collective-permute-done((bf16[4,96,768]{2,1,0:T(8,128)(2,1)S(1)}, bf16[4,96,768]{2,1,0:T(8,128)(2,1)S(1)}, u32[]{:S(2)}, u32[]{:S(2)}) %collective-permute-start.42) | collective-permute-done | bytes 589856 | tf_op jit(solution)/shard_map/ppermute | solution.py:604
  427.8 3.9 collective-permute-start.43
  432.5 1.6 collective-permute-start.45
  434.1 1.5 collective-permute-start.50
  436.4 1.8 collective-permute-done.50
  438.2 6.0 %collective-permute-done.44 = bf16[96,768]{1,0:T(8,128)(2,1)S(1)} collective-permute-done((bf16[96,768]{1,0:T(8,128)(2,1)S(1)}, bf16[96,768]{1,0:T(8,128)(2,1)S(1)}, u32[]{:S(2)}, u32[]{:S(2)}) %collective-permute-start.44) | collective-permute-done | bytes 147488 | tf_op jit(solution)/shard_map/ppermute | solution.py:592
  444.3 1.3 collective-permute-start.46
  445.7 1.2 collective-permute-done.51
  448.3 1.2 collective-permute-done.46
  465.0 1.1 pad_maximum_fusion.2
  466.1 1.1 pad_maximum_fusion.1
  (256 shorter events, 44.8 us)
Async XLA Ops:
  7.2 115.5 %all-gather.5.cloned.1.call-start = ((), (), s32[]{:S(2)}) async-start(), calls=%async_computation | async-start | bytes 5750784 | tf_op jit(solution)/shard_map/all_gather | solution.py:819
  14.7 169.8 %all-gather.7.cloned.1.call-start = ((), (), s32[]{:S(2)}) async-start(), calls=%async_computation.1 | async-start | bytes 2654208 | tf_op jit(solution)/shard_map/all_gather | solution.py:825
  15.8 57.0 %copy-start.20 = (bf16[96,2,768]{2,0,1:T(8,128)(2,1)}, bf16[96,2,768]{2,0,1:T(8,128)(2,1)S(1)}, u32[]{:S(2)}) copy-start(bf16[96,2,768]{2,0,1:T(8,128)(2,1)S(1)} %copy.128) | copy-start | bytes 884740
  15.8 14.9 %collective-permute-start.1 = (bf16[2,96,768]{2,1,0:T(8,128)(2,1)S(1)}, bf16[2,96,768]{2,1,0:T(8,128)(2,1)S(1)}, u32[]{:S(2)}, u32[]{:S(2)}) collective-permute-start(bf16[2,96,768]{2,1,0:T(8,128)(2,1)S(1)} %bitcast.171), channel_id=1, source_target_pairs={{0,8},{4,12},{8,0},{12,4},{16,24},{20,28},{24,16},{28,20},{1,9},{5... | collective-permute-start | bytes 884744 | tf_op jit(solution)/shard_map/ppermute | solution.py:592
  18.9 11.8 %collective-permute-start = (bf16[2,96,768]{2,1,0:T(8,128)(2,1)S(1)}, bf16[2,96,768]{2,1,0:T(8,128)(2,1)S(1)}, u32[]{:S(2)}, u32[]{:S(2)}) collective-permute-start(bf16[2,96,768]{2,1,0:T(8,128)(2,1)S(1)} %bitcast.172), channel_id=1, source_target_pairs={{0,4},{4,0},{8,12},{12,8},{16,20},{20,16},{24,28},{28,24},{1,5},{5... | collective-permute-start | bytes 884744 | tf_op jit(solution)/shard_map/ppermute | solution.py:592
  20.4 19.3 %collective-permute-start.4 = (bf16[2,96,768]{2,1,0:T(8,128)(2,1)S(1)}, bf16[2,96,768]{2,1,0:T(8,128)(2,1)S(1)}, u32[]{:S(2)}, u32[]{:S(2)}) collective-permute-start(bf16[2,96,768]{2,1,0:T(8,128)(2,1)S(1)} %bitcast.173), channel_id=1, source_target_pairs={{0,1},{1,0},{2,3},{3,2},{4,5},{5,4},{6,7},{7,6},{8,9},{9,8},{10,11... | collective-permute-start | bytes 884744 | tf_op jit(solution)/shard_map/ppermute | solution.py:597
  20.4 32.4 %collective-permute-start.3 = (bf16[2,96,768]{2,1,0:T(8,128)(2,1)S(1)}, bf16[2,96,768]{2,1,0:T(8,128)(2,1)S(1)}, u32[]{:S(2)}, u32[]{:S(2)}) collective-permute-start(bf16[2,96,768]{2,1,0:T(8,128)(2,1)S(1)} %bitcast.174), channel_id=1, source_target_pairs={{0,16},{4,20},{8,24},{12,28},{16,0},{20,4},{24,8},{28,12},{1,17},{... | collective-permute-start | bytes 884744 | tf_op jit(solution)/shard_map/ppermute | solution.py:592
  30.7 22.3 %copy-start.27 = (bf16[2,96,768]{2,1,0:T(8,128)(2,1)}, bf16[2,96,768]{2,1,0:T(8,128)(2,1)S(1)}, u32[]{:S(2)}) copy-start(bf16[2,96,768]{2,1,0:T(8,128)(2,1)S(1)} %collective-permute-done.refs_3_) | copy-start | bytes 884740
  30.7 22.1 %collective-permute-start.2 = (bf16[2,96,768]{2,1,0:T(8,128)(2,1)S(1)}, bf16[2,96,768]{2,1,0:T(8,128)(2,1)S(1)}, u32[]{:S(2)}, u32[]{:S(2)}) collective-permute-start(bf16[2,96,768]{2,1,0:T(8,128)(2,1)S(1)} %collective-permute-done.1.refs_4_), channel_id=1, source_target_pairs={{0,4},{4,0},{8,12},{12,8},{16,20},{20,16},{24,28},{28,24},{1,5},{5... | collective-permute-start | bytes 884744 | tf_op jit(solution)/shard_map/ppermute | solution.py:592
  35.9 16.9 %collective-permute-start.5 = (bf16[2,96,768]{2,1,0:T(8,128)(2,1)S(1)}, bf16[2,96,768]{2,1,0:T(8,128)(2,1)S(1)}, u32[]{:S(2)}, u32[]{:S(2)}) collective-permute-start(bf16[2,96,768]{2,1,0:T(8,128)(2,1)S(1)} %collective-permute-done.refs_3_), channel_id=1, source_target_pairs={{0,1},{1,0},{2,3},{3,2},{4,5},{5,4},{6,7},{7,6},{8,9},{9,8},{10,11... | collective-permute-start | bytes 884744 | tf_op jit(solution)/shard_map/ppermute | solution.py:597
  35.9 17.1 %collective-permute-start.7 = (bf16[2,96,768]{2,1,0:T(8,128)(2,1)S(1)}, bf16[2,96,768]{2,1,0:T(8,128)(2,1)S(1)}, u32[]{:S(2)}, u32[]{:S(2)}) collective-permute-start(bf16[2,96,768]{2,1,0:T(8,128)(2,1)S(1)} %bitcast.175), channel_id=1, source_target_pairs={{0,24},{4,28},{8,16},{12,20},{16,8},{20,12},{24,0},{28,4},{1,25},{... | collective-permute-start | bytes 884744 | tf_op jit(solution)/shard_map/ppermute | solution.py:592
  39.7 13.3 %collective-permute-start.8 = (bf16[2,96,768]{2,1,0:T(8,128)(2,1)S(1)}, bf16[2,96,768]{2,1,0:T(8,128)(2,1)S(1)}, u32[]{:S(2)}, u32[]{:S(2)}) collective-permute-start(bf16[2,96,768]{2,1,0:T(8,128)(2,1)S(1)} %collective-permute-done.1.refs_4_), channel_id=1, source_target_pairs={{0,1},{1,0},{2,3},{3,2},{4,5},{5,4},{6,7},{7,6},{8,9},{9,8},{10,11... | collective-permute-start | bytes 884744 | tf_op jit(solution)/shard_map/ppermute | solution.py:597
  52.8 1.6 collective-permute-start.9
  52.8 9.4 %collective-permute-start.6 = (bf16[2,96,768]{2,1,0:T(8,128)(2,1)S(1)}, bf16[2,96,768]{2,1,0:T(8,128)(2,1)S(1)}, u32[]{:S(2)}, u32[]{:S(2)}) collective-permute-start(bf16[2,96,768]{2,1,0:T(8,128)(2,1)S(1)} %collective-permute-done.3.refs_6_), channel_id=1, source_target_pairs={{0,4},{4,0},{8,12},{12,8},{16,20},{20,16},{24,28},{28,24},{1,5},{5... | collective-permute-start | bytes 884744 | tf_op jit(solution)/shard_map/ppermute | solution.py:592
  62.3 8.7 %collective-permute-start.10 = (bf16[2,96,768]{2,1,0:T(8,128)(2,1)S(1)}, bf16[2,96,768]{2,1,0:T(8,128)(2,1)S(1)}, u32[]{:S(2)}, u32[]{:S(2)}) collective-permute-start(bf16[2,96,768]{2,1,0:T(8,128)(2,1)S(1)} %collective-permute-done.7.refs_8_), channel_id=1, source_target_pairs={{0,4},{4,0},{8,12},{12,8},{16,20},{20,16},{24,28},{28,24},{1,5},{5... | collective-permute-start | bytes 884744 | tf_op jit(solution)/shard_map/ppermute | solution.py:592
  62.5 9.0 %collective-permute-start.13 = (bf16[2,96,768]{2,1,0:T(8,128)(2,1)S(1)}, bf16[2,96,768]{2,1,0:T(8,128)(2,1)S(1)}, u32[]{:S(2)}, u32[]{:S(2)}) collective-permute-start(bf16[2,96,768]{2,1,0:T(8,128)(2,1)S(1)} %collective-permute-done.7.refs_8_), channel_id=1, source_target_pairs={{0,1},{1,0},{2,3},{3,2},{4,5},{5,4},{6,7},{7,6},{8,9},{9,8},{10,11... | collective-permute-start | bytes 884744 | tf_op jit(solution)/shard_map/ppermute | solution.py:597
  62.5 9.1 %collective-permute-start.11 = (bf16[2,96,768]{2,1,0:T(8,128)(2,1)S(1)}, bf16[2,96,768]{2,1,0:T(8,128)(2,1)S(1)}, u32[]{:S(2)}, u32[]{:S(2)}) collective-permute-start(bf16[2,96,768]{2,1,0:T(8,128)(2,1)S(1)} %collective-permute-done.3.refs_6_), channel_id=1, source_target_pairs={{0,1},{1,0},{2,3},{3,2},{4,5},{5,4},{6,7},{7,6},{8,9},{9,8},{10,11... | collective-permute-start | bytes 884744 | tf_op jit(solution)/shard_map/ppermute | solution.py:597
  63.1 8.6 %collective-permute-start.12 = (bf16[2,96,768]{2,1,0:T(8,128)(2,1)S(1)}, bf16[2,96,768]{2,1,0:T(8,128)(2,1)}, u32[]{:S(2)}, u32[]{:S(2)}) collective-permute-start(bf16[2,96,768]{2,1,0:T(8,128)(2,1)S(1)} %collective-permute-done.6.refs_7_), channel_id=1, source_target_pairs={{0,1},{1,0},{2,3},{3,2},{4,5},{5,4},{6,7},{7,6},{8,9},{9,8},{10,11... | collective-permute-start | bytes 884744 | tf_op jit(solution)/shard_map/ppermute | solution.py:597
  71.0 1.7 collective-permute-start.14
  72.8 51.7 %copy-start.16 = (bf16[2,1,8,128,768]{4,3,2,1,0:T(8,128)(2,1)S(1)}, bf16[2,1,8,128,768]{4,3,2,1,0:T(8,128)(2,1)}, u32[]{:S(2)}) copy-start(bf16[2,1,8,128,768]{4,3,2,1,0:T(8,128)(2,1)} %param.15) | copy-start | bytes 9437188
  122.7 8.8 %collective-permute-start.15 = (bf16[8,2,208,768]{3,2,1,0:T(8,128)(2,1)}, bf16[8,2,208,768]{3,2,1,0:T(8,128)(2,1)}, u32[]{:S(2)}, u32[]{:S(2)}) collective-permute-start(bf16[8,2,208,768]{3,2,1,0:T(8,128)(2,1)} %bitcast.156), channel_id=1, source_target_pairs={{0,1},{1,0},{2,3},{3,2},{4,5},{5,4},{6,7},{7,6},{8,9},{9,8},{10,11... | collective-permute-start | bytes 15335432 | tf_op jit(solution)/shard_map/ppermute | solution.py:597
  141.2 23.3 %collective-permute-start.17 = (f32[2,16,768]{2,1,0:T(8,128)S(1)}, f32[2,16,768]{2,1,0:T(8,128)S(1)}, u32[]{:S(2)}, u32[]{:S(2)}) collective-permute-start(f32[2,16,768]{2,1,0:T(8,128)S(1)} %get-tuple-element.296), channel_id=1, source_target_pairs={{0,16},{4,20},{8,24},{12,28},{16,0},{20,4},{24,8},{28,12},{1,17},{... | collective-permute-start | bytes 294920 | tf_op jit(solution)/shard_map/ppermute | solution.py:592
  142.6 21.9 %collective-permute-start.16 = (f32[2,16,768]{2,1,0:T(8,128)S(1)}, f32[2,16,768]{2,1,0:T(8,128)S(1)}, u32[]{:S(2)}, u32[]{:S(2)}) collective-permute-start(f32[2,16,768]{2,1,0:T(8,128)S(1)} %get-tuple-element.296), channel_id=1, source_target_pairs={{0,8},{4,12},{8,0},{12,4},{16,24},{20,28},{24,16},{28,20},{1,9},{5... | collective-permute-start | bytes 294920 | tf_op jit(solution)/shard_map/ppermute | solution.py:592
  143.5 21.1 %collective-permute-start.18 = (f32[2,16,768]{2,1,0:T(8,128)S(1)}, f32[2,16,768]{2,1,0:T(8,128)S(1)}, u32[]{:S(2)}, u32[]{:S(2)}) collective-permute-start(f32[2,16,768]{2,1,0:T(8,128)S(1)} %get-tuple-element.296), channel_id=1, source_target_pairs={{0,24},{4,28},{8,16},{12,20},{16,8},{20,12},{24,0},{28,4},{1,25},{... | collective-permute-start | bytes 294920 | tf_op jit(solution)/shard_map/ppermute | solution.py:592
  184.5 13.1 %collective-permute-start.20 = (bf16[8,2,96,768]{3,2,1,0:T(8,128)(2,1)}, bf16[8,2,96,768]{3,2,1,0:T(8,128)(2,1)}, u32[]{:S(2)}, u32[]{:S(2)}) collective-permute-start(bf16[8,2,96,768]{3,2,1,0:T(8,128)(2,1)} %bitcast.198), channel_id=1, source_target_pairs={{0,1},{1,0},{2,3},{3,2},{4,5},{5,4},{6,7},{7,6},{8,9},{9,8},{10,11... | collective-permute-start | bytes 7077896 | tf_op jit(solution)/shard_map/ppermute | solution.py:597
  185.0 11.6 %collective-permute-start.19 = (f32[4,2,16,768]{3,2,1,0:T(8,128)S(1)}, f32[4,2,16,768]{3,2,1,0:T(8,128)S(1)}, u32[]{:S(2)}, u32[]{:S(2)}) collective-permute-start(f32[4,2,16,768]{3,2,1,0:T(8,128)S(1)} %copy-done.19), channel_id=1, source_target_pairs={{0,4},{4,0},{8,12},{12,8},{16,20},{20,16},{24,28},{28,24},{1,5},{5... | collective-permute-start | bytes 1179656 | tf_op jit(solution)/shard_map/ppermute | solution.py:592
  210.4 12.3 %collective-permute-start.21 = (bf16[2,96,768]{2,1,0:T(8,128)(2,1)S(1)}, bf16[2,96,768]{2,1,0:T(8,128)(2,1)S(1)}, u32[]{:S(2)}, u32[]{:S(2)}) collective-permute-start(bf16[2,96,768]{2,1,0:T(8,128)(2,1)S(1)} %dynamic-slice_bitcast_fusion.refs_6_), channel_id=1, source_target_pairs={{0,1},{1,0},{2,3},{3,2},{4,5},{5,4},{6,7},{7,6},{8,9},{9,8},{10,11... | collective-permute-start | bytes 884744 | tf_op jit(solution)/shard_map/ppermute | solution.py:597
  222.9 18.3 %collective-permute-start.22 = (bf16[96,768]{1,0:T(8,128)(2,1)S(1)}, bf16[96,768]{1,0:T(8,128)(2,1)S(1)}, u32[]{:S(2)}, u32[]{:S(2)}) collective-permute-start(bf16[96,768]{1,0:T(8,128)(2,1)S(1)} %fusion.6.refs_0_), channel_id=1, source_target_pairs={{0,2},{1,3},{2,0},{3,1},{4,6},{5,7},{6,4},{7,5},{8,10},{9,11},{10,... | collective-permute-start | bytes 442376 | tf_op jit(solution)/shard_map/ppermute | solution.py:597
  241.0 33.5 %collective-permute-start.23 = (bf16[2,8,96,768]{3,2,1,0:T(8,128)(2,1)}, bf16[2,8,96,768]{3,2,1,0:T(8,128)(2,1)S(1)}, u32[]{:S(2)}, u32[]{:S(2)}) collective-permute-start(bf16[2,8,96,768]{3,2,1,0:T(8,128)(2,1)} %get-tuple-element.138.refs_7_), channel_id=1, source_target_pairs={{0,1},{1,0},{2,3},{3,2},{4,5},{5,4},{6,7},{7,6},{8,9},{9,8},{10,11... | collective-permute-start | bytes 7077896 | tf_op jit(solution)/shard_map/ppermute | solution.py:597
  241.8 32.7 %copy-start.5 = (bf16[2,8,96,768]{3,2,1,0:T(8,128)(2,1)S(1)}, bf16[2,8,96,768]{3,2,1,0:T(8,128)(2,1)}, u32[]{:S(2)}) copy-start(bf16[2,8,96,768]{3,2,1,0:T(8,128)(2,1)} %get-tuple-element.146) | copy-start | bytes 7077892
  241.8 32.7 %copy-start.13 = (s32[2]{0:T(128)S(1)}, s32[2]{0:T(128)}, u32[]{:S(2)}) copy-start(s32[2]{0:T(128)} %pad_add_fusion.1.refs_0_.ids_ref) | copy-start | bytes 28
  277.8 74.0 %collective-permute-start.28 = (bf16[4,96,768]{2,1,0:T(8,128)(2,1)}, bf16[4,96,768]{2,1,0:T(8,128)(2,1)S(1)}, u32[]{:S(2)}, u32[]{:S(2)}) collective-permute-start(bf16[4,96,768]{2,1,0:T(8,128)(2,1)} %get-tuple-element.166), channel_id=1, source_target_pairs={{0,4},{4,0},{8,12},{12,8},{16,20},{20,16},{24,28},{28,24},{1,5},{5... | collective-permute-start | bytes 1769480 | tf_op jit(solution)/shard_map/ppermute | solution.py:592
  278.1 73.3 %collective-permute-start.29 = (bf16[4,96,768]{2,1,0:T(8,128)(2,1)}, bf16[4,96,768]{2,1,0:T(8,128)(2,1)S(1)}, u32[]{:S(2)}, u32[]{:S(2)}) collective-permute-start(bf16[4,96,768]{2,1,0:T(8,128)(2,1)} %get-tuple-element.168), channel_id=1, source_target_pairs={{0,2},{1,3},{2,0},{3,1},{4,6},{5,7},{6,4},{7,5},{8,10},{9,11},{10,... | collective-permute-start | bytes 1769480 | tf_op jit(solution)/shard_map/ppermute | solution.py:597
  279.0 33.7 %collective-permute-start.30 = (bf16[4,96,768]{2,1,0:T(8,128)(2,1)}, bf16[4,96,768]{2,1,0:T(8,128)(2,1)}, u32[]{:S(2)}, u32[]{:S(2)}) collective-permute-start(bf16[4,96,768]{2,1,0:T(8,128)(2,1)} %get-tuple-element.170), channel_id=1, source_target_pairs={{0,6},{1,7},{2,4},{3,5},{4,2},{5,3},{6,0},{7,1},{8,14},{9,15},{10,... | collective-permute-start | bytes 1769480 | tf_op jit(solution)/shard_map/ppermute | solution.py:604
  291.4 15.1 %collective-permute-start.24 = (bf16[2,768,768]{2,1,0:T(8,128)(2,1)}, bf16[2,768,768]{2,1,0:T(8,128)(2,1)S(1)}, u32[]{:S(2)}, u32[]{:S(2)}) collective-permute-start(bf16[2,768,768]{2,1,0:T(8,128)(2,1)} %cols_grads.2.refs_0_), channel_id=1, source_target_pairs={{0,1},{1,0},{2,3},{3,2},{4,5},{5,4},{6,7},{7,6},{8,9},{9,8},{10,11... | collective-permute-start | bytes 7077896 | tf_op jit(solution)/shard_map/ppermute | solution.py:597
  311.5 44.2 %collective-permute-start.25 = (bf16[4,96,768]{2,1,0:T(8,128)(2,1)}, bf16[4,96,768]{2,1,0:T(8,128)(2,1)S(1)}, u32[]{:S(2)}, u32[]{:S(2)}) collective-permute-start(bf16[4,96,768]{2,1,0:T(8,128)(2,1)} %get-tuple-element.159), channel_id=1, source_target_pairs={{0,4},{4,0},{8,12},{12,8},{16,20},{20,16},{24,28},{28,24},{1,5},{5... | collective-permute-start | bytes 1769480 | tf_op jit(solution)/shard_map/ppermute | solution.py:592
  311.8 44.7 %collective-permute-start.26 = (bf16[4,96,768]{2,1,0:T(8,128)(2,1)}, bf16[4,96,768]{2,1,0:T(8,128)(2,1)S(1)}, u32[]{:S(2)}, u32[]{:S(2)}) collective-permute-start(bf16[4,96,768]{2,1,0:T(8,128)(2,1)} %get-tuple-element.161), channel_id=1, source_target_pairs={{0,2},{1,3},{2,0},{3,1},{4,6},{5,7},{6,4},{7,5},{8,10},{9,11},{10,... | collective-permute-start | bytes 1769480 | tf_op jit(solution)/shard_map/ppermute | solution.py:597
  312.6 45.6 %collective-permute-start.27 = (bf16[4,96,768]{2,1,0:T(8,128)(2,1)}, bf16[4,96,768]{2,1,0:T(8,128)(2,1)S(1)}, u32[]{:S(2)}, u32[]{:S(2)}) collective-permute-start(bf16[4,96,768]{2,1,0:T(8,128)(2,1)} %get-tuple-element.163), channel_id=1, source_target_pairs={{0,6},{1,7},{2,4},{3,5},{4,2},{5,3},{6,0},{7,1},{8,14},{9,15},{10,... | collective-permute-start | bytes 1769480 | tf_op jit(solution)/shard_map/ppermute | solution.py:604
  315.0 36.4 %copy-start.39 = (f32[4,16,768]{2,1,0:T(8,128)S(1)}, f32[4,16,768]{2,1,0:T(8,128)}, u32[]{:S(2)}) copy-start(f32[4,16,768]{2,1,0:T(8,128)} %fusion.5.refs_1_) | copy-start | bytes 589828
  315.0 36.8 %copy-start.3 = (bf16[4,96,768]{2,1,0:T(8,128)(2,1)S(1)}, bf16[4,96,768]{2,1,0:T(8,128)(2,1)}, u32[]{:S(2)}) copy-start(bf16[4,96,768]{2,1,0:T(8,128)(2,1)} %copy-done.2) | copy-start | bytes 1769476
  351.4 36.8 %collective-permute-start.38 = (f32[4,16,768]{2,1,0:T(8,128)S(1)}, f32[4,16,768]{2,1,0:T(8,128)S(1)}, u32[]{:S(2)}, u32[]{:S(2)}) collective-permute-start(f32[4,16,768]{2,1,0:T(8,128)S(1)} %copy-done.39), channel_id=1, source_target_pairs={{0,16},{4,20},{8,24},{12,28},{16,0},{20,4},{24,8},{28,12},{1,17},{... | collective-permute-start | bytes 589832 | tf_op jit(solution)/shard_map/ppermute | solution.py:592
  353.8 32.6 %collective-permute-start.32 = (bf16[96,768]{1,0:T(8,128)(2,1)S(1)}, bf16[96,768]{1,0:T(8,128)(2,1)S(1)}, u32[]{:S(2)}, u32[]{:S(2)}) collective-permute-start(bf16[96,768]{1,0:T(8,128)(2,1)S(1)} %get-tuple-element.173), channel_id=1, source_target_pairs={{0,8},{4,12},{8,0},{12,4},{16,24},{20,28},{24,16},{28,20},{1,9},{5... | collective-permute-start | bytes 442376 | tf_op jit(solution)/shard_map/ppermute | solution.py:592
  355.7 29.1 %collective-permute-start.33 = (bf16[96,768]{1,0:T(8,128)(2,1)S(1)}, bf16[96,768]{1,0:T(8,128)(2,1)S(1)}, u32[]{:S(2)}, u32[]{:S(2)}) collective-permute-start(bf16[96,768]{1,0:T(8,128)(2,1)S(1)} %get-tuple-element.175), channel_id=1, source_target_pairs={{0,16},{4,20},{8,24},{12,28},{16,0},{20,4},{24,8},{28,12},{1,17},{... | collective-permute-start | bytes 442376 | tf_op jit(solution)/shard_map/ppermute | solution.py:592
  356.5 27.2 %collective-permute-start.34 = (bf16[96,768]{1,0:T(8,128)(2,1)S(1)}, bf16[96,768]{1,0:T(8,128)(2,1)S(1)}, u32[]{:S(2)}, u32[]{:S(2)}) collective-permute-start(bf16[96,768]{1,0:T(8,128)(2,1)S(1)} %get-tuple-element.177), channel_id=1, source_target_pairs={{0,24},{4,28},{8,16},{12,20},{16,8},{20,12},{24,0},{28,4},{1,25},{... | collective-permute-start | bytes 442376 | tf_op jit(solution)/shard_map/ppermute | solution.py:592
  371.5 27.3 %copy-start.12 = (bf16[96,768]{1,0:T(8,128)(2,1)S(1)}, bf16[96,768]{1,0:T(8,128)(2,1)}, u32[]{:S(2)}) copy-start(bf16[96,768]{1,0:T(8,128)(2,1)} %copy-done.11) | copy-start | bytes 442372
  371.5 27.4 %collective-permute-start.31 = (bf16[2,768,768]{2,1,0:T(8,128)(2,1)}, bf16[2,768,768]{2,1,0:T(8,128)(2,1)S(1)}, u32[]{:S(2)}, u32[]{:S(2)}) collective-permute-start(bf16[2,768,768]{2,1,0:T(8,128)(2,1)} %joint_grads.2.refs_0_), channel_id=1, source_target_pairs={{0,1},{1,0},{2,3},{3,2},{4,5},{5,4},{6,7},{7,6},{8,9},{9,8},{10,11... | collective-permute-start | bytes 7077896 | tf_op jit(solution)/shard_map/ppermute | solution.py:597
  383.7 15.0 %collective-permute-start.35 = (bf16[96,768]{1,0:T(8,128)(2,1)S(1)}, bf16[96,768]{1,0:T(8,128)(2,1)S(1)}, u32[]{:S(2)}, u32[]{:S(2)}) collective-permute-start(bf16[96,768]{1,0:T(8,128)(2,1)S(1)} %get-tuple-element.179), channel_id=1, source_target_pairs={{0,8},{4,12},{8,0},{12,4},{16,24},{20,28},{24,16},{28,20},{1,9},{5... | collective-permute-start | bytes 442376 | tf_op jit(solution)/shard_map/ppermute | solution.py:592
  384.8 14.0 %collective-permute-start.36 = (bf16[96,768]{1,0:T(8,128)(2,1)S(1)}, bf16[96,768]{1,0:T(8,128)(2,1)S(1)}, u32[]{:S(2)}, u32[]{:S(2)}) collective-permute-start(bf16[96,768]{1,0:T(8,128)(2,1)S(1)} %get-tuple-element.181), channel_id=1, source_target_pairs={{0,16},{4,20},{8,24},{12,28},{16,0},{20,4},{24,8},{28,12},{1,17},{... | collective-permute-start | bytes 442376 | tf_op jit(solution)/shard_map/ppermute | solution.py:592
  386.5 11.6 %collective-permute-start.37 = (bf16[96,768]{1,0:T(8,128)(2,1)S(1)}, bf16[96,768]{1,0:T(8,128)(2,1)S(1)}, u32[]{:S(2)}, u32[]{:S(2)}) collective-permute-start(bf16[96,768]{1,0:T(8,128)(2,1)S(1)} %get-tuple-element.183), channel_id=1, source_target_pairs={{0,24},{4,28},{8,16},{12,20},{16,8},{20,12},{24,0},{28,4},{1,25},{... | collective-permute-start | bytes 442376 | tf_op jit(solution)/shard_map/ppermute | solution.py:592
  388.3 9.5 %collective-permute-start.39 = (f32[2,16,768]{2,1,0:T(8,128)S(1)}, f32[2,16,768]{2,1,0:T(8,128)S(1)}, u32[]{:S(2)}, u32[]{:S(2)}) collective-permute-start(f32[2,16,768]{2,1,0:T(8,128)S(1)} %dynamic-slice_bitcast_fusion.6), channel_id=1, source_target_pairs={{0,8},{4,12},{8,0},{12,4},{16,24},{20,28},{24,16},{28,20},{1,9},{5... | collective-permute-start | bytes 294920 | tf_op jit(solution)/shard_map/ppermute | solution.py:592
  400.4 16.3 %collective-permute-start.40 = (bf16[4,96,768]{2,1,0:T(8,128)(2,1)S(1)}, bf16[4,96,768]{2,1,0:T(8,128)(2,1)S(1)}, u32[]{:S(2)}, u32[]{:S(2)}) collective-permute-start(bf16[4,96,768]{2,1,0:T(8,128)(2,1)S(1)} %get-tuple-element.189), channel_id=1, source_target_pairs={{0,4},{4,0},{8,12},{12,8},{16,20},{20,16},{24,28},{28,24},{1,5},{5... | collective-permute-start | bytes 1769480 | tf_op jit(solution)/shard_map/ppermute | solution.py:592
  400.8 16.0 %collective-permute-start.41 = (bf16[4,96,768]{2,1,0:T(8,128)(2,1)S(1)}, bf16[4,96,768]{2,1,0:T(8,128)(2,1)S(1)}, u32[]{:S(2)}, u32[]{:S(2)}) collective-permute-start(bf16[4,96,768]{2,1,0:T(8,128)(2,1)S(1)} %get-tuple-element.190), channel_id=1, source_target_pairs={{0,2},{1,3},{2,0},{3,1},{4,6},{5,7},{6,4},{7,5},{8,10},{9,11},{10,... | collective-permute-start | bytes 1769480 | tf_op jit(solution)/shard_map/ppermute | solution.py:597
  401.7 25.3 %collective-permute-start.42 = (bf16[4,96,768]{2,1,0:T(8,128)(2,1)S(1)}, bf16[4,96,768]{2,1,0:T(8,128)(2,1)S(1)}, u32[]{:S(2)}, u32[]{:S(2)}) collective-permute-start(bf16[4,96,768]{2,1,0:T(8,128)(2,1)S(1)} %get-tuple-element.191), channel_id=1, source_target_pairs={{0,6},{1,7},{2,4},{3,5},{4,2},{5,3},{6,0},{7,1},{8,14},{9,15},{10,... | collective-permute-start | bytes 1769480 | tf_op jit(solution)/shard_map/ppermute | solution.py:604
  426.9 23.3 %copy-start.48 = (s32[4]{0:T(128)S(1)}, s32[4]{0:T(128)}, u32[]{:S(2)}) copy-start(s32[4]{0:T(128)} %constant.117.clone) | copy-start | bytes 52
  427.8 10.4 %collective-permute-start.43 = (bf16[96,768]{1,0:T(8,128)(2,1)S(1)}, bf16[96,768]{1,0:T(8,128)(2,1)S(1)}, u32[]{:S(2)}, u32[]{:S(2)}) collective-permute-start(bf16[96,768]{1,0:T(8,128)(2,1)S(1)} %get-tuple-element.193), channel_id=1, source_target_pairs={{0,8},{4,12},{8,0},{12,4},{16,24},{20,28},{24,16},{28,20},{1,9},{5... | collective-permute-start | bytes 442376 | tf_op jit(solution)/shard_map/ppermute | solution.py:592
  431.6 12.6 %collective-permute-start.44 = (bf16[96,768]{1,0:T(8,128)(2,1)S(1)}, bf16[96,768]{1,0:T(8,128)(2,1)S(1)}, u32[]{:S(2)}, u32[]{:S(2)}) collective-permute-start(bf16[96,768]{1,0:T(8,128)(2,1)S(1)} %get-tuple-element.194), channel_id=1, source_target_pairs={{0,16},{4,20},{8,24},{12,28},{16,0},{20,4},{24,8},{28,12},{1,17},{... | collective-permute-start | bytes 442376 | tf_op jit(solution)/shard_map/ppermute | solution.py:592
  432.5 11.7 %collective-permute-start.45 = (bf16[96,768]{1,0:T(8,128)(2,1)S(1)}, bf16[96,768]{1,0:T(8,128)(2,1)S(1)}, u32[]{:S(2)}, u32[]{:S(2)}) collective-permute-start(bf16[96,768]{1,0:T(8,128)(2,1)S(1)} %get-tuple-element.195), channel_id=1, source_target_pairs={{0,24},{4,28},{8,16},{12,20},{16,8},{20,12},{24,0},{28,4},{1,25},{... | collective-permute-start | bytes 442376 | tf_op jit(solution)/shard_map/ppermute | solution.py:592
  434.1 4.1 collective-permute-start.50
  435.6 10.1 %collective-permute-start.48 = (bf16[3,96,768]{2,1,0:T(8,128)(2,1)S(1)}, bf16[3,96,768]{2,1,0:T(8,128)(2,1)S(1)}, u32[]{:S(2)}, u32[]{:S(2)}) collective-permute-start(bf16[3,96,768]{2,1,0:T(8,128)(2,1)S(1)} %get-tuple-element.292), channel_id=1, source_target_pairs={{0,2},{1,3},{2,0},{3,1},{4,6},{5,7},{6,4},{7,5},{8,10},{9,11},{10,... | collective-permute-start | bytes 1327112 | tf_op jit(solution)/shard_map/ppermute | solution.py:597
  444.3 5.2 %collective-permute-start.46 = (bf16[96,768]{1,0:T(8,128)(2,1)S(1)}, bf16[96,768]{1,0:T(8,128)(2,1)S(1)}, u32[]{:S(2)}, u32[]{:S(2)}) collective-permute-start(bf16[96,768]{1,0:T(8,128)(2,1)S(1)} %add_convert_fusion), channel_id=1, source_target_pairs={{0,2},{1,3},{2,0},{3,1},{4,6},{5,7},{6,4},{7,5},{8,10},{9,11},{10,... | collective-permute-start | bytes 442376 | tf_op jit(solution)/shard_map/ppermute | solution.py:597
  445.6 1.3 collective-permute-start.51
  447.5 11.2 %collective-permute-start.52 = (f32[16,768]{1,0:T(8,128)}, f32[16,768]{1,0:T(8,128)}, u32[]{:S(2)}, u32[]{:S(2)}) collective-permute-start(f32[16,768]{1,0:T(8,128)} %add.243), channel_id=1, source_target_pairs={{0,2},{1,3},{2,0},{3,1},{4,6},{5,7},{6,4},{7,5},{8,10},{9,11},{10,... | collective-permute-start | bytes 147464 | tf_op jit(solution)/shard_map/ppermute | solution.py:597
  449.6 11.1 %collective-permute-start.47 = (bf16[2,96,768]{2,1,0:T(8,128)(2,1)S(1)}, bf16[2,96,768]{2,1,0:T(8,128)(2,1)S(1)}, u32[]{:S(2)}, u32[]{:S(2)}) collective-permute-start(bf16[2,96,768]{2,1,0:T(8,128)(2,1)S(1)} %pad_maximum_fusion.13), channel_id=1, source_target_pairs={{0,1},{1,0},{2,3},{3,2},{4,5},{5,4},{6,7},{7,6},{8,9},{9,8},{10,11... | collective-permute-start | bytes 884744 | tf_op jit(solution)/shard_map/ppermute | solution.py:597
  449.7 12.8 %collective-permute-start.49 = (bf16[2,3,96,768]{3,2,1,0:T(8,128)(2,1)S(1)}, bf16[2,3,96,768]{3,2,1,0:T(8,128)(2,1)S(1)}, u32[]{:S(2)}, u32[]{:S(2)}) collective-permute-start(bf16[2,3,96,768]{3,2,1,0:T(8,128)(2,1)S(1)} %pad_maximum_fusion.3), channel_id=1, source_target_pairs={{0,1},{1,0},{2,3},{3,2},{4,5},{5,4},{6,7},{7,6},{8,9},{9,8},{10,11... | collective-permute-start | bytes 2654216 | tf_op jit(solution)/shard_map/ppermute | solution.py:597
  (41 other events, 384.1 us)
Sparse Core Ops, SparseCore 0:
  14.8 107.8 all-gather.4
  125.5 53.0 all-gather.6

commit v3 on v2

--- a/solution.py
+++ b/solution.py
@@ -233,8 +233,11 @@
     )
 
 
-def ffn_rows(pre_ref, wup_ref, wdown_ref, gains_ref, shifts_ref, low_ref, act_ref, slope_ref, pre2_ref):
-    width = pre_ref.shape[1]
+def ffn_rows(
+    seg_length, pre_ref, cot_ref, wup_ref, wdown_ref, gains_ref, shifts_ref,
+    low_ref, act_ref, slope_ref, out_ref, branch_ref, grad_ref, sums_ref,
+):
+    rows, width = pre_ref.shape
     unit, unused = norm_parts(pre_ref[...])
     total = unit * gains_ref[0:1].astype(F32) + shifts_ref[0:1].astype(F32)
     low = total.astype(BF16)
@@ -248,43 +251,59 @@
         slope_ref[:, cols] = slope.astype(BF16)
         total = total + dot_nn(act_ref[:, cols], down_block(wdown_ref, part))
         held = ahead
-    pre2_ref[...] = total
-
-
-def ffn_forward(pre_first, w_up, w_down, gains, shifts, block, span, prior=(), after=()):
+    gain = gains_ref[1:2].astype(F32)
+    unit, inverse = norm_parts(total)
+    out_ref[...] = (unit * gain + shifts_ref[1:2].astype(F32)).astype(BF16)
+    grad = cot_ref[...].astype(F32)
+    pre_grad = norm_back(grad, unit, inverse, gain)
+    grad_ref[...] = pre_grad
+    branch_ref[...] = pre_grad.astype(BF16)
+
+    @pl.when(pl.program_id(0) == 0)
+    def start_sums():
+        sums_ref[...] = jnp.zeros_like(sums_ref)
+
+    inner = jnp.where(lax.broadcasted_iota(jnp.int32, grad.shape, 0) % seg_length == 0, 0.0, grad)
+    sums_ref[1:2] += jnp.sum(inner * unit, axis=0, keepdims=True)
+    sums_ref[4:5] += jnp.sum(inner, axis=0, keepdims=True)
+
+
+def ffn_forward(pre_first, cot, w_up, w_down, gains, shifts, seg_length, block, span, prior=(), after=()):
     rows, width = pre_first.shape
-    wide = shape_of((rows, 4 * width), BF16)
+    wide, low = shape_of((rows, 4 * width), BF16), shape_of((rows, width), BF16)
     return rows_call(
-        ffn_rows, "ffn_forward", block, span, [pre_first],
+        partial(ffn_rows, seg_length), "ffn_forward", block, span, [pre_first, cot],
         [(value, whole(value.shape)) for value in (w_up, w_down, gains, shifts)],
-        [shape_of((rows, width), BF16), wide, wide, shape_of((rows, width), F32)], 8 * width * width, prior, after,
-    )
-
-
-def edge_rows(pre_ref, wup_ref, wdown_ref, gains_ref, shifts_ref, out_ref):
+        [low, wide, wide, low, low, shape_of((rows, width), F32)], 8 * width * width, prior, after,
+        extra=[shape_of((8, width), F32)],
+    )
+
+
+def edge_rows(pre_ref, wup_ref, wdown_ref, gains_ref, shifts_ref, out_ref, total_ref):
     unit, unused = norm_parts(pre_ref[...])
     total = unit * gains_ref[0:1].astype(F32) + shifts_ref[0:1].astype(F32)
     low = total.astype(BF16)
     for part in range(4):
         act, unused = gelu_parts(dot_nn(low, square(wup_ref[part])))
         total = total + dot_nn(act.astype(BF16), down_block(wdown_ref, part))
+    total_ref[...] = total
     unit, unused = norm_parts(total)
     out_ref[...] = unit * gains_ref[1:2].astype(F32) + shifts_ref[1:2].astype(F32)
 
 
-def edge_first_kernel(ids_ref, pre_ref, gains_ref, shifts_ref, half_ref, other_ref, out_ref, wup_ref, wdown_ref, sems):
+def edge_first_kernel(ids_ref, pre_ref, gains_ref, shifts_ref, half_ref, other_ref, out_ref, total_ref, wup_ref, wdown_ref, sems):
     parts = (half_ref, other_ref)
     up = fetch_halves(ids_ref, parts, wup_ref, sems)
     down = fetch_halves(ids_ref, parts, wdown_ref, sems, wup_ref.shape[2], True)
     for copy in up + down:
         copy.wait()
-    edge_rows(pre_ref, wup_ref, wdown_ref, gains_ref, shifts_ref, out_ref)
+    edge_rows(pre_ref, wup_ref, wdown_ref, gains_ref, shifts_ref, out_ref, total_ref)
 
 
 def edge_forward(pre_edge, weights, gains, shifts, pieces=None, ids=None):
     rows, width = pre_edge.shape
     norms = [(gains, whole(gains.shape)), (shifts, whole(shifts.shape))]
-    outs = [shape_of((rows, width), F32)]
+    outs = [shape_of((rows, width), F32)] * 2
     if pieces is None:
         return rows_call(
             edge_rows, "edge_forward", rows, (0, 1), [pre_edge], [(value, whole(value.shape)) for value in weights] + norms,
@@ -294,43 +313,6 @@
     return rows_call(
         edge_first_kernel, "edge_forward", rows, (0, 1), [pre_edge], norms + [(part, ANYWHERE) for part in parts], outs,
         60 * width * width, extra=shapes, ids=ids, scratch=[pltpu.SemaphoreType.DMA((8,))],
-    )
-
-
-def norm_rows(seg_length, cot_ref, pre2_ref, edge_ref, cls_ref, gains_ref, shifts_ref, out_ref, branch_ref, grad_ref, sums_ref):
-    rows, width = cot_ref.shape
-    top = lax.broadcasted_iota(jnp.int32, (seg_length, width), 0) == 0
-
-    def with_edge(values, edge):
-        parts = [
-            jnp.where(top, edge[seg], values[seg * seg_length : (seg + 1) * seg_length]) for seg in range(rows // seg_length)
-        ]
-        return jnp.concatenate(parts, axis=0) if len(parts) > 1 else parts[0]
-
-    gain = gains_ref[1:2].astype(F32)
-    unit, inverse = norm_parts(pre2_ref[...])
-    out_ref[...] = with_edge(unit * gain + shifts_ref[1:2].astype(F32), cls_ref).astype(BF16)
-    grad = with_edge(cot_ref[...].astype(F32), edge_ref)
-    pre_grad = norm_back(grad, unit, inverse, gain)
-    grad_ref[...] = pre_grad
-    branch_ref[...] = pre_grad.astype(BF16)
-
-    @pl.when(pl.program_id(0) == 0)
-    def start_sums():
-        sums_ref[...] = jnp.zeros_like(sums_ref)
-
-    sums_ref[1:2] += jnp.sum(grad * unit, axis=0, keepdims=True)
-    sums_ref[4:5] += jnp.sum(grad, axis=0, keepdims=True)
-
-
-def norm_backward(cot, pre_second, edge, cls_new, gains, shifts, seg_length, block, after):
-    rows, width = cot.shape
-    return rows_call(
-        partial(norm_rows, seg_length), "norm_backward", block, (0, rows // block),
-        [cot, pre_second, (edge, seg_length), (cls_new, seg_length)],
-        [(gains, whole(gains.shape)), (shifts, whole(shifts.shape))],
-        [shape_of((rows, width), BF16), shape_of((rows, width), BF16), shape_of((rows, width), F32)], 2 * width,
-        after=after, extra=[shape_of((8, width), F32)],
     )
 
 
@@ -366,8 +348,8 @@
     )
 
 
-def attention_back_rows(seg_length, grad1_ref, low1_ref, proj_ref, probs_ref, wqo_ref, gradp_ref, input_ref, gradm_ref):
-    rows, width = grad1_ref.shape
+def attention_back_rows(seg_length, low1_ref, proj_ref, probs_ref, wqo_ref, gradp_ref, gradm_ref):
+    rows, width = low1_ref.shape
     pairs = width // PAIR
     gradm_ref[...] = dot_nt(low1_ref[...], square(wqo_ref[3])).astype(BF16)
     first_half = lane_half((seg_length, PAIR))
@@ -381,30 +363,43 @@
             )
             for place, grad in zip(cols, grads):
                 gradp_ref[span, place] = grad.astype(BF16)
+
+
+def attention_backward(low1, proj, probs, w_qo, seg_length, block, after=()):
+    rows, width = low1.shape
+    return rows_call(
+        partial(attention_back_rows, seg_length), "attention_backward", block, (0, rows // block),
+        [low1, proj, (probs, seg_length)], [(w_qo, whole(w_qo.shape))],
+        [shape_of((rows, 3 * width), BF16)],
+        width * (width + 16 * seg_length), (), after, scratch=[pltpu.VMEM((block, width), BF16)], weight=SHORT,
+    )[0]
+
+
+def input_rows(grad1_ref, gradp_ref, wqo_ref, input_ref):
+    width = grad1_ref.shape[1]
     total = grad1_ref[...]
     for part in range(3):
         total = total + dot_nt(gradp_ref[:, part * width : (part + 1) * width], square(wqo_ref[part]))
     input_ref[...] = total
 
 
-def attention_backward(grad1, low1, proj, probs, w_qo, seg_length, block, span, prior=(), after=()):
+def input_gradient(grad1, gradp, w_qo, block, after):
     rows, width = grad1.shape
     return rows_call(
-        partial(attention_back_rows, seg_length), "attention_backward", block, span,
-        [grad1, low1, proj, (probs, seg_length)], [(w_qo, whole(w_qo.shape))],
-        [shape_of((rows, 3 * width), BF16), shape_of((rows, width), F32)],
-        width * (4 * width + 16 * seg_length), prior, after, scratch=[pltpu.VMEM((block, width), BF16)], weight=SHORT,
-    )
+        input_rows, "input_gradient", block, (0, rows // block), [grad1, gradp], [(w_qo, whole(w_qo.shape))],
+        [shape_of((rows, width), F32)], 3 * width * width, (), after, weight=LONG,
+    )[0]
 
 
 def cross_kernel(
-    local, fetch, ids_ref, rows_ref, cot_ref, keyc_ref, keyr_ref, place_ref, table_ref, gains_ref, shifts_ref, *refs
+    local, fetch, ids_ref, rows_ref, cot_ref, total_ref, keyc_ref, keyr_ref, place_ref, table_ref, gains_ref, shifts_ref, *refs
 ):
     parts, refs = (refs[:2], refs[2:]) if fetch else (refs[:1], refs[1:])
-    new_ref, edge_ref, low_ref, gradp_ref, mixed_ref, gradz_ref, sums_ref, table_grad_ref, proj_ref, probs_ref, gradm_ref = refs[:11]
+    new_ref, branch_ref, edge_ref, low_ref, gradp_ref, mixed_ref, gradz_ref, sums_ref, table_grad_ref = refs[:9]
+    proj_ref, probs_ref, gradm_ref = refs[9:12]
     wc_ref = parts[0]
     if fetch:
-        wc_ref, sems = refs[11:]
+        wc_ref, sems = refs[12:]
         for copy in fetch_halves(ids_ref, parts, wc_ref, sems):
             copy.wait()
     count, width = rows_ref.shape
@@ -428,7 +423,7 @@
     pre_third = embedded + dot_nn(mixed_ref[...], square(wc_ref[3]))
     unit, inverse = norm_parts(pre_third)
     gain = gains_ref[2:3].astype(F32)
-    new_ref[...] = unit[:local] * gain + shifts_ref[2:3].astype(F32)
+    new_ref[...] = (unit[:local] * gain + shifts_ref[2:3].astype(F32)).astype(BF16)
     grad_out = cot_ref[...]
     grad_third = norm_back(grad_out, unit, inverse, gain)
     sums_ref[...] = jnp.zeros_like(sums_ref)
@@ -446,22 +441,28 @@
     grad_edge = grad_third[:local]
     for part in range(3):
         grad_edge = grad_edge + dot_nt(gradp_ref[:local, part * width : (part + 1) * width], square(wc_ref[part]))
-    edge_ref[...] = grad_edge
+    unit, inverse = norm_parts(total_ref[...])
+    sums_ref[1:2] = jnp.sum(grad_edge * unit, axis=0, keepdims=True)
+    sums_ref[4:5] = jnp.sum(grad_edge, axis=0, keepdims=True)
+    pre_grad = norm_back(grad_edge, unit, inverse, gains_ref[1:2].astype(F32))
+    edge_ref[...] = pre_grad
+    branch_ref[...] = pre_grad.astype(BF16)
     table_grad_ref[...] = lax.dot_general(
         picks[:local].astype(F32), grad_edge, (((0,), (0,)), ((), ())),
         precision=lax.Precision.HIGHEST, preferred_element_type=F32,
     )
 
 
-def cross_block(ids, local, edge_rows, edge_cot, key_col, key_row, place, table, gains, shifts, parts, shape):
+def cross_block(ids, local, edge_rows, edge_cot, edge_total, key_col, key_row, place, table, gains, shifts, parts, shape):
     count, width = edge_rows.shape
-    read = [edge_rows, edge_cot, key_col, key_row, place, table, gains, shifts]
+    read = [edge_rows, edge_cot, edge_total, key_col, key_row, place, table, gains, shifts]
     part_specs, fetched = [whole(part.shape) for part in parts], []
     if shape is not None:
         part_specs = [ANYWHERE] * len(parts)
         fetched = [pltpu.VMEM(shape.shape, BF16), pltpu.SemaphoreType.DMA((4,))]
     shapes = (
-        jax.ShapeDtypeStruct((local, width), F32),
+        jax.ShapeDtypeStruct((local, width), BF16),
+        jax.ShapeDtypeStruct((local, width), BF16),
         jax.ShapeDtypeStruct((local, width), F32),
         jax.ShapeDtypeStruct((count, width), BF16),
         jax.ShapeDtypeStruct((count, 3 * width), BF16),
@@ -490,8 +491,14 @@
     )(ids, *read, *parts)
 
 
-def cols_grad_kernel(ids_ref, left_ref, right_ref, *refs):
-    refs[-1][0] = dot_tn(left_ref[...], right_ref[...]).astype(BF16)
+def cols_grad_kernel(side, ids_ref, left_ref, right_ref, rider_ref, *refs):
+    out_ref = refs[-1]
+    owners, rows = rider_ref.shape[0], left_ref.shape[1] // rider_ref.shape[0]
+    block = half_block(side, pl.program_id(0), ids_ref)
+    product = dot_tn(left_ref[...], right_ref[...]).astype(BF16)
+    out_ref[0, :, :rows] = product.reshape(owners, rows, product.shape[1])
+    rider = rider_ref[...]
+    out_ref[0, :, rows:] = jnp.where(block == 0, rider, jnp.zeros_like(rider))
 
 
 def joint_grad_kernel(side, ids_ref, left_ref, last_left_ref, right_ref, last_right_ref, *refs):
@@ -510,16 +517,16 @@
     return 2 * ((ids[1] & 1) ^ side) + step
 
 
-def half_grads(kernel, name, side, ids, operands, specs, after, weight):
+def half_grads(kernel, name, ids, operands, specs, shape, after, weight):
     rows, width = operands[0].shape
     return pl.pallas_call(
         kernel,
-        out_shape=jax.ShapeDtypeStruct((2, width, width), BF16),
+        out_shape=jax.ShapeDtypeStruct((2,) + shape, BF16),
         grid_spec=pltpu.PrefetchScalarGridSpec(
             num_scalar_prefetch=1,
             grid=(2,),
             in_specs=specs + [ANYWHERE] * len(after),
-            out_specs=pl.BlockSpec((1, width, width), lambda j, ids: (j, 0, 0)),
+            out_specs=pl.BlockSpec((1,) + shape, lambda j, ids: (j,) + (0,) * len(shape)),
         ),
         compiler_params=pltpu.CompilerParams(vmem_limit_bytes=56 * MIB),
         cost_estimate=cost(4 * rows * width * width, 10 * rows * width, weight),
@@ -527,13 +534,27 @@
     )(ids, *operands, *after)
 
 
-def cols_grads(side, ids, left, right, after, weight):
+def plain_cols_kernel(ids_ref, left_ref, right_ref, *refs):
+    refs[-1][0] = dot_tn(left_ref[...], right_ref[...]).astype(BF16)
+
+
+def cols_grads(side, ids, left, right, rider, after, weight):
     rows, width = left.shape
+    owners, extra, unused = rider.shape
     specs = [
         whole(left.shape),
         pl.BlockSpec((rows, width), lambda j, ids: (0, half_block(side, j, ids))),
     ]
-    return half_grads(cols_grad_kernel, "cols_grads", side, ids, [left, right], specs, after, weight)
+    if width // owners % 16 == 0:
+        return half_grads(
+            partial(cols_grad_kernel, side), "cols_grads", ids, [left, right, rider], specs + [whole(rider.shape)],
+            (owners, width // owners + extra, width), after, weight,
+        )
+    product = half_grads(plain_cols_kernel, "cols_grads", ids, [left, right], specs, (width, width), after, weight)
+    first = half_block(side, 0, ids) == 0
+    rider = jnp.where(first, rider, jnp.zeros_like(rider))
+    rider = jnp.stack([rider, jnp.zeros_like(rider)], axis=0)
+    return jnp.concatenate([product.reshape(2, owners, width // owners, width), rider], axis=2)
 
 
 def joint_grads(side, ids, left, last_left, right, last_right, after, weight):
@@ -545,7 +566,7 @@
         whole(left.shape),
     ]
     operands = [left, last_left, right, last_right]
-    return half_grads(partial(joint_grad_kernel, side), "joint_grads", side, ids, operands, specs, after, weight)
+    return half_grads(partial(joint_grad_kernel, side), "joint_grads", ids, operands, specs, (width, width), after, weight)
 
 
 def rows_grad_kernel(ids_ref, left_ref, right_ref, *refs):
@@ -693,26 +714,33 @@
     )(ids, keep.reshape(shape), came.reshape(shape))
 
 
-def settle_kernel(ids_ref, a_ref, b_ref, c_ref, d_ref, *outs):
-    far = ids_ref[0] >> 1
-    for mask, out in enumerate(outs):
-        place = far ^ mask
-        total = (a_ref[place].astype(F32) + b_ref[place].astype(F32)) + (c_ref[place].astype(F32) + d_ref[place].astype(F32))
-        out[...] = total.astype(BF16)
-
-
-def settle(ids, parts):
-    far, rows, width = parts[0].shape
+def settle_kernel(ids_ref, *refs):
+    far = refs[0].shape[0]
+    parts, outs = refs[:-far], refs[-far:]
+    start = 0
+    for first in range(0, len(parts), 4):
+        rows = parts[first].shape[1]
+        for mask, out in enumerate(outs):
+            a, b, c, d = (part[(ids_ref[0] >> 1) ^ mask].astype(F32) for part in parts[first : first + 4])
+            out[start : start + rows] = ((a + b) + (c + d)).astype(BF16)
+        start += rows
+
+
+def settle(ids, *groups):
+    far, unused, width = groups[0][0].shape
+    heights = [group[0].shape[1] for group in groups]
+    if len(groups) > 1 and any(rows % 16 for rows in heights):
+        return [jnp.concatenate(parts, axis=0) for parts in zip(*[settle(ids, group) for group in groups])]
     whole_spec = pl.BlockSpec(memory_space=pltpu.VMEM)
     return pl.pallas_call(
         settle_kernel,
-        out_shape=(jax.ShapeDtypeStruct((rows, width), BF16),) * far,
-        in_specs=[pl.BlockSpec(memory_space=pltpu.SMEM)] + [whole_spec] * 4,
+        out_shape=(jax.ShapeDtypeStruct((sum(heights), width), BF16),) * far,
+        in_specs=[pl.BlockSpec(memory_space=pltpu.SMEM)] + [whole_spec] * (4 * len(groups)),
         out_specs=[whole_spec] * far,
         compiler_params=pltpu.CompilerParams(vmem_limit_bytes=32 * MIB),
-        cost_estimate=cost(0, 10 * far * rows * width),
+        cost_estimate=cost(0, 10 * far * sum(heights) * width),
         name="settle",
-    )(ids, *parts)
+    )(ids, *[part for group in groups for part in group])
 
 
 def halve(value, axis, bit):
@@ -730,19 +758,23 @@
         self.came = rep_swap(send, 1)
 
     def spread(self, *first):
-        came = later(self.came, *first)
+        came = after_all(self.came, first)
         self.stay, *sends = spread(self.ids, self.keep.reshape(self.shape), came.reshape(self.shape))
         self.came = [seg_swap(sends[0], 1), rep_swap(sends[1], 2), both_swap(sends[2], 1, 2)]
 
-    def settle(self, *first):
-        self.own, *others = settle(self.ids, [self.stay] + [later(value, *first) for value in self.came])
-        self.came = [seg_swap(other, 2 * mask) for mask, other in enumerate(others, 1)]
-
-    def finish(self, *first):
-        total = self.own.astype(F32)
-        for value in self.came:
-            total = total + later(value, *first).astype(F32)
-        return total.astype(BF16)
+    def parts(self, *first):
+        return [self.stay] + [after_all(value, first) for value in self.came]
+
+
+def swap_far(others):
+    return [seg_swap(other, 2 * mask) for mask, other in enumerate(others, 1)]
+
+
+def add_up(own, came, *first):
+    total = own.astype(F32)
+    for value in came:
+        total = total + after_all(value, first).astype(F32)
+    return total.astype(BF16)
 
 
 class Sharing:
@@ -761,35 +793,6 @@
             lax.dynamic_index_in_dim(held, order[self.ids[1] ^ owner], 0, keepdims=False).astype(F32)
             for owner in (0, 2, 1, 3)
         ]
-
-
-class SmallReduction:
-    def __init__(self, ids, value):
-        self.ids, self.mask = ids, lax.axis_size("seg") // 2
-        self.split(value)
-
-    def split(self, value):
-        bit = (self.ids[0] // self.mask) & 1
-        self.own, self.other = halve(value.reshape((2, self.mask) + value.shape[1:]), 0, bit)
-        self.came = seg_swap(self.other, self.mask)
-        self.mask //= 2
-
-    def step(self, *first):
-        value = self.own + later(self.came, *first)
-        if self.mask:
-            self.split(value)
-        elif value.ndim == 3:
-            self.own = self.other = value[0]
-            self.came = rep_swap(self.own, 1)
-        else:
-            self.own = self.other = value
-            self.came = rep_swap(self.own, 2)
-            self.last = True
-
-    def finish(self, *first):
-        while not getattr(self, "last", False):
-            self.step(*first)
-        return self.own + later(self.came, *first)
 
 
 def body(tokens, cotangent, doc_counts, w_qkv, w_out, w_up, w_down, c_qkv, c_out, pos_table, norm_gains, norm_shifts):
@@ -844,7 +847,7 @@
     everything = (0, steps)
     if aligned:
         proj, probs, mixed, pre_first, full_qo = attention_forward(
-            flat, None, seg_length, block, everything, pieces=qo_pieces, ids=ids
+            flat, None, seg_length, block, everything, after=[keys, places], pieces=qo_pieces, ids=ids
         )
     else:
         full_qo = put_in_place(ids, qo_pieces).reshape(4, 1, width, width)
@@ -863,90 +866,97 @@
 
     pre_edge = pre_first.reshape(local, seg_length, width)[:, 0]
     if aligned:
-        edge, full_up, full_down = edge_forward(
+        edge, edge_total, full_up, full_down = edge_forward(
             pre_edge, None, gains, shifts, ([ffn_half, ffn_other], shapes), ids
         )
     else:
         full_up = joined([ffn_half, ffn_other], 0, False)
         full_down = joined([ffn_half, ffn_other], shard_rows, True)
-        edge = edge_forward(pre_edge, [full_up, full_down], gains, shifts)[0]
+        edge, edge_total = edge_forward(pre_edge, [full_up, full_down], gains, shifts)
     edge_cot = cot.reshape(local, seg_length, width)[:, 0].astype(F32)
     edges = Gather(jnp.stack([edge, edge_cot], axis=0))
-    kept = ffn_forward(pre_first, full_up, full_down, gains, shifts, block, halves_of[0], after=[edge])
+    small_block, small_steps = block // 2, steps
+    *kept, sums2a = ffn_forward(
+        pre_first, cot, full_up, full_down, gains, shifts, seg_length, small_block, (0, small_steps), after=[edge]
+    )
     edges.across(kept[0])
-    low, act, slope, pre_second = ffn_forward(
-        pre_first, full_up, full_down, gains, shifts, block, halves_of[1], prior=kept, after=[edges.evens]
-    )
-    edges = edges.finish(pre_second)
-    cross_half = later(cross_half, pre_second)
+    low, act, slope, out, branch, grad2, sums2b = ffn_forward(
+        pre_first, cot, full_up, full_down, gains, shifts, seg_length, small_block, (small_steps, small_steps), prior=kept,
+        after=[edges.evens],
+    )
+    edges = edges.finish(low)
+    cross_half = later(cross_half, low)
     cross_parts, cross_shape = [cross_half, rep_swap(cross_half, 1)], shapes[0]
     if not aligned:
         cross_parts, cross_shape = [joined(cross_parts, 0, False)], None
-    cls_new, grad_edge, c_low, c_gradp, c_mixed, c_gradz, c_sums, table_grad = cross_block(
-        ids, local, edges[:, 0].reshape(-1, width), edges[:, 1].reshape(-1, width),
+    cls_new, cls_branch, cls_grad, c_low, c_gradp, c_mixed, c_gradz, c_sums, table_grad = cross_block(
+        ids, local, edges[:, 0].reshape(-1, width), edges[:, 1].reshape(-1, width), edge_total,
         keys[:, None], jnp.concatenate([keys, keys])[None, :], places, table, gains, shifts, cross_parts, cross_shape,
     )
-    own_low = lax.dynamic_slice_in_dim(c_low, me * shard_rows, shard_rows, 1)
-    own_mixed = lax.dynamic_slice_in_dim(c_mixed, me * shard_rows, shard_rows, 1)
+
+    def with_edge(values, edge):
+        whole_rows = values.reshape(local, seg_length, width)
+        return lax.dynamic_update_slice(whole_rows, edge[:, None], (0, 0, 0)).reshape(rows, width)
+
+    branch, grad2 = with_edge(branch, cls_branch), with_edge(grad2, cls_grad)
+    send_down, keep_down = rows_grads(ids, act, branch, count, [])
+    down = Reduction(ids, send_down, keep_down)
+    *kept, sums1a = ffn_backward(
+        branch, grad2, pre_first, slope, full_up, full_down, gains, block, halves_of[0], LONG, after=[send_down]
+    )
+    down.spread(kept[0])
+    grad_hidden, grad1, low1, sums1b = ffn_backward(
+        branch, grad2, pre_first, slope, full_up, full_down, gains, block, halves_of[1], SHORT, prior=kept, after=[down.stay]
+    )
+    norm_sums = (sums2a + sums2b + sums1a + sums1b + c_sums).reshape(8, count, norm_cols).transpose(1, 0, 2)
+    norm_sums = jnp.pad(norm_sums, ((0, 0), (0, 0), (0, width - norm_cols)))
+    rider = jnp.concatenate([norm_sums, table_grad.reshape(count, table_rows, width)], axis=1).astype(BF16)
+    send_up = cols_grads(1, ids, low, grad_hidden, rider, [], SHORT)
+    own_down, *others = settle(ids, down.parts(send_up))
+    came_down = swap_far(others)
+    keep_up = cols_grads(0, ids, low, grad_hidden, rider, [send_up, own_down], LONG)
+    up = Reduction(ids, send_up, keep_up)
+    up.spread(keep_up, *came_down[:1])
+    grad_proj = attention_backward(low1, proj, probs, full_qo, seg_length, block, after=[up.stay])
+    down_share = add_up(own_down, came_down, grad_proj)
+    send_qo = joint_grads(1, ids, flat, mixed, grad_proj, low1, [], SHORT)
+    own_up, *others = settle(ids, up.parts(send_qo))
+    came_up = swap_far(others)
+    keep_qo = joint_grads(0, ids, flat, mixed, grad_proj, low1, [send_qo, own_up], LONG)
+    qo = Reduction(ids, send_qo, keep_qo)
+    qo.spread(keep_qo, *came_up[:2])
+    input_grad = input_gradient(grad1, grad_proj, full_qo, block, [qo.stay])
+    own, *others = settle(ids, qo.parts(input_grad))
+    came = swap_far(others)
+    early = Sharing(ids, jnp.concatenate([down_share, add_up(own_up, came_up, own)], axis=0))
+    own_low = lax.dynamic_slice_in_dim(later(c_low, own), me * shard_rows, shard_rows, 1)
+    own_mixed = lax.dynamic_slice_in_dim(later(c_mixed, own), me * shard_rows, shard_rows, 1)
     grad_c = shares_of(jnp.concatenate([dot_tn(own_low, c_gradp), dot_tn(own_mixed, c_gradz)], axis=1)).astype(BF16)
     c_own, c_other = halve(grad_c.reshape(2, 2, shard_rows, width), 0, rep & 1)
-    c_came = rep_swap(c_other, 1)
-    layer_out, branch, grad2, sums2 = norm_backward(
-        cot, pre_second, grad_edge[:, None], cls_new[:, None], gains, shifts, seg_length, block, [c_other]
-    )
-    c_own, c_other = halve(c_own.astype(F32) + later(c_came, branch).astype(F32), 0, rep >> 1)
-    c_other = c_other.astype(BF16)
-    c_came = rep_swap(c_other, 2)
-    send_down, keep_down = rows_grads(ids, act, branch, count, [c_other])
-    c_share = (c_own + later(c_came, send_down).astype(F32)).astype(BF16)
-    down = Reduction(ids, send_down, keep_down)
-    grad_hidden, grad1, low1, sums1 = ffn_backward(
-        branch, grad2, pre_first, slope, full_up, full_down, gains, block, everything, LONG, after=[send_down, c_share]
-    )
-    down.spread(grad1)
-    send_up = cols_grads(1, ids, low, grad_hidden, [down.stay], SHORT)
-    norm_sums = (later(sums2, send_up) + sums1 + c_sums).reshape(8, count, norm_cols).transpose(1, 0, 2)
-    norm_sums = jnp.pad(norm_sums, ((0, 0), (0, 0), (0, width - norm_cols)))
-    tiny = SmallReduction(ids, jnp.concatenate([norm_sums, table_grad.reshape(count, table_rows, width)], axis=1))
-    keep_up = cols_grads(0, ids, low, grad_hidden, [send_up, tiny.other], LONG)
-    up = Reduction(ids, send_up, keep_up)
-    up.spread(keep_up)
-    grad_proj, input_grad = attention_backward(
-        grad1, low1, proj, probs, full_qo, seg_length, block, everything, after=[up.stay]
-    )
-    down.settle(grad_proj)
-    up.settle(grad_proj)
-    send_qo = joint_grads(1, ids, flat, mixed, grad_proj, low1, [up.own, down.own], SHORT)
-    keep_qo = joint_grads(0, ids, flat, mixed, grad_proj, low1, [send_qo], LONG)
-    qo = Reduction(ids, send_qo, keep_qo)
-    tiny.step(send_qo)
-    early = Sharing(ids, jnp.stack([down.finish(keep_qo), up.finish(keep_qo), c_share], axis=0))
-    tiny.step(keep_qo)
-    qo.spread(early.value, tiny.other)
-    early.step(qo.came[0])
-    tiny.step(qo.came[0])
-    qo.settle()
-    early_shares = early.finish(qo.own)
-    tiny.step(qo.own)
-    qo_share = qo.finish()
-    summed = tiny.finish(qo_share)
-    late = Sharing(ids, qo_share)
-    late.step()
-    late_shares = late.finish()
-
-    def side_by_side(parts):
-        return jnp.concatenate(parts, axis=1)
+    c_own, c_other = halve(c_own.astype(F32) + rep_swap(c_other, 1).astype(F32), 0, rep >> 1)
+    c_came = rep_swap(c_other.astype(BF16), 2)
+    late = Sharing(ids, add_up(own, came))
+    early.step(late.value)
+    crossing = Sharing(ids, (c_own + later(c_came, late.value).astype(F32)).astype(BF16))
+    layer_out = with_edge(later(out, crossing.value), cls_new)
+    late.step(layer_out)
+    crossing.step(late.value)
+    early_shares = early.finish(late.value)
+    starts = (0, shard_rows, 2 * shard_rows, 2 * shard_rows + 16)
+    down_parts, up_parts, riders = [[part[first:last] for part in early_shares] for first, last in zip(starts, starts[1:])]
+    grad_up, grad_down, summed = jnp.concatenate(up_parts, axis=1), jnp.concatenate(down_parts, axis=0), riders[0]
+    qo_parts, c_parts = late.finish(), crossing.finish()
 
     return (
         layer_out.reshape(tokens.shape),
         input_grad.reshape(tokens.shape),
-        side_by_side(late_shares[:3]),
-        late_shares[3],
-        side_by_side([part[1] for part in early_shares]),
-        jnp.concatenate([part[0] for part in early_shares], axis=0),
-        side_by_side([part[2] for part in early_shares[:3]]),
-        early_shares[3][2],
-        summed[8:],
+        jnp.concatenate(qo_parts[:3], axis=1),
+        qo_parts[3],
+        grad_up,
+        grad_down,
+        jnp.concatenate(c_parts[:3], axis=1),
+        c_parts[3],
+        summed[8 : 8 + table_rows],
         summed[:3, :norm_cols],
         summed[3:6, :norm_cols],
     )

time: 479 us -> 466 us (0.973)
  waiting for transfers between devices: 113 us -> 89.6 us
  Pallas kernels: 235 us -> 243 us
  starting transfers between devices: 55.7 us -> 48.8 us
  local copies, waits for them, and re-layouts: 29.4 us -> 35.6 us
    ppermute x26 -> x23, waiting for transfers between devices: 74.6 us -> 53 us  [seg_swap(): return lax.ppermute(value, 'seg', [(i, i ^ mask) for i in range(count)])]
    pallas_call x7 -> x8, Pallas kernels: 155 us -> 163 us  [rows_call(): pl.pallas_call(run, out_shape=tuple((jax.ShapeDtypeStruct(shape.shape, sh...]
    dynamic_update_slice x0 -> x3, local copies, waits for them, and re-layouts: none -> 5.84 us  [with_edge(): lax.dynamic_update_slice(whole_rows, edge[:, None], (0, 0, 0))]
    ppermute x26 -> x23, starting transfers between devices: 39.4 us -> 35.8 us  [seg_swap(): return lax.ppermute(value, 'seg', [(i, i ^ mask) for i in range(count)])]
    unnamed x105 -> x104, local copies, waits for them, and re-layouts: 8.93 us -> 10.2 us
  transfers between devices with their start and end apart: 55 -> 52, of which waited for: 18 -> 12; matrix products, arithmetic and copies ran while one was open for 6% -> 6% of each run, Pallas kernels for 46% -> 46%
where the time goes in v3:
time: 466 us; the launch traced here: 460 us
  Pallas kernels  243 us (52%)
  waiting for transfers between devices  89.6 us (19%)
  starting transfers between devices  48.8 us (10%)
  local copies, waits for them, and re-layouts  35.6 us (8%)
  between operations  23.5 us (5%)
  other arithmetic  16.9 us (4%)
    pallas_call x8, Pallas kernels, rows_call(): pl.pallas_call(run, out_shape=tuple((jax.ShapeDtypeStruct(shape.shape, sh...  163 us
    ppermute x23, waiting for transfers between devices, seg_swap(): return lax.ppermute(value, 'seg', [(i, i ^ mask) for i in range(count)])  53 us
    pallas_call x4, Pallas kernels, half_grads(): pl.pallas_call(kernel, out_shape=jax.ShapeDtypeStruct((2,) + shape, BF16)...  44.4 us
    ppermute x23, starting transfers between devices, seg_swap(): return lax.ppermute(value, 'seg', [(i, i ^ mask) for i in range(count)])  35.8 us
    all_gather x1, waiting for transfers between devices, body(): ffn_half = lax.all_gather(ffn_piece, 'seg', axis=0)  20.6 us
    pallas_call x1, Pallas kernels, rows_grads(): pl.pallas_call(rows_grad_kernel, out_shape=(half, half), grid_spec=pltpu....  16.5 us
    ppermute x3, waiting for transfers between devices, both_swap(): return lax.ppermute(value, ('seg', 'rep'), pairs)  10.5 us
    unnamed x104, local copies, waits for them, and re-layouts  10.2 us
  transfers between devices with their start and end apart: 52, of which 12 were waited for; matrix products, arithmetic and copies ran while one was open for 6% of the time, Pallas kernels for 46%

profile of v3, /device:TPU:0, one launch (start us, length us, event | category | flops | bytes accessed | tf_op | source)
XLA Modules:
  0.0 460.2 jit_solution(1588262732540156526)
XLA Ops:
  9.2 1.8 reshape.229
  12.4 1.3 dynamic-slice_bitcast_fusion.1
  16.5 3.1 collective-permute-start.1
  19.6 1.5 collective-permute-start
  21.1 2.6 collective-permute-start.3
  23.7 7.5 %collective-permute-done.1.refs_4_ = bf16[2,96,768]{2,1,0:T(8,128)(2,1)S(1)} collective-permute-done((bf16[2,96,768]{2,1,0:T(8,128)(2,1)S(1)}, bf16[2,96,768]{2,1,0:T(8,128)(2,1)S(1)}, u32[]{:S(2)}, u32[]{:S(2)}) %collective-permute-start.1) | collective-permute-done | bytes 294944 | tf_op jit(solution)/shard_map/ppermute | solution.py:613
  31.2 5.2 %collective-permute-start.2 = (bf16[2,96,768]{2,1,0:T(8,128)(2,1)S(1)}, bf16[2,96,768]{2,1,0:T(8,128)(2,1)S(1)}, u32[]{:S(2)}, u32[]{:S(2)}) collective-permute-start(bf16[2,96,768]{2,1,0:T(8,128)(2,1)S(1)} %collective-permute-done.1.refs_4_), channel_id=1, source_target_pairs={{0,4},{4,0},{8,12},{12,8},{16,20},{20,16},{24,28},{28,24},{1,5},{5... | collective-permute-start | bytes 884744 | tf_op jit(solution)/shard_map/ppermute | solution.py:613
  36.4 3.4 collective-permute-start.7
  40.1 13.5 %collective-permute-done.3.refs_6_ = bf16[2,96,768]{2,1,0:T(8,128)(2,1)S(1)} collective-permute-done((bf16[2,96,768]{2,1,0:T(8,128)(2,1)S(1)}, bf16[2,96,768]{2,1,0:T(8,128)(2,1)S(1)}, u32[]{:S(2)}, u32[]{:S(2)}) %collective-permute-start.3) | collective-permute-done | bytes 294944 | tf_op jit(solution)/shard_map/ppermute | solution.py:613
  54.1 1.3 collective-permute-done.9.refs_13_
  55.3 7.9 %collective-permute-done.6.refs_7_ = bf16[2,96,768]{2,1,0:T(8,128)(2,1)S(1)} collective-permute-done((bf16[2,96,768]{2,1,0:T(8,128)(2,1)S(1)}, bf16[2,96,768]{2,1,0:T(8,128)(2,1)S(1)}, u32[]{:S(2)}, u32[]{:S(2)}) %collective-permute-start.6) | collective-permute-done | bytes 294944 | tf_op jit(solution)/shard_map/ppermute | solution.py:613
  64.3 7.7 %collective-permute-done.10.refs_9_ = bf16[2,96,768]{2,1,0:T(8,128)(2,1)} collective-permute-done((bf16[2,96,768]{2,1,0:T(8,128)(2,1)S(1)}, bf16[2,96,768]{2,1,0:T(8,128)(2,1)}, u32[]{:S(2)}, u32[]{:S(2)}) %collective-permute-start.10) | collective-permute-done | bytes 294944 | tf_op jit(solution)/shard_map/ppermute | solution.py:613
  74.2 28.6 %attention_forward.1 = (bf16[2048,2304]{1,0:T(8,128)(2,1)}, bf16[16,6,128,256]{3,2,1,0:T(8,128)(2,1)}, bf16[2048,768]{1,0:T(8,128)(2,1)}, f32[2048,768]{1,0:T(8,128)}, bf16[4,8,96,768]{3,2,1,0:T(8,128)(2,1)}) custom-call(s32[2]{0:T(128)} %pad_add_fusion.1.refs_0_.ids_ref, bf16[2048,768]{1,0:T(8,128)(2,1)} %bitcast.153, bf16[2,96,768]{2,1,0:T(8,128)(2,1)} %bitcast.178, ...), custom_call_target="tpu_custom_call" | custom-call | flops 12884901 | bytes 18874 | tf_op jit(solution)/shard_map/attention_forward/pallas_call | solution.py:127
  102.8 20.6 %all-gather.5.cloned.1.call-done = bf16[16,208,768]{2,1,0:T(8,128)(2,1)} async-done(((bf16[2,208,768]{2,1,0:T(8,128)(2,1)}), bf16[16,208,768]{2,1,0:T(8,128)(2,1)}) %all-gather.5.cloned.1.call-update) | async-done | bytes 5111824 | tf_op jit(solution)/shard_map/all_gather | solution.py:822
  123.4 1.7 copy.131
  125.2 1.7 copy.147
  130.7 1.6 collective-permute-done.15.refs_5_
  132.2 9.3 %edge_forward.1 = (f32[16,768]{1,0:T(8,128)}, f32[16,768]{1,0:T(8,128)}, bf16[4,8,96,768]{3,2,1,0:T(8,128)(2,1)}, bf16[8,4,96,768]{3,2,1,0:T(8,128)(2,1)}) custom-call(s32[2]{0:T(128)} %pad_add_fusion.1.refs_0_.ids_ref, f32[16,768]{1,0:T(8,128)} %bitcast.186, bf16[3,768]{1,0:T(4,128)(2,1)} %slice.100.refs_2_.refs_4_.gains_ref.refs_6_, ...), custom_call_target="tpu_custom_call" | custom-call | flops 1132462080 | bytes 9908736 | tf_op jit(solution)/shard_map/edge_forward/pallas_call | solution.py:127
  142.4 1.4 collective-permute-start.17
  144.6 2.2 collective-permute-start.18
  146.8 21.3 %ffn_forward.2 = (bf16[2048,768]{1,0:T(8,128)(2,1)}, bf16[2048,3072]{1,0:T(8,128)(2,1)}, bf16[2048,3072]{1,0:T(8,128)(2,1)}, bf16[2048,768]{1,0:T(8,128)(2,1)}, ...) custom-call(f32[2048,768]{1,0:T(8,128)} %get-tuple-element.115.refs_0_.refs_2_, ...), custom_call_target="tpu_custom_call" | custom-call | flops 9663676416 | bytes 29901312 | tf_op jit(solution)/shard_map/ffn_forward/pallas_call | solution.py:127
  169.0 21.8 %ffn_forward.3 = (bf16[2048,768]{1,0:T(8,128)(2,1)}, bf16[2048,3072]{1,0:T(8,128)(2,1)}, bf16[2048,3072]{1,0:T(8,128)(2,1)}, bf16[2048,768]{1,0:T(8,128)(2,1)}, ...) custom-call(f32[2048,768]{1,0:T(8,128)} %get-tuple-element.115.refs_, ...), custom_call_target="tpu_custom_call", output_to_operand_aliasing={{0}: (6, {}), {1}: (7, {}), {2}: (8, {}), {3}: (9, {}), {4}... | custom-call | flops 9663676416 | bytes 29901312 | tf_op jit(solution)/shard_map/ffn_forward/pallas_call | solution.py:127
  192.6 1.5 slice_bitcast_fusion.8.table_ref
  194.1 8.3 %collective-permute-done.19 = f32[4,2,16,768]{3,2,1,0:T(8,128)S(1)} collective-permute-done((f32[4,2,16,768]{3,2,1,0:T(8,128)S(1)}, f32[4,2,16,768]{3,2,1,0:T(8,128)S(1)}, u32[]{:S(2)}, u32[]{:S(2)}) %collective-permute-start.19) | collective-permute-done | bytes 393248 | tf_op jit(solution)/shard_map/ppermute | solution.py:613
  203.5 10.0 %cross_block.1 = (bf16[16,768]{1,0:T(8,128)(2,1)}, bf16[16,768]{1,0:T(8,128)(2,1)}, f32[16,768]{1,0:T(8,128)}, bf16[128,768]{1,0:T(8,128)(2,1)}, bf16[128,2304]{...) custom-call(s32[2]{0:T(128)} %pad_add_fusion.1.refs_0_.ids_ref, ...), custom_call_target="tpu_custom_call" | custom-call | flops 10000000000 | bytes 4718592 | tf_op jit(solution)/shard_map/cross_block/pallas_call | solution.py:474
  215.1 2.0 dynamic_update_slice.9
  217.0 16.5 %rows_grads.1 = (bf16[2,8,96,768]{3,2,1,0:T(8,128)(2,1)}, bf16[2,8,96,768]{3,2,1,0:T(8,128)(2,1)}) custom-call(s32[2]{0:T(128)} %pad_add_fusion.1.refs_0_.ids_ref, bf16[2048,3072]{1,0:T(8,128)(2,1)} %get-tuple-element.143.left_ref, bf16[2048,768]{1,0:T(8,128)(2,1)} %bitcast.148), custom_call_target="tpu_custom_call" | custom-call | flops 9663676416 | bytes 15728640 | tf_op jit(solution)/shard_map/rows_grads/pallas_call | solution.py:588
  233.5 2.0 dynamic_update_slice.10
  235.5 20.6 %ffn_backward.2 = (bf16[2048,3072]{1,0:T(8,128)(2,1)}, f32[2048,768]{1,0:T(8,128)}, bf16[2048,768]{1,0:T(8,128)(2,1)}, f32[8,768]{1,0:T(8,128)}) custom-call(bf16[2048,768]{1,0:T(8,128)(2,1)} %bitcast.149, f32[2048,768]{1,0:T(8,128)} %bitcast.145, f32[2048,768]{1,0:T(8,128)} %get-tuple-element.115.refs_0_.refs_2_, ...), custom_call_target="tpu_custom_call" | custom-call | flops 57982058496 | bytes 179394048 | tf_op jit(solution)/shard_map/ffn_backward/pallas_call | solution.py:127
  256.1 2.4 spread.3
  259.6 1.5 collective-permute-start.23
  261.1 1.7 collective-permute-start.24
  262.8 20.5 %ffn_backward.3 = (bf16[2048,3072]{1,0:T(8,128)(2,1)}, f32[2048,768]{1,0:T(8,128)}, bf16[2048,768]{1,0:T(8,128)(2,1)}, f32[8,768]{1,0:T(8,128)}) custom-call(bf16[2048,768]{1,0:T(8,128)(2,1)} %bitcast.150, f32[2048,768]{1,0:T(8,128)} %bitcast.146, ...), custom_call_target="tpu_custom_call", output_to_operand_aliasing={{0}: (7, {}), {1}: (8, {}), {2}: (9, {})} | custom-call | flops 9663676 | bytes 29899 | tf_op jit(solution)/shard_map/ffn_backward/pallas_call | solution.py:127
  284.9 10.3 %cols_grads.2.refs_0_ = bf16[2,8,112,768]{3,2,1,0:T(8,128)(2,1)} custom-call(s32[2]{0:T(128)} %pad_add_fusion.1.refs_0_.ids_ref, bf16[2048,768]{1,0:T(8,128)(2,1)} %get-tuple-element.131.left_ref, bf16[2048,3072]{1,0:T(8,128)(2,1)} %get-tuple-element.154.right_ref, bf16[8,16,768]{2,1,0:T(8,128)(2,1)} %fusion.2.rider_ref), custom_call_target="tpu_custom_call" | custom-call | flops 4831838 | bytes 15728 | tf_op jit(solution)/shard_map/cols_grads/pallas_call | solution.py:522
  295.2 1.5 settle.3
  297.3 10.1 %cols_grads.3 = bf16[2,8,112,768]{3,2,1,0:T(8,128)(2,1)} custom-call(s32[2]{0:T(128)} %pad_add_fusion.1.refs_0_.ids_ref, bf16[2048,768]{1,0:T(8,128)(2,1)} %get-tuple-element.131.left_ref, bf16[2048,3072]{1,0:T(8,128)(2,1)} %get-tuple-element.154.right_ref, bf16[8,16,768]{2,1,0:T(8,128)(2,1)} %fusion.2.rider_ref, ...), custom_call_target="tpu_custom_call" | custom-call | flops 28991029248 | bytes 94371840 | tf_op jit(solution)/shard_map/cols_grads/pallas_call | solution.py:522
  307.5 1.8 copy-done.4
  309.3 2.5 spread.4
  312.7 1.3 collective-permute-start.29
  314.5 1.7 collective-permute-start.27
  316.1 1.9 collective-permute-start.44
  318.0 1.6 collective-permute-start.43
  319.6 26.7 %attention_backward.1.right_ref.refs_1_ = bf16[2048,2304]{1,0:T(8,128)(2,1)} custom-call(bf16[2048,768]{1,0:T(8,128)(2,1)} %get-tuple-element.151.refs_0_.last_right_ref, bf16[2048,2304]{1,0:T(8,128)(2,1)} %get-tuple-element.116.refs_1_, bf16[16,6,128,256]{3,2,1,0:T(8,128)(2,1)} %get-tuple-element.152.refs_2_, ...), custom_call_target="tpu_custom_call" | custom-call | flops 8858370 | bytes 16515 | tf_op jit(solution)/shard_map/attention_backward/pallas_call | solution.py:127
  346.4 12.1 %joint_grads.2.refs_0_ = bf16[2,768,768]{2,1,0:T(8,128)(2,1)} custom-call(s32[2]{0:T(128)} %pad_add_fusion.1.refs_0_.ids_ref, bf16[2048,768]{1,0:T(8,128)(2,1)} %bitcast.154, bf16[2048,768]{1,0:T(8,128)(2,1)} %get-tuple-element.137.last_left_ref, bf16[2048,2304]{1,0:T(8,128)(2,1)} %attention_backward.1.right_ref.refs_1_, ...), custom_call_target="tpu_custom_call" | custom-call | flops 4831838 | bytes 15728 | tf_op jit(solution)/shard_map/joint_grads/pallas_call | solution.py:522
  358.5 1.7 add_convert_fusion.1
  362.7 1.3 collective-permute-start.32
  364.0 11.8 %joint_grads.3 = bf16[2,768,768]{2,1,0:T(8,128)(2,1)} custom-call(s32[2]{0:T(128)} %pad_add_fusion.1.refs_0_.ids_ref, bf16[2048,768]{1,0:T(8,128)(2,1)} %bitcast.155, bf16[2048,768]{1,0:T(8,128)(2,1)} %get-tuple-element.137.last_left_ref, bf16[2048,2304]{1,0:T(8,128)(2,1)} %attention_backward.1.right_ref.refs_1_, ...), custom_call_target="tpu_custom_call" | custom-call | flops 28991029248 | bytes 94371840 | tf_op jit(solution)/shard_map/joint_grads/pallas_call | solution.py:522
  375.9 2.2 collective-permute-start.45
  378.1 1.7 copy-done.5
  379.8 1.5 spread.5
  382.4 1.5 collective-permute-start.34
  383.9 1.7 collective-permute-start.35
  385.5 14.5 %input_gradient.1 = f32[2048,768]{1,0:T(8,128)} custom-call(f32[2048,768]{1,0:T(8,128)} %get-tuple-element.183.refs_0_, bf16[2048,2304]{1,0:T(8,128)(2,1)} %attention_backward.1.right_ref.refs_1_, bf16[4,8,96,768]{3,2,1,0:T(8,128)(2,1)} %get-tuple-element.153.refs_3_.refs_2_, bf16[4,96,768]{2,1,0:T(8,128)(2,1)} %copy-done.9), custom_call_target="tpu_custom_call" | custom-call | flops 43486543872 | bytes 80216064 | tf_op jit(solution)/shard_map/input_gradient/pallas_call | solution.py:127
  400.0 10.5 %collective-permute-done.35.refs_3_ = bf16[4,96,768]{2,1,0:T(8,128)(2,1)S(1)} collective-permute-done((bf16[4,96,768]{2,1,0:T(8,128)(2,1)S(1)}, bf16[4,96,768]{2,1,0:T(8,128)(2,1)S(1)}, u32[]{:S(2)}, u32[]{:S(2)}) %collective-permute-start.35) | collective-permute-done | bytes 589856 | tf_op jit(solution)/shard_map/ppermute | solution.py:625
  411.4 1.2 convolution_convert_fusion.1
  412.6 1.2 convolution_convert_fusion
  414.5 2.1 collective-permute-start.39
  416.6 2.2 collective-permute-start.40
  419.8 1.3 collective-permute-done.38
  421.1 6.9 %collective-permute-done.39 = bf16[96,768]{1,0:T(8,128)(2,1)S(1)} collective-permute-done((bf16[96,768]{1,0:T(8,128)(2,1)S(1)}, bf16[96,768]{1,0:T(8,128)(2,1)S(1)}, u32[]{:S(2)}, u32[]{:S(2)}) %collective-permute-start.39) | collective-permute-done | bytes 147488 | tf_op jit(solution)/shard_map/ppermute | solution.py:613
  428.7 1.6 collective-permute-start.37
  439.8 1.9 dynamic_update_slice.11
  442.7 2.4 collective-permute-done.48
  451.8 1.1 pad_maximum_fusion.1
  (252 shorter events, 41.5 us)
Async XLA Ops:
  7.2 116.2 %all-gather.5.cloned.1.call-start = ((), (), s32[]{:S(2)}) async-start(), calls=%async_computation | async-start | bytes 5750784 | tf_op jit(solution)/shard_map/all_gather | solution.py:822
  14.7 39.2 %copy-start.48 = (s32[2,1,3]{2,1,0:T(1,128)S(1)}, s32[2,1,3]{2,1,0:T(1,128)}, u32[]{:S(2)}) copy-start(s32[2,1,3]{2,1,0:T(1,128)} %param.17) | copy-start | bytes 76
  15.6 175.2 %all-gather.7.cloned.1.call-start = ((), (), s32[]{:S(2)}) async-start(), calls=%async_computation.1 | async-start | bytes 2654208 | tf_op jit(solution)/shard_map/all_gather | solution.py:828
  16.5 57.6 %copy-start.22 = (bf16[96,2,768]{2,0,1:T(8,128)(2,1)}, bf16[96,2,768]{2,0,1:T(8,128)(2,1)S(1)}, u32[]{:S(2)}) copy-start(bf16[96,2,768]{2,0,1:T(8,128)(2,1)S(1)} %copy.148) | copy-start | bytes 884740
  16.5 14.7 %collective-permute-start.1 = (bf16[2,96,768]{2,1,0:T(8,128)(2,1)S(1)}, bf16[2,96,768]{2,1,0:T(8,128)(2,1)S(1)}, u32[]{:S(2)}, u32[]{:S(2)}) collective-permute-start(bf16[2,96,768]{2,1,0:T(8,128)(2,1)S(1)} %bitcast.173), channel_id=1, source_target_pairs={{0,8},{4,12},{8,0},{12,4},{16,24},{20,28},{24,16},{28,20},{1,9},{5... | collective-permute-start | bytes 884744 | tf_op jit(solution)/shard_map/ppermute | solution.py:613
  19.6 11.6 %collective-permute-start = (bf16[2,96,768]{2,1,0:T(8,128)(2,1)S(1)}, bf16[2,96,768]{2,1,0:T(8,128)(2,1)S(1)}, u32[]{:S(2)}, u32[]{:S(2)}) collective-permute-start(bf16[2,96,768]{2,1,0:T(8,128)(2,1)S(1)} %bitcast.174), channel_id=1, source_target_pairs={{0,4},{4,0},{8,12},{12,8},{16,20},{20,16},{24,28},{28,24},{1,5},{5... | collective-permute-start | bytes 884744 | tf_op jit(solution)/shard_map/ppermute | solution.py:613
  21.1 18.8 %collective-permute-start.4 = (bf16[2,96,768]{2,1,0:T(8,128)(2,1)S(1)}, bf16[2,96,768]{2,1,0:T(8,128)(2,1)S(1)}, u32[]{:S(2)}, u32[]{:S(2)}) collective-permute-start(bf16[2,96,768]{2,1,0:T(8,128)(2,1)S(1)} %bitcast.175), channel_id=1, source_target_pairs={{0,1},{1,0},{2,3},{3,2},{4,5},{5,4},{6,7},{7,6},{8,9},{9,8},{10,11... | collective-permute-start | bytes 884744 | tf_op jit(solution)/shard_map/ppermute | solution.py:618
  21.1 32.5 %collective-permute-start.3 = (bf16[2,96,768]{2,1,0:T(8,128)(2,1)S(1)}, bf16[2,96,768]{2,1,0:T(8,128)(2,1)S(1)}, u32[]{:S(2)}, u32[]{:S(2)}) collective-permute-start(bf16[2,96,768]{2,1,0:T(8,128)(2,1)S(1)} %bitcast.176), channel_id=1, source_target_pairs={{0,16},{4,20},{8,24},{12,28},{16,0},{20,4},{24,8},{28,12},{1,17},{... | collective-permute-start | bytes 884744 | tf_op jit(solution)/shard_map/ppermute | solution.py:613
  31.2 42.8 %copy-start.27 = (bf16[2,96,768]{2,1,0:T(8,128)(2,1)}, bf16[2,96,768]{2,1,0:T(8,128)(2,1)S(1)}, u32[]{:S(2)}) copy-start(bf16[2,96,768]{2,1,0:T(8,128)(2,1)S(1)} %collective-permute-done.1.refs_4_) | copy-start | bytes 884740
  31.2 42.8 %copy-start.28 = (bf16[2,96,768]{2,1,0:T(8,128)(2,1)}, bf16[2,96,768]{2,1,0:T(8,128)(2,1)S(1)}, u32[]{:S(2)}) copy-start(bf16[2,96,768]{2,1,0:T(8,128)(2,1)S(1)} %collective-permute-done.refs_3_) | copy-start | bytes 884740
  31.2 22.4 %collective-permute-start.2 = (bf16[2,96,768]{2,1,0:T(8,128)(2,1)S(1)}, bf16[2,96,768]{2,1,0:T(8,128)(2,1)S(1)}, u32[]{:S(2)}, u32[]{:S(2)}) collective-permute-start(bf16[2,96,768]{2,1,0:T(8,128)(2,1)S(1)} %collective-permute-done.1.refs_4_), channel_id=1, source_target_pairs={{0,4},{4,0},{8,12},{12,8},{16,20},{20,16},{24,28},{28,24},{1,5},{5... | collective-permute-start | bytes 884744 | tf_op jit(solution)/shard_map/ppermute | solution.py:613
  36.4 17.2 %collective-permute-start.5 = (bf16[2,96,768]{2,1,0:T(8,128)(2,1)S(1)}, bf16[2,96,768]{2,1,0:T(8,128)(2,1)S(1)}, u32[]{:S(2)}, u32[]{:S(2)}) collective-permute-start(bf16[2,96,768]{2,1,0:T(8,128)(2,1)S(1)} %collective-permute-done.refs_3_), channel_id=1, source_target_pairs={{0,1},{1,0},{2,3},{3,2},{4,5},{5,4},{6,7},{7,6},{8,9},{9,8},{10,11... | collective-permute-start | bytes 884744 | tf_op jit(solution)/shard_map/ppermute | solution.py:618
  36.4 17.6 %collective-permute-start.7 = (bf16[2,96,768]{2,1,0:T(8,128)(2,1)S(1)}, bf16[2,96,768]{2,1,0:T(8,128)(2,1)S(1)}, u32[]{:S(2)}, u32[]{:S(2)}) collective-permute-start(bf16[2,96,768]{2,1,0:T(8,128)(2,1)S(1)} %bitcast.177), channel_id=1, source_target_pairs={{0,24},{4,28},{8,16},{12,20},{16,8},{20,12},{24,0},{28,4},{1,25},{... | collective-permute-start | bytes 884744 | tf_op jit(solution)/shard_map/ppermute | solution.py:613
  39.9 34.2 %copy-start.29 = (bf16[2,96,768]{2,1,0:T(8,128)(2,1)}, bf16[2,96,768]{2,1,0:T(8,128)(2,1)S(1)}, u32[]{:S(2)}) copy-start(bf16[2,96,768]{2,1,0:T(8,128)(2,1)S(1)} %collective-permute-done.4.refs_10_) | copy-start | bytes 884740
  39.9 14.2 %collective-permute-start.8 = (bf16[2,96,768]{2,1,0:T(8,128)(2,1)S(1)}, bf16[2,96,768]{2,1,0:T(8,128)(2,1)S(1)}, u32[]{:S(2)}, u32[]{:S(2)}) collective-permute-start(bf16[2,96,768]{2,1,0:T(8,128)(2,1)S(1)} %collective-permute-done.1.refs_4_), channel_id=1, source_target_pairs={{0,1},{1,0},{2,3},{3,2},{4,5},{5,4},{6,7},{7,6},{8,9},{9,8},{10,11... | collective-permute-start | bytes 884744 | tf_op jit(solution)/shard_map/ppermute | solution.py:618
  53.7 1.6 collective-permute-start.9
  53.8 9.4 %collective-permute-start.6 = (bf16[2,96,768]{2,1,0:T(8,128)(2,1)S(1)}, bf16[2,96,768]{2,1,0:T(8,128)(2,1)S(1)}, u32[]{:S(2)}, u32[]{:S(2)}) collective-permute-start(bf16[2,96,768]{2,1,0:T(8,128)(2,1)S(1)} %collective-permute-done.3.refs_6_), channel_id=1, source_target_pairs={{0,4},{4,0},{8,12},{12,8},{16,20},{20,16},{24,28},{28,24},{1,5},{5... | collective-permute-start | bytes 884744 | tf_op jit(solution)/shard_map/ppermute | solution.py:613
  63.2 8.8 %collective-permute-start.10 = (bf16[2,96,768]{2,1,0:T(8,128)(2,1)S(1)}, bf16[2,96,768]{2,1,0:T(8,128)(2,1)}, u32[]{:S(2)}, u32[]{:S(2)}) collective-permute-start(bf16[2,96,768]{2,1,0:T(8,128)(2,1)S(1)} %collective-permute-done.7.refs_8_), channel_id=1, source_target_pairs={{0,4},{4,0},{8,12},{12,8},{16,20},{20,16},{24,28},{28,24},{1,5},{5... | collective-permute-start | bytes 884744 | tf_op jit(solution)/shard_map/ppermute | solution.py:613
  63.6 10.4 %collective-permute-start.13 = (bf16[2,96,768]{2,1,0:T(8,128)(2,1)S(1)}, bf16[2,96,768]{2,1,0:T(8,128)(2,1)}, u32[]{:S(2)}, u32[]{:S(2)}) collective-permute-start(bf16[2,96,768]{2,1,0:T(8,128)(2,1)S(1)} %collective-permute-done.7.refs_8_), channel_id=1, source_target_pairs={{0,1},{1,0},{2,3},{3,2},{4,5},{5,4},{6,7},{7,6},{8,9},{9,8},{10,11... | collective-permute-start | bytes 884744 | tf_op jit(solution)/shard_map/ppermute | solution.py:618
  63.7 10.4 %collective-permute-start.11 = (bf16[2,96,768]{2,1,0:T(8,128)(2,1)S(1)}, bf16[2,96,768]{2,1,0:T(8,128)(2,1)}, u32[]{:S(2)}, u32[]{:S(2)}) collective-permute-start(bf16[2,96,768]{2,1,0:T(8,128)(2,1)S(1)} %collective-permute-done.3.refs_6_), channel_id=1, source_target_pairs={{0,1},{1,0},{2,3},{3,2},{4,5},{5,4},{6,7},{7,6},{8,9},{9,8},{10,11... | collective-permute-start | bytes 884744 | tf_op jit(solution)/shard_map/ppermute | solution.py:618
  64.2 9.9 %collective-permute-start.12 = (bf16[2,96,768]{2,1,0:T(8,128)(2,1)S(1)}, bf16[2,96,768]{2,1,0:T(8,128)(2,1)}, u32[]{:S(2)}, u32[]{:S(2)}) collective-permute-start(bf16[2,96,768]{2,1,0:T(8,128)(2,1)S(1)} %collective-permute-done.6.refs_7_), channel_id=1, source_target_pairs={{0,1},{1,0},{2,3},{3,2},{4,5},{5,4},{6,7},{7,6},{8,9},{9,8},{10,11... | collective-permute-start | bytes 884744 | tf_op jit(solution)/shard_map/ppermute | solution.py:618
  72.0 2.1 collective-permute-start.14
  74.2 51.0 %copy-start.20 = (bf16[2,1,8,128,768]{4,3,2,1,0:T(8,128)(2,1)S(1)}, bf16[2,1,8,128,768]{4,3,2,1,0:T(8,128)(2,1)}, u32[]{:S(2)}) copy-start(bf16[2,1,8,128,768]{4,3,2,1,0:T(8,128)(2,1)} %param.16) | copy-start | bytes 9437188
  123.4 8.8 %collective-permute-start.15 = (bf16[8,2,208,768]{3,2,1,0:T(8,128)(2,1)}, bf16[8,2,208,768]{3,2,1,0:T(8,128)(2,1)}, u32[]{:S(2)}, u32[]{:S(2)}) collective-permute-start(bf16[8,2,208,768]{3,2,1,0:T(8,128)(2,1)} %bitcast.156), channel_id=1, source_target_pairs={{0,1},{1,0},{2,3},{3,2},{4,5},{5,4},{6,7},{7,6},{8,9},{9,8},{10,11... | collective-permute-start | bytes 15335432 | tf_op jit(solution)/shard_map/ppermute | solution.py:618
  142.4 25.8 %collective-permute-start.17 = (f32[2,16,768]{2,1,0:T(8,128)S(1)}, f32[2,16,768]{2,1,0:T(8,128)S(1)}, u32[]{:S(2)}, u32[]{:S(2)}) collective-permute-start(f32[2,16,768]{2,1,0:T(8,128)S(1)} %get-tuple-element.311), channel_id=1, source_target_pairs={{0,16},{4,20},{8,24},{12,28},{16,0},{20,4},{24,8},{28,12},{1,17},{... | collective-permute-start | bytes 294920 | tf_op jit(solution)/shard_map/ppermute | solution.py:613
  143.8 24.4 %collective-permute-start.16 = (f32[2,16,768]{2,1,0:T(8,128)S(1)}, f32[2,16,768]{2,1,0:T(8,128)S(1)}, u32[]{:S(2)}, u32[]{:S(2)}) collective-permute-start(f32[2,16,768]{2,1,0:T(8,128)S(1)} %get-tuple-element.311), channel_id=1, source_target_pairs={{0,8},{4,12},{8,0},{12,4},{16,24},{20,28},{24,16},{28,20},{1,9},{5... | collective-permute-start | bytes 294920 | tf_op jit(solution)/shard_map/ppermute | solution.py:613
  144.6 23.5 %collective-permute-start.18 = (f32[2,16,768]{2,1,0:T(8,128)S(1)}, f32[2,16,768]{2,1,0:T(8,128)S(1)}, u32[]{:S(2)}, u32[]{:S(2)}) collective-permute-start(f32[2,16,768]{2,1,0:T(8,128)S(1)} %get-tuple-element.311), channel_id=1, source_target_pairs={{0,24},{4,28},{8,16},{12,20},{16,8},{20,12},{24,0},{28,4},{1,25},{... | collective-permute-start | bytes 294920 | tf_op jit(solution)/shard_map/ppermute | solution.py:613
  169.0 21.9 %copy-start.21 = (f32[4,2,16,768]{3,2,1,0:T(8,128)S(1)}, f32[4,2,16,768]{3,2,1,0:T(8,128)}, u32[]{:S(2)}) copy-start(f32[4,2,16,768]{3,2,1,0:T(8,128)} %get-tuple-element.307.refs_12_) | copy-start | bytes 1179652
  169.0 23.1 %copy-start.49 = (s32[128]{0:T(128)S(1)}, s32[128]{0:T(128)}, u32[]{:S(2)}) copy-start(s32[128]{0:T(128)} %add.182.refs_18_) | copy-start | bytes 1540
  190.8 12.7 %collective-permute-start.20 = (bf16[8,2,96,768]{3,2,1,0:T(8,128)(2,1)}, bf16[8,2,96,768]{3,2,1,0:T(8,128)(2,1)}, u32[]{:S(2)}, u32[]{:S(2)}) collective-permute-start(bf16[8,2,96,768]{3,2,1,0:T(8,128)(2,1)} %bitcast.198), channel_id=1, source_target_pairs={{0,1},{1,0},{2,3},{3,2},{4,5},{5,4},{6,7},{7,6},{8,9},{9,8},{10,11... | collective-permute-start | bytes 7077896 | tf_op jit(solution)/shard_map/ppermute | solution.py:618
  190.9 11.5 %collective-permute-start.19 = (f32[4,2,16,768]{3,2,1,0:T(8,128)S(1)}, f32[4,2,16,768]{3,2,1,0:T(8,128)S(1)}, u32[]{:S(2)}, u32[]{:S(2)}) collective-permute-start(f32[4,2,16,768]{3,2,1,0:T(8,128)S(1)} %copy-done.21), channel_id=1, source_target_pairs={{0,4},{4,0},{8,12},{12,8},{16,20},{20,16},{24,28},{28,24},{1,5},{5... | collective-permute-start | bytes 1179656 | tf_op jit(solution)/shard_map/ppermute | solution.py:613
  233.5 22.6 %collective-permute-start.21 = (bf16[2,8,96,768]{3,2,1,0:T(8,128)(2,1)}, bf16[2,8,96,768]{3,2,1,0:T(8,128)(2,1)S(1)}, u32[]{:S(2)}, u32[]{:S(2)}) collective-permute-start(bf16[2,8,96,768]{3,2,1,0:T(8,128)(2,1)} %get-tuple-element.144.refs_7_), channel_id=1, source_target_pairs={{0,1},{1,0},{2,3},{3,2},{4,5},{5,4},{6,7},{7,6},{8,9},{9,8},{10,11... | collective-permute-start | bytes 7077896 | tf_op jit(solution)/shard_map/ppermute | solution.py:618
  235.4 20.6 %copy-start.15 = (s32[2]{0:T(128)S(1)}, s32[2]{0:T(128)}, u32[]{:S(2)}) copy-start(s32[2]{0:T(128)} %pad_add_fusion.1.refs_0_.ids_ref) | copy-start | bytes 28
  259.2 35.9 %collective-permute-start.22 = (bf16[4,96,768]{2,1,0:T(8,128)(2,1)S(1)}, bf16[4,96,768]{2,1,0:T(8,128)(2,1)S(1)}, u32[]{:S(2)}, u32[]{:S(2)}) collective-permute-start(bf16[4,96,768]{2,1,0:T(8,128)(2,1)S(1)} %get-tuple-element.161), channel_id=1, source_target_pairs={{0,4},{4,0},{8,12},{12,8},{16,20},{20,16},{24,28},{28,24},{1,5},{5... | collective-permute-start | bytes 1769480 | tf_op jit(solution)/shard_map/ppermute | solution.py:613
  259.6 35.5 %collective-permute-start.23 = (bf16[4,96,768]{2,1,0:T(8,128)(2,1)S(1)}, bf16[4,96,768]{2,1,0:T(8,128)(2,1)S(1)}, u32[]{:S(2)}, u32[]{:S(2)}) collective-permute-start(bf16[4,96,768]{2,1,0:T(8,128)(2,1)S(1)} %get-tuple-element.163), channel_id=1, source_target_pairs={{0,2},{1,3},{2,0},{3,1},{4,6},{5,7},{6,4},{7,5},{8,10},{9,11},{10,... | collective-permute-start | bytes 1769480 | tf_op jit(solution)/shard_map/ppermute | solution.py:618
  261.1 34.1 %collective-permute-start.24 = (bf16[4,96,768]{2,1,0:T(8,128)(2,1)}, bf16[4,96,768]{2,1,0:T(8,128)(2,1)S(1)}, u32[]{:S(2)}, u32[]{:S(2)}) collective-permute-start(bf16[4,96,768]{2,1,0:T(8,128)(2,1)} %get-tuple-element.165), channel_id=1, source_target_pairs={{0,6},{1,7},{2,4},{3,5},{4,2},{5,3},{6,0},{7,1},{8,14},{9,15},{10,... | collective-permute-start | bytes 1769480 | tf_op jit(solution)/shard_map/ppermute | solution.py:625
  295.1 12.4 %collective-permute-start.25 = (bf16[2,8,112,768]{3,2,1,0:T(8,128)(2,1)}, bf16[2,8,112,768]{3,2,1,0:T(8,128)(2,1)S(1)}, u32[]{:S(2)}, u32[]{:S(2)}) collective-permute-start(bf16[2,8,112,768]{3,2,1,0:T(8,128)(2,1)} %cols_grads.2.refs_0_), channel_id=1, source_target_pairs={{0,1},{1,0},{2,3},{3,2},{4,5},{5,4},{6,7},{7,6},{8,9},{9,8},{10,11... | collective-permute-start | bytes 8257544 | tf_op jit(solution)/shard_map/ppermute | solution.py:618
  297.3 10.2 %collective-permute-start.26 = (bf16[96,768]{1,0:T(8,128)(2,1)S(1)}, bf16[96,768]{1,0:T(8,128)(2,1)S(1)}, u32[]{:S(2)}, u32[]{:S(2)}) collective-permute-start(bf16[96,768]{1,0:T(8,128)(2,1)S(1)} %get-tuple-element.168), channel_id=1, source_target_pairs={{0,8},{4,12},{8,0},{12,4},{16,24},{20,28},{24,16},{28,20},{1,9},{5... | collective-permute-start | bytes 442376 | tf_op jit(solution)/shard_map/ppermute | solution.py:613
  312.7 47.6 %collective-permute-start.29 = (bf16[4,112,768]{2,1,0:T(8,128)(2,1)}, bf16[4,112,768]{2,1,0:T(8,128)(2,1)S(1)}, u32[]{:S(2)}, u32[]{:S(2)}) collective-permute-start(bf16[4,112,768]{2,1,0:T(8,128)(2,1)} %get-tuple-element.175), channel_id=1, source_target_pairs={{0,6},{1,7},{2,4},{3,5},{4,2},{5,3},{6,0},{7,1},{8,14},{9,15},{10,... | collective-permute-start | bytes 2064392 | tf_op jit(solution)/shard_map/ppermute | solution.py:625
  313.9 46.3 %collective-permute-start.28 = (bf16[4,112,768]{2,1,0:T(8,128)(2,1)S(1)}, bf16[4,112,768]{2,1,0:T(8,128)(2,1)S(1)}, u32[]{:S(2)}, u32[]{:S(2)}) collective-permute-start(bf16[4,112,768]{2,1,0:T(8,128)(2,1)S(1)} %get-tuple-element.173), channel_id=1, source_target_pairs={{0,2},{1,3},{2,0},{3,1},{4,6},{5,7},{6,4},{7,5},{8,10},{9,11},{10,... | collective-permute-start | bytes 2064392 | tf_op jit(solution)/shard_map/ppermute | solution.py:618
  314.5 45.8 %collective-permute-start.27 = (bf16[4,112,768]{2,1,0:T(8,128)(2,1)S(1)}, bf16[4,112,768]{2,1,0:T(8,128)(2,1)S(1)}, u32[]{:S(2)}, u32[]{:S(2)}) collective-permute-start(bf16[4,112,768]{2,1,0:T(8,128)(2,1)S(1)} %get-tuple-element.171), channel_id=1, source_target_pairs={{0,4},{4,0},{8,12},{12,8},{16,20},{20,16},{24,28},{28,24},{1,5},{5... | collective-permute-start | bytes 2064392 | tf_op jit(solution)/shard_map/ppermute | solution.py:613
  316.1 30.2 %collective-permute-start.44 = (bf16[96,768]{1,0:T(8,128)(2,1)}, bf16[96,768]{1,0:T(8,128)(2,1)}, u32[]{:S(2)}, u32[]{:S(2)}) collective-permute-start(bf16[96,768]{1,0:T(8,128)(2,1)} %get-tuple-element.204), channel_id=1, source_target_pairs={{0,24},{4,28},{8,16},{12,20},{16,8},{20,12},{24,0},{28,4},{1,25},{... | collective-permute-start | bytes 442376 | tf_op jit(solution)/shard_map/ppermute | solution.py:613
  318.0 28.3 %collective-permute-start.43 = (bf16[96,768]{1,0:T(8,128)(2,1)}, bf16[96,768]{1,0:T(8,128)(2,1)}, u32[]{:S(2)}, u32[]{:S(2)}) collective-permute-start(bf16[96,768]{1,0:T(8,128)(2,1)} %get-tuple-element.202), channel_id=1, source_target_pairs={{0,16},{4,20},{8,24},{12,28},{16,0},{20,4},{24,8},{28,12},{1,17},{... | collective-permute-start | bytes 442376 | tf_op jit(solution)/shard_map/ppermute | solution.py:613
  358.5 19.6 %collective-permute-start.30 = (bf16[2,768,768]{2,1,0:T(8,128)(2,1)}, bf16[2,768,768]{2,1,0:T(8,128)(2,1)S(1)}, u32[]{:S(2)}, u32[]{:S(2)}) collective-permute-start(bf16[2,768,768]{2,1,0:T(8,128)(2,1)} %joint_grads.2.refs_0_), channel_id=1, source_target_pairs={{0,1},{1,0},{2,3},{3,2},{4,5},{5,4},{6,7},{7,6},{8,9},{9,8},{10,11... | collective-permute-start | bytes 7077896 | tf_op jit(solution)/shard_map/ppermute | solution.py:618
  361.8 16.2 %collective-permute-start.31 = (bf16[112,768]{1,0:T(8,128)(2,1)S(1)}, bf16[112,768]{1,0:T(8,128)(2,1)S(1)}, u32[]{:S(2)}, u32[]{:S(2)}) collective-permute-start(bf16[112,768]{1,0:T(8,128)(2,1)S(1)} %get-tuple-element.178), channel_id=1, source_target_pairs={{0,8},{4,12},{8,0},{12,4},{16,24},{20,28},{24,16},{28,20},{1,9},{5... | collective-permute-start | bytes 516104 | tf_op jit(solution)/shard_map/ppermute | solution.py:613
  362.7 15.3 %collective-permute-start.32 = (bf16[112,768]{1,0:T(8,128)(2,1)S(1)}, bf16[112,768]{1,0:T(8,128)(2,1)S(1)}, u32[]{:S(2)}, u32[]{:S(2)}) collective-permute-start(bf16[112,768]{1,0:T(8,128)(2,1)S(1)} %get-tuple-element.179), channel_id=1, source_target_pairs={{0,16},{4,20},{8,24},{12,28},{16,0},{20,4},{24,8},{28,12},{1,17},{... | collective-permute-start | bytes 516104 | tf_op jit(solution)/shard_map/ppermute | solution.py:613
  375.9 35.5 %collective-permute-start.45 = (bf16[112,768]{1,0:T(8,128)(2,1)S(1)}, bf16[112,768]{1,0:T(8,128)(2,1)S(1)}, u32[]{:S(2)}, u32[]{:S(2)}) collective-permute-start(bf16[112,768]{1,0:T(8,128)(2,1)S(1)} %get-tuple-element.208), channel_id=1, source_target_pairs={{0,24},{4,28},{8,16},{12,20},{16,8},{20,12},{24,0},{28,4},{1,25},{... | collective-permute-start | bytes 516104 | tf_op jit(solution)/shard_map/ppermute | solution.py:613
  382.0 18.0 %collective-permute-start.33 = (bf16[4,96,768]{2,1,0:T(8,128)(2,1)S(1)}, bf16[4,96,768]{2,1,0:T(8,128)(2,1)S(1)}, u32[]{:S(2)}, u32[]{:S(2)}) collective-permute-start(bf16[4,96,768]{2,1,0:T(8,128)(2,1)S(1)} %get-tuple-element.182), channel_id=1, source_target_pairs={{0,4},{4,0},{8,12},{12,8},{16,20},{20,16},{24,28},{28,24},{1,5},{5... | collective-permute-start | bytes 1769480 | tf_op jit(solution)/shard_map/ppermute | solution.py:613
  382.4 17.6 %collective-permute-start.34 = (bf16[4,96,768]{2,1,0:T(8,128)(2,1)S(1)}, bf16[4,96,768]{2,1,0:T(8,128)(2,1)S(1)}, u32[]{:S(2)}, u32[]{:S(2)}) collective-permute-start(bf16[4,96,768]{2,1,0:T(8,128)(2,1)S(1)} %get-tuple-element.185), channel_id=1, source_target_pairs={{0,2},{1,3},{2,0},{3,1},{4,6},{5,7},{6,4},{7,5},{8,10},{9,11},{10,... | collective-permute-start | bytes 1769480 | tf_op jit(solution)/shard_map/ppermute | solution.py:618
  383.9 26.7 %collective-permute-start.35 = (bf16[4,96,768]{2,1,0:T(8,128)(2,1)S(1)}, bf16[4,96,768]{2,1,0:T(8,128)(2,1)S(1)}, u32[]{:S(2)}, u32[]{:S(2)}) collective-permute-start(bf16[4,96,768]{2,1,0:T(8,128)(2,1)S(1)} %get-tuple-element.187), channel_id=1, source_target_pairs={{0,6},{1,7},{2,4},{3,5},{4,2},{5,3},{6,0},{7,1},{8,14},{9,15},{10,... | collective-permute-start | bytes 1769480 | tf_op jit(solution)/shard_map/ppermute | solution.py:625
  385.5 25.0 %copy-start.10 = (bf16[4,96,768]{2,1,0:T(8,128)(2,1)S(1)}, bf16[4,96,768]{2,1,0:T(8,128)(2,1)}, u32[]{:S(2)}) copy-start(bf16[4,96,768]{2,1,0:T(8,128)(2,1)} %copy-done.9) | copy-start | bytes 1769476
  385.5 25.9 %copy-start.37 = (bf16[128,768]{1,0:T(8,128)(2,1)S(1)}, bf16[128,768]{1,0:T(8,128)(2,1)}, u32[]{:S(2)}) copy-start(bf16[128,768]{1,0:T(8,128)(2,1)} %get-tuple-element.194) | copy-start | bytes 589828
  414.3 24.3 %copy-start.42 = (bf16[16,768]{1,0:T(8,128)(2,1)S(1)}, bf16[16,768]{1,0:T(8,128)(2,1)}, u32[]{:S(2)}) copy-start(bf16[16,768]{1,0:T(8,128)(2,1)} %get-tuple-element.200) | copy-start | bytes 73732
  414.4 6.6 %collective-permute-start.38 = (bf16[96,768]{1,0:T(8,128)(2,1)S(1)}, bf16[96,768]{1,0:T(8,128)(2,1)S(1)}, u32[]{:S(2)}, u32[]{:S(2)}) collective-permute-start(bf16[96,768]{1,0:T(8,128)(2,1)S(1)} %get-tuple-element.195), channel_id=1, source_target_pairs={{0,8},{4,12},{8,0},{12,4},{16,24},{20,28},{24,16},{28,20},{1,9},{5... | collective-permute-start | bytes 442376 | tf_op jit(solution)/shard_map/ppermute | solution.py:613
  414.5 13.4 %collective-permute-start.39 = (bf16[96,768]{1,0:T(8,128)(2,1)S(1)}, bf16[96,768]{1,0:T(8,128)(2,1)S(1)}, u32[]{:S(2)}, u32[]{:S(2)}) collective-permute-start(bf16[96,768]{1,0:T(8,128)(2,1)S(1)} %get-tuple-element.196), channel_id=1, source_target_pairs={{0,16},{4,20},{8,24},{12,28},{16,0},{20,4},{24,8},{28,12},{1,17},{... | collective-permute-start | bytes 442376 | tf_op jit(solution)/shard_map/ppermute | solution.py:613
  416.6 11.3 %collective-permute-start.40 = (bf16[96,768]{1,0:T(8,128)(2,1)S(1)}, bf16[96,768]{1,0:T(8,128)(2,1)S(1)}, u32[]{:S(2)}, u32[]{:S(2)}) collective-permute-start(bf16[96,768]{1,0:T(8,128)(2,1)S(1)} %get-tuple-element.197), channel_id=1, source_target_pairs={{0,24},{4,28},{8,16},{12,20},{16,8},{20,12},{24,0},{28,4},{1,25},{... | collective-permute-start | bytes 442376 | tf_op jit(solution)/shard_map/ppermute | solution.py:613
  418.9 9.7 %collective-permute-start.36 = (bf16[2,96,768]{2,1,0:T(8,128)(2,1)S(1)}, bf16[2,96,768]{2,1,0:T(8,128)(2,1)S(1)}, u32[]{:S(2)}, u32[]{:S(2)}) collective-permute-start(bf16[2,96,768]{2,1,0:T(8,128)(2,1)S(1)} %dynamic-slice_bitcast_fusion), channel_id=1, source_target_pairs={{0,1},{1,0},{2,3},{3,2},{4,5},{5,4},{6,7},{7,6},{8,9},{9,8},{10,11... | collective-permute-start | bytes 884744 | tf_op jit(solution)/shard_map/ppermute | solution.py:618
  419.1 19.7 %collective-permute-start.46 = (bf16[208,768]{1,0:T(8,128)(2,1)S(1)}, bf16[208,768]{1,0:T(8,128)(2,1)S(1)}, u32[]{:S(2)}, u32[]{:S(2)}) collective-permute-start(bf16[208,768]{1,0:T(8,128)(2,1)S(1)} %get-tuple-element.309), channel_id=1, source_target_pairs={{0,2},{1,3},{2,0},{3,1},{4,6},{5,7},{6,4},{7,5},{8,10},{9,11},{10,... | collective-permute-start | bytes 958472 | tf_op jit(solution)/shard_map/ppermute | solution.py:618
  428.0 10.7 %collective-permute-start.41 = (bf16[96,768]{1,0:T(8,128)(2,1)S(1)}, bf16[96,768]{1,0:T(8,128)(2,1)S(1)}, u32[]{:S(2)}, u32[]{:S(2)}) collective-permute-start(bf16[96,768]{1,0:T(8,128)(2,1)S(1)} %add_convert_fusion.2), channel_id=1, source_target_pairs={{0,2},{1,3},{2,0},{3,1},{4,6},{5,7},{6,4},{7,5},{8,10},{9,11},{10,... | collective-permute-start | bytes 442376 | tf_op jit(solution)/shard_map/ppermute | solution.py:618
  428.7 10.1 %collective-permute-start.37 = (bf16[96,768]{1,0:T(8,128)(2,1)S(1)}, bf16[96,768]{1,0:T(8,128)(2,1)S(1)}, u32[]{:S(2)}, u32[]{:S(2)}) collective-permute-start(bf16[96,768]{1,0:T(8,128)(2,1)S(1)} %fusion.3), channel_id=1, source_target_pairs={{0,2},{1,3},{2,0},{3,1},{4,6},{5,7},{6,4},{7,5},{8,10},{9,11},{10,... | collective-permute-start | bytes 442376 | tf_op jit(solution)/shard_map/ppermute | solution.py:618
  438.8 3.0 collective-permute-start.42
  438.9 6.3 %collective-permute-start.48 = (bf16[96,768]{1,0:T(8,128)(2,1)S(1)}, bf16[96,768]{1,0:T(8,128)(2,1)S(1)}, u32[]{:S(2)}, u32[]{:S(2)}) collective-permute-start(bf16[96,768]{1,0:T(8,128)(2,1)S(1)} %fusion.1), channel_id=1, source_target_pairs={{0,2},{1,3},{2,0},{3,1},{4,6},{5,7},{6,4},{7,5},{8,10},{9,11},{10,... | collective-permute-start | bytes 442376 | tf_op jit(solution)/shard_map/ppermute | solution.py:618
  439.5 9.3 %collective-permute-start.47 = (bf16[2,208,768]{2,1,0:T(8,128)(2,1)S(1)}, bf16[2,208,768]{2,1,0:T(8,128)(2,1)S(1)}, u32[]{:S(2)}, u32[]{:S(2)}) collective-permute-start(bf16[2,208,768]{2,1,0:T(8,128)(2,1)S(1)} %pad_maximum_fusion.5), channel_id=1, source_target_pairs={{0,1},{1,0},{2,3},{3,2},{4,5},{5,4},{6,7},{7,6},{8,9},{9,8},{10,11... | collective-permute-start | bytes 1916936 | tf_op jit(solution)/shard_map/ppermute | solution.py:618
  445.2 1.8 collective-permute-start.49
  (38 other events, 405.7 us)
Sparse Core Ops, SparseCore 0:
  15.7 107.6 all-gather.4
  126.2 53.1 all-gather.6

commit v4 on v3

--- a/solution.py
+++ b/solution.py
@@ -14,6 +14,7 @@
 BF16 = jnp.bfloat16
 MIB = 1 << 20
 LONG, SHORT = 6.0, 0.001
+CLS_ACT, CLS_SLOPE, CLS_LOW, CLS_PRE, CLS_TOTAL, CLS_OUT, CLS_COT, CLS_BLOCKS = 0, 4, 8, 9, 10, 11, 12, 13
 
 
 def dot_nn(left, right):
@@ -235,9 +236,16 @@
 
 def ffn_rows(
     seg_length, pre_ref, cot_ref, wup_ref, wdown_ref, gains_ref, shifts_ref,
-    low_ref, act_ref, slope_ref, out_ref, branch_ref, grad_ref, sums_ref,
+    low_ref, act_ref, slope_ref, out_ref, branch_ref, grad_ref, sums_ref, cls_ref,
 ):
     rows, width = pre_ref.shape
+    segs = rows // seg_length
+
+    def keep_cls(block, values):
+        for seg in range(segs):
+            row = values[seg * seg_length : seg * seg_length + 1].astype(F32)
+            cls_ref[pl.ds(pl.program_id(0) * segs + seg, 1), block * width : (block + 1) * width] = row
+
     unit, unused = norm_parts(pre_ref[...])
     total = unit * gains_ref[0:1].astype(F32) + shifts_ref[0:1].astype(F32)
     low = total.astype(BF16)
@@ -247,14 +255,24 @@
         cols = slice(part * width, (part + 1) * width)
         ahead = dot_nn(low, square(wup_ref[part + 1])) if part < 3 else None
         act, slope = gelu_parts(held)
-        act_ref[:, cols] = act.astype(BF16)
-        slope_ref[:, cols] = slope.astype(BF16)
+        act, slope = act.astype(BF16), slope.astype(BF16)
+        act_ref[:, cols] = act
+        slope_ref[:, cols] = slope
+        keep_cls(CLS_ACT + part, act)
+        keep_cls(CLS_SLOPE + part, slope)
         total = total + dot_nn(act_ref[:, cols], down_block(wdown_ref, part))
         held = ahead
     gain = gains_ref[1:2].astype(F32)
     unit, inverse = norm_parts(total)
-    out_ref[...] = (unit * gain + shifts_ref[1:2].astype(F32)).astype(BF16)
-    grad = cot_ref[...].astype(F32)
+    out = unit * gain + shifts_ref[1:2].astype(F32)
+    out_ref[...] = out.astype(BF16)
+    keep_cls(CLS_LOW, low)
+    keep_cls(CLS_PRE, pre_ref)
+    keep_cls(CLS_TOTAL, total)
+    keep_cls(CLS_OUT, out)
+    keep_cls(CLS_COT, cot_ref)
+    is_cls = lax.broadcasted_iota(jnp.int32, total.shape, 0) % seg_length == 0
+    grad = jnp.where(is_cls, 0.0, cot_ref[...].astype(F32))
     pre_grad = norm_back(grad, unit, inverse, gain)
     grad_ref[...] = pre_grad
     branch_ref[...] = pre_grad.astype(BF16)
@@ -263,56 +281,40 @@
     def start_sums():
         sums_ref[...] = jnp.zeros_like(sums_ref)
 
-    inner = jnp.where(lax.broadcasted_iota(jnp.int32, grad.shape, 0) % seg_length == 0, 0.0, grad)
-    sums_ref[1:2] += jnp.sum(inner * unit, axis=0, keepdims=True)
-    sums_ref[4:5] += jnp.sum(inner, axis=0, keepdims=True)
-
-
-def ffn_forward(pre_first, cot, w_up, w_down, gains, shifts, seg_length, block, span, prior=(), after=()):
+    sums_ref[1:2] += jnp.sum(grad * unit, axis=0, keepdims=True)
+    sums_ref[4:5] += jnp.sum(grad, axis=0, keepdims=True)
+
+
+def ffn_first_kernel(seg_length, ids_ref, pre_ref, cot_ref, gains_ref, shifts_ref, half_ref, other_ref, *refs):
+    *outs, wup_ref, wdown_ref, sems = refs
+
+    @pl.when(pl.program_id(0) == 0)
+    def fetch():
+        parts = (half_ref, other_ref)
+        up = fetch_halves(ids_ref, parts, wup_ref, sems)
+        down = fetch_halves(ids_ref, parts, wdown_ref, sems, wup_ref.shape[2], True)
+        for copy in up + down:
+            copy.wait()
+
+    ffn_rows(seg_length, pre_ref, cot_ref, wup_ref, wdown_ref, gains_ref, shifts_ref, *outs)
+
+
+def ffn_forward(pre_first, cot, weights, gains, shifts, seg_length, block, pieces=None, ids=None):
     rows, width = pre_first.shape
+    span = (0, rows // block)
     wide, low = shape_of((rows, 4 * width), BF16), shape_of((rows, width), BF16)
-    return rows_call(
-        partial(ffn_rows, seg_length), "ffn_forward", block, span, [pre_first, cot],
-        [(value, whole(value.shape)) for value in (w_up, w_down, gains, shifts)],
-        [low, wide, wide, low, low, shape_of((rows, width), F32)], 8 * width * width, prior, after,
-        extra=[shape_of((8, width), F32)],
-    )
-
-
-def edge_rows(pre_ref, wup_ref, wdown_ref, gains_ref, shifts_ref, out_ref, total_ref):
-    unit, unused = norm_parts(pre_ref[...])
-    total = unit * gains_ref[0:1].astype(F32) + shifts_ref[0:1].astype(F32)
-    low = total.astype(BF16)
-    for part in range(4):
-        act, unused = gelu_parts(dot_nn(low, square(wup_ref[part])))
-        total = total + dot_nn(act.astype(BF16), down_block(wdown_ref, part))
-    total_ref[...] = total
-    unit, unused = norm_parts(total)
-    out_ref[...] = unit * gains_ref[1:2].astype(F32) + shifts_ref[1:2].astype(F32)
-
-
-def edge_first_kernel(ids_ref, pre_ref, gains_ref, shifts_ref, half_ref, other_ref, out_ref, total_ref, wup_ref, wdown_ref, sems):
-    parts = (half_ref, other_ref)
-    up = fetch_halves(ids_ref, parts, wup_ref, sems)
-    down = fetch_halves(ids_ref, parts, wdown_ref, sems, wup_ref.shape[2], True)
-    for copy in up + down:
-        copy.wait()
-    edge_rows(pre_ref, wup_ref, wdown_ref, gains_ref, shifts_ref, out_ref, total_ref)
-
-
-def edge_forward(pre_edge, weights, gains, shifts, pieces=None, ids=None):
-    rows, width = pre_edge.shape
-    norms = [(gains, whole(gains.shape)), (shifts, whole(shifts.shape))]
-    outs = [shape_of((rows, width), F32)] * 2
+    outs = [low, wide, wide, low, low, shape_of((rows, width), F32)]
+    extra = [shape_of((8, width), F32), shape_of((rows // seg_length, CLS_BLOCKS * width), F32)]
     if pieces is None:
         return rows_call(
-            edge_rows, "edge_forward", rows, (0, 1), [pre_edge], [(value, whole(value.shape)) for value in weights] + norms,
-            outs, 60 * width * width,
+            partial(ffn_rows, seg_length), "ffn_forward", block, span, [pre_first, cot],
+            [(value, whole(value.shape)) for value in (*weights, gains, shifts)], outs, 8 * width * width, extra=extra,
         )
     parts, shapes = pieces
     return rows_call(
-        edge_first_kernel, "edge_forward", rows, (0, 1), [pre_edge], norms + [(part, ANYWHERE) for part in parts], outs,
-        60 * width * width, extra=shapes, ids=ids, scratch=[pltpu.SemaphoreType.DMA((8,))],
+        partial(ffn_first_kernel, seg_length), "ffn_forward", block, span, [pre_first, cot],
+        [(gains, whole(gains.shape)), (shifts, whole(shifts.shape))] + [(part, ANYWHERE) for part in parts], outs,
+        8 * width * width, extra=extra + shapes, ids=ids, scratch=[pltpu.SemaphoreType.DMA((8,))],
     )
 
 
@@ -392,23 +394,34 @@
 
 
 def cross_kernel(
-    local, fetch, ids_ref, rows_ref, cot_ref, total_ref, keyc_ref, keyr_ref, place_ref, table_ref, gains_ref, shifts_ref, *refs
+    local, fetch, ids_ref, rows_ref, cls_ref, keyc_ref, keyr_ref, place_ref, table_ref, gains_ref, shifts_ref,
+    wup_hbm, wdown_hbm, *refs
 ):
     parts, refs = (refs[:2], refs[2:]) if fetch else (refs[:1], refs[1:])
-    new_ref, branch_ref, edge_ref, low_ref, gradp_ref, mixed_ref, gradz_ref, sums_ref, table_grad_ref = refs[:9]
-    proj_ref, probs_ref, gradm_ref = refs[9:12]
+    new_ref, branch_ref, grad_c_ref, sums_ref, table_grad_ref, hidden_ref, grad1_ref, low1_ref, turned_ref = refs[:9]
+    proj_ref, probs_ref, gradm_ref, mixed_ref, gradp_ref, lying_ref, wup_ref, wdown_ref, ffn_sems = refs[9:18]
+    ffn_copies = [
+        pltpu.make_async_copy(wdown_hbm, wdown_ref, ffn_sems.at[0]), pltpu.make_async_copy(wup_hbm, wup_ref, ffn_sems.at[1]),
+    ]
     wc_ref = parts[0]
     if fetch:
-        wc_ref, sems = refs[12:]
-        for copy in fetch_halves(ids_ref, parts, wc_ref, sems):
+        wc_ref, sems = refs[18:]
+        copies = fetch_halves(ids_ref, parts, wc_ref, sems)
+    for copy in ffn_copies:
+        copy.start()
+    if fetch:
+        for copy in copies:
             copy.wait()
-    count, width = rows_ref.shape
+    count, width = rows_ref.shape[0], rows_ref.shape[1] // 2
+
+    def cls(block):
+        return cls_ref[:, block * width : (block + 1) * width]
+
     pairs = width // PAIR
     entries = table_ref.shape[0]
     picks = place_ref[...] == lax.broadcasted_iota(jnp.int32, (count, entries), 1)
-    embedded = rows_ref[...] + dot_nn(picks.astype(BF16), table_ref[...])
+    embedded = rows_ref[:, :width] + dot_nn(picks.astype(BF16), table_ref[...])
     low = embedded.astype(BF16)
-    low_ref[...] = low
     for part in range(3):
         proj_ref[:, part * width : (part + 1) * width] = dot_nn(low, square(wc_ref[part])).astype(BF16)
     first_half = lane_half((count, PAIR))
@@ -424,13 +437,12 @@
     unit, inverse = norm_parts(pre_third)
     gain = gains_ref[2:3].astype(F32)
     new_ref[...] = (unit[:local] * gain + shifts_ref[2:3].astype(F32)).astype(BF16)
-    grad_out = cot_ref[...]
+    grad_out = rows_ref[:, width:]
     grad_third = norm_back(grad_out, unit, inverse, gain)
     sums_ref[...] = jnp.zeros_like(sums_ref)
     sums_ref[2:3] = jnp.sum(grad_out[:local] * unit[:local], axis=0, keepdims=True)
     sums_ref[5:6] = jnp.sum(grad_out[:local], axis=0, keepdims=True)
     gradz = grad_third.astype(BF16)
-    gradz_ref[...] = gradz
     gradm_ref[...] = dot_nt(gradz, square(wc_ref[3])).astype(BF16)
     for pair, cols in enumerate(places):
         grads = pair_backward(
@@ -441,21 +453,44 @@
     grad_edge = grad_third[:local]
     for part in range(3):
         grad_edge = grad_edge + dot_nt(gradp_ref[:local, part * width : (part + 1) * width], square(wc_ref[part]))
-    unit, inverse = norm_parts(total_ref[...])
+    rows = grad_c_ref.shape[1]
+    own = pl.ds(pl.multiple_of(ids_ref[0] * rows, 8), rows)
+    lying_ref[...] = low.astype(F32).T
+    own_low = lying_ref[own, :].astype(BF16)
+    for part in range(3):
+        grad_c_ref[part] = dot_nn(own_low, gradp_ref[:, part * width : (part + 1) * width]).astype(BF16)
+    lying_ref[...] = mixed_ref[...].astype(F32).T
+    grad_c_ref[3] = dot_nn(lying_ref[own, :].astype(BF16), gradz).astype(BF16)
+    unit, inverse = norm_parts(cls(CLS_TOTAL))
     sums_ref[1:2] = jnp.sum(grad_edge * unit, axis=0, keepdims=True)
     sums_ref[4:5] = jnp.sum(grad_edge, axis=0, keepdims=True)
-    pre_grad = norm_back(grad_edge, unit, inverse, gains_ref[1:2].astype(F32))
-    edge_ref[...] = pre_grad
-    branch_ref[...] = pre_grad.astype(BF16)
+    total = norm_back(grad_edge, unit, inverse, gains_ref[1:2].astype(F32))
+    branch = total.astype(BF16)
+    branch_ref[...] = branch
+    for part in range(4):
+        turned_ref[part * width : (part + 1) * width] = cls(CLS_ACT + part).T.astype(BF16)
+    for copy in ffn_copies:
+        copy.wait()
+    for part in range(4):
+        grad_act = dot_nt(branch, down_block(wdown_ref, part))
+        grad_hidden = (grad_act * cls(CLS_SLOPE + part)).astype(BF16)
+        hidden_ref[:, part * width : (part + 1) * width] = grad_hidden
+        total = total + dot_nt(grad_hidden, square(wup_ref[part]))
+    unit, inverse = norm_parts(cls(CLS_PRE))
+    grad1 = norm_back(total, unit, inverse, gains_ref[0:1].astype(F32))
+    grad1_ref[...] = grad1
+    low1_ref[...] = grad1.astype(BF16)
+    sums_ref[0:1] = jnp.sum(total * unit, axis=0, keepdims=True)
+    sums_ref[3:4] = jnp.sum(total, axis=0, keepdims=True)
     table_grad_ref[...] = lax.dot_general(
         picks[:local].astype(F32), grad_edge, (((0,), (0,)), ((), ())),
         precision=lax.Precision.HIGHEST, preferred_element_type=F32,
     )
 
 
-def cross_block(ids, local, edge_rows, edge_cot, edge_total, key_col, key_row, place, table, gains, shifts, parts, shape):
-    count, width = edge_rows.shape
-    read = [edge_rows, edge_cot, edge_total, key_col, key_row, place, table, gains, shifts]
+def cross_block(ids, edges, cls, key_col, key_row, place, table, gains, shifts, w_up, w_down, parts, shape):
+    local, count, width = cls.shape[0], edges.shape[0], table.shape[1]
+    read = [edges, cls, key_col, key_row, place, table, gains, shifts]
     part_specs, fetched = [whole(part.shape) for part in parts], []
     if shape is not None:
         part_specs = [ANYWHERE] * len(parts)
@@ -463,13 +498,13 @@
     shapes = (
         jax.ShapeDtypeStruct((local, width), BF16),
         jax.ShapeDtypeStruct((local, width), BF16),
-        jax.ShapeDtypeStruct((local, width), F32),
-        jax.ShapeDtypeStruct((count, width), BF16),
-        jax.ShapeDtypeStruct((count, 3 * width), BF16),
-        jax.ShapeDtypeStruct((count, width), BF16),
-        jax.ShapeDtypeStruct((count, width), BF16),
+        jax.ShapeDtypeStruct((4, width // lax.axis_size("seg"), width), BF16),
         jax.ShapeDtypeStruct((8, width), F32),
         jax.ShapeDtypeStruct(table.shape, F32),
+        jax.ShapeDtypeStruct((local, 4 * width), BF16),
+        jax.ShapeDtypeStruct((local, width), F32),
+        jax.ShapeDtypeStruct((local, width), BF16),
+        jax.ShapeDtypeStruct((4 * width, local), BF16),
     )
     return pl.pallas_call(
         partial(cross_kernel, local, shape is not None),
@@ -477,25 +512,36 @@
         grid_spec=pltpu.PrefetchScalarGridSpec(
             num_scalar_prefetch=1,
             grid=(1,),
-            in_specs=[whole(value.shape) for value in read] + part_specs,
+            in_specs=[whole(value.shape) for value in read] + [ANYWHERE] * 2 + part_specs,
             out_specs=[whole(value.shape) for value in shapes],
             scratch_shapes=[
                 pltpu.VMEM((count, 3 * width), BF16),
                 pltpu.VMEM((width // PAIR, count, 2 * count), BF16),
                 pltpu.VMEM((count, width), BF16),
+                pltpu.VMEM((count, width), BF16),
+                pltpu.VMEM((count, 3 * width), BF16),
+                pltpu.VMEM((width, count), F32),
+                pltpu.VMEM(w_up.shape, BF16),
+                pltpu.VMEM(w_down.shape, BF16),
+                pltpu.SemaphoreType.DMA((2,)),
             ] + fetched,
         ),
         compiler_params=pltpu.CompilerParams(vmem_limit_bytes=56 * MIB),
         cost_estimate=cost(10_000_000_000, width * width * 8),
         name="cross_block",
-    )(ids, *read, *parts)
-
-
-def cols_grad_kernel(side, ids_ref, left_ref, right_ref, rider_ref, *refs):
+    )(ids, *read, w_up, w_down, *parts)
+
+
+def with_cls(left_ref, right_ref, cls_left_ref, cls_right_ref):
+    cls_product = dot_tn(cls_left_ref[...].astype(BF16), cls_right_ref[...])
+    return (dot_tn(left_ref[...], right_ref[...]) + cls_product).astype(BF16)
+
+
+def cols_grad_kernel(side, ids_ref, left_ref, right_ref, cls_left_ref, cls_right_ref, rider_ref, *refs):
     out_ref = refs[-1]
     owners, rows = rider_ref.shape[0], left_ref.shape[1] // rider_ref.shape[0]
     block = half_block(side, pl.program_id(0), ids_ref)
-    product = dot_tn(left_ref[...], right_ref[...]).astype(BF16)
+    product = with_cls(left_ref, right_ref, cls_left_ref, cls_right_ref)
     out_ref[0, :, :rows] = product.reshape(owners, rows, product.shape[1])
     rider = rider_ref[...]
     out_ref[0, :, rows:] = jnp.where(block == 0, rider, jnp.zeros_like(rider))
@@ -534,23 +580,26 @@
     )(ids, *operands, *after)
 
 
-def plain_cols_kernel(ids_ref, left_ref, right_ref, *refs):
-    refs[-1][0] = dot_tn(left_ref[...], right_ref[...]).astype(BF16)
-
-
-def cols_grads(side, ids, left, right, rider, after, weight):
+def plain_cols_kernel(ids_ref, left_ref, right_ref, cls_left_ref, cls_right_ref, *refs):
+    refs[-1][0] = with_cls(left_ref, right_ref, cls_left_ref, cls_right_ref)
+
+
+def cols_grads(side, ids, left, right, cls_left, cls_right, rider, after, weight):
     rows, width = left.shape
     owners, extra, unused = rider.shape
     specs = [
         whole(left.shape),
         pl.BlockSpec((rows, width), lambda j, ids: (0, half_block(side, j, ids))),
+        pl.BlockSpec((cls_left.shape[0], width), lambda j, ids: (0, CLS_LOW), pipeline_mode=pl.Buffered(1)),
+        pl.BlockSpec((cls_left.shape[0], width), lambda j, ids: (0, half_block(side, j, ids))),
     ]
+    operands = [left, right, cls_left, cls_right]
     if width // owners % 16 == 0:
         return half_grads(
-            partial(cols_grad_kernel, side), "cols_grads", ids, [left, right, rider], specs + [whole(rider.shape)],
+            partial(cols_grad_kernel, side), "cols_grads", ids, operands + [rider], specs + [whole(rider.shape)],
             (owners, width // owners + extra, width), after, weight,
         )
-    product = half_grads(plain_cols_kernel, "cols_grads", ids, [left, right], specs, (width, width), after, weight)
+    product = half_grads(plain_cols_kernel, "cols_grads", ids, operands, specs, (width, width), after, weight)
     first = half_block(side, 0, ids) == 0
     rider = jnp.where(first, rider, jnp.zeros_like(rider))
     rider = jnp.stack([rider, jnp.zeros_like(rider)], axis=0)
@@ -683,11 +732,16 @@
         return jnp.stack([self.evens, later(self.came, *first)], axis=1).reshape((-1,) + self.piece.shape)
 
 
-def spread_kernel(ids_ref, keep_ref, came_ref, stay_ref, x_ref, y_ref, xy_ref):
-    near, across = ids_ref[0] & 1, ids_ref[1] >> 1
+def spread_kernel(ids_ref, keep_ref, came_ref, *refs):
+    stay_ref, x_ref, y_ref, xy_ref = refs[-4:]
+    near, across, core = ids_ref[0] & 1, ids_ref[1] >> 1, ids_ref[1] & 1
 
     def total(share, side):
-        return (keep_ref[share, 0, side].astype(F32) + came_ref[share, 0, side].astype(F32)).astype(BF16)
+        value = keep_ref[share, 0, side].astype(F32) + came_ref[share, 0, side].astype(F32)
+        if len(refs) > 4:
+            for left_ref, right_ref in (refs[:2], refs[2:4]):
+                value = value + dot_nn(left_ref[0, side, 2 * core + share], right_ref[...])
+        return value.astype(BF16)
 
     stay_ref[0] = total(across, near)
     x_ref[0] = total(across, 1 - near)
@@ -695,23 +749,28 @@
     xy_ref[0] = total(1 - across, 1 - near)
 
 
-def spread(ids, keep, came):
+def spread(ids, keep, came, product=()):
     unused, count, rows, width = keep.shape
     far = count // 2
     shape = (2, far, 2, rows, width)
     in_spec = pl.BlockSpec((2, 1, 2, rows, width), lambda j: (0, j, 0, 0, 0))
     out_spec = pl.BlockSpec((1, rows, width), lambda j: (j, 0, 0))
     out = jax.ShapeDtypeStruct((far, rows, width), BF16)
+    specs = [pl.BlockSpec(memory_space=pltpu.SMEM), in_spec, in_spec]
+    if product:
+        depth = product[1].shape[0]
+        product = [value.reshape(far, 2, 4, rows, depth) if i % 2 == 0 else value for i, value in enumerate(product)]
+        specs += [pl.BlockSpec((1, 2, 4, rows, depth), lambda j: (j, 0, 0, 0, 0)), whole(product[1].shape)] * 2
     return pl.pallas_call(
         spread_kernel,
         out_shape=(out,) * 4,
         grid=(far,),
-        in_specs=[pl.BlockSpec(memory_space=pltpu.SMEM), in_spec, in_spec],
+        in_specs=specs,
         out_specs=[out_spec] * 4,
         compiler_params=pltpu.CompilerParams(vmem_limit_bytes=32 * MIB),
         cost_estimate=cost(0, 12 * count * rows * width),
         name="spread",
-    )(ids, keep.reshape(shape), came.reshape(shape))
+    )(ids, keep.reshape(shape), came.reshape(shape), *product)
 
 
 def settle_kernel(ids_ref, *refs):
@@ -757,9 +816,9 @@
         self.keep = keep
         self.came = rep_swap(send, 1)
 
-    def spread(self, *first):
+    def spread(self, *first, product=()):
         came = after_all(self.came, first)
-        self.stay, *sends = spread(self.ids, self.keep.reshape(self.shape), came.reshape(self.shape))
+        self.stay, *sends = spread(self.ids, self.keep.reshape(self.shape), came.reshape(self.shape), product)
         self.came = [seg_swap(sends[0], 1), rep_swap(sends[1], 2), both_swap(sends[2], 1, 2)]
 
     def parts(self, *first):
@@ -788,10 +847,9 @@
 
     def finish(self, *first):
         held = jnp.concatenate([self.value, later(self.came, *first)], axis=0)
-        order = jnp.array([0, 2, 1, 3], jnp.int32)
+        places = [self.ids[1] ^ owner for owner in (0, 2, 1, 3)]
         return [
-            lax.dynamic_index_in_dim(held, order[self.ids[1] ^ owner], 0, keepdims=False).astype(F32)
-            for owner in (0, 2, 1, 3)
+            lax.dynamic_index_in_dim(held, 2 * (place & 1) + place // 2, 0, keepdims=False).astype(F32) for place in places
         ]
 
 
@@ -864,98 +922,96 @@
         both = jnp.where((rep & 1) == 0, jnp.concatenate([own, other], axis=1), jnp.concatenate([other, own], axis=1))
         return (both if owner_first else both.transpose(1, 0, 2, 3)).reshape(4, 1, width, width)
 
-    pre_edge = pre_first.reshape(local, seg_length, width)[:, 0]
+    small_block = 2 * seg_length
     if aligned:
-        edge, edge_total, full_up, full_down = edge_forward(
-            pre_edge, None, gains, shifts, ([ffn_half, ffn_other], shapes), ids
+        low, act, slope, out, branch, grad2, sums2, cls, full_up, full_down = ffn_forward(
+            pre_first, cot, None, gains, shifts, seg_length, small_block, ([ffn_half, ffn_other], shapes), ids
         )
     else:
         full_up = joined([ffn_half, ffn_other], 0, False)
         full_down = joined([ffn_half, ffn_other], shard_rows, True)
-        edge, edge_total = edge_forward(pre_edge, [full_up, full_down], gains, shifts)
-    edge_cot = cot.reshape(local, seg_length, width)[:, 0].astype(F32)
-    edges = Gather(jnp.stack([edge, edge_cot], axis=0))
-    small_block, small_steps = block // 2, steps
-    *kept, sums2a = ffn_forward(
-        pre_first, cot, full_up, full_down, gains, shifts, seg_length, small_block, (0, small_steps), after=[edge]
+        low, act, slope, out, branch, grad2, sums2, cls = ffn_forward(
+            pre_first, cot, [full_up, full_down], gains, shifts, seg_length, small_block
+        )
+
+    def with_edge(values, edge):
+        whole_rows = values.reshape(local, seg_length, values.shape[1])
+        return lax.dynamic_update_slice(whole_rows, edge[:, None], (0, 0, 0)).reshape(values.shape)
+
+    edges = Gather(cls[:, CLS_OUT * width : (CLS_COT + 1) * width])
+    send_down, keep_down = rows_grads(ids, act, branch, count, [edges.piece])
+    down = Reduction(ids, send_down, keep_down)
+    edges.across(send_down)
+    cross_half = later(cross_half, send_down)
+    cross_other = rep_swap(cross_half, 1)
+    *kept, sums1a = ffn_backward(
+        branch, grad2, pre_first, slope, full_up, full_down, gains, block, halves_of[0], LONG, after=[edges.evens, cross_half]
     )
-    edges.across(kept[0])
-    low, act, slope, out, branch, grad2, sums2b = ffn_forward(
-        pre_first, cot, full_up, full_down, gains, shifts, seg_length, small_block, (small_steps, small_steps), prior=kept,
-        after=[edges.evens],
-    )
-    edges = edges.finish(low)
-    cross_half = later(cross_half, low)
-    cross_parts, cross_shape = [cross_half, rep_swap(cross_half, 1)], shapes[0]
+    edges = edges.finish(kept[0]).reshape(-1, 2 * width)
+    cross_parts, cross_shape = [cross_half, later(cross_other, kept[0])], shapes[0]
     if not aligned:
         cross_parts, cross_shape = [joined(cross_parts, 0, False)], None
-    cls_new, cls_branch, cls_grad, c_low, c_gradp, c_mixed, c_gradz, c_sums, table_grad = cross_block(
-        ids, local, edges[:, 0].reshape(-1, width), edges[:, 1].reshape(-1, width), edge_total,
-        keys[:, None], jnp.concatenate([keys, keys])[None, :], places, table, gains, shifts, cross_parts, cross_shape,
+    cls_new, cls_branch, grad_c, c_sums, table_grad, *cls_back = cross_block(
+        ids, edges, cls, keys[:, None], jnp.concatenate([keys, keys])[None, :], places, table, gains, shifts, full_up,
+        full_down, cross_parts, cross_shape,
     )
-
-    def with_edge(values, edge):
-        whole_rows = values.reshape(local, seg_length, width)
-        return lax.dynamic_update_slice(whole_rows, edge[:, None], (0, 0, 0)).reshape(rows, width)
-
-    branch, grad2 = with_edge(branch, cls_branch), with_edge(grad2, cls_grad)
-    send_down, keep_down = rows_grads(ids, act, branch, count, [])
-    down = Reduction(ids, send_down, keep_down)
-    *kept, sums1a = ffn_backward(
-        branch, grad2, pre_first, slope, full_up, full_down, gains, block, halves_of[0], LONG, after=[send_down]
-    )
-    down.spread(kept[0])
+    cls_hidden, cls_grad1, cls_low1, cls_turned = cls_back
+    operands = [cls_turned, cls_branch]
+    c_own, c_other = halve(grad_c.reshape(2, 2, shard_rows, width), 0, rep & 1)
+    c_came = rep_swap(c_other, 1)
+    down.spread(kept[0], product=operands + [rep_swap(value, 1) for value in operands])
     grad_hidden, grad1, low1, sums1b = ffn_backward(
         branch, grad2, pre_first, slope, full_up, full_down, gains, block, halves_of[1], SHORT, prior=kept, after=[down.stay]
     )
-    norm_sums = (sums2a + sums2b + sums1a + sums1b + c_sums).reshape(8, count, norm_cols).transpose(1, 0, 2)
+    low1 = with_edge(low1, cls_low1)
+    norm_sums = (sums2 + sums1a + sums1b + c_sums).reshape(8, count, norm_cols).transpose(1, 0, 2)
     norm_sums = jnp.pad(norm_sums, ((0, 0), (0, 0), (0, width - norm_cols)))
     rider = jnp.concatenate([norm_sums, table_grad.reshape(count, table_rows, width)], axis=1).astype(BF16)
-    send_up = cols_grads(1, ids, low, grad_hidden, rider, [], SHORT)
+    send_up = cols_grads(1, ids, low, grad_hidden, cls, cls_hidden, rider, [], SHORT)
     own_down, *others = settle(ids, down.parts(send_up))
     came_down = swap_far(others)
-    keep_up = cols_grads(0, ids, low, grad_hidden, rider, [send_up, own_down], LONG)
+    keep_up = cols_grads(0, ids, low, grad_hidden, cls, cls_hidden, rider, [send_up, own_down], LONG)
     up = Reduction(ids, send_up, keep_up)
     up.spread(keep_up, *came_down[:1])
     grad_proj = attention_backward(low1, proj, probs, full_qo, seg_length, block, after=[up.stay])
     down_share = add_up(own_down, came_down, grad_proj)
+    c_own, c_other = halve(c_own.astype(F32) + later(c_came, grad_proj).astype(F32), 0, rep >> 1)
+    c_came = rep_swap(c_other.astype(BF16), 2)
     send_qo = joint_grads(1, ids, flat, mixed, grad_proj, low1, [], SHORT)
     own_up, *others = settle(ids, up.parts(send_qo))
     came_up = swap_far(others)
     keep_qo = joint_grads(0, ids, flat, mixed, grad_proj, low1, [send_qo, own_up], LONG)
     qo = Reduction(ids, send_qo, keep_qo)
     qo.spread(keep_qo, *came_up[:2])
-    input_grad = input_gradient(grad1, grad_proj, full_qo, block, [qo.stay])
+    input_grad = input_gradient(with_edge(later(grad1, qo.stay), cls_grad1), grad_proj, full_qo, block, [qo.stay])
     own, *others = settle(ids, qo.parts(input_grad))
     came = swap_far(others)
-    early = Sharing(ids, jnp.concatenate([down_share, add_up(own_up, came_up, own)], axis=0))
-    own_low = lax.dynamic_slice_in_dim(later(c_low, own), me * shard_rows, shard_rows, 1)
-    own_mixed = lax.dynamic_slice_in_dim(later(c_mixed, own), me * shard_rows, shard_rows, 1)
-    grad_c = shares_of(jnp.concatenate([dot_tn(own_low, c_gradp), dot_tn(own_mixed, c_gradz)], axis=1)).astype(BF16)
-    c_own, c_other = halve(grad_c.reshape(2, 2, shard_rows, width), 0, rep & 1)
-    c_own, c_other = halve(c_own.astype(F32) + rep_swap(c_other, 1).astype(F32), 0, rep >> 1)
-    c_came = rep_swap(c_other.astype(BF16), 2)
+    c_share = (c_own + later(c_came, own).astype(F32)).astype(BF16)
+    early = Sharing(ids, jnp.concatenate([down_share, add_up(own_up, came_up, own), c_share], axis=0))
     late = Sharing(ids, add_up(own, came))
     early.step(late.value)
-    crossing = Sharing(ids, (c_own + later(c_came, late.value).astype(F32)).astype(BF16))
-    layer_out = with_edge(later(out, crossing.value), cls_new)
-    late.step(layer_out)
-    crossing.step(late.value)
-    early_shares = early.finish(late.value)
-    starts = (0, shard_rows, 2 * shard_rows, 2 * shard_rows + 16)
-    down_parts, up_parts, riders = [[part[first:last] for part in early_shares] for first, last in zip(starts, starts[1:])]
-    grad_up, grad_down, summed = jnp.concatenate(up_parts, axis=1), jnp.concatenate(down_parts, axis=0), riders[0]
-    qo_parts, c_parts = late.finish(), crossing.finish()
+    layer_out = with_edge(later(out, late.value), cls_new)
+    early_shares = early.finish(layer_out)
+    starts = (0, shard_rows, 2 * shard_rows, 2 * shard_rows + 16, 3 * shard_rows + 16)
+    down_parts, up_parts, riders, c_parts = [
+        [part[first:last] for part in early_shares] for first, last in zip(starts, starts[1:])
+    ]
+    done = [
+        jnp.concatenate(up_parts, axis=1),
+        jnp.concatenate(down_parts, axis=0),
+        jnp.concatenate(c_parts[:3], axis=1),
+        c_parts[3],
+    ]
+    summed = riders[0]
+    late.step(layer_out, *done)
+    qo_parts = late.finish()
 
     return (
         layer_out.reshape(tokens.shape),
         input_grad.reshape(tokens.shape),
         jnp.concatenate(qo_parts[:3], axis=1),
         qo_parts[3],
-        grad_up,
-        grad_down,
-        jnp.concatenate(c_parts[:3], axis=1),
-        c_parts[3],
+        *done,
         summed[8 : 8 + table_rows],
         summed[:3, :norm_cols],
         summed[3:6, :norm_cols],

time: 466 us -> 446 us (0.957)
  waiting for transfers between devices: 89.6 us -> 74.7 us
  between operations: 23.5 us -> 15.4 us
  starting transfers between devices: 48.8 us -> 54.9 us
    ppermute x23, waiting for transfers between devices: 53 us -> 37.4 us  [seg_swap(): return lax.ppermute(value, 'seg', [(i, i ^ mask) for i in range(count)])]
    pallas_call x8 -> x6, Pallas kernels: 163 us -> 152 us  [rows_call(): pl.pallas_call(run, out_shape=tuple((jax.ShapeDtypeStruct(shape.shape, sh...]
    ppermute x3, waiting for transfers between devices: 10.5 us -> 0.01 us  [both_swap(): return lax.ppermute(value, ('seg', 'rep'), pairs)]
    ppermute x24, waiting for transfers between devices: 5.31 us -> 12.7 us  [rep_swap(): return lax.ppermute(value, 'rep', [(i, i ^ mask) for i in range(count)])]
    pallas_call x1, Pallas kernels: 9.96 us -> 14.7 us  [cross_block(): pl.pallas_call(partial(cross_kernel, local, shape is not None), out_shape...]
    unnamed x104 -> x128, local copies, waits for them, and re-layouts: 10.2 us -> 11.9 us
  transfers between devices with their start and end apart: 52 -> 52, of which waited for: 12 -> 11; matrix products, arithmetic and copies ran while one was open for 6% -> 7% of each run, Pallas kernels for 46% -> 54%
where the time goes in v4:
time: 446 us; the launch traced here: 440 us
  Pallas kernels  242 us (54%)
  waiting for transfers between devices  74.7 us (17%)
  starting transfers between devices  54.9 us (12%)
  local copies, waits for them, and re-layouts  36.9 us (8%)
  other arithmetic  16.6 us (4%)
  between operations  15.4 us (3%)
    pallas_call x6, Pallas kernels, rows_call(): pl.pallas_call(run, out_shape=tuple((jax.ShapeDtypeStruct(shape.shape, sh...  152 us
    pallas_call x4, Pallas kernels, half_grads(): pl.pallas_call(kernel, out_shape=jax.ShapeDtypeStruct((2,) + shape, BF16)...  45.7 us
    ppermute x23, starting transfers between devices, seg_swap(): return lax.ppermute(value, 'seg', [(i, i ^ mask) for i in range(count)])  39.9 us
    ppermute x23, waiting for transfers between devices, seg_swap(): return lax.ppermute(value, 'seg', [(i, i ^ mask) for i in range(count)])  37.4 us
    all_gather x1, waiting for transfers between devices, body(): ffn_half = lax.all_gather(ffn_piece, 'seg', axis=0)  24.7 us
    pallas_call x1, Pallas kernels, rows_grads(): pl.pallas_call(rows_grad_kernel, out_shape=(half, half), grid_spec=pltpu....  16.8 us
    pallas_call x1, Pallas kernels, cross_block(): pl.pallas_call(partial(cross_kernel, local, shape is not None), out_shape...  14.7 us
    ppermute x24, waiting for transfers between devices, rep_swap(): return lax.ppermute(value, 'rep', [(i, i ^ mask) for i in range(count)])  12.7 us
  transfers between devices with their start and end apart: 52, of which 11 were waited for; matrix products, arithmetic and copies ran while one was open for 7% of the time, Pallas kernels for 54%

profile of v4, /device:TPU:0, one launch (start us, length us, event | category | flops | bytes accessed | tf_op | source)
XLA Modules:
  0.0 440.4 jit_solution(3457340237372515067)
XLA Ops:
  7.3 1.2 pad_maximum_fusion.8
  13.4 3.1 collective-permute-start.1
  16.5 1.5 collective-permute-start
  17.9 2.6 collective-permute-start.3
  20.5 11.0 %collective-permute-done.1.refs_4_ = bf16[2,96,768]{2,1,0:T(8,128)(2,1)S(1)} collective-permute-done((bf16[2,96,768]{2,1,0:T(8,128)(2,1)S(1)}, bf16[2,96,768]{2,1,0:T(8,128)(2,1)S(1)}, u32[]{:S(2)}, u32[]{:S(2)}) %collective-permute-start.1) | collective-permute-done | bytes 294944 | tf_op jit(solution)/shard_map/ppermute | solution.py:662
  31.5 5.1 %collective-permute-start.2 = (bf16[2,96,768]{2,1,0:T(8,128)(2,1)S(1)}, bf16[2,96,768]{2,1,0:T(8,128)(2,1)S(1)}, u32[]{:S(2)}, u32[]{:S(2)}) collective-permute-start(bf16[2,96,768]{2,1,0:T(8,128)(2,1)S(1)} %collective-permute-done.1.refs_4_), channel_id=1, source_target_pairs={{0,4},{4,0},{8,12},{12,8},{16,20},{20,16},{24,28},{28,24},{1,5},{5... | collective-permute-start | bytes 884744 | tf_op jit(solution)/shard_map/ppermute | solution.py:662
  36.7 3.7 collective-permute-start.7
  41.4 2.1 collective-permute-start.6
  43.6 9.3 %collective-permute-done.7.refs_8_ = bf16[2,96,768]{2,1,0:T(8,128)(2,1)S(1)} collective-permute-done((bf16[2,96,768]{2,1,0:T(8,128)(2,1)S(1)}, bf16[2,96,768]{2,1,0:T(8,128)(2,1)S(1)}, u32[]{:S(2)}, u32[]{:S(2)}) %collective-permute-start.7) | collective-permute-done | bytes 294944 | tf_op jit(solution)/shard_map/ppermute | solution.py:662
  53.0 1.5 collective-permute-start.10
  55.3 6.8 %collective-permute-done.10.refs_9_ = bf16[2,96,768]{2,1,0:T(8,128)(2,1)} collective-permute-done((bf16[2,96,768]{2,1,0:T(8,128)(2,1)S(1)}, bf16[2,96,768]{2,1,0:T(8,128)(2,1)}, u32[]{:S(2)}, u32[]{:S(2)}) %collective-permute-start.10) | collective-permute-done | bytes 294944 | tf_op jit(solution)/shard_map/ppermute | solution.py:662
  65.6 28.5 %attention_forward.1 = (bf16[2048,2304]{1,0:T(8,128)(2,1)}, bf16[16,6,128,256]{3,2,1,0:T(8,128)(2,1)}, bf16[2048,768]{1,0:T(8,128)(2,1)}, f32[2048,768]{1,0:T(8,128)}, bf16[4,8,96,768]{3,2,1,0:T(8,128)(2,1)}) custom-call(s32[2]{0:T(128)} %pad_add_fusion.1.refs_0_.ids_ref, bf16[2048,768]{1,0:T(8,128)(2,1)} %bitcast.126, bf16[2,96,768]{2,1,0:T(8,128)(2,1)} %bitcast.140, ...), custom_call_target="tpu_custom_call" | custom-call | flops 12884901 | bytes 18874 | tf_op jit(solution)/shard_map/attention_forward/pallas_call | solution.py:128
  94.0 24.7 %all-gather.5.cloned.1.call-done = bf16[16,208,768]{2,1,0:T(8,128)(2,1)} async-done(((bf16[2,208,768]{2,1,0:T(8,128)(2,1)}), bf16[16,208,768]{2,1,0:T(8,128)(2,1)}) %all-gather.5.cloned.1.call-update) | async-done | bytes 5111824 | tf_op jit(solution)/shard_map/all_gather | solution.py:880
  122.9 1.5 slice_bitcast_fusion.12.table_ref
  124.4 3.1 collective-permute-done.15.refs_6_
  127.5 41.8 %ffn_forward.1 = (bf16[2048,768]{1,0:T(8,128)(2,1)}, bf16[2048,3072]{1,0:T(8,128)(2,1)}, bf16[2048,3072]{1,0:T(8,128)(2,1)}, bf16[2048,768]{1,0:T(8,128)(2,1)}, ...) custom-call(s32[2]{0:T(128)} %pad_add_fusion.1.refs_0_.ids_ref, ...), custom_call_target="tpu_custom_call" | custom-call | flops 19327352832 | bytes 35332608 | tf_op jit(solution)/shard_map/ffn_forward/pallas_call | solution.py:128
  170.8 1.7 collective-permute-start.17
  172.5 2.2 collective-permute-start.18
  174.7 16.8 %rows_grads.1 = (bf16[2,8,96,768]{3,2,1,0:T(8,128)(2,1)}, bf16[2,8,96,768]{3,2,1,0:T(8,128)(2,1)}) custom-call(s32[2]{0:T(128)} %pad_add_fusion.1.refs_0_.ids_ref, bf16[2048,3072]{1,0:T(8,128)(2,1)} %get-tuple-element.119.left_ref, bf16[2048,768]{1,0:T(8,128)(2,1)} %get-tuple-element.113.right_ref.refs_0_, f32[16,1536]{1,0:T(8,128)} %copy-done.51), custom_call_target="tpu_custom_call" | custom-call | flops 9663676416 | bytes 15728640 | tf_op jit(solution)/shard_map/rows_grads/pallas_call | solution.py:637
  192.8 20.4 %ffn_backward.2 = (bf16[2048,3072]{1,0:T(8,128)(2,1)}, f32[2048,768]{1,0:T(8,128)}, bf16[2048,768]{1,0:T(8,128)(2,1)}, f32[8,768]{1,0:T(8,128)}) custom-call(bf16[2048,768]{1,0:T(8,128)(2,1)} %get-tuple-element.113.right_ref.refs_0_, f32[2048,768]{1,0:T(8,128)} %get-tuple-element.114.refs_1_, f32[2048,768]{1,0:T(8,128)} %get-tuple-element.108.refs_1_.refs_2_, ...), custom_call_target="tpu_custom_call" | custom-call | flops 57982058496 | bytes 179394048 | tf_op jit(solution)/shard_map/ffn_backward/pallas_call | solution.py:128
  214.3 1.4 copy-done.62
  215.7 14.7 %cross_block.1 = (bf16[16,768]{1,0:T(8,128)(2,1)}, bf16[16,768]{1,0:T(8,128)(2,1)}, bf16[4,96,768]{2,1,0:T(8,128)(2,1)}, f32[8,768]{1,0:T(8,128)}, f32[64,768]{1...) custom-call(s32[2]{0:T(128)} %pad_add_fusion.1.refs_0_.ids_ref, ...), custom_call_target="tpu_custom_call" | custom-call | flops 10000000000 | bytes 4718592 | tf_op jit(solution)/shard_map/cross_block/pallas_call | solution.py:509
  230.5 1.4 copy.116
  233.6 1.1 copy-done.2
  235.5 4.5 %spread.3 = (bf16[4,96,768]{2,1,0:T(8,128)(2,1)S(1)}, bf16[4,96,768]{2,1,0:T(8,128)(2,1)}, bf16[4,96,768]{2,1,0:T(8,128)(2,1)}, bf16[4,96,768]{2,1,0:T(8,128)(2,1)}) custom-call(s32[2]{0:T(128)S(1)} %copy-done.16, bf16[2,4,2,96,768]{4,3,2,1,0:T(8,128)(2,1)S(1)} %bitcast.119, bf16[2,4,2,96,768]{4,3,2,1,0:T(8,128)(2,1)} %bitcast.21.came_ref, ...), custom_call_target="tpu_custom_call" | custom-call | bytes 7077888 | tf_op jit(solution)/shard_map/spread/pallas_call | solution.py:764
  240.8 2.4 collective-permute-start.26
  244.3 20.5 %ffn_backward.3 = (bf16[2048,3072]{1,0:T(8,128)(2,1)}, f32[2048,768]{1,0:T(8,128)}, bf16[2048,768]{1,0:T(8,128)(2,1)}, f32[8,768]{1,0:T(8,128)}) custom-call(bf16[2048,768]{1,0:T(8,128)(2,1)} %get-tuple-element.113.right_ref.refs_0_, f32[2048,768]{1,0:T(8,128)} %get-tuple-element.114.refs_1_, ...), custom_call_target="tpu_custom_call", output_to_operand_aliasing={{0}: (7, {}), {1}: (8, {}), {2}: (9, {})} | custom-call | flops 9663676 | bytes 29899 | tf_op jit(solution)/shard_map/ffn_backward/pallas_call | solution.py:128
  266.4 10.7 %cols_grads.2.refs_0_ = bf16[2,8,112,768]{3,2,1,0:T(8,128)(2,1)} custom-call(s32[2]{0:T(128)} %pad_add_fusion.1.refs_0_.ids_ref, bf16[2048,768]{1,0:T(8,128)(2,1)} %get-tuple-element.140.left_ref, bf16[2048,3072]{1,0:T(8,128)(2,1)} %get-tuple-element.141.right_ref, f32[16,9984]{1,0:T(8,128)} %get-tuple-element.118.cls_ref.cls_left_ref, ...), custom_call_target="tpu_custom_call" | custom-call | flops 4831838 | bytes 15728 | tf_op jit(solution)/shard_map/cols_grads/pallas_call | solution.py:568
  278.4 1.4 settle.3
  280.5 2.2 collective-permute-start.42
  282.7 2.2 collective-permute-start.43
  284.9 11.1 %cols_grads.3 = bf16[2,8,112,768]{3,2,1,0:T(8,128)(2,1)} custom-call(s32[2]{0:T(128)} %pad_add_fusion.1.refs_0_.ids_ref, bf16[2048,768]{1,0:T(8,128)(2,1)} %get-tuple-element.140.left_ref, bf16[2048,3072]{1,0:T(8,128)(2,1)} %get-tuple-element.141.right_ref, f32[16,9984]{1,0:T(8,128)} %get-tuple-element.118.cls_ref.cls_left_ref, ...), custom_call_target="tpu_custom_call" | custom-call | flops 28991029248 | bytes 94371840 | tf_op jit(solution)/shard_map/cols_grads/pallas_call | solution.py:568
  296.0 1.8 copy-done.5
  297.9 2.5 spread.4
  301.2 2.4 collective-permute-start.31
  306.8 1.9 dynamic_update_slice.9
  308.7 27.1 %attention_backward.1.right_ref.refs_1_ = bf16[2048,2304]{1,0:T(8,128)(2,1)} custom-call(bf16[2048,768]{1,0:T(8,128)(2,1)} %bitcast.123, bf16[2048,2304]{1,0:T(8,128)(2,1)} %get-tuple-element.109.refs_1_, bf16[16,6,128,256]{3,2,1,0:T(8,128)(2,1)} %get-tuple-element.138.refs_2_, bf16[4,8,96,768]{3,2,1,0:T(8,128)(2,1)} %get-tuple-element.139.refs_3_.refs_2_, ...), custom_call_target="tpu_custom_call" | custom-call | flops 8858370 | bytes 16515 | tf_op jit(solution)/shard_map/attention_backward/pallas_call | solution.py:128
  335.9 11.8 %joint_grads.2.refs_0_ = bf16[2,768,768]{2,1,0:T(8,128)(2,1)} custom-call(s32[2]{0:T(128)} %pad_add_fusion.1.refs_0_.ids_ref, bf16[2048,768]{1,0:T(8,128)(2,1)} %bitcast.127, bf16[2048,768]{1,0:T(8,128)(2,1)} %get-tuple-element.112.last_left_ref, bf16[2048,2304]{1,0:T(8,128)(2,1)} %attention_backward.1.right_ref.refs_1_, bf16[2048,768]{1,0:T(8,128)(2,1)} %bitcast.124), custom_call_target="tpu_custom_call" | custom-call | flops 4831838 | bytes 15728 | tf_op jit(solution)/shard_map/joint_grads/pallas_call | solution.py:568
  347.7 1.1 convert_add_fusion
  349.6 1.5 collective-permute-start.46
  351.1 1.6 add_convert_fusion.1
  352.8 1.5 settle.4
  355.0 2.1 collective-permute-start.34
  357.0 12.0 %joint_grads.3 = bf16[2,768,768]{2,1,0:T(8,128)(2,1)} custom-call(s32[2]{0:T(128)} %pad_add_fusion.1.refs_0_.ids_ref, bf16[2048,768]{1,0:T(8,128)(2,1)} %bitcast.128, bf16[2048,768]{1,0:T(8,128)(2,1)} %get-tuple-element.112.last_left_ref, bf16[2048,2304]{1,0:T(8,128)(2,1)} %attention_backward.1.right_ref.refs_1_, bf16[2048,768]{1,0:T(8,128)(2,1)} %bitcast.125, ...), custom_call_target="tpu_custom_call" | custom-call | flops 28991029248 | bytes 94371840 | tf_op jit(solution)/shard_map/joint_grads/pallas_call | solution.py:568
  369.1 2.3 collective-permute-start.44
  371.4 1.8 copy-done.7
  373.2 1.5 spread.5
  375.5 1.3 collective-permute-start.37
  376.8 1.5 collective-permute-start.36
  379.0 2.0 dynamic_update_slice.10
  380.9 14.2 %input_gradient.1 = f32[2048,768]{1,0:T(8,128)} custom-call(f32[2048,768]{1,0:T(8,128)} %bitcast.130, bf16[2048,2304]{1,0:T(8,128)(2,1)} %attention_backward.1.right_ref.refs_1_, bf16[4,8,96,768]{3,2,1,0:T(8,128)(2,1)} %get-tuple-element.139.refs_3_.refs_2_, bf16[4,96,768]{2,1,0:T(8,128)(2,1)} %copy-done.10), custom_call_target="tpu_custom_call" | custom-call | flops 43486543872 | bytes 80216064 | tf_op jit(solution)/shard_map/input_gradient/pallas_call | solution.py:128
  395.2 8.4 %collective-permute-done.36.refs_2_ = bf16[4,96,768]{2,1,0:T(8,128)(2,1)S(1)} collective-permute-done((bf16[4,96,768]{2,1,0:T(8,128)(2,1)S(1)}, bf16[4,96,768]{2,1,0:T(8,128)(2,1)S(1)}, u32[]{:S(2)}, u32[]{:S(2)}) %collective-permute-start.36) | collective-permute-done | bytes 589856 | tf_op jit(solution)/shard_map/ppermute | solution.py:667
  404.5 0.9 fusion.1
  405.5 1.0 add_convert_fusion
  407.2 2.1 collective-permute-start.39
  409.3 2.3 collective-permute-start.40
  411.6 3.0 collective-permute-done.38
  414.7 6.5 %collective-permute-done.39 = bf16[96,768]{1,0:T(8,128)(2,1)S(1)} collective-permute-done((bf16[96,768]{1,0:T(8,128)(2,1)S(1)}, bf16[96,768]{1,0:T(8,128)(2,1)S(1)}, u32[]{:S(2)}, u32[]{:S(2)}) %collective-permute-start.39) | collective-permute-done | bytes 147488 | tf_op jit(solution)/shard_map/ppermute | solution.py:662
  421.6 1.6 collective-permute-start.41
  423.1 1.9 dynamic_update_slice.11
  426.6 1.0 pad_maximum_fusion.4
  427.6 1.1 pad_maximum_fusion.1
  428.7 1.1 pad_maximum_fusion.2
  432.4 1.0 maximum_convert_fusion
  (264 shorter events, 39.0 us)
Async XLA Ops:
  7.2 111.5 %all-gather.5.cloned.1.call-start = ((), (), s32[]{:S(2)}) async-start(), calls=%async_computation | async-start | bytes 5750784 | tf_op jit(solution)/shard_map/all_gather | solution.py:880
  12.4 31.1 %copy-start.58 = (s32[2,1,3]{2,1,0:T(1,128)S(1)}, s32[2,1,3]{2,1,0:T(1,128)}, u32[]{:S(2)}) copy-start(s32[2,1,3]{2,1,0:T(1,128)} %param.14) | copy-start | bytes 76
  12.4 179.1 %all-gather.7.cloned.1.call-start = ((), (), s32[]{:S(2)}) async-start(), calls=%async_computation.1 | async-start | bytes 2654208 | tf_op jit(solution)/shard_map/all_gather | solution.py:886
  13.3 52.1 %copy-start.24 = (bf16[96,2,768]{2,0,1:T(8,128)(2,1)}, bf16[96,2,768]{2,0,1:T(8,128)(2,1)S(1)}, u32[]{:S(2)}) copy-start(bf16[96,2,768]{2,0,1:T(8,128)(2,1)S(1)} %copy.127) | copy-start | bytes 884740
  13.4 18.1 %collective-permute-start.1 = (bf16[2,96,768]{2,1,0:T(8,128)(2,1)S(1)}, bf16[2,96,768]{2,1,0:T(8,128)(2,1)S(1)}, u32[]{:S(2)}, u32[]{:S(2)}) collective-permute-start(bf16[2,96,768]{2,1,0:T(8,128)(2,1)S(1)} %bitcast.135), channel_id=1, source_target_pairs={{0,8},{4,12},{8,0},{12,4},{16,24},{20,28},{24,16},{28,20},{1,9},{5... | collective-permute-start | bytes 884744 | tf_op jit(solution)/shard_map/ppermute | solution.py:662
  16.5 15.1 %collective-permute-start = (bf16[2,96,768]{2,1,0:T(8,128)(2,1)S(1)}, bf16[2,96,768]{2,1,0:T(8,128)(2,1)S(1)}, u32[]{:S(2)}, u32[]{:S(2)}) collective-permute-start(bf16[2,96,768]{2,1,0:T(8,128)(2,1)S(1)} %bitcast.136), channel_id=1, source_target_pairs={{0,4},{4,0},{8,12},{12,8},{16,20},{20,16},{24,28},{28,24},{1,5},{5... | collective-permute-start | bytes 884744 | tf_op jit(solution)/shard_map/ppermute | solution.py:662
  17.9 22.4 %collective-permute-start.3 = (bf16[2,96,768]{2,1,0:T(8,128)(2,1)S(1)}, bf16[2,96,768]{2,1,0:T(8,128)(2,1)S(1)}, u32[]{:S(2)}, u32[]{:S(2)}) collective-permute-start(bf16[2,96,768]{2,1,0:T(8,128)(2,1)S(1)} %bitcast.137), channel_id=1, source_target_pairs={{0,16},{4,20},{8,24},{12,28},{16,0},{20,4},{24,8},{28,12},{1,17},{... | collective-permute-start | bytes 884744 | tf_op jit(solution)/shard_map/ppermute | solution.py:662
  20.5 20.1 %collective-permute-start.4 = (bf16[2,96,768]{2,1,0:T(8,128)(2,1)S(1)}, bf16[2,96,768]{2,1,0:T(8,128)(2,1)S(1)}, u32[]{:S(2)}, u32[]{:S(2)}) collective-permute-start(bf16[2,96,768]{2,1,0:T(8,128)(2,1)S(1)} %bitcast.138), channel_id=1, source_target_pairs={{0,1},{1,0},{2,3},{3,2},{4,5},{5,4},{6,7},{7,6},{8,9},{9,8},{10,11... | collective-permute-start | bytes 884744 | tf_op jit(solution)/shard_map/ppermute | solution.py:667
  31.5 33.9 %copy-start.31 = (bf16[2,96,768]{2,1,0:T(8,128)(2,1)}, bf16[2,96,768]{2,1,0:T(8,128)(2,1)S(1)}, u32[]{:S(2)}) copy-start(bf16[2,96,768]{2,1,0:T(8,128)(2,1)S(1)} %collective-permute-done.1.refs_4_) | copy-start | bytes 884740
  31.5 34.0 %copy-start.32 = (bf16[2,96,768]{2,1,0:T(8,128)(2,1)}, bf16[2,96,768]{2,1,0:T(8,128)(2,1)S(1)}, u32[]{:S(2)}) copy-start(bf16[2,96,768]{2,1,0:T(8,128)(2,1)S(1)} %collective-permute-done.refs_3_) | copy-start | bytes 884740
  31.5 9.9 %collective-permute-start.2 = (bf16[2,96,768]{2,1,0:T(8,128)(2,1)S(1)}, bf16[2,96,768]{2,1,0:T(8,128)(2,1)S(1)}, u32[]{:S(2)}, u32[]{:S(2)}) collective-permute-start(bf16[2,96,768]{2,1,0:T(8,128)(2,1)S(1)} %collective-permute-done.1.refs_4_), channel_id=1, source_target_pairs={{0,4},{4,0},{8,12},{12,8},{16,20},{20,16},{24,28},{28,24},{1,5},{5... | collective-permute-start | bytes 884744 | tf_op jit(solution)/shard_map/ppermute | solution.py:662
  36.7 4.7 %collective-permute-start.5 = (bf16[2,96,768]{2,1,0:T(8,128)(2,1)S(1)}, bf16[2,96,768]{2,1,0:T(8,128)(2,1)S(1)}, u32[]{:S(2)}, u32[]{:S(2)}) collective-permute-start(bf16[2,96,768]{2,1,0:T(8,128)(2,1)S(1)} %collective-permute-done.refs_3_), channel_id=1, source_target_pairs={{0,1},{1,0},{2,3},{3,2},{4,5},{5,4},{6,7},{7,6},{8,9},{9,8},{10,11... | collective-permute-start | bytes 884744 | tf_op jit(solution)/shard_map/ppermute | solution.py:667
  36.7 16.3 %collective-permute-start.7 = (bf16[2,96,768]{2,1,0:T(8,128)(2,1)S(1)}, bf16[2,96,768]{2,1,0:T(8,128)(2,1)S(1)}, u32[]{:S(2)}, u32[]{:S(2)}) collective-permute-start(bf16[2,96,768]{2,1,0:T(8,128)(2,1)S(1)} %bitcast.139), channel_id=1, source_target_pairs={{0,24},{4,28},{8,16},{12,20},{16,8},{20,12},{24,0},{28,4},{1,25},{... | collective-permute-start | bytes 884744 | tf_op jit(solution)/shard_map/ppermute | solution.py:662
  40.4 25.1 %copy-start.33 = (bf16[2,96,768]{2,1,0:T(8,128)(2,1)}, bf16[2,96,768]{2,1,0:T(8,128)(2,1)S(1)}, u32[]{:S(2)}) copy-start(bf16[2,96,768]{2,1,0:T(8,128)(2,1)S(1)} %collective-permute-done.3.refs_6_) | copy-start | bytes 884740
  40.4 12.6 %collective-permute-start.8 = (bf16[2,96,768]{2,1,0:T(8,128)(2,1)S(1)}, bf16[2,96,768]{2,1,0:T(8,128)(2,1)S(1)}, u32[]{:S(2)}, u32[]{:S(2)}) collective-permute-start(bf16[2,96,768]{2,1,0:T(8,128)(2,1)S(1)} %collective-permute-done.1.refs_4_), channel_id=1, source_target_pairs={{0,1},{1,0},{2,3},{3,2},{4,5},{5,4},{6,7},{7,6},{8,9},{9,8},{10,11... | collective-permute-start | bytes 884744 | tf_op jit(solution)/shard_map/ppermute | solution.py:667
  40.6 24.9 %copy-start.34 = (bf16[2,96,768]{2,1,0:T(8,128)(2,1)}, bf16[2,96,768]{2,1,0:T(8,128)(2,1)S(1)}, u32[]{:S(2)}) copy-start(bf16[2,96,768]{2,1,0:T(8,128)(2,1)S(1)} %collective-permute-done.4.refs_10_) | copy-start | bytes 884740
  41.4 24.1 %copy-start.35 = (bf16[2,96,768]{2,1,0:T(8,128)(2,1)}, bf16[2,96,768]{2,1,0:T(8,128)(2,1)S(1)}, u32[]{:S(2)}) copy-start(bf16[2,96,768]{2,1,0:T(8,128)(2,1)S(1)} %collective-permute-done.2.refs_5_) | copy-start | bytes 884740
  41.4 24.1 %copy-start.36 = (bf16[2,96,768]{2,1,0:T(8,128)(2,1)}, bf16[2,96,768]{2,1,0:T(8,128)(2,1)S(1)}, u32[]{:S(2)}) copy-start(bf16[2,96,768]{2,1,0:T(8,128)(2,1)S(1)} %collective-permute-done.5.refs_11_) | copy-start | bytes 884740
  41.4 11.6 %collective-permute-start.6 = (bf16[2,96,768]{2,1,0:T(8,128)(2,1)S(1)}, bf16[2,96,768]{2,1,0:T(8,128)(2,1)S(1)}, u32[]{:S(2)}, u32[]{:S(2)}) collective-permute-start(bf16[2,96,768]{2,1,0:T(8,128)(2,1)S(1)} %collective-permute-done.3.refs_6_), channel_id=1, source_target_pairs={{0,4},{4,0},{8,12},{12,8},{16,20},{20,16},{24,28},{28,24},{1,5},{5... | collective-permute-start | bytes 884744 | tf_op jit(solution)/shard_map/ppermute | solution.py:662
  43.5 9.5 %collective-permute-start.9 = (bf16[2,96,768]{2,1,0:T(8,128)(2,1)S(1)}, bf16[2,96,768]{2,1,0:T(8,128)(2,1)S(1)}, u32[]{:S(2)}, u32[]{:S(2)}) collective-permute-start(bf16[2,96,768]{2,1,0:T(8,128)(2,1)S(1)} %collective-permute-done.2.refs_5_), channel_id=1, source_target_pairs={{0,1},{1,0},{2,3},{3,2},{4,5},{5,4},{6,7},{7,6},{8,9},{9,8},{10,11... | collective-permute-start | bytes 884744 | tf_op jit(solution)/shard_map/ppermute | solution.py:667
  53.0 9.1 %collective-permute-start.10 = (bf16[2,96,768]{2,1,0:T(8,128)(2,1)S(1)}, bf16[2,96,768]{2,1,0:T(8,128)(2,1)}, u32[]{:S(2)}, u32[]{:S(2)}) collective-permute-start(bf16[2,96,768]{2,1,0:T(8,128)(2,1)S(1)} %collective-permute-done.7.refs_8_), channel_id=1, source_target_pairs={{0,4},{4,0},{8,12},{12,8},{16,20},{20,16},{24,28},{28,24},{1,5},{5... | collective-permute-start | bytes 884744 | tf_op jit(solution)/shard_map/ppermute | solution.py:662
  54.7 10.8 %collective-permute-start.11 = (bf16[2,96,768]{2,1,0:T(8,128)(2,1)S(1)}, bf16[2,96,768]{2,1,0:T(8,128)(2,1)}, u32[]{:S(2)}, u32[]{:S(2)}) collective-permute-start(bf16[2,96,768]{2,1,0:T(8,128)(2,1)S(1)} %collective-permute-done.3.refs_6_), channel_id=1, source_target_pairs={{0,1},{1,0},{2,3},{3,2},{4,5},{5,4},{6,7},{7,6},{8,9},{9,8},{10,11... | collective-permute-start | bytes 884744 | tf_op jit(solution)/shard_map/ppermute | solution.py:667
  54.7 10.7 %collective-permute-start.13 = (bf16[2,96,768]{2,1,0:T(8,128)(2,1)S(1)}, bf16[2,96,768]{2,1,0:T(8,128)(2,1)}, u32[]{:S(2)}, u32[]{:S(2)}) collective-permute-start(bf16[2,96,768]{2,1,0:T(8,128)(2,1)S(1)} %collective-permute-done.7.refs_8_), channel_id=1, source_target_pairs={{0,1},{1,0},{2,3},{3,2},{4,5},{5,4},{6,7},{7,6},{8,9},{9,8},{10,11... | collective-permute-start | bytes 884744 | tf_op jit(solution)/shard_map/ppermute | solution.py:667
  55.2 10.2 %collective-permute-start.12 = (bf16[2,96,768]{2,1,0:T(8,128)(2,1)S(1)}, bf16[2,96,768]{2,1,0:T(8,128)(2,1)}, u32[]{:S(2)}, u32[]{:S(2)}) collective-permute-start(bf16[2,96,768]{2,1,0:T(8,128)(2,1)S(1)} %collective-permute-done.6.refs_7_), channel_id=1, source_target_pairs={{0,1},{1,0},{2,3},{3,2},{4,5},{5,4},{6,7},{7,6},{8,9},{9,8},{10,11... | collective-permute-start | bytes 884744 | tf_op jit(solution)/shard_map/ppermute | solution.py:667
  62.1 3.3 collective-permute-start.14
  65.6 54.6 %copy-start.59 = (s32[128]{0:T(128)S(1)}, s32[128]{0:T(128)}, u32[]{:S(2)}) copy-start(s32[128]{0:T(128)} %add.155.refs_18_) | copy-start | bytes 1540
  118.7 8.8 %collective-permute-start.15 = (bf16[8,2,208,768]{3,2,1,0:T(8,128)(2,1)}, bf16[8,2,208,768]{3,2,1,0:T(8,128)(2,1)}, u32[]{:S(2)}, u32[]{:S(2)}) collective-permute-start(bf16[8,2,208,768]{3,2,1,0:T(8,128)(2,1)} %bitcast.157), channel_id=1, source_target_pairs={{0,1},{1,0},{2,3},{3,2},{4,5},{5,4},{6,7},{7,6},{8,9},{9,8},{10,11... | collective-permute-start | bytes 15335432 | tf_op jit(solution)/shard_map/ppermute | solution.py:667
  170.2 21.8 %collective-permute-start.16 = (f32[16,1536]{1,0:T(8,128)S(1)}, f32[16,1536]{1,0:T(8,128)S(1)}, u32[]{:S(2)}, u32[]{:S(2)}) collective-permute-start(f32[16,1536]{1,0:T(8,128)S(1)} %get-tuple-element.287.refs_0_), channel_id=1, source_target_pairs={{0,8},{4,12},{8,0},{12,4},{16,24},{20,28},{24,16},{28,20},{1,9},{5... | collective-permute-start | bytes 294920 | tf_op jit(solution)/shard_map/ppermute | solution.py:662
  170.8 21.2 %collective-permute-start.17 = (f32[16,1536]{1,0:T(8,128)S(1)}, f32[16,1536]{1,0:T(8,128)S(1)}, u32[]{:S(2)}, u32[]{:S(2)}) collective-permute-start(f32[16,1536]{1,0:T(8,128)S(1)} %get-tuple-element.287.refs_0_), channel_id=1, source_target_pairs={{0,16},{4,20},{8,24},{12,28},{16,0},{20,4},{24,8},{28,12},{1,17},{... | collective-permute-start | bytes 294920 | tf_op jit(solution)/shard_map/ppermute | solution.py:662
  172.5 19.6 %collective-permute-start.18 = (f32[16,1536]{1,0:T(8,128)S(1)}, f32[16,1536]{1,0:T(8,128)S(1)}, u32[]{:S(2)}, u32[]{:S(2)}) collective-permute-start(f32[16,1536]{1,0:T(8,128)S(1)} %get-tuple-element.287.refs_0_), channel_id=1, source_target_pairs={{0,24},{4,28},{8,16},{12,20},{16,8},{20,12},{24,0},{28,4},{1,25},{... | collective-permute-start | bytes 294920 | tf_op jit(solution)/shard_map/ppermute | solution.py:662
  191.5 40.9 %collective-permute-start.19 = (bf16[2,8,96,768]{3,2,1,0:T(8,128)(2,1)}, bf16[2,8,96,768]{3,2,1,0:T(8,128)(2,1)}, u32[]{:S(2)}, u32[]{:S(2)}) collective-permute-start(bf16[2,8,96,768]{3,2,1,0:T(8,128)(2,1)} %get-tuple-element.120), channel_id=1, source_target_pairs={{0,1},{1,0},{2,3},{3,2},{4,5},{5,4},{6,7},{7,6},{8,9},{9,8},{10,11... | collective-permute-start | bytes 7077896 | tf_op jit(solution)/shard_map/ppermute | solution.py:667
  191.5 22.8 %collective-permute-start.21 = (bf16[8,2,96,768]{3,2,1,0:T(8,128)(2,1)}, bf16[8,2,96,768]{3,2,1,0:T(8,128)(2,1)S(1)}, u32[]{:S(2)}, u32[]{:S(2)}) collective-permute-start(bf16[8,2,96,768]{3,2,1,0:T(8,128)(2,1)} %bitcast.164), channel_id=1, source_target_pairs={{0,1},{1,0},{2,3},{3,2},{4,5},{5,4},{6,7},{7,6},{8,9},{9,8},{10,11... | collective-permute-start | bytes 7077896 | tf_op jit(solution)/shard_map/ppermute | solution.py:667
  192.1 21.2 %collective-permute-start.20 = (f32[4,16,1536]{2,1,0:T(8,128)S(1)}, f32[4,16,1536]{2,1,0:T(8,128)S(1)}, u32[]{:S(2)}, u32[]{:S(2)}) collective-permute-start(f32[4,16,1536]{2,1,0:T(8,128)S(1)} %get-tuple-element.295.refs_7_), channel_id=1, source_target_pairs={{0,4},{4,0},{8,12},{12,8},{16,20},{20,16},{24,28},{28,24},{1,5},{5... | collective-permute-start | bytes 1179656 | tf_op jit(solution)/shard_map/ppermute | solution.py:662
  231.8 1.4 collective-permute-start.22
  231.9 1.6 collective-permute-start.23
  240.8 37.6 %collective-permute-start.26 = (bf16[4,96,768]{2,1,0:T(8,128)(2,1)}, bf16[4,96,768]{2,1,0:T(8,128)(2,1)S(1)}, u32[]{:S(2)}, u32[]{:S(2)}) collective-permute-start(bf16[4,96,768]{2,1,0:T(8,128)(2,1)} %get-tuple-element.152), channel_id=1, source_target_pairs={{0,6},{1,7},{2,4},{3,5},{4,2},{5,3},{6,0},{7,1},{8,14},{9,15},{10,... | collective-permute-start | bytes 1769480 | tf_op jit(solution)/shard_map/ppermute | solution.py:674
  243.1 35.3 %collective-permute-start.25 = (bf16[4,96,768]{2,1,0:T(8,128)(2,1)}, bf16[4,96,768]{2,1,0:T(8,128)(2,1)S(1)}, u32[]{:S(2)}, u32[]{:S(2)}) collective-permute-start(bf16[4,96,768]{2,1,0:T(8,128)(2,1)} %get-tuple-element.150), channel_id=1, source_target_pairs={{0,2},{1,3},{2,0},{3,1},{4,6},{5,7},{6,4},{7,5},{8,10},{9,11},{10,... | collective-permute-start | bytes 1769480 | tf_op jit(solution)/shard_map/ppermute | solution.py:667
  243.6 34.8 %collective-permute-start.24 = (bf16[4,96,768]{2,1,0:T(8,128)(2,1)}, bf16[4,96,768]{2,1,0:T(8,128)(2,1)S(1)}, u32[]{:S(2)}, u32[]{:S(2)}) collective-permute-start(bf16[4,96,768]{2,1,0:T(8,128)(2,1)} %get-tuple-element.148), channel_id=1, source_target_pairs={{0,4},{4,0},{8,12},{12,8},{16,20},{20,16},{24,28},{28,24},{1,5},{5... | collective-permute-start | bytes 1769480 | tf_op jit(solution)/shard_map/ppermute | solution.py:662
  244.3 20.6 %copy-start.53 = (f32[8,768]{1,0:T(8,128)S(1)}, f32[8,768]{1,0:T(8,128)}, u32[]{:S(2)}) copy-start(f32[8,768]{1,0:T(8,128)} %get-tuple-element.143) | copy-start | bytes 73732
  244.3 20.6 %copy-start.54 = (f32[8,768]{1,0:T(8,128)S(1)}, f32[8,768]{1,0:T(8,128)}, u32[]{:S(2)}) copy-start(f32[8,768]{1,0:T(8,128)} %get-tuple-element.144) | copy-start | bytes 73732
  277.1 18.9 %collective-permute-start.27 = (bf16[2,8,112,768]{3,2,1,0:T(8,128)(2,1)}, bf16[2,8,112,768]{3,2,1,0:T(8,128)(2,1)S(1)}, u32[]{:S(2)}, u32[]{:S(2)}) collective-permute-start(bf16[2,8,112,768]{3,2,1,0:T(8,128)(2,1)} %cols_grads.2.refs_0_), channel_id=1, source_target_pairs={{0,1},{1,0},{2,3},{3,2},{4,5},{5,4},{6,7},{7,6},{8,9},{9,8},{10,11... | collective-permute-start | bytes 8257544 | tf_op jit(solution)/shard_map/ppermute | solution.py:667
  277.9 69.8 %collective-permute-start.45 = (bf16[2,96,768]{2,1,0:T(8,128)(2,1)}, bf16[2,96,768]{2,1,0:T(8,128)(2,1)}, u32[]{:S(2)}, u32[]{:S(2)}) collective-permute-start(bf16[2,96,768]{2,1,0:T(8,128)(2,1)} %dynamic-slice_bitcast_fusion), channel_id=1, source_target_pairs={{0,1},{1,0},{2,3},{3,2},{4,5},{5,4},{6,7},{7,6},{8,9},{9,8},{10,11... | collective-permute-start | bytes 884744 | tf_op jit(solution)/shard_map/ppermute | solution.py:667
  280.5 15.5 %collective-permute-start.28 = (bf16[96,768]{1,0:T(8,128)(2,1)S(1)}, bf16[96,768]{1,0:T(8,128)(2,1)S(1)}, u32[]{:S(2)}, u32[]{:S(2)}) collective-permute-start(bf16[96,768]{1,0:T(8,128)(2,1)S(1)} %get-tuple-element.155), channel_id=1, source_target_pairs={{0,8},{4,12},{8,0},{12,4},{16,24},{20,28},{24,16},{28,20},{1,9},{5... | collective-permute-start | bytes 442376 | tf_op jit(solution)/shard_map/ppermute | solution.py:662
  280.5 23.5 %collective-permute-start.42 = (bf16[96,768]{1,0:T(8,128)(2,1)S(1)}, bf16[96,768]{1,0:T(8,128)(2,1)S(1)}, u32[]{:S(2)}, u32[]{:S(2)}) collective-permute-start(bf16[96,768]{1,0:T(8,128)(2,1)S(1)} %get-tuple-element.185), channel_id=1, source_target_pairs={{0,16},{4,20},{8,24},{12,28},{16,0},{20,4},{24,8},{28,12},{1,17},{... | collective-permute-start | bytes 442376 | tf_op jit(solution)/shard_map/ppermute | solution.py:662
  282.7 53.1 %collective-permute-start.43 = (bf16[96,768]{1,0:T(8,128)(2,1)}, bf16[96,768]{1,0:T(8,128)(2,1)}, u32[]{:S(2)}, u32[]{:S(2)}) collective-permute-start(bf16[96,768]{1,0:T(8,128)(2,1)} %get-tuple-element.187), channel_id=1, source_target_pairs={{0,24},{4,28},{8,16},{12,20},{16,8},{20,12},{24,0},{28,4},{1,25},{... | collective-permute-start | bytes 442376 | tf_op jit(solution)/shard_map/ppermute | solution.py:662
  301.2 51.6 %collective-permute-start.31 = (bf16[4,112,768]{2,1,0:T(8,128)(2,1)}, bf16[4,112,768]{2,1,0:T(8,128)(2,1)S(1)}, u32[]{:S(2)}, u32[]{:S(2)}) collective-permute-start(bf16[4,112,768]{2,1,0:T(8,128)(2,1)} %get-tuple-element.162), channel_id=1, source_target_pairs={{0,6},{1,7},{2,4},{3,5},{4,2},{5,3},{6,0},{7,1},{8,14},{9,15},{10,... | collective-permute-start | bytes 2064392 | tf_op jit(solution)/shard_map/ppermute | solution.py:674
  303.5 49.3 %collective-permute-start.30 = (bf16[4,112,768]{2,1,0:T(8,128)(2,1)S(1)}, bf16[4,112,768]{2,1,0:T(8,128)(2,1)S(1)}, u32[]{:S(2)}, u32[]{:S(2)}) collective-permute-start(bf16[4,112,768]{2,1,0:T(8,128)(2,1)S(1)} %get-tuple-element.160), channel_id=1, source_target_pairs={{0,2},{1,3},{2,0},{3,1},{4,6},{5,7},{6,4},{7,5},{8,10},{9,11},{10,... | collective-permute-start | bytes 2064392 | tf_op jit(solution)/shard_map/ppermute | solution.py:667
  304.7 48.1 %collective-permute-start.29 = (bf16[4,112,768]{2,1,0:T(8,128)(2,1)S(1)}, bf16[4,112,768]{2,1,0:T(8,128)(2,1)S(1)}, u32[]{:S(2)}, u32[]{:S(2)}) collective-permute-start(bf16[4,112,768]{2,1,0:T(8,128)(2,1)S(1)} %get-tuple-element.158), channel_id=1, source_target_pairs={{0,4},{4,0},{8,12},{12,8},{16,20},{20,16},{24,28},{28,24},{1,5},{5... | collective-permute-start | bytes 2064392 | tf_op jit(solution)/shard_map/ppermute | solution.py:662
  347.7 23.7 %collective-permute-start.32 = (bf16[2,768,768]{2,1,0:T(8,128)(2,1)}, bf16[2,768,768]{2,1,0:T(8,128)(2,1)S(1)}, u32[]{:S(2)}, u32[]{:S(2)}) collective-permute-start(bf16[2,768,768]{2,1,0:T(8,128)(2,1)} %joint_grads.2.refs_0_), channel_id=1, source_target_pairs={{0,1},{1,0},{2,3},{3,2},{4,5},{5,4},{6,7},{7,6},{8,9},{9,8},{10,11... | collective-permute-start | bytes 7077896 | tf_op jit(solution)/shard_map/ppermute | solution.py:667
  349.6 54.9 %collective-permute-start.46 = (bf16[96,768]{1,0:T(8,128)(2,1)}, bf16[96,768]{1,0:T(8,128)(2,1)}, u32[]{:S(2)}, u32[]{:S(2)}) collective-permute-start(bf16[96,768]{1,0:T(8,128)(2,1)} %fusion.4), channel_id=1, source_target_pairs={{0,2},{1,3},{2,0},{3,1},{4,6},{5,7},{6,4},{7,5},{8,10},{9,11},{10,... | collective-permute-start | bytes 442376 | tf_op jit(solution)/shard_map/ppermute | solution.py:667
  355.0 16.4 %collective-permute-start.33 = (bf16[112,768]{1,0:T(8,128)(2,1)S(1)}, bf16[112,768]{1,0:T(8,128)(2,1)S(1)}, u32[]{:S(2)}, u32[]{:S(2)}) collective-permute-start(bf16[112,768]{1,0:T(8,128)(2,1)S(1)} %get-tuple-element.165), channel_id=1, source_target_pairs={{0,8},{4,12},{8,0},{12,4},{16,24},{20,28},{24,16},{28,20},{1,9},{5... | collective-permute-start | bytes 516104 | tf_op jit(solution)/shard_map/ppermute | solution.py:662
  355.0 16.4 %collective-permute-start.34 = (bf16[112,768]{1,0:T(8,128)(2,1)S(1)}, bf16[112,768]{1,0:T(8,128)(2,1)S(1)}, u32[]{:S(2)}, u32[]{:S(2)}) collective-permute-start(bf16[112,768]{1,0:T(8,128)(2,1)S(1)} %get-tuple-element.166), channel_id=1, source_target_pairs={{0,16},{4,20},{8,24},{12,28},{16,0},{20,4},{24,8},{28,12},{1,17},{... | collective-permute-start | bytes 516104 | tf_op jit(solution)/shard_map/ppermute | solution.py:662
  369.1 35.4 %collective-permute-start.44 = (bf16[112,768]{1,0:T(8,128)(2,1)}, bf16[112,768]{1,0:T(8,128)(2,1)}, u32[]{:S(2)}, u32[]{:S(2)}) collective-permute-start(bf16[112,768]{1,0:T(8,128)(2,1)} %get-tuple-element.191), channel_id=1, source_target_pairs={{0,24},{4,28},{8,16},{12,20},{16,8},{20,12},{24,0},{28,4},{1,25},{... | collective-permute-start | bytes 516104 | tf_op jit(solution)/shard_map/ppermute | solution.py:662
  375.5 19.7 %collective-permute-start.37 = (bf16[4,96,768]{2,1,0:T(8,128)(2,1)S(1)}, bf16[4,96,768]{2,1,0:T(8,128)(2,1)S(1)}, u32[]{:S(2)}, u32[]{:S(2)}) collective-permute-start(bf16[4,96,768]{2,1,0:T(8,128)(2,1)S(1)} %get-tuple-element.176), channel_id=1, source_target_pairs={{0,6},{1,7},{2,4},{3,5},{4,2},{5,3},{6,0},{7,1},{8,14},{9,15},{10,... | collective-permute-start | bytes 1769480 | tf_op jit(solution)/shard_map/ppermute | solution.py:674
  376.8 26.8 %collective-permute-start.36 = (bf16[4,96,768]{2,1,0:T(8,128)(2,1)S(1)}, bf16[4,96,768]{2,1,0:T(8,128)(2,1)S(1)}, u32[]{:S(2)}, u32[]{:S(2)}) collective-permute-start(bf16[4,96,768]{2,1,0:T(8,128)(2,1)S(1)} %get-tuple-element.174), channel_id=1, source_target_pairs={{0,2},{1,3},{2,0},{3,1},{4,6},{5,7},{6,4},{7,5},{8,10},{9,11},{10,... | collective-permute-start | bytes 1769480 | tf_op jit(solution)/shard_map/ppermute | solution.py:667
  378.3 25.3 %collective-permute-start.35 = (bf16[4,96,768]{2,1,0:T(8,128)(2,1)S(1)}, bf16[4,96,768]{2,1,0:T(8,128)(2,1)S(1)}, u32[]{:S(2)}, u32[]{:S(2)}) collective-permute-start(bf16[4,96,768]{2,1,0:T(8,128)(2,1)S(1)} %get-tuple-element.169), channel_id=1, source_target_pairs={{0,4},{4,0},{8,12},{12,8},{16,20},{20,16},{24,28},{28,24},{1,5},{5... | collective-permute-start | bytes 1769480 | tf_op jit(solution)/shard_map/ppermute | solution.py:662
  380.9 22.7 %copy-start.11 = (bf16[4,96,768]{2,1,0:T(8,128)(2,1)S(1)}, bf16[4,96,768]{2,1,0:T(8,128)(2,1)}, u32[]{:S(2)}) copy-start(bf16[4,96,768]{2,1,0:T(8,128)(2,1)} %copy-done.10) | copy-start | bytes 1769476
  406.6 14.7 %collective-permute-start.47 = (bf16[304,768]{1,0:T(8,128)(2,1)S(1)}, bf16[304,768]{1,0:T(8,128)(2,1)S(1)}, u32[]{:S(2)}, u32[]{:S(2)}) collective-permute-start(bf16[304,768]{1,0:T(8,128)(2,1)S(1)} %get-tuple-element.293), channel_id=1, source_target_pairs={{0,2},{1,3},{2,0},{3,1},{4,6},{5,7},{6,4},{7,5},{8,10},{9,11},{10,... | collective-permute-start | bytes 1400840 | tf_op jit(solution)/shard_map/ppermute | solution.py:667
  407.2 7.4 %collective-permute-start.38 = (bf16[96,768]{1,0:T(8,128)(2,1)S(1)}, bf16[96,768]{1,0:T(8,128)(2,1)S(1)}, u32[]{:S(2)}, u32[]{:S(2)}) collective-permute-start(bf16[96,768]{1,0:T(8,128)(2,1)S(1)} %get-tuple-element.179), channel_id=1, source_target_pairs={{0,8},{4,12},{8,0},{12,4},{16,24},{20,28},{24,16},{28,20},{1,9},{5... | collective-permute-start | bytes 442376 | tf_op jit(solution)/shard_map/ppermute | solution.py:662
  407.2 13.9 %collective-permute-start.39 = (bf16[96,768]{1,0:T(8,128)(2,1)S(1)}, bf16[96,768]{1,0:T(8,128)(2,1)S(1)}, u32[]{:S(2)}, u32[]{:S(2)}) collective-permute-start(bf16[96,768]{1,0:T(8,128)(2,1)S(1)} %get-tuple-element.180), channel_id=1, source_target_pairs={{0,16},{4,20},{8,24},{12,28},{16,0},{20,4},{24,8},{28,12},{1,17},{... | collective-permute-start | bytes 442376 | tf_op jit(solution)/shard_map/ppermute | solution.py:662
  409.3 11.8 %collective-permute-start.40 = (bf16[96,768]{1,0:T(8,128)(2,1)S(1)}, bf16[96,768]{1,0:T(8,128)(2,1)S(1)}, u32[]{:S(2)}, u32[]{:S(2)}) collective-permute-start(bf16[96,768]{1,0:T(8,128)(2,1)S(1)} %get-tuple-element.181), channel_id=1, source_target_pairs={{0,24},{4,28},{8,16},{12,20},{16,8},{20,12},{24,0},{28,4},{1,25},{... | collective-permute-start | bytes 442376 | tf_op jit(solution)/shard_map/ppermute | solution.py:662
  421.3 3.7 collective-permute-start.48
  421.6 8.3 %collective-permute-start.41 = (bf16[96,768]{1,0:T(8,128)(2,1)S(1)}, bf16[96,768]{1,0:T(8,128)(2,1)S(1)}, u32[]{:S(2)}, u32[]{:S(2)}) collective-permute-start(bf16[96,768]{1,0:T(8,128)(2,1)S(1)} %add_convert_fusion.2), channel_id=1, source_target_pairs={{0,2},{1,3},{2,0},{3,1},{4,6},{5,7},{6,4},{7,5},{8,10},{9,11},{10,... | collective-permute-start | bytes 442376 | tf_op jit(solution)/shard_map/ppermute | solution.py:667
  429.9 1.6 collective-permute-start.49
  (51 other events, 384.2 us)
Sparse Core Ops, SparseCore 0:
  12.6 106.0 all-gather.4
  121.5 50.1 all-gather.6
